TPU v7x, 32 devices: a whole 2x2x4 slice. The times are simulated.
32 devices in a mesh: parts: 2 (over x), query: 16 (over z, y, core).
Axes of the slice: x: 2, y: 2, z: 4, core: 2. Of those that a mesh axis runs over, the one named last changes fastest.
Arguments:
- train_inputs: bfloat16 [2, 256, 4096], P(None, ('parts', 'query')), parts along dimension 1, may hold values from -6 to 6
- train_outgrads: bfloat16 [2, 256, 12288], P(None, 'parts', 'query'), parts along dimension 1, may hold values from -0.0039978027 to 0.0039978027
- sequence_ids: int32 [256], P('parts'), parts along dimension 0, may hold values from 0 to 3, never falling along the last dimension, each value on 1 to 64 neighbouring positions
- query_inputs: bfloat16 [2, 256, 4096], P(None, 'query'), may hold values from -6 to 6
- query_outgrads: bfloat16 [2, 256, 12288], P(None, None, 'query'), may hold values from -0.0039978027 to 0.0039978027
- eigenvalues: float32 [2, 12288, 4096], P(None, 'query'), may hold values from 0.01 to 10
- input_basis: bfloat16 [64, 128, 128], P('query'), may hold values from -0.5 to 0.5
- slot_list: int32 [64], replicated, may hold values from 0 to 63, as said below
- output_basis: bfloat16 [2, 192, 64, 64], P(None, 'query'), may hold values from -0.75 to 0.75
Outputs:
- scores: float32 [16, 8], P(None, 'parts'), parts along dimension 1
- rotated_inputs: bfloat16 [2, 256, 4096], P(None, ('parts', 'query')), parts along dimension 1
There are 2 independent parts, one for each index of `parts`. A program takes and returns all parts, laid end to end along the dimension named above; an argument that names none is the same for every part. Nothing has to cross between parts.
Inputs may be any that keep to these rules, and one draw needn't show every extreme that they name: `slot_list`: the entries are distinct slots; slot p belongs to device p // 4 of the query axis. Every device holds 4 tiles.
All inputs are finite; a program needn't handle non-finite values.
Results may differ from a plain program's by a relative error of at most 0.0071.
Values may be sent and summed in bfloat16 or wider, within the bound.
No kernel may reach another device: no remote copies, remote signals or barrier semaphores. Data moves between devices by JAX's collectives and lax.ppermute only.
A program may use at most 192 MiB of HBM per device.

v0:
```python
import jax
import jax.numpy as jnp
from jax import lax
from jax.sharding import PartitionSpec as P

D = 4096
LAYERS = 2
TILE_A = 128
TILE_S = 64
SEQS = 4
QUERIES = 16
QLEN = 16


damping = 0.05


def rotate_blocks(rows, block_tiles, width):
    layer_count, row_count, feature_count = rows.shape
    blocks = rows.reshape(layer_count, row_count, feature_count // width, width)
    shaped = block_tiles.reshape(layer_count, feature_count // width, width, width)
    turned = jnp.einsum("lrbi,lbij->lrbj", blocks, shaped, preferred_element_type=jnp.float32)
    return turned.reshape(layer_count, row_count, feature_count).astype(jnp.bfloat16)


def body(
    train_inputs,
    train_outgrads,
    sequence_ids,
    query_inputs,
    query_outgrads,
    eigenvalues,
    input_basis,
    slot_list,
    output_basis,
):
    every_slot = lax.all_gather(input_basis, "query", axis=0, tiled=True)
    basis_tiles = jnp.take(every_slot, slot_list, axis=0)
    rotated_out = rotate_blocks(train_inputs, basis_tiles, TILE_A)
    own_query = rotate_blocks(query_inputs, basis_tiles, TILE_A)
    rotated_train, rotated_query = (
        lax.all_gather(rotated_out, "query", axis=1, tiled=True),
        lax.all_gather(own_query, "query", axis=1, tiled=True),
    )
    grads_rot = rotate_blocks(train_outgrads, output_basis, TILE_S)
    query_rot = rotate_blocks(query_outgrads, output_basis, TILE_S)
    token_count = grads_rot.shape[1]
    slab_width = grads_rot.shape[2]
    weights = 1.0 / (eigenvalues + damping)
    onehot = (sequence_ids[:, None] == jnp.arange(SEQS, dtype=jnp.int32)[None, :]).astype(
        jnp.bfloat16
    )
    totals = jnp.zeros((SEQS, QUERIES * QLEN), jnp.float32)
    for layer_index in range(LAYERS):
        masked = (onehot[:, :, None] * grads_rot[layer_index][:, None, :]).reshape(
            token_count, SEQS * slab_width
        )
        gram_block = lax.dot_general(
            masked,
            rotated_train[layer_index],
            (((0,), (0,)), ((), ())),
            preferred_element_type=jnp.float32,
        )
        scaled = (gram_block.reshape(SEQS, slab_width, D) * weights[layer_index][None]).astype(
            jnp.bfloat16
        )
        projected = jnp.einsum(
            "sij,uj->siu", scaled, rotated_query[layer_index], preferred_element_type=jnp.float32
        )
        totals = totals + jnp.einsum(
            "siu,ui->su", projected, query_rot[layer_index].astype(jnp.float32)
        )
    partial_value = jnp.sum(totals.reshape(SEQS, QUERIES, QLEN), axis=2).T
    scores = lax.psum(partial_value, "query")
    return (scores, rotated_out)


def solution(mesh):
    return jax.shard_map(
        body,
        mesh=mesh,
        in_specs=(
            P(None, ("parts", "query"), None),
            P(None, "parts", "query"),
            P("parts"),
            P(None, "query", None),
            P(None, None, "query"),
            P(None, "query", None),
            P("query", None, None),
            P(),
            P(None, "query", None, None),
        ),
        out_specs=(P(None, "parts"), P(None, ("parts", "query"), None)),
        check_vma=False,
    )
```

profile of v0, /device:TPU:0, one launch (start us, length us, event | category | flops | bytes accessed | tf_op | source)
XLA Modules:
  0.0 223.0 jit_solution(12092274137243276574)
XLA Ops:
  7.2 0.0 copy-start
  7.2 0.0 all-gather.4.cloned.1.call-start
  7.2 0.7 all-gather.4.cloned.1.call-update
  7.9 0.0 all-gather.6.cloned.1.call-start
  8.0 0.7 compare_and_fusion
  8.6 0.1 broadcast_in_dim.18
  8.7 0.7 compare_select_fusion
  9.4 44.9 %all-gather.4.cloned.1.call-done = bf16[64,128,128]{2,1,0:T(8,128)(2,1)} async-done(((bf16[4,128,128]{2,1,0:T(8,128)(2,1)}), bf16[64,128,128]{2,1,0:T(8,128)(2,1)}) %all-gather.4.cloned.1.call-update) | async-done | bytes 2097168 | tf_op jit(solution)/shard_map/all_gather | solution.py:37
  54.3 2.5 %gather_fusion = bf16[64,128,128]{2,1,0:T(8,128)(2,1)S(1)} fusion(bf16[64,128,128]{2,1,0:T(8,128)(2,1)} %all-gather.4.cloned.1.call-done, s32[1024]{0:T(1024)S(1)} %pad_clamp_fusion), kind=kCustom, calls=%fused_computation | custom fusion | bytes 4194560 | tf_op jit(solution)/shard_map/jit(_take)/gather | solution.py:38
  56.9 1.4 fusion.15
  58.3 0.0 all-gather.6.cloned.1.call-update
  58.3 0.0 copy-start.7
  58.3 0.0 all-gather.8.cloned.1.call-start
  58.4 0.7 fusion.13
  59.1 0.8 copy.61
  59.8 0.0 all-gather.8.cloned.1.call-update
  59.9 0.3 copy.32
  60.1 1.2 copy.34
  61.4 0.3 fusion.11
  61.7 0.7 fusion.41
  62.4 0.4 fusion.10
  62.8 0.1 fusion.40
  62.9 1.1 bitcast_convert_fusion
  64.0 17.6 %add_divide_fusion = f32[2,768,4096]{2,1,0:T(8,128)} fusion(f32[2,768,4096]{2,1,0:T(8,128)} %param.14), kind=kLoop, calls=%fused_computation.7 | loop fusion | flops 12582912 | bytes 50331648 | tf_op jit(solution)/shard_map/div | solution.py:49
  81.6 18.5 %slice_bitcast_fusion = (f32[768,4096]{1,0:T(8,128)}, f32[768,4096]{1,0:T(8,128)}) fusion(f32[2,768,4096]{2,1,0:T(8,128)} %add_divide_fusion), kind=kLoop, calls=%fused_computation.10 | loop fusion | bytes 50331648 | tf_op jit(solution)/shard_map/mul | solution.py:64
  100.1 50.1 %all-gather.8.cloned.1.call-done = bf16[2,256,4096]{2,1,0:T(8,128)(2,1)} async-done(((bf16[2,16,4096]{2,1,0:T(8,128)(2,1)}), bf16[2,256,4096]{2,1,0:T(8,128)(2,1)}) %all-gather.8.cloned.1.call-update) | async-done | bytes 4194320 | tf_op jit(solution)/shard_map/all_gather | solution.py:43
  150.2 17.4 %multiply_reduce_fusion.1 = f32[256,4]{0,1:T(4,128)S(1)} fusion(f32[256,768]{0,1:T(8,128)} %get-tuple-element.9, bf16[2,256,4096]{2,1,0:T(8,128)(2,1)} %all-gather.8.cloned.1.call-done, f32[768,4096]{1,0:T(8,128)} %get-tuple-element.3, bf16[2,128,4096]{2,1,0:T(8,128)(2,1)} %all-gather.6.cloned.1.call-done, bf16[128,768]{0,1:T(8,128)(2,1)S(1)} %bitcast.87, ...), kind=kOutput, calls=%fused_computation.13 | convolution fusion | flops 9690807296 | bytes 16716800 | tf_op jit(solution)/shard_map/sij,uj->siu/dot_general | solution.py:67
  167.6 0.0 copy-start.1
  167.6 16.9 %multiply_reduce_fusion = f32[256,4]{0,1:T(4,128)S(1)} fusion(f32[256,768]{0,1:T(8,128)S(1)} %get-tuple-element.8, bf16[2,256,4096]{2,1,0:T(8,128)(2,1)} %all-gather.8.cloned.1.call-done, f32[768,4096]{1,0:T(8,128)} %get-tuple-element.2, bf16[2,128,4096]{2,1,0:T(8,128)(2,1)S(1)} %copy-done.2, bf16[128,768]{0,1:T(8,128)(2,1)S(1)} %bitcast.86, ...), kind=kOutput, calls=%fused_computation.12 | convolution fusion | flops 9690807296 | bytes 16716800 | tf_op jit(solution)/shard_map/sij,uj->siu/dot_general | solution.py:67
  184.6 0.1 reshape.85
  184.6 0.1 reduce_sum.9
  184.7 31.7 %psum.7 = f32[16,4]{0,1:T(4,128)} all-reduce(f32[16,4]{0,1:T(4,128)S(1)} %bitcast.93), channel_id=1, replica_groups=mesh['parts'=2,'query'=16] {'query'}, use_global_device_ids=true, to_apply=%region_1.2 | all-reduce | flops 64 | bytes 512 | tf_op jit(solution)/shard_map/psum | solution.py:74
  (17 shorter events, 0.0 us)
Async XLA Ops:
  7.2 54.2 %copy-start = (bf16[2,12,64,64]{3,2,1,0:T(8,128)(2,1)S(1)}, bf16[2,12,64,64]{3,2,1,0:T(8,128)(2,1)}, u32[]{:S(2)}) copy-start(bf16[2,12,64,64]{3,2,1,0:T(8,128)(2,1)} %param.17) | copy-start | bytes 589828
  7.2 49.7 %copy-start.6 = (bf16[2,8,4096]{2,1,0:T(8,128)(2,1)S(1)}, bf16[2,8,4096]{2,1,0:T(8,128)(2,1)}, u32[]{:S(2)}) copy-start(bf16[2,8,4096]{2,1,0:T(8,128)(2,1)} %param.9) | copy-start | bytes 393220
  7.2 47.1 %all-gather.4.cloned.1.call-start = ((), (), s32[]{:S(2)}) async-start(), calls=%async_computation | async-start | bytes 2228224 | tf_op jit(solution)/shard_map/all_gather | solution.py:37
  7.9 92.2 %all-gather.6.cloned.1.call-start = ((), (), s32[]{:S(2)}) async-start(), calls=%async_computation.1 | async-start | bytes 2228224 | tf_op jit(solution)/shard_map/all_gather | solution.py:42
  9.4 49.0 %copy-start.5 = (bf16[2,16,4096]{2,1,0:T(8,128)(2,1)S(1)}, bf16[2,16,4096]{2,1,0:T(8,128)(2,1)}, u32[]{:S(2)}) copy-start(bf16[2,16,4096]{2,1,0:T(8,128)(2,1)} %param.12) | copy-start | bytes 786436
  58.3 1.6 copy-start.4
  58.3 3.1 %copy-start.7 = (s32[128]{0:T(128)S(1)}, s32[128]{0:T(128)}, u32[]{:S(2)}) copy-start(s32[128]{0:T(128)} %param.11) | copy-start | bytes 1540
  58.3 91.9 %all-gather.8.cloned.1.call-start = ((), (), s32[]{:S(2)}) async-start(), calls=%async_computation.2 | async-start | bytes 4456448 | tf_op jit(solution)/shard_map/all_gather | solution.py:43
  81.6 68.6 %copy-start.3 = (bf16[1,128,12,64]{1,3,2,0:T(8,128)(2,1)S(1)}, bf16[1,128,12,64]{1,3,2,0:T(8,128)(2,1)}, u32[]{:S(2)}) copy-start(bf16[1,128,12,64]{1,3,2,0:T(8,128)(2,1)} %get-tuple-element.7) | copy-start | bytes 589828
  150.2 17.4 %copy-start.2 = (bf16[2,128,4096]{2,1,0:T(8,128)(2,1)S(1)}, bf16[2,128,4096]{2,1,0:T(8,128)(2,1)}, u32[]{:S(2)}) copy-start(bf16[2,128,4096]{2,1,0:T(8,128)(2,1)} %all-gather.6.cloned.1.call-done) | copy-start | bytes 6291460
  167.6 48.8 %copy-start.1 = (bf16[2,12,64,64]{3,2,1,0:T(8,128)(2,1)S(1)}, bf16[2,12,64,64]{3,2,1,0:T(8,128)(2,1)}, u32[]{:S(2)}) copy-start(bf16[2,12,64,64]{3,2,1,0:T(8,128)(2,1)} %param.17) | copy-start | bytes 589828
Sparse Core Ops, SparseCore 0:
  10.2 44.0 all-gather.3
  58.4 40.1 all-gather.5
  100.8 49.3 all-gather.7
where the time goes:
time: 223 us
  waiting for transfers between devices  95.8 us (43%)
  matrix products  37.1 us (17%)
  blocking collectives  31.7 us (14%)
  local copies, waits for them, and re-layouts  24.2 us (11%)
  other arithmetic  20.1 us (9%)
  between operations  13.9 us (6%)
    all_gather x1, waiting for transfers between devices, body(): lax.all_gather(own_query, 'query', axis=1, tiled=True)  50.1 us
    all_gather x1, waiting for transfers between devices, body(): every_slot = lax.all_gather(input_basis, 'query', axis=0, tiled=True)  44.9 us
    dot_general x2, matrix products, body(): jnp.einsum('sij,uj->siu', scaled, rotated_query[layer_index], preferred_e...  34.3 us
    psum x1, blocking collectives, body(): scores = lax.psum(partial_value, 'query')  31.7 us
    mul x1, local copies, waits for them, and re-layouts, body(): gram_block.reshape(SEQS, slab_width, D) * weights[layer_index][None]  18.5 us
    div x1, other arithmetic, body(): weights = 1.0 / (eigenvalues + damping)  17.6 us
  transfers between devices with their start and end apart: 3, of which 2 were waited for; matrix products, arithmetic and copies ran while one was open for 19% of the time, Pallas kernels for 0%

commit v1 on v0

--- a/solution.py
+++ b/solution.py
@@ -1,6 +1,8 @@
 import jax
 import jax.numpy as jnp
 from jax import lax
+from jax.experimental import pallas as pl
+from jax.experimental.pallas import tpu as pltpu
 from jax.sharding import PartitionSpec as P
 
 D = 4096
@@ -23,7 +25,7 @@
     return turned.reshape(layer_count, row_count, feature_count).astype(jnp.bfloat16)
 
 
-def body(
+def general_body(
     train_inputs,
     train_outgrads,
     sequence_ids,
@@ -75,9 +77,195 @@
     return (scores, rotated_out)
 
 
+NQ = 16
+HALF = 32
+UNIT = 40
+SWAP = [(0, 1), (1, 0)]
+
+
+def hop(value, bits):
+    return lax.ppermute(value, "query", [(i, i ^ bits) for i in range(NQ)])
+
+
+def score_kernel(info, *refs):
+    units = refs[:NQ]
+    grads, query_grads, codes, eigen, totals, own_rows, held, rows, acc, sems = refs[NQ:]
+    step = pl.program_id(0)
+    me = info[0]
+
+    @pl.when(step == 0)
+    def _():
+        copies = [
+            pltpu.make_async_copy(units[d], held.at[me ^ d], sems.at[d]) for d in range(NQ)
+        ]
+        for copy in copies:
+            copy.start()
+        acc[...] = jnp.zeros_like(acc)
+        for copy in copies:
+            copy.wait()
+
+    layer = info[1 + step]
+    owner = step // 2
+    slot = step % 2
+    basis = held[owner, pl.ds(HALF + 4 * slot, 4)].reshape(TILE_A, TILE_A)
+    tile = held[:, step]
+    train = tile[:, :16].reshape(256, TILE_A)
+    query = tile[:, 16:].reshape(256, TILE_A)
+    turned = jnp.dot(train, basis, preferred_element_type=jnp.float32)
+    rows[...] = turned.astype(jnp.bfloat16)
+    own_rows[0] = rows[pl.ds(pl.multiple_of(me * 16, 16), 16), :]
+    train_t = turned.T.astype(jnp.bfloat16)
+    query_t = (
+        jnp.dot(query, basis, preferred_element_type=jnp.float32).T.astype(jnp.bfloat16)
+    ).astype(jnp.float32)
+    weights = 1.0 / (eigen[0].T + damping)
+    code = codes[...]
+    zero = jnp.zeros_like(train_t)
+    left = jnp.concatenate(
+        [jnp.where(code == s, train_t, zero) for s in range(2 * SEQS)], axis=0
+    )
+    projected = None
+    for c in range(3):
+        cols = pl.ds(c * 256, 256)
+        gram = jnp.dot(left, grads[layer, :, cols], preferred_element_type=jnp.float32)
+        w = weights[:, c * 256 : (c + 1) * 256]
+        scaled = (gram.reshape(2 * SEQS, TILE_A, 256) * w[None]).astype(jnp.bfloat16)
+        term = jnp.dot(
+            scaled.reshape(2 * SEQS * TILE_A, 256),
+            query_grads[layer, cols, :],
+            preferred_element_type=jnp.float32,
+        )
+        projected = term if projected is None else projected + term
+    product = projected.reshape(2 * SEQS, TILE_A, 256) * query_t[None]
+    acc[...] += jnp.sum(product.reshape(2 * SEQS, TILE_A // 8, 8, 256), axis=1)
+
+    @pl.when(step == pl.num_programs(0) - 1)
+    def _():
+        totals[...] = jnp.sum(acc[...], axis=1)
+
+
+def paired_body(
+    train_inputs,
+    train_outgrads,
+    sequence_ids,
+    query_inputs,
+    query_outgrads,
+    eigenvalues,
+    input_basis,
+    slot_list,
+    output_basis,
+):
+    x = lax.axis_index("parts")
+    me = lax.axis_index("query")
+    ids = jnp.arange(64, dtype=jnp.int32)
+    tile_of = jnp.sum(jnp.where(slot_list[None, :] == ids[:, None], ids[None, :], 0), axis=1)
+    by_half = tile_of.reshape(NQ, 2, 2)
+    mine = lax.dynamic_index_in_dim(by_half, x, 1, False).reshape(HALF)
+    theirs = lax.dynamic_index_in_dim(by_half, 1 - x, 1, False).reshape(HALF)
+
+    def tiles(rows):
+        return rows.reshape(LAYERS, rows.shape[1], 32, TILE_A).transpose(0, 2, 1, 3).reshape(
+            64, rows.shape[1], TILE_A
+        )
+
+    train_tiles = tiles(train_inputs)
+    train_mine = jnp.take(train_tiles, mine, axis=0, mode="clip")
+    train_theirs = jnp.take(train_tiles, theirs, axis=0, mode="clip")
+    train_other = lax.ppermute(train_theirs, "parts", SWAP)
+    query_mine = jnp.take(tiles(query_inputs), mine, axis=0, mode="clip")
+    first = jnp.where(x == 0, train_mine, train_other)
+    second = jnp.where(x == 0, train_other, train_mine)
+    basis_mine = lax.dynamic_slice_in_dim(input_basis, 2 * x, 2, 0).reshape(8, 32, TILE_A)
+    unit = jnp.concatenate(
+        [jnp.concatenate([first, second, query_mine], axis=1), basis_mine], axis=0
+    )
+    units = [None] * NQ
+    units[0] = unit
+    for d in (4, 12, 8):
+        units[d] = hop(unit, d)
+    for d in (0, 4, 12, 8):
+        units[d ^ 2] = hop(units[d], 2)
+    for d in (0, 2, 4, 6, 12, 14, 8, 10):
+        units[d ^ 1] = hop(units[d], 1)
+
+    id_block = jnp.broadcast_to(
+        sequence_ids.astype(jnp.bfloat16)[None, :, None], (LAYERS, 128, TILE_A)
+    )
+    sent = jnp.concatenate([train_outgrads, id_block], axis=2)
+    other = lax.ppermute(sent, "parts", SWAP)
+    both = jnp.stack(
+        [jnp.where(x == 0, sent, other), jnp.where(x == 0, other, sent)], axis=0
+    ).reshape(2, LAYERS, NQ, 8, 896)
+    both = both.transpose(1, 2, 0, 3, 4).reshape(LAYERS, 256, 896)
+    part_of = (jnp.arange(256, dtype=jnp.int32) // 8) % 2
+    codes = (both[0, :, 768].astype(jnp.int32) + SEQS * part_of).reshape(1, 256)
+    grads_rot = rotate_blocks(both[:, :, :768], output_basis, TILE_S)
+    query_rot = rotate_blocks(query_outgrads, output_basis, TILE_S).transpose(0, 2, 1)
+
+    info = jnp.concatenate([me.reshape(1).astype(jnp.int32), mine // 32, mine % 32])
+    any_spec = pl.BlockSpec(memory_space=pl.ANY)
+
+    def whole(shape):
+        return pl.BlockSpec(shape, lambda n, s: (0,) * len(shape))
+
+    totals, own_rows = pl.pallas_call(
+        score_kernel,
+        grid_spec=pltpu.PrefetchScalarGridSpec(
+            num_scalar_prefetch=1,
+            grid=(HALF,),
+            in_specs=[any_spec] * NQ
+            + [
+                whole((LAYERS, 256, 768)),
+                whole((LAYERS, 768, 256)),
+                whole((1, 256)),
+                pl.BlockSpec((1, 768, TILE_A), lambda n, s: (s[1 + n], 0, s[1 + HALF + n])),
+            ],
+            out_specs=[
+                whole((2 * SEQS, 256)),
+                pl.BlockSpec((1, 16, TILE_A), lambda n, s: (n, 0, 0)),
+            ],
+            scratch_shapes=[
+                pltpu.VMEM((NQ, UNIT, 32, TILE_A), jnp.bfloat16),
+                pltpu.VMEM((256, TILE_A), jnp.bfloat16),
+                pltpu.VMEM((2 * SEQS, 8, 256), jnp.float32),
+                pltpu.SemaphoreType.DMA((NQ,)),
+            ],
+        ),
+        out_shape=[
+            jax.ShapeDtypeStruct((2 * SEQS, 256), jnp.float32),
+            jax.ShapeDtypeStruct((HALF, 16, TILE_A), jnp.bfloat16),
+        ],
+        compiler_params=pltpu.CompilerParams(vmem_limit_bytes=40 * 1024 * 1024),
+        cost_estimate=pl.CostEstimate(
+            flops=26 * 10**9, bytes_accessed=19 * 10**6, transcendentals=0
+        ),
+    )(info, *units, grads_rot, query_rot, codes, eigenvalues)
+
+    halves = totals.reshape(2, SEQS, 256)
+    keep = lax.dynamic_index_in_dim(halves, x, 0, False)
+    give = lax.dynamic_index_in_dim(halves, 1 - x, 0, False)
+    total = keep + lax.ppermute(give, "parts", SWAP)
+    for bits in (1, 2, 4, 8):
+        total = total + hop(total, bits)
+    scores = jnp.sum(total.reshape(SEQS, QUERIES, QLEN), axis=2).T
+
+    pair = own_rows.reshape(HALF, 2, 8, TILE_A)
+    kept = lax.dynamic_index_in_dim(pair, x, 1, False)
+    came = lax.ppermute(lax.dynamic_index_in_dim(pair, 1 - x, 1, False), "parts", SWAP)
+    low = jnp.where(x == 0, kept, came).reshape(NQ, 1, 2, 8, TILE_A)
+    high = jnp.where(x == 0, came, kept).reshape(NQ, 1, 2, 8, TILE_A)
+    by_slot = jnp.concatenate([low, high], axis=1).reshape(64, 8, TILE_A)
+    ordered = jnp.take(by_slot, slot_list, axis=0, mode="clip")
+    rotated_out = (
+        ordered.reshape(LAYERS, 32, 8, TILE_A).transpose(0, 2, 1, 3).reshape(LAYERS, 8, D)
+    )
+    return (scores, rotated_out)
+
+
 def solution(mesh):
+    paired = mesh.shape["parts"] == 2 and mesh.shape["query"] == NQ
     return jax.shard_map(
-        body,
+        paired_body if paired else general_body,
         mesh=mesh,
         in_specs=(
             P(None, ("parts", "query"), None),

time: 223 us -> 139 us (0.62)
  waiting for transfers between devices: 95.8 us -> 35.9 us
  Pallas kernels: 0 us -> 55.2 us
  matrix products: 37.1 us -> 2.9 us
  blocking collectives: 31.7 us -> 0 us
  starting transfers between devices: 0.12 us -> 24.3 us
  other arithmetic: 20.1 us -> 5.63 us
  between operations: 13.9 us -> 0.98 us
  local copies, waits for them, and re-layouts: 24.2 us -> 13.7 us
    all_gather x3 -> x0, waiting for transfers between devices: 95.1 us -> none  [the longest x1 50.1 us: body(): lax.all_gather(own_query, 'query', axis=1, tiled=True)]
    pallas_call x0 -> x1, Pallas kernels: none -> 55.2 us  [paired_body(): pl.pallas_call(score_kernel, grid_spec=pltpu.PrefetchScalarGridSpec(num_s...]
    ppermute x0 -> x23, waiting for transfers between devices: none -> 35.9 us  [the longest x19 33.8 us: hop(): return lax.ppermute(value, 'query', [(i, i ^ bits) for i in range(NQ)])]
    dot_general x2 -> x0, matrix products: 34.3 us -> none  [body(): jnp.einsum('sij,uj->siu', scaled, rotated_query[layer_index], preferred_e...]
    psum x1 -> x0, blocking collectives: 31.7 us -> none  [body(): scores = lax.psum(partial_value, 'query')]
    ppermute x0 -> x23, starting transfers between devices: none -> 24.3 us  [the longest x19 18.2 us: hop(): return lax.ppermute(value, 'query', [(i, i ^ bits) for i in range(NQ)])]
    mul x1 -> x0, local copies, waits for them, and re-layouts: 18.5 us -> none  [body(): gram_block.reshape(SEQS, slab_width, D) * weights[layer_index][None]]
    div x1 -> x0, other arithmetic: 17.6 us -> none  [body(): weights = 1.0 / (eigenvalues + damping)]
  transfers between devices with their start and end apart: 3 -> 23, of which waited for: 2 -> 10; matrix products, arithmetic and copies ran while one was open for 19% -> 10% of each run, Pallas kernels for 0% -> 0%
where the time goes in v1:
time: 139 us
  Pallas kernels  55.2 us (40%)
  waiting for transfers between devices  35.9 us (26%)
  starting transfers between devices  24.3 us (17%)
  local copies, waits for them, and re-layouts  13.7 us (10%)
  other arithmetic  5.63 us (4%)
  matrix products  2.9 us (2%)
    pallas_call x1, Pallas kernels, paired_body(): pl.pallas_call(score_kernel, grid_spec=pltpu.PrefetchScalarGridSpec(num_s...  55.2 us
    ppermute x19, waiting for transfers between devices, hop(): return lax.ppermute(value, 'query', [(i, i ^ bits) for i in range(NQ)])  33.8 us
    ppermute x19, starting transfers between devices, hop(): return lax.ppermute(value, 'query', [(i, i ^ bits) for i in range(NQ)])  18.2 us
    unnamed x22, local copies, waits for them, and re-layouts  5.44 us
    ppermute x1, starting transfers between devices, paired_body(): train_other = lax.ppermute(train_theirs, 'parts', SWAP)  3 us
    dot_general x2, matrix products, rotate_blocks(): jnp.einsum('lrbi,lbij->lrbj', blocks, shaped, preferred_element_type=jnp....  2.9 us
  transfers between devices with their start and end apart: 23, of which 10 were waited for; matrix products, arithmetic and copies ran while one was open for 10% of the time, Pallas kernels for 0%

profile of v1, /device:TPU:0, one launch (start us, length us, event | category | flops | bytes accessed | tf_op | source)
XLA Modules:
  0.0 138.6 jit_solution(3642780418801620636)
XLA Ops:
  1.8 1.5 %gather_fusion.1 = bf16[32,8,128]{2,1,0:T(8,128)(2,1)S(1)} fusion(bf16[64,8,128]{2,1,0:T(8,128)(2,1)} %bitcast.80, s32[1024]{0:T(1024)S(1)} %pad_clamp_fusion.1), kind=kCustom, calls=%fused_computation.1 | custom fusion | bytes 131200 | tf_op jit(solution)/shard_map/jit(_take)/gather | solution.py:173
  3.3 3.0 %collective-permute-start = (bf16[32,8,128]{2,1,0:T(8,128)(2,1)S(1)}, bf16[32,8,128]{2,1,0:T(8,128)(2,1)S(1)}, u32[]{:S(2)}, u32[]{:S(2)}) collective-permute-start(bf16[32,8,128]{2,1,0:T(8,128)(2,1)S(1)} %gather_fusion.1), channel_id=1, source_target_pairs={{0,16},{16,0},{1,17},{17,1},{2,18},{18,2},{3,19},{19,3},{4,20},{20... | collective-permute-start | bytes 196616 | tf_op jit(solution)/shard_map/ppermute | solution.py:174
  7.0 1.0 pad_maximum_fusion.1
  8.3 1.5 %gather_fusion = bf16[32,8,128]{2,1,0:T(8,128)(2,1)S(1)} fusion(bf16[64,8,128]{2,1,0:T(8,128)(2,1)} %bitcast.81, s32[1024]{0:T(1024)S(1)} %pad_clamp_fusion.2), kind=kCustom, calls=%fused_computation | custom fusion | bytes 131200 | tf_op jit(solution)/shard_map/jit(_take)/gather | solution.py:172
  9.8 1.0 copy.51
  11.7 4.1 %collective-permute-start.12 = (bf16[40,32,128]{2,1,0:T(8,128)(2,1)S(1)}, bf16[40,32,128]{2,1,0:T(8,128)(2,1)S(1)}, u32[]{:S(2)}, u32[]{:S(2)}) collective-permute-start(bf16[40,32,128]{2,1,0:T(8,128)(2,1)S(1)} %pad_maximum_fusion.2.refs_0_), channel_id=1, source_target_pairs={{0,12},{1,13},{2,14},{3,15},{4,8},{5,9},{6,10},{7,11},{8,4},{9,5},... | collective-permute-start | bytes 983048 | tf_op jit(solution)/shard_map/ppermute | solution.py:87
  17.2 1.7 %collective-permute-start.2 = (bf16[40,32,128]{2,1,0:T(8,128)(2,1)S(1)}, bf16[40,32,128]{2,1,0:T(8,128)(2,1)S(1)}, u32[]{:S(2)}, u32[]{:S(2)}) collective-permute-start(bf16[40,32,128]{2,1,0:T(8,128)(2,1)S(1)} %pad_maximum_fusion.2.refs_0_), channel_id=1, source_target_pairs={{0,2},{1,3},{2,0},{3,1},{4,6},{5,7},{6,4},{7,5},{8,10},{9,11},{10,... | collective-permute-start | bytes 983048 | tf_op jit(solution)/shard_map/ppermute | solution.py:87
  18.9 5.6 %collective-permute-done.12.refs_12_ = bf16[40,32,128]{2,1,0:T(8,128)(2,1)S(1)} collective-permute-done((bf16[40,32,128]{2,1,0:T(8,128)(2,1)S(1)}, bf16[40,32,128]{2,1,0:T(8,128)(2,1)S(1)}, u32[]{:S(2)}, u32[]{:S(2)}) %collective-permute-start.12) | collective-permute-done | bytes 327712 | tf_op jit(solution)/shard_map/ppermute | solution.py:87
  24.6 1.8 %collective-permute-start.14 = (bf16[40,32,128]{2,1,0:T(8,128)(2,1)S(1)}, bf16[40,32,128]{2,1,0:T(8,128)(2,1)}, u32[]{:S(2)}, u32[]{:S(2)}) collective-permute-start(bf16[40,32,128]{2,1,0:T(8,128)(2,1)S(1)} %collective-permute-done.12.refs_12_), channel_id=1, source_target_pairs={{0,2},{1,3},{2,0},{3,1},{4,6},{5,7},{6,4},{7,5},{8,10},{9,11},{10,... | collective-permute-start | bytes 983048 | tf_op jit(solution)/shard_map/ppermute | solution.py:87
  26.4 1.2 select_bitcast_fusion.1
  27.5 15.6 %collective-permute-done.8.refs_8_ = bf16[40,32,128]{2,1,0:T(8,128)(2,1)S(1)} collective-permute-done((bf16[40,32,128]{2,1,0:T(8,128)(2,1)S(1)}, bf16[40,32,128]{2,1,0:T(8,128)(2,1)S(1)}, u32[]{:S(2)}, u32[]{:S(2)}) %collective-permute-start.8) | collective-permute-done | bytes 327712 | tf_op jit(solution)/shard_map/ppermute | solution.py:87
  43.2 1.5 %collective-permute-start.10 = (bf16[40,32,128]{2,1,0:T(8,128)(2,1)S(1)}, bf16[40,32,128]{2,1,0:T(8,128)(2,1)}, u32[]{:S(2)}, u32[]{:S(2)}) collective-permute-start(bf16[40,32,128]{2,1,0:T(8,128)(2,1)S(1)} %collective-permute-done.8.refs_8_), channel_id=1, source_target_pairs={{0,2},{1,3},{2,0},{3,1},{4,6},{5,7},{6,4},{7,5},{8,10},{9,11},{10,... | collective-permute-start | bytes 983048 | tf_op jit(solution)/shard_map/ppermute | solution.py:87
  46.8 0.9 copy-done.5
  47.8 1.2 copy.38
  49.0 2.5 %convolution_convert_fusion.1 = bf16[2,12,256,64]{2,3,1,0:T(8,128)(2,1)} fusion(bf16[2,256,12,64]{1,3,2,0:T(8,128)(2,1)} %bitcast.70, bf16[2,12,64,64]{3,2,1,0:T(8,128)(2,1)S(1)} %copy-done), kind=kOutput, calls=%fused_computation.5 | convolution fusion | flops 50724864 | bytes 1769472 | tf_op jit(solution)/shard_map/lrbi,lbij->lrbj/dot_general | solution.py:24
  51.5 1.4 %copy.42.refs_16_ = bf16[2,256,768]{2,1,0:T(8,128)(2,1)S(1)} copy(bf16[2,256,768]{1,2,0:T(8,128)(2,1)} %bitcast.71) | data formatting | bytes 1572864 | tf_op jit(solution)/shard_map/convert_element_type | solution.py:25
  54.3 6.1 %collective-permute-done.6.refs_6_ = bf16[40,32,128]{2,1,0:T(8,128)(2,1)} collective-permute-done((bf16[40,32,128]{2,1,0:T(8,128)(2,1)S(1)}, bf16[40,32,128]{2,1,0:T(8,128)(2,1)}, u32[]{:S(2)}, u32[]{:S(2)}) %collective-permute-start.6) | collective-permute-done | bytes 327712 | tf_op jit(solution)/shard_map/ppermute | solution.py:87
  60.4 1.0 convert_reduce_fusion
  61.4 0.8 collective-permute-done.7.refs_7_
  62.3 1.0 copy-done.2
  63.2 1.0 copy-done.4
  64.2 55.2 %shard_map.104 = (f32[8,256]{1,0:T(8,128)S(1)}, bf16[32,16,128]{2,1,0:T(8,128)(2,1)S(1)}) custom-call(s32[65]{0:T(128)S(1)} %pad_add_fusion.info, bf16[40,32,128]{2,1,0:T(8,128)(2,1)S(1)} %pad_maximum_fusion.2.refs_0_, bf16[40,32,128]{2,1,0:T(8,128)(2,1)S(1)} %copy-done.4, bf16[40,32,128]{2,1,0:T(8,128)(2,1)S(1)} %copy-done.2, ...), custom_call_target="tpu_custom_call" | custom-call | flops 25999998976 | bytes 19000000 | tf_op jit(solution)/shard_map/pallas_call | solution.py:211
  119.5 1.6 %collective-permute-start.17 = (f32[4,256]{1,0:T(4,128)S(1)}, f32[4,256]{1,0:T(4,128)S(1)}, u32[]{:S(2)}, u32[]{:S(2)}) collective-permute-start(f32[4,256]{1,0:T(4,128)S(1)} %dynamic-slice_bitcast_fusion.1), channel_id=1, source_target_pairs={{0,16},{16,0},{1,17},{17,1},{2,18},{18,2},{3,19},{19,3},{4,20},{20... | collective-permute-start | bytes 12296 | tf_op jit(solution)/shard_map/ppermute | solution.py:247
  121.0 2.1 %collective-permute-done.17 = f32[4,256]{1,0:T(4,128)S(1)} collective-permute-done((f32[4,256]{1,0:T(4,128)S(1)}, f32[4,256]{1,0:T(4,128)S(1)}, u32[]{:S(2)}, u32[]{:S(2)}) %collective-permute-start.17) | collective-permute-done | bytes 4128 | tf_op jit(solution)/shard_map/ppermute | solution.py:247
  123.2 1.2 collective-permute-done.18
  124.3 1.5 %collective-permute-start.19 = (f32[4,256]{1,0:T(4,128)S(1)}, f32[4,256]{1,0:T(4,128)S(1)}, u32[]{:S(2)}, u32[]{:S(2)}) collective-permute-start(f32[4,256]{1,0:T(4,128)S(1)} %add.77), channel_id=1, source_target_pairs={{0,2},{1,3},{2,0},{3,1},{4,6},{5,7},{6,4},{7,5},{8,10},{9,11},{10,... | collective-permute-start | bytes 12296 | tf_op jit(solution)/shard_map/ppermute | solution.py:87
  125.9 2.1 %collective-permute-done.19 = f32[4,256]{1,0:T(4,128)S(1)} collective-permute-done((f32[4,256]{1,0:T(4,128)S(1)}, f32[4,256]{1,0:T(4,128)S(1)}, u32[]{:S(2)}, u32[]{:S(2)}) %collective-permute-start.19) | collective-permute-done | bytes 4128 | tf_op jit(solution)/shard_map/ppermute | solution.py:87
  127.9 1.7 %collective-permute-start.20 = (f32[4,256]{1,0:T(4,128)S(1)}, f32[4,256]{1,0:T(4,128)S(1)}, u32[]{:S(2)}, u32[]{:S(2)}) collective-permute-start(f32[4,256]{1,0:T(4,128)S(1)} %add.78), channel_id=1, source_target_pairs={{0,4},{1,5},{2,6},{3,7},{4,0},{5,1},{6,2},{7,3},{8,12},{9,13},{10,... | collective-permute-start | bytes 12296 | tf_op jit(solution)/shard_map/ppermute | solution.py:87
  129.6 1.5 %collective-permute-start.22 = (bf16[32,8,128]{2,1,0:T(8,128)(2,1)S(1)}, bf16[32,8,128]{2,1,0:T(8,128)(2,1)S(1)}, u32[]{:S(2)}, u32[]{:S(2)}) collective-permute-start(bf16[32,8,128]{2,1,0:T(8,128)(2,1)S(1)} %dynamic-slice_bitcast_fusion), channel_id=1, source_target_pairs={{0,16},{16,0},{1,17},{17,1},{2,18},{18,2},{3,19},{19,3},{4,20},{20... | collective-permute-start | bytes 196616 | tf_op jit(solution)/shard_map/ppermute | solution.py:254
  131.6 3.4 %collective-permute-start.21 = (f32[4,256]{1,0:T(4,128)S(1)}, f32[4,256]{1,0:T(4,128)S(1)}, u32[]{:S(2)}, u32[]{:S(2)}) collective-permute-start(f32[4,256]{1,0:T(4,128)S(1)} %add.79), channel_id=1, source_target_pairs={{0,8},{1,9},{2,10},{3,11},{4,12},{5,13},{6,14},{7,15},{8,0},{9,1},... | collective-permute-start | bytes 12296 | tf_op jit(solution)/shard_map/ppermute | solution.py:87
  135.0 1.6 %collective-permute-done.21 = f32[4,256]{1,0:T(4,128)S(1)} collective-permute-done((f32[4,256]{1,0:T(4,128)S(1)}, f32[4,256]{1,0:T(4,128)S(1)}, u32[]{:S(2)}, u32[]{:S(2)}) %collective-permute-start.21) | collective-permute-done | bytes 4128 | tf_op jit(solution)/shard_map/ppermute | solution.py:87
  137.4 1.3 gather_fusion.3
  (80 shorter events, 9.1 us)
Async XLA Ops:
  0.6 15.5 %copy-start = (bf16[2,12,64,64]{3,2,1,0:T(8,128)(2,1)S(1)}, bf16[2,12,64,64]{3,2,1,0:T(8,128)(2,1)}, u32[]{:S(2)}) copy-start(bf16[2,12,64,64]{3,2,1,0:T(8,128)(2,1)} %param.17) | copy-start | bytes 589828
  1.7 9.9 %copy-start.8 = (bf16[4,128,128]{2,1,0:T(8,128)(2,1)S(1)}, bf16[4,128,128]{2,1,0:T(8,128)(2,1)}, u32[]{:S(2)}) copy-start(bf16[4,128,128]{2,1,0:T(8,128)(2,1)} %param.15) | copy-start | bytes 393220
  3.3 8.3 %collective-permute-start = (bf16[32,8,128]{2,1,0:T(8,128)(2,1)S(1)}, bf16[32,8,128]{2,1,0:T(8,128)(2,1)S(1)}, u32[]{:S(2)}, u32[]{:S(2)}) collective-permute-start(bf16[32,8,128]{2,1,0:T(8,128)(2,1)S(1)} %gather_fusion.1), channel_id=1, source_target_pairs={{0,16},{16,0},{1,17},{17,1},{2,18},{18,2},{3,19},{19,3},{4,20},{20... | collective-permute-start | bytes 196616 | tf_op jit(solution)/shard_map/ppermute | solution.py:174
  8.1 7.7 %copy-start.7 = (bf16[2,256,768]{2,1,0:T(8,128)(2,1)S(1)}, bf16[2,256,768]{2,1,0:T(8,128)(2,1)}, u32[]{:S(2)}) copy-start(bf16[2,256,768]{2,1,0:T(8,128)(2,1)} %param.13) | copy-start | bytes 2359300
  8.1 16.5 %collective-permute-start.16 = (bf16[2,128,896]{2,1,0:T(8,128)(2,1)S(1)}, bf16[2,128,896]{2,1,0:T(8,128)(2,1)}, u32[]{:S(2)}, u32[]{:S(2)}) collective-permute-start(bf16[2,128,896]{2,1,0:T(8,128)(2,1)S(1)} %pad_maximum_fusion.1), channel_id=1, source_target_pairs={{0,16},{16,0},{1,17},{17,1},{2,18},{18,2},{3,19},{19,3},{4,20},{20... | collective-permute-start | bytes 1376264 | tf_op jit(solution)/shard_map/ppermute | solution.py:195
  11.7 12.9 %collective-permute-start.12 = (bf16[40,32,128]{2,1,0:T(8,128)(2,1)S(1)}, bf16[40,32,128]{2,1,0:T(8,128)(2,1)S(1)}, u32[]{:S(2)}, u32[]{:S(2)}) collective-permute-start(bf16[40,32,128]{2,1,0:T(8,128)(2,1)S(1)} %pad_maximum_fusion.2.refs_0_), channel_id=1, source_target_pairs={{0,12},{1,13},{2,14},{3,15},{4,8},{5,9},{6,10},{7,11},{8,4},{9,5},... | collective-permute-start | bytes 983048 | tf_op jit(solution)/shard_map/ppermute | solution.py:87
  15.8 10.5 %copy-start.6 = (bf16[2,128,768]{2,1,0:T(8,128)(2,1)S(1)}, bf16[2,128,768]{2,1,0:T(8,128)(2,1)}, u32[]{:S(2)}) copy-start(bf16[2,128,768]{2,1,0:T(8,128)(2,1)} %param.10) | copy-start | bytes 1179652
  16.5 26.6 %collective-permute-start.8 = (bf16[40,32,128]{2,1,0:T(8,128)(2,1)S(1)}, bf16[40,32,128]{2,1,0:T(8,128)(2,1)S(1)}, u32[]{:S(2)}, u32[]{:S(2)}) collective-permute-start(bf16[40,32,128]{2,1,0:T(8,128)(2,1)S(1)} %pad_maximum_fusion.2.refs_0_), channel_id=1, source_target_pairs={{0,8},{1,9},{2,10},{3,11},{4,12},{5,13},{6,14},{7,15},{8,0},{9,1},... | collective-permute-start | bytes 983048 | tf_op jit(solution)/shard_map/ppermute | solution.py:87
  16.6 26.6 %collective-permute-start.4 = (bf16[40,32,128]{2,1,0:T(8,128)(2,1)S(1)}, bf16[40,32,128]{2,1,0:T(8,128)(2,1)S(1)}, u32[]{:S(2)}, u32[]{:S(2)}) collective-permute-start(bf16[40,32,128]{2,1,0:T(8,128)(2,1)S(1)} %pad_maximum_fusion.2.refs_0_), channel_id=1, source_target_pairs={{0,4},{1,5},{2,6},{3,7},{4,0},{5,1},{6,2},{7,3},{8,12},{9,13},{10,... | collective-permute-start | bytes 983048 | tf_op jit(solution)/shard_map/ppermute | solution.py:87
  17.2 27.5 %collective-permute-start.2 = (bf16[40,32,128]{2,1,0:T(8,128)(2,1)S(1)}, bf16[40,32,128]{2,1,0:T(8,128)(2,1)S(1)}, u32[]{:S(2)}, u32[]{:S(2)}) collective-permute-start(bf16[40,32,128]{2,1,0:T(8,128)(2,1)S(1)} %pad_maximum_fusion.2.refs_0_), channel_id=1, source_target_pairs={{0,2},{1,3},{2,0},{3,1},{4,6},{5,7},{6,4},{7,5},{8,10},{9,11},{10,... | collective-permute-start | bytes 983048 | tf_op jit(solution)/shard_map/ppermute | solution.py:87
  24.5 20.4 %collective-permute-start.1 = (bf16[40,32,128]{2,1,0:T(8,128)(2,1)S(1)}, bf16[40,32,128]{2,1,0:T(8,128)(2,1)S(1)}, u32[]{:S(2)}, u32[]{:S(2)}) collective-permute-start(bf16[40,32,128]{2,1,0:T(8,128)(2,1)S(1)} %pad_maximum_fusion.2.refs_0_), channel_id=1, source_target_pairs={{0,1},{1,0},{2,3},{3,2},{4,5},{5,4},{6,7},{7,6},{8,9},{9,8},{10,11... | collective-permute-start | bytes 983048 | tf_op jit(solution)/shard_map/ppermute | solution.py:87
  24.6 28.3 %collective-permute-start.14 = (bf16[40,32,128]{2,1,0:T(8,128)(2,1)S(1)}, bf16[40,32,128]{2,1,0:T(8,128)(2,1)}, u32[]{:S(2)}, u32[]{:S(2)}) collective-permute-start(bf16[40,32,128]{2,1,0:T(8,128)(2,1)S(1)} %collective-permute-done.12.refs_12_), channel_id=1, source_target_pairs={{0,2},{1,3},{2,0},{3,1},{4,6},{5,7},{6,4},{7,5},{8,10},{9,11},{10,... | collective-permute-start | bytes 983048 | tf_op jit(solution)/shard_map/ppermute | solution.py:87
  43.2 9.8 %collective-permute-start.13 = (bf16[40,32,128]{2,1,0:T(8,128)(2,1)S(1)}, bf16[40,32,128]{2,1,0:T(8,128)(2,1)}, u32[]{:S(2)}, u32[]{:S(2)}) collective-permute-start(bf16[40,32,128]{2,1,0:T(8,128)(2,1)S(1)} %collective-permute-done.12.refs_12_), channel_id=1, source_target_pairs={{0,1},{1,0},{2,3},{3,2},{4,5},{5,4},{6,7},{7,6},{8,9},{9,8},{10,11... | collective-permute-start | bytes 983048 | tf_op jit(solution)/shard_map/ppermute | solution.py:87
  43.2 10.6 %collective-permute-start.10 = (bf16[40,32,128]{2,1,0:T(8,128)(2,1)S(1)}, bf16[40,32,128]{2,1,0:T(8,128)(2,1)}, u32[]{:S(2)}, u32[]{:S(2)}) collective-permute-start(bf16[40,32,128]{2,1,0:T(8,128)(2,1)S(1)} %collective-permute-done.8.refs_8_), channel_id=1, source_target_pairs={{0,2},{1,3},{2,0},{3,1},{4,6},{5,7},{6,4},{7,5},{8,10},{9,11},{10,... | collective-permute-start | bytes 983048 | tf_op jit(solution)/shard_map/ppermute | solution.py:87
  44.7 9.1 %collective-permute-start.9 = (bf16[40,32,128]{2,1,0:T(8,128)(2,1)S(1)}, bf16[40,32,128]{2,1,0:T(8,128)(2,1)}, u32[]{:S(2)}, u32[]{:S(2)}) collective-permute-start(bf16[40,32,128]{2,1,0:T(8,128)(2,1)S(1)} %collective-permute-done.8.refs_8_), channel_id=1, source_target_pairs={{0,1},{1,0},{2,3},{3,2},{4,5},{5,4},{6,7},{7,6},{8,9},{9,8},{10,11... | collective-permute-start | bytes 983048 | tf_op jit(solution)/shard_map/ppermute | solution.py:87
  45.4 0.8 copy-start.3
  46.2 14.2 %collective-permute-start.6 = (bf16[40,32,128]{2,1,0:T(8,128)(2,1)S(1)}, bf16[40,32,128]{2,1,0:T(8,128)(2,1)}, u32[]{:S(2)}, u32[]{:S(2)}) collective-permute-start(bf16[40,32,128]{2,1,0:T(8,128)(2,1)S(1)} %collective-permute-done.4.refs_4_), channel_id=1, source_target_pairs={{0,2},{1,3},{2,0},{3,1},{4,6},{5,7},{6,4},{7,5},{8,10},{9,11},{10,... | collective-permute-start | bytes 983048 | tf_op jit(solution)/shard_map/ppermute | solution.py:87
  46.8 0.9 copy-start.5
  52.9 8.5 %collective-permute-start.5 = (bf16[40,32,128]{2,1,0:T(8,128)(2,1)S(1)}, bf16[40,32,128]{2,1,0:T(8,128)(2,1)S(1)}, u32[]{:S(2)}, u32[]{:S(2)}) collective-permute-start(bf16[40,32,128]{2,1,0:T(8,128)(2,1)S(1)} %collective-permute-done.4.refs_4_), channel_id=1, source_target_pairs={{0,1},{1,0},{2,3},{3,2},{4,5},{5,4},{6,7},{7,6},{8,9},{9,8},{10,11... | collective-permute-start | bytes 983048 | tf_op jit(solution)/shard_map/ppermute | solution.py:87
  53.0 8.4 %collective-permute-start.3 = (bf16[40,32,128]{2,1,0:T(8,128)(2,1)}, bf16[40,32,128]{2,1,0:T(8,128)(2,1)S(1)}, u32[]{:S(2)}, u32[]{:S(2)}) collective-permute-start(bf16[40,32,128]{2,1,0:T(8,128)(2,1)} %copy-done.1), channel_id=1, source_target_pairs={{0,1},{1,0},{2,3},{3,2},{4,5},{5,4},{6,7},{7,6},{8,9},{9,8},{10,11... | collective-permute-start | bytes 983048 | tf_op jit(solution)/shard_map/ppermute | solution.py:87
  53.8 7.6 %collective-permute-start.15 = (bf16[40,32,128]{2,1,0:T(8,128)(2,1)}, bf16[40,32,128]{2,1,0:T(8,128)(2,1)S(1)}, u32[]{:S(2)}, u32[]{:S(2)}) collective-permute-start(bf16[40,32,128]{2,1,0:T(8,128)(2,1)} %collective-permute-done.14.refs_14_), channel_id=1, source_target_pairs={{0,1},{1,0},{2,3},{3,2},{4,5},{5,4},{6,7},{7,6},{8,9},{9,8},{10,11... | collective-permute-start | bytes 983048 | tf_op jit(solution)/shard_map/ppermute | solution.py:87
  53.8 7.6 %collective-permute-start.11 = (bf16[40,32,128]{2,1,0:T(8,128)(2,1)}, bf16[40,32,128]{2,1,0:T(8,128)(2,1)S(1)}, u32[]{:S(2)}, u32[]{:S(2)}) collective-permute-start(bf16[40,32,128]{2,1,0:T(8,128)(2,1)} %collective-permute-done.10.refs_10_), channel_id=1, source_target_pairs={{0,1},{1,0},{2,3},{3,2},{4,5},{5,4},{6,7},{7,6},{8,9},{9,8},{10,11... | collective-permute-start | bytes 983048 | tf_op jit(solution)/shard_map/ppermute | solution.py:87
  60.4 1.8 %collective-permute-start.7 = (bf16[40,32,128]{2,1,0:T(8,128)(2,1)}, bf16[40,32,128]{2,1,0:T(8,128)(2,1)S(1)}, u32[]{:S(2)}, u32[]{:S(2)}) collective-permute-start(bf16[40,32,128]{2,1,0:T(8,128)(2,1)} %collective-permute-done.6.refs_6_), channel_id=1, source_target_pairs={{0,1},{1,0},{2,3},{3,2},{4,5},{5,4},{6,7},{7,6},{8,9},{9,8},{10,11... | collective-permute-start | bytes 983048 | tf_op jit(solution)/shard_map/ppermute | solution.py:87
  62.3 1.0 copy-start.2
  63.2 1.0 copy-start.4
  64.2 70.8 %copy-start.9 = (s32[64]{0:T(128)S(1)}, s32[64]{0:T(128)}, u32[]{:S(2)}) copy-start(s32[64]{0:T(128)} %param.16) | copy-start | bytes 772
  119.5 3.7 %collective-permute-start.17 = (f32[4,256]{1,0:T(4,128)S(1)}, f32[4,256]{1,0:T(4,128)S(1)}, u32[]{:S(2)}, u32[]{:S(2)}) collective-permute-start(f32[4,256]{1,0:T(4,128)S(1)} %dynamic-slice_bitcast_fusion.1), channel_id=1, source_target_pairs={{0,16},{16,0},{1,17},{17,1},{2,18},{18,2},{3,19},{19,3},{4,20},{20... | collective-permute-start | bytes 12296 | tf_op jit(solution)/shard_map/ppermute | solution.py:247
  123.2 1.2 collective-permute-start.18
  124.3 3.6 %collective-permute-start.19 = (f32[4,256]{1,0:T(4,128)S(1)}, f32[4,256]{1,0:T(4,128)S(1)}, u32[]{:S(2)}, u32[]{:S(2)}) collective-permute-start(f32[4,256]{1,0:T(4,128)S(1)} %add.77), channel_id=1, source_target_pairs={{0,2},{1,3},{2,0},{3,1},{4,6},{5,7},{6,4},{7,5},{8,10},{9,11},{10,... | collective-permute-start | bytes 12296 | tf_op jit(solution)/shard_map/ppermute | solution.py:87
  127.9 3.6 %collective-permute-start.20 = (f32[4,256]{1,0:T(4,128)S(1)}, f32[4,256]{1,0:T(4,128)S(1)}, u32[]{:S(2)}, u32[]{:S(2)}) collective-permute-start(f32[4,256]{1,0:T(4,128)S(1)} %add.78), channel_id=1, source_target_pairs={{0,4},{1,5},{2,6},{3,7},{4,0},{5,1},{6,2},{7,3},{8,12},{9,13},{10,... | collective-permute-start | bytes 12296 | tf_op jit(solution)/shard_map/ppermute | solution.py:87
  129.6 7.7 %collective-permute-start.22 = (bf16[32,8,128]{2,1,0:T(8,128)(2,1)S(1)}, bf16[32,8,128]{2,1,0:T(8,128)(2,1)S(1)}, u32[]{:S(2)}, u32[]{:S(2)}) collective-permute-start(bf16[32,8,128]{2,1,0:T(8,128)(2,1)S(1)} %dynamic-slice_bitcast_fusion), channel_id=1, source_target_pairs={{0,16},{16,0},{1,17},{17,1},{2,18},{18,2},{3,19},{19,3},{4,20},{20... | collective-permute-start | bytes 196616 | tf_op jit(solution)/shard_map/ppermute | solution.py:254
  131.6 5.0 %collective-permute-start.21 = (f32[4,256]{1,0:T(4,128)S(1)}, f32[4,256]{1,0:T(4,128)S(1)}, u32[]{:S(2)}, u32[]{:S(2)}) collective-permute-start(f32[4,256]{1,0:T(4,128)S(1)} %add.79), channel_id=1, source_target_pairs={{0,8},{1,9},{2,10},{3,11},{4,12},{5,13},{6,14},{7,15},{8,0},{9,1},... | collective-permute-start | bytes 12296 | tf_op jit(solution)/shard_map/ppermute | solution.py:87
  (1 other events, 0.7 us)

commit v2 on v0

--- a/solution.py
+++ b/solution.py
@@ -1,6 +1,8 @@
 import jax
 import jax.numpy as jnp
 from jax import lax
+from jax.experimental import pallas as pl
+from jax.experimental.pallas import tpu as pltpu
 from jax.sharding import PartitionSpec as P
 
 D = 4096
@@ -23,7 +25,7 @@
     return turned.reshape(layer_count, row_count, feature_count).astype(jnp.bfloat16)
 
 
-def body(
+def general_body(
     train_inputs,
     train_outgrads,
     sequence_ids,
@@ -75,9 +77,261 @@
     return (scores, rotated_out)
 
 
+NQ = 16
+WAVES = 2
+GROUPS = 2 * SEQS
+TOKENS = 256
+UNIT = 20
+SWAP = [(0, 1), (1, 0)]
+BF = jnp.bfloat16
+
+
+def hop(value, bits):
+    return lax.ppermute(value, "query", [(i, i ^ bits) for i in range(NQ)])
+
+
+def pack_kernel(info, own, other, query, basis, *units):
+    x = info[0]
+
+    for wave in range(WAVES):
+        unit = units[wave]
+
+        @pl.loop(0, NQ)
+        def _(owner):
+            tile = info[1 + wave * NQ + owner]
+            layer = tile // 32
+            cols = pl.ds(pl.multiple_of((tile % 32) * TILE_A, TILE_A), TILE_A)
+            mine = own[layer, :, cols].astype(jnp.float32)
+            came = other[layer, :, cols].astype(jnp.float32)
+            first = jnp.where(x == 0, mine, came)
+            second = jnp.where(x == 0, came, mine)
+            unit[owner, :16, :] = jnp.concatenate([first, second], axis=0).astype(BF)
+            unit[owner, 16:, :] = query[layer, :, cols]
+
+        unit[NQ:] = basis[2 * x + wave].reshape(4, 32, TILE_A)
+
+
+def score_kernel(wave, info, *refs):
+    units = refs[:NQ]
+    grads, query_grads, codes, eigen, before, totals, own_rows = refs[NQ : NQ + 7]
+    held, turned_rows, train_t, query_t, eig, scaled0, scaled1, weights, acc = refs[NQ + 7 : NQ + 16]
+    unit_sems, eig_sems = refs[NQ + 16 :]
+    scaled = (scaled0, scaled1)
+    me = info[0]
+    copies = [
+        pltpu.make_async_copy(units[d], held.at[me ^ d], unit_sems.at[d]) for d in range(NQ)
+    ]
+    for copy in copies:
+        copy.start()
+
+    def eig_copy(n):
+        tile = info[1 + wave * NQ + n]
+        cols = pl.ds(pl.multiple_of((tile % 32) * TILE_A, TILE_A), TILE_A)
+        return pltpu.make_async_copy(eigen.at[tile // 32, :, cols], eig.at[n], eig_sems.at[n])
+
+    for n in range(NQ):
+        eig_copy(n).start()
+    acc[...] = jnp.zeros_like(acc)
+    for copy in copies:
+        copy.wait()
+
+    @pl.loop(0, NQ)
+    def _(n):
+        basis = held[n, NQ:].reshape(TILE_A, TILE_A)
+        tile = held[:, n]
+        train = tile[:, :16].reshape(TOKENS, TILE_A)
+        query = tile[:, 16:].reshape(TOKENS, TILE_A)
+        turned = jnp.dot(train, basis, preferred_element_type=jnp.float32)
+        turned_rows[...] = turned.astype(BF)
+        own_rows[n] = turned_rows[pl.ds(pl.multiple_of(me * 16, 16), 16), :]
+        train_t[n] = turned.T.astype(BF)
+        query_t[n] = jnp.dot(query, basis, preferred_element_type=jnp.float32).T.astype(BF)
+
+    def weigh(n, k):
+        weights[k] = 1.0 / (eig[n].T + damping)
+
+    def gram(n, k):
+        layer = info[1 + wave * NQ + n] // 32
+        code = codes[...]
+        rows = train_t[n]
+        zero = jnp.zeros_like(rows)
+        for h in range(2):
+            left = jnp.concatenate(
+                [jnp.where(code == s, rows, zero) for s in range(4 * h, 4 * h + 4)], axis=0
+            )
+            for c in range(3):
+                cols = slice(c * 256, (c + 1) * 256)
+                part = jnp.dot(left, grads[layer, :, cols], preferred_element_type=jnp.float32)
+                part = part.reshape(4, TILE_A, 256) * weights[k, :, cols][None]
+                scaled[k][h * 512 : (h + 1) * 512, cols] = part.astype(BF).reshape(512, 256)
+
+    def project(n, k):
+        layer = info[1 + wave * NQ + n] // 32
+        query = query_t[n].astype(jnp.float32)
+        for h in range(2):
+            part = jnp.dot(
+                scaled[k][h * 512 : (h + 1) * 512, :],
+                query_grads[layer],
+                preferred_element_type=jnp.float32,
+            )
+            part = part.reshape(4, TILE_A, TOKENS) * query[None]
+            acc[4 * h : 4 * h + 4] += jnp.sum(part.reshape(4, TILE_A // 8, 8, TOKENS), axis=1)
+
+    eig_copy(0).wait()
+    weigh(0, 0)
+    eig_copy(1).wait()
+    weigh(1, 1)
+    gram(0, 0)
+
+    @pl.loop(0, NQ - 2, step=2)
+    def _(n):
+        eig_copy(n + 2).wait()
+        eig_copy(n + 3).wait()
+        gram(n + 1, 1)
+        project(n, 0)
+        weigh(n + 2, 0)
+        gram(n + 2, 0)
+        project(n + 1, 1)
+        weigh(n + 3, 1)
+
+    gram(NQ - 1, 1)
+    project(NQ - 2, 0)
+    project(NQ - 1, 1)
+    totals[...] = before[...] + jnp.sum(acc[...], axis=1)
+
+
+VMEM = pl.BlockSpec(memory_space=pltpu.VMEM)
+SMEM = pl.BlockSpec(memory_space=pltpu.SMEM)
+ANY = pl.BlockSpec(memory_space=pl.ANY)
+
+
+def score_wave(wave, info, units, grads, query_grads, codes, eigenvalues, before):
+    width = grads.shape[2]
+
+    def kernel(*refs):
+        score_kernel(wave, *refs)
+
+    return pl.pallas_call(
+        kernel,
+        in_specs=[SMEM] + [ANY] * NQ + [VMEM, VMEM, VMEM, ANY, VMEM],
+        out_specs=[VMEM, VMEM],
+        out_shape=[
+            jax.ShapeDtypeStruct((GROUPS, TOKENS), jnp.float32),
+            jax.ShapeDtypeStruct((NQ, 16, TILE_A), BF),
+        ],
+        scratch_shapes=[
+            pltpu.VMEM((NQ, UNIT, 32, TILE_A), BF),
+            pltpu.VMEM((TOKENS, TILE_A), BF),
+            pltpu.VMEM((NQ, TILE_A, TOKENS), BF),
+            pltpu.VMEM((NQ, TILE_A, TOKENS), BF),
+            pltpu.VMEM((NQ, width, TILE_A), jnp.float32),
+            pltpu.VMEM((GROUPS * TILE_A, width), BF),
+            pltpu.VMEM((GROUPS * TILE_A, width), BF),
+            pltpu.VMEM((2, TILE_A, width), jnp.float32),
+            pltpu.VMEM((GROUPS, 8, TOKENS), jnp.float32),
+            pltpu.SemaphoreType.DMA((NQ,)),
+            pltpu.SemaphoreType.DMA((NQ,)),
+        ],
+        compiler_params=pltpu.CompilerParams(vmem_limit_bytes=40 * 1024 * 1024),
+        cost_estimate=pl.CostEstimate(
+            flops=20 * 10**9, bytes_accessed=10 * 10**6, transcendentals=0
+        ),
+    )(info, *units, grads, query_grads, codes, eigenvalues, before)
+
+
+def gather_units(unit):
+    units = [None] * NQ
+    units[0] = unit
+    for d in (4, 12, 8):
+        units[d] = hop(unit, d)
+    for d in (0, 4, 12, 8):
+        units[d ^ 2] = hop(units[d], 2)
+    for d in (0, 2, 4, 6, 12, 14, 8, 10):
+        units[d ^ 1] = hop(units[d], 1)
+    return units
+
+
+def paired_body(
+    train_inputs,
+    train_outgrads,
+    sequence_ids,
+    query_inputs,
+    query_outgrads,
+    eigenvalues,
+    input_basis,
+    slot_list,
+    output_basis,
+):
+    x = lax.axis_index("parts")
+    me = lax.axis_index("query")
+    train_other = lax.ppermute(train_inputs, "parts", SWAP)
+    ids = jnp.arange(64, dtype=jnp.int32)
+    tile_of = jnp.sum(jnp.where(slot_list[None, :] == ids[:, None], ids[None, :], 0), axis=1)
+    mine = lax.dynamic_index_in_dim(tile_of.reshape(NQ, 2, WAVES), x, 1, False)
+    mine = mine.T.reshape(WAVES * NQ)
+
+    packed = pl.pallas_call(
+        pack_kernel,
+        in_specs=[SMEM, VMEM, VMEM, VMEM, VMEM],
+        out_specs=[VMEM] * WAVES,
+        out_shape=[jax.ShapeDtypeStruct((UNIT, 32, TILE_A), BF)] * WAVES,
+    )(
+        jnp.concatenate([x.reshape(1).astype(jnp.int32), mine]),
+        train_inputs,
+        train_other,
+        query_inputs,
+        input_basis,
+    )
+    waves = [gather_units(unit) for unit in packed]
+
+    slab = train_outgrads.shape[2]
+    id_block = jnp.broadcast_to(sequence_ids.astype(BF)[None, :, None], (LAYERS, 128, TILE_A))
+    sent = jnp.concatenate([train_outgrads, id_block], axis=2)
+    other = lax.ppermute(sent, "parts", SWAP)
+    both = jnp.stack(
+        [jnp.where(x == 0, sent, other), jnp.where(x == 0, other, sent)], axis=0
+    ).reshape(2, LAYERS, NQ, 8, slab + TILE_A)
+    both = both.transpose(1, 2, 0, 3, 4).reshape(LAYERS, TOKENS, slab + TILE_A)
+    part_of = (jnp.arange(TOKENS, dtype=jnp.int32) // 8) % 2
+    codes = (both[0, :, slab].astype(jnp.int32) + SEQS * part_of).reshape(1, TOKENS)
+    grads_rot = rotate_blocks(both[:, :, :slab], output_basis, TILE_S)
+    query_rot = rotate_blocks(query_outgrads, output_basis, TILE_S).transpose(0, 2, 1)
+
+    info = jnp.concatenate([me.reshape(1).astype(jnp.int32), mine])
+    totals = jnp.zeros((GROUPS, TOKENS), jnp.float32)
+    own_rows = [None] * WAVES
+    for wave in range(WAVES):
+        totals, own_rows[wave] = score_wave(
+            wave, info, waves[wave], grads_rot, query_rot, codes, eigenvalues, totals
+        )
+
+    halves = totals.reshape(2, SEQS, TOKENS)
+    keep = lax.dynamic_index_in_dim(halves, x, 0, False)
+    give = lax.dynamic_index_in_dim(halves, 1 - x, 0, False)
+    total = keep + lax.ppermute(give, "parts", SWAP)
+    for bits in (1, 2, 4, 8):
+        total = total + hop(total, bits)
+    scores = jnp.sum(total.reshape(SEQS, QUERIES, QLEN), axis=2).T
+
+    slots = [None] * 4
+    for wave in range(WAVES):
+        pair = own_rows[wave].reshape(NQ, 2, 8, TILE_A)
+        kept = lax.dynamic_index_in_dim(pair, x, 1, False)
+        came = lax.ppermute(lax.dynamic_index_in_dim(pair, 1 - x, 1, False), "parts", SWAP)
+        slots[wave] = jnp.where(x == 0, kept, came)
+        slots[2 + wave] = jnp.where(x == 0, came, kept)
+    by_slot = jnp.stack(slots, axis=1).reshape(64, 8, TILE_A)
+    ordered = jnp.take(by_slot, slot_list, axis=0, mode="clip")
+    rotated_out = (
+        ordered.reshape(LAYERS, 32, 8, TILE_A).transpose(0, 2, 1, 3).reshape(LAYERS, 8, D)
+    )
+    return (scores, rotated_out)
+
+
 def solution(mesh):
+    paired = mesh.shape["parts"] == 2 and mesh.shape["query"] == NQ
     return jax.shard_map(
-        body,
+        paired_body if paired else general_body,
         mesh=mesh,
         in_specs=(
             P(None, ("parts", "query"), None),

time: 223 us -> 142 us (0.64)
  waiting for transfers between devices: 95.8 us -> 23.7 us
  Pallas kernels: 0 us -> 49.8 us
  starting transfers between devices: 0.12 us -> 43.3 us
  matrix products: 37.1 us -> 2.88 us
  blocking collectives: 31.7 us -> 0 us
  other arithmetic: 20.1 us -> 6.97 us
  between operations: 13.9 us -> 0.95 us
  local copies, waits for them, and re-layouts: 24.2 us -> 13.8 us
    all_gather x3 -> x0, waiting for transfers between devices: 95.1 us -> none  [the longest x1 50.1 us: body(): lax.all_gather(own_query, 'query', axis=1, tiled=True)]
    pallas_call x0 -> x3, Pallas kernels: none -> 49.8 us  [the longest x2 47.4 us: score_wave(): pl.pallas_call(kernel, in_specs=[SMEM] + [ANY] * NQ + [VMEM, VMEM, VMEM,...]
    ppermute x0 -> x39, starting transfers between devices: none -> 43.3 us  [the longest x34 32.1 us: hop(): return lax.ppermute(value, 'query', [(i, i ^ bits) for i in range(NQ)])]
    dot_general x2 -> x0, matrix products: 34.3 us -> none  [body(): jnp.einsum('sij,uj->siu', scaled, rotated_query[layer_index], preferred_e...]
    psum x1 -> x0, blocking collectives: 31.7 us -> none  [body(): scores = lax.psum(partial_value, 'query')]
    ppermute x0 -> x39, waiting for transfers between devices: none -> 23.7 us  [the longest x34 19.9 us: hop(): return lax.ppermute(value, 'query', [(i, i ^ bits) for i in range(NQ)])]
    mul x1 -> x0, local copies, waits for them, and re-layouts: 18.5 us -> none  [body(): gram_block.reshape(SEQS, slab_width, D) * weights[layer_index][None]]
    div x1 -> x0, other arithmetic: 17.6 us -> none  [body(): weights = 1.0 / (eigenvalues + damping)]
  transfers between devices with their start and end apart: 3 -> 39, of which waited for: 2 -> 15; matrix products, arithmetic and copies ran while one was open for 19% -> 11% of each run, Pallas kernels for 0% -> 17%
where the time goes in v2:
time: 142 us; the launch traced here: 141 us
  Pallas kernels  49.8 us (35%)
  starting transfers between devices  43.3 us (30%)
  waiting for transfers between devices  23.7 us (17%)
  local copies, waits for them, and re-layouts  13.8 us (10%)
  other arithmetic  6.97 us (5%)
  matrix products  2.88 us (2%)
    pallas_call x2, Pallas kernels, score_wave(): pl.pallas_call(kernel, in_specs=[SMEM] + [ANY] * NQ + [VMEM, VMEM, VMEM,...  47.4 us
    ppermute x34, starting transfers between devices, hop(): return lax.ppermute(value, 'query', [(i, i ^ bits) for i in range(NQ)])  32.1 us
    ppermute x34, waiting for transfers between devices, hop(): return lax.ppermute(value, 'query', [(i, i ^ bits) for i in range(NQ)])  19.9 us
    unnamed x43, local copies, waits for them, and re-layouts  7.42 us
    ppermute x1, starting transfers between devices, paired_body(): total = keep + lax.ppermute(give, 'parts', SWAP)  3.67 us
    slice x2, local copies, waits for them, and re-layouts, paired_body(): grads_rot = rotate_blocks(both[:, :, :slab], output_basis, TILE_S)  3.22 us
    ppermute x2, starting transfers between devices, paired_body(): lax.ppermute(lax.dynamic_index_in_dim(pair, 1 - x, 1, False), 'parts', SWAP)  3.11 us
    ppermute x1, starting transfers between devices, paired_body(): train_other = lax.ppermute(train_inputs, 'parts', SWAP)  3 us
  transfers between devices with their start and end apart: 39, of which 15 were waited for; matrix products, arithmetic and copies ran while one was open for 11% of the time, Pallas kernels for 17%

profile of v2, /device:TPU:0, one launch (start us, length us, event | category | flops | bytes accessed | tf_op | source)
XLA Modules:
  0.0 141.4 jit_solution(5864712369662928451)
XLA Ops:
  0.7 3.0 %collective-permute-start = (bf16[2,8,4096]{2,1,0:T(8,128)(2,1)}, bf16[2,8,4096]{2,1,0:T(8,128)(2,1)S(1)}, u32[]{:S(2)}, u32[]{:S(2)}) collective-permute-start(bf16[2,8,4096]{2,1,0:T(8,128)(2,1)} %own.1), channel_id=1, source_target_pairs={{0,16},{16,0},{1,17},{17,1},{2,18},{18,2},{3,19},{19,3},{4,20},{20... | collective-permute-start | bytes 393224 | tf_op jit(solution)/shard_map/ppermute | solution.py:267
  5.4 2.0 %collective-permute-done.other = bf16[2,8,4096]{2,1,0:T(8,128)(2,1)S(1)} collective-permute-done((bf16[2,8,4096]{2,1,0:T(8,128)(2,1)}, bf16[2,8,4096]{2,1,0:T(8,128)(2,1)S(1)}, u32[]{:S(2)}, u32[]{:S(2)}) %collective-permute-start) | collective-permute-done | bytes 131104 | tf_op jit(solution)/shard_map/ppermute | solution.py:267
  8.0 2.4 %shard_map.104 = (bf16[20,32,128]{2,1,0:T(8,128)(2,1)}, bf16[20,32,128]{2,1,0:T(8,128)(2,1)}) custom-call(s32[33]{0:T(128)} %get-tuple-element.20.info, bf16[2,8,4096]{2,1,0:T(8,128)(2,1)} %own.1, bf16[2,8,4096]{2,1,0:T(8,128)(2,1)} %copy-done.19, bf16[2,16,4096]{2,1,0:T(8,128)(2,1)} %query.1, bf16[4,128,128]{2,1,0:T(8,128)(2,1)} %basis.1), custom_call_target="tpu_custom_call" | custom-call | tf_op jit(solution)/shard_map/pallas_call | solution.py:273
  10.4 1.8 %collective-permute-start.20 = (bf16[20,32,128]{2,1,0:T(8,128)(2,1)}, bf16[20,32,128]{2,1,0:T(8,128)(2,1)S(1)}, u32[]{:S(2)}, u32[]{:S(2)}) collective-permute-start(bf16[20,32,128]{2,1,0:T(8,128)(2,1)} %get-tuple-element.9.refs_1_), channel_id=1, source_target_pairs={{0,4},{1,5},{2,6},{3,7},{4,0},{5,1},{6,2},{7,3},{8,12},{9,13},{10,... | collective-permute-start | bytes 491528 | tf_op jit(solution)/shard_map/ppermute | solution.py:90
  12.2 2.6 %collective-permute-start.24 = (bf16[20,32,128]{2,1,0:T(8,128)(2,1)}, bf16[20,32,128]{2,1,0:T(8,128)(2,1)S(1)}, u32[]{:S(2)}, u32[]{:S(2)}) collective-permute-start(bf16[20,32,128]{2,1,0:T(8,128)(2,1)} %get-tuple-element.9.refs_1_), channel_id=1, source_target_pairs={{0,8},{1,9},{2,10},{3,11},{4,12},{5,13},{6,14},{7,15},{8,0},{9,1},... | collective-permute-start | bytes 491528 | tf_op jit(solution)/shard_map/ppermute | solution.py:90
  15.6 1.8 %pad_maximum_fusion.1 = bf16[2,128,896]{2,1,0:T(8,128)(2,1)} fusion(bf16[2,128,128]{2,1,0:T(8,128)(2,1)S(1)} %broadcast_in_dim.30, bf16[2,128,768]{2,1,0:T(8,128)(2,1)} %param.10), kind=kLoop, calls=%fused_computation.4 | loop fusion | flops 917504 | bytes 917504 | tf_op jit(solution)/shard_map/concatenate | solution.py:289
  17.4 1.5 %collective-permute-start.16 = (bf16[2,128,896]{2,1,0:T(8,128)(2,1)}, bf16[2,128,896]{2,1,0:T(8,128)(2,1)}, u32[]{:S(2)}, u32[]{:S(2)}) collective-permute-start(bf16[2,128,896]{2,1,0:T(8,128)(2,1)} %pad_maximum_fusion.1), channel_id=1, source_target_pairs={{0,16},{16,0},{1,17},{17,1},{2,18},{18,2},{3,19},{19,3},{4,20},{20... | collective-permute-start | bytes 1376264 | tf_op jit(solution)/shard_map/ppermute | solution.py:290
  19.1 1.5 %collective-permute-start.18 = (bf16[20,32,128]{2,1,0:T(8,128)(2,1)}, bf16[20,32,128]{2,1,0:T(8,128)(2,1)S(1)}, u32[]{:S(2)}, u32[]{:S(2)}) collective-permute-start(bf16[20,32,128]{2,1,0:T(8,128)(2,1)} %get-tuple-element.9.refs_1_), channel_id=1, source_target_pairs={{0,2},{1,3},{2,0},{3,1},{4,6},{5,7},{6,4},{7,5},{8,10},{9,11},{10,... | collective-permute-start | bytes 491528 | tf_op jit(solution)/shard_map/ppermute | solution.py:90
  20.6 3.0 %collective-permute-done.24.refs_9_ = bf16[20,32,128]{2,1,0:T(8,128)(2,1)S(1)} collective-permute-done((bf16[20,32,128]{2,1,0:T(8,128)(2,1)}, bf16[20,32,128]{2,1,0:T(8,128)(2,1)S(1)}, u32[]{:S(2)}, u32[]{:S(2)}) %collective-permute-start.24) | collective-permute-done | bytes 163872 | tf_op jit(solution)/shard_map/ppermute | solution.py:90
  23.9 2.8 %collective-permute-done.28.refs_13_ = bf16[20,32,128]{2,1,0:T(8,128)(2,1)S(1)} collective-permute-done((bf16[20,32,128]{2,1,0:T(8,128)(2,1)}, bf16[20,32,128]{2,1,0:T(8,128)(2,1)S(1)}, u32[]{:S(2)}, u32[]{:S(2)}) %collective-permute-start.28) | collective-permute-done | bytes 163872 | tf_op jit(solution)/shard_map/ppermute | solution.py:90
  26.7 7.6 %collective-permute-start.12 = (bf16[20,32,128]{2,1,0:T(8,128)(2,1)S(1)}, bf16[20,32,128]{2,1,0:T(8,128)(2,1)S(1)}, u32[]{:S(2)}, u32[]{:S(2)}) collective-permute-start(bf16[20,32,128]{2,1,0:T(8,128)(2,1)S(1)} %copy-done.1), channel_id=1, source_target_pairs={{0,12},{1,13},{2,14},{3,15},{4,8},{5,9},{6,10},{7,11},{8,4},{9,5},... | collective-permute-start | bytes 491528 | tf_op jit(solution)/shard_map/ppermute | solution.py:90
  34.3 2.8 %collective-permute-start.4 = (bf16[20,32,128]{2,1,0:T(8,128)(2,1)S(1)}, bf16[20,32,128]{2,1,0:T(8,128)(2,1)}, u32[]{:S(2)}, u32[]{:S(2)}) collective-permute-start(bf16[20,32,128]{2,1,0:T(8,128)(2,1)S(1)} %copy-done.1), channel_id=1, source_target_pairs={{0,4},{1,5},{2,6},{3,7},{4,0},{5,1},{6,2},{7,3},{8,12},{9,13},{10,... | collective-permute-start | bytes 491528 | tf_op jit(solution)/shard_map/ppermute | solution.py:90
  37.1 1.5 %collective-permute-start.2 = (bf16[20,32,128]{2,1,0:T(8,128)(2,1)S(1)}, bf16[20,32,128]{2,1,0:T(8,128)(2,1)S(1)}, u32[]{:S(2)}, u32[]{:S(2)}) collective-permute-start(bf16[20,32,128]{2,1,0:T(8,128)(2,1)S(1)} %copy-done.1), channel_id=1, source_target_pairs={{0,2},{1,3},{2,0},{3,1},{4,6},{5,7},{6,4},{7,5},{8,10},{9,11},{10,... | collective-permute-start | bytes 491528 | tf_op jit(solution)/shard_map/ppermute | solution.py:90
  39.1 2.0 %collective-permute-done.12.refs_13_ = bf16[20,32,128]{2,1,0:T(8,128)(2,1)S(1)} collective-permute-done((bf16[20,32,128]{2,1,0:T(8,128)(2,1)S(1)}, bf16[20,32,128]{2,1,0:T(8,128)(2,1)S(1)}, u32[]{:S(2)}, u32[]{:S(2)}) %collective-permute-start.12) | collective-permute-done | bytes 163872 | tf_op jit(solution)/shard_map/ppermute | solution.py:90
  41.1 1.5 %collective-permute-start.22 = (bf16[20,32,128]{2,1,0:T(8,128)(2,1)S(1)}, bf16[20,32,128]{2,1,0:T(8,128)(2,1)S(1)}, u32[]{:S(2)}, u32[]{:S(2)}) collective-permute-start(bf16[20,32,128]{2,1,0:T(8,128)(2,1)S(1)} %collective-permute-done.20.refs_5_), channel_id=1, source_target_pairs={{0,2},{1,3},{2,0},{3,1},{4,6},{5,7},{6,4},{7,5},{8,10},{9,11},{10,... | collective-permute-start | bytes 491528 | tf_op jit(solution)/shard_map/ppermute | solution.py:90
  42.7 2.5 %collective-permute-start.26 = (bf16[20,32,128]{2,1,0:T(8,128)(2,1)S(1)}, bf16[20,32,128]{2,1,0:T(8,128)(2,1)S(1)}, u32[]{:S(2)}, u32[]{:S(2)}) collective-permute-start(bf16[20,32,128]{2,1,0:T(8,128)(2,1)S(1)} %collective-permute-done.24.refs_9_), channel_id=1, source_target_pairs={{0,2},{1,3},{2,0},{3,1},{4,6},{5,7},{6,4},{7,5},{8,10},{9,11},{10,... | collective-permute-start | bytes 491528 | tf_op jit(solution)/shard_map/ppermute | solution.py:90
  48.7 2.3 %copy.38 = bf16[2,256,768]{1,2,0:T(8,128)(2,1)} copy(bf16[2,256,768]{2,1,0:T(8,128)(2,1)} %slice.10) | data formatting | bytes 1572864 | tf_op jit(solution)/shard_map/slice | solution.py:297
  51.5 1.9 %collective-permute-done.30.refs_15_ = bf16[20,32,128]{2,1,0:T(8,128)(2,1)S(1)} collective-permute-done((bf16[20,32,128]{2,1,0:T(8,128)(2,1)S(1)}, bf16[20,32,128]{2,1,0:T(8,128)(2,1)S(1)}, u32[]{:S(2)}, u32[]{:S(2)}) %collective-permute-start.30) | collective-permute-done | bytes 163872 | tf_op jit(solution)/shard_map/ppermute | solution.py:90
  53.4 1.5 %collective-permute-start.10 = (bf16[20,32,128]{2,1,0:T(8,128)(2,1)S(1)}, bf16[20,32,128]{2,1,0:T(8,128)(2,1)}, u32[]{:S(2)}, u32[]{:S(2)}) collective-permute-start(bf16[20,32,128]{2,1,0:T(8,128)(2,1)S(1)} %collective-permute-done.8.refs_9_), channel_id=1, source_target_pairs={{0,2},{1,3},{2,0},{3,1},{4,6},{5,7},{6,4},{7,5},{8,10},{9,11},{10,... | collective-permute-start | bytes 491528 | tf_op jit(solution)/shard_map/ppermute | solution.py:90
  55.5 1.5 %collective-permute-start.6 = (bf16[20,32,128]{2,1,0:T(8,128)(2,1)}, bf16[20,32,128]{2,1,0:T(8,128)(2,1)}, u32[]{:S(2)}, u32[]{:S(2)}) collective-permute-start(bf16[20,32,128]{2,1,0:T(8,128)(2,1)} %collective-permute-done.4.refs_5_), channel_id=1, source_target_pairs={{0,2},{1,3},{2,0},{3,1},{4,6},{5,7},{6,4},{7,5},{8,10},{9,11},{10,... | collective-permute-start | bytes 491528 | tf_op jit(solution)/shard_map/ppermute | solution.py:90
  57.0 2.5 %convolution_convert_fusion.1 = bf16[2,12,256,64]{2,3,1,0:T(8,128)(2,1)} fusion(bf16[2,256,12,64]{1,3,2,0:T(8,128)(2,1)} %bitcast.81, bf16[2,12,64,64]{3,2,1,0:T(8,128)(2,1)S(1)} %copy-done), kind=kOutput, calls=%fused_computation.2 | convolution fusion | flops 50724864 | bytes 1769472 | tf_op jit(solution)/shard_map/lrbi,lbij->lrbj/dot_general | solution.py:24
  62.6 1.6 %collective-permute-done.14.refs_15_ = bf16[20,32,128]{2,1,0:T(8,128)(2,1)} collective-permute-done((bf16[20,32,128]{2,1,0:T(8,128)(2,1)S(1)}, bf16[20,32,128]{2,1,0:T(8,128)(2,1)}, u32[]{:S(2)}, u32[]{:S(2)}) %collective-permute-start.14) | collective-permute-done | bytes 163872 | tf_op jit(solution)/shard_map/ppermute | solution.py:90
  64.2 1.9 %collective-permute-done.6.refs_7_ = bf16[20,32,128]{2,1,0:T(8,128)(2,1)} collective-permute-done((bf16[20,32,128]{2,1,0:T(8,128)(2,1)}, bf16[20,32,128]{2,1,0:T(8,128)(2,1)}, u32[]{:S(2)}, u32[]{:S(2)}) %collective-permute-start.6) | collective-permute-done | bytes 163872 | tf_op jit(solution)/shard_map/ppermute | solution.py:90
  73.4 23.8 %shard_map.105 = (f32[8,256]{1,0:T(8,128)S(1)}, bf16[16,16,128]{2,1,0:T(8,128)(2,1)S(1)}) custom-call(s32[33]{0:T(128)S(1)} %get-tuple-element.21.refs_0_, bf16[20,32,128]{2,1,0:T(8,128)(2,1)S(1)} %copy-done.2, bf16[20,32,128]{2,1,0:T(8,128)(2,1)S(1)} %copy-done.4, bf16[20,32,128]{2,1,0:T(8,128)(2,1)S(1)} %collective-permute-done.18.refs_3_, ...), custom_call_target="tpu_custom_call" | custom-call | flops 20000000000 | bytes 10000000 | tf_op jit(solution)/shard_map/pallas_call | solution.py:214
  97.3 23.6 %shard_map.106 = (f32[8,256]{1,0:T(8,128)S(1)}, bf16[16,16,128]{2,1,0:T(8,128)(2,1)S(1)}) custom-call(s32[33]{0:T(128)S(1)} %get-tuple-element.21.refs_0_, bf16[20,32,128]{2,1,0:T(8,128)(2,1)S(1)} %copy-done.1, bf16[20,32,128]{2,1,0:T(8,128)(2,1)S(1)} %copy-done.6, bf16[20,32,128]{2,1,0:T(8,128)(2,1)S(1)} %collective-permute-done.2.refs_3_, ...), custom_call_target="tpu_custom_call" | custom-call | flops 20000000000 | bytes 10000000 | tf_op jit(solution)/shard_map/pallas_call | solution.py:214
  120.9 3.7 %collective-permute-start.32 = (f32[4,256]{1,0:T(4,128)S(1)}, f32[4,256]{1,0:T(4,128)S(1)}, u32[]{:S(2)}, u32[]{:S(2)}) collective-permute-start(f32[4,256]{1,0:T(4,128)S(1)} %dynamic-slice_bitcast_fusion.2), channel_id=1, source_target_pairs={{0,16},{16,0},{1,17},{17,1},{2,18},{18,2},{3,19},{19,3},{4,20},{20... | collective-permute-start | bytes 12296 | tf_op jit(solution)/shard_map/ppermute | solution.py:311
  124.6 1.6 %collective-permute-done.32 = f32[4,256]{1,0:T(4,128)S(1)} collective-permute-done((f32[4,256]{1,0:T(4,128)S(1)}, f32[4,256]{1,0:T(4,128)S(1)}, u32[]{:S(2)}, u32[]{:S(2)}) %collective-permute-start.32) | collective-permute-done | bytes 4128 | tf_op jit(solution)/shard_map/ppermute | solution.py:311
  127.3 1.5 %collective-permute-start.34 = (f32[4,256]{1,0:T(4,128)S(1)}, f32[4,256]{1,0:T(4,128)S(1)}, u32[]{:S(2)}, u32[]{:S(2)}) collective-permute-start(f32[4,256]{1,0:T(4,128)S(1)} %add.66), channel_id=1, source_target_pairs={{0,2},{1,3},{2,0},{3,1},{4,6},{5,7},{6,4},{7,5},{8,10},{9,11},{10,... | collective-permute-start | bytes 12296 | tf_op jit(solution)/shard_map/ppermute | solution.py:90
  128.9 2.1 %collective-permute-done.34 = f32[4,256]{1,0:T(4,128)S(1)} collective-permute-done((f32[4,256]{1,0:T(4,128)S(1)}, f32[4,256]{1,0:T(4,128)S(1)}, u32[]{:S(2)}, u32[]{:S(2)}) %collective-permute-start.34) | collective-permute-done | bytes 4128 | tf_op jit(solution)/shard_map/ppermute | solution.py:90
  131.6 1.6 %collective-permute-start.37 = (bf16[16,8,128]{2,1,0:T(8,128)(2,1)S(1)}, bf16[16,8,128]{2,1,0:T(8,128)(2,1)S(1)}, u32[]{:S(2)}, u32[]{:S(2)}) collective-permute-start(bf16[16,8,128]{2,1,0:T(8,128)(2,1)S(1)} %dynamic-slice_bitcast_fusion.1), channel_id=1, source_target_pairs={{0,16},{16,0},{1,17},{17,1},{2,18},{18,2},{3,19},{19,3},{4,20},{20... | collective-permute-start | bytes 98312 | tf_op jit(solution)/shard_map/ppermute | solution.py:320
  134.6 1.6 %collective-permute-start.36 = (f32[4,256]{1,0:T(4,128)S(1)}, f32[4,256]{1,0:T(4,128)S(1)}, u32[]{:S(2)}, u32[]{:S(2)}) collective-permute-start(f32[4,256]{1,0:T(4,128)S(1)} %add.68), channel_id=1, source_target_pairs={{0,8},{1,9},{2,10},{3,11},{4,12},{5,13},{6,14},{7,15},{8,0},{9,1},... | collective-permute-start | bytes 12296 | tf_op jit(solution)/shard_map/ppermute | solution.py:90
  136.2 1.5 %collective-permute-start.38 = (bf16[16,8,128]{2,1,0:T(8,128)(2,1)S(1)}, bf16[16,8,128]{2,1,0:T(8,128)(2,1)S(1)}, u32[]{:S(2)}, u32[]{:S(2)}) collective-permute-start(bf16[16,8,128]{2,1,0:T(8,128)(2,1)S(1)} %dynamic-slice_bitcast_fusion), channel_id=1, source_target_pairs={{0,16},{16,0},{1,17},{17,1},{2,18},{18,2},{3,19},{19,3},{4,20},{20... | collective-permute-start | bytes 98312 | tf_op jit(solution)/shard_map/ppermute | solution.py:320
  (127 shorter events, 25.8 us)
Async XLA Ops:
  0.7 6.7 %collective-permute-start = (bf16[2,8,4096]{2,1,0:T(8,128)(2,1)}, bf16[2,8,4096]{2,1,0:T(8,128)(2,1)S(1)}, u32[]{:S(2)}, u32[]{:S(2)}) collective-permute-start(bf16[2,8,4096]{2,1,0:T(8,128)(2,1)} %own.1), channel_id=1, source_target_pairs={{0,16},{16,0},{1,17},{17,1},{2,18},{18,2},{3,19},{19,3},{4,20},{20... | collective-permute-start | bytes 393224 | tf_op jit(solution)/shard_map/ppermute | solution.py:267
  10.4 10.2 %collective-permute-start.20 = (bf16[20,32,128]{2,1,0:T(8,128)(2,1)}, bf16[20,32,128]{2,1,0:T(8,128)(2,1)S(1)}, u32[]{:S(2)}, u32[]{:S(2)}) collective-permute-start(bf16[20,32,128]{2,1,0:T(8,128)(2,1)} %get-tuple-element.9.refs_1_), channel_id=1, source_target_pairs={{0,4},{1,5},{2,6},{3,7},{4,0},{5,1},{6,2},{7,3},{8,12},{9,13},{10,... | collective-permute-start | bytes 491528 | tf_op jit(solution)/shard_map/ppermute | solution.py:90
  12.2 11.4 %collective-permute-start.24 = (bf16[20,32,128]{2,1,0:T(8,128)(2,1)}, bf16[20,32,128]{2,1,0:T(8,128)(2,1)S(1)}, u32[]{:S(2)}, u32[]{:S(2)}) collective-permute-start(bf16[20,32,128]{2,1,0:T(8,128)(2,1)} %get-tuple-element.9.refs_1_), channel_id=1, source_target_pairs={{0,8},{1,9},{2,10},{3,11},{4,12},{5,13},{6,14},{7,15},{8,0},{9,1},... | collective-permute-start | bytes 491528 | tf_op jit(solution)/shard_map/ppermute | solution.py:90
  17.4 27.9 %collective-permute-start.16 = (bf16[2,128,896]{2,1,0:T(8,128)(2,1)}, bf16[2,128,896]{2,1,0:T(8,128)(2,1)}, u32[]{:S(2)}, u32[]{:S(2)}) collective-permute-start(bf16[2,128,896]{2,1,0:T(8,128)(2,1)} %pad_maximum_fusion.1), channel_id=1, source_target_pairs={{0,16},{16,0},{1,17},{17,1},{2,18},{18,2},{3,19},{19,3},{4,20},{20... | collective-permute-start | bytes 1376264 | tf_op jit(solution)/shard_map/ppermute | solution.py:290
  18.9 7.8 %collective-permute-start.28 = (bf16[20,32,128]{2,1,0:T(8,128)(2,1)}, bf16[20,32,128]{2,1,0:T(8,128)(2,1)S(1)}, u32[]{:S(2)}, u32[]{:S(2)}) collective-permute-start(bf16[20,32,128]{2,1,0:T(8,128)(2,1)} %get-tuple-element.9.refs_1_), channel_id=1, source_target_pairs={{0,12},{1,13},{2,14},{3,15},{4,8},{5,9},{6,10},{7,11},{8,4},{9,5},... | collective-permute-start | bytes 491528 | tf_op jit(solution)/shard_map/ppermute | solution.py:90
  19.1 15.2 %collective-permute-start.18 = (bf16[20,32,128]{2,1,0:T(8,128)(2,1)}, bf16[20,32,128]{2,1,0:T(8,128)(2,1)S(1)}, u32[]{:S(2)}, u32[]{:S(2)}) collective-permute-start(bf16[20,32,128]{2,1,0:T(8,128)(2,1)} %get-tuple-element.9.refs_1_), channel_id=1, source_target_pairs={{0,2},{1,3},{2,0},{3,1},{4,6},{5,7},{6,4},{7,5},{8,10},{9,11},{10,... | collective-permute-start | bytes 491528 | tf_op jit(solution)/shard_map/ppermute | solution.py:90
  20.6 16.5 %collective-permute-start.17 = (bf16[20,32,128]{2,1,0:T(8,128)(2,1)}, bf16[20,32,128]{2,1,0:T(8,128)(2,1)S(1)}, u32[]{:S(2)}, u32[]{:S(2)}) collective-permute-start(bf16[20,32,128]{2,1,0:T(8,128)(2,1)} %get-tuple-element.9.refs_1_), channel_id=1, source_target_pairs={{0,1},{1,0},{2,3},{3,2},{4,5},{5,4},{6,7},{7,6},{8,9},{9,8},{10,11... | collective-permute-start | bytes 491528 | tf_op jit(solution)/shard_map/ppermute | solution.py:90
  23.6 15.0 %collective-permute-start.8 = (bf16[20,32,128]{2,1,0:T(8,128)(2,1)}, bf16[20,32,128]{2,1,0:T(8,128)(2,1)S(1)}, u32[]{:S(2)}, u32[]{:S(2)}) collective-permute-start(bf16[20,32,128]{2,1,0:T(8,128)(2,1)} %get-tuple-element.8.refs_1_), channel_id=1, source_target_pairs={{0,8},{1,9},{2,10},{3,11},{4,12},{5,13},{6,14},{7,15},{8,0},{9,1},... | collective-permute-start | bytes 491528 | tf_op jit(solution)/shard_map/ppermute | solution.py:90
  26.7 14.4 %collective-permute-start.12 = (bf16[20,32,128]{2,1,0:T(8,128)(2,1)S(1)}, bf16[20,32,128]{2,1,0:T(8,128)(2,1)S(1)}, u32[]{:S(2)}, u32[]{:S(2)}) collective-permute-start(bf16[20,32,128]{2,1,0:T(8,128)(2,1)S(1)} %copy-done.1), channel_id=1, source_target_pairs={{0,12},{1,13},{2,14},{3,15},{4,8},{5,9},{6,10},{7,11},{8,4},{9,5},... | collective-permute-start | bytes 491528 | tf_op jit(solution)/shard_map/ppermute | solution.py:90
  34.3 8.3 %collective-permute-start.4 = (bf16[20,32,128]{2,1,0:T(8,128)(2,1)S(1)}, bf16[20,32,128]{2,1,0:T(8,128)(2,1)}, u32[]{:S(2)}, u32[]{:S(2)}) collective-permute-start(bf16[20,32,128]{2,1,0:T(8,128)(2,1)S(1)} %copy-done.1), channel_id=1, source_target_pairs={{0,4},{1,5},{2,6},{3,7},{4,0},{5,1},{6,2},{7,3},{8,12},{9,13},{10,... | collective-permute-start | bytes 491528 | tf_op jit(solution)/shard_map/ppermute | solution.py:90
  37.1 5.6 %collective-permute-start.2 = (bf16[20,32,128]{2,1,0:T(8,128)(2,1)S(1)}, bf16[20,32,128]{2,1,0:T(8,128)(2,1)S(1)}, u32[]{:S(2)}, u32[]{:S(2)}) collective-permute-start(bf16[20,32,128]{2,1,0:T(8,128)(2,1)S(1)} %copy-done.1), channel_id=1, source_target_pairs={{0,2},{1,3},{2,0},{3,1},{4,6},{5,7},{6,4},{7,5},{8,10},{9,11},{10,... | collective-permute-start | bytes 491528 | tf_op jit(solution)/shard_map/ppermute | solution.py:90
  38.6 6.6 %collective-permute-start.1 = (bf16[20,32,128]{2,1,0:T(8,128)(2,1)S(1)}, bf16[20,32,128]{2,1,0:T(8,128)(2,1)S(1)}, u32[]{:S(2)}, u32[]{:S(2)}) collective-permute-start(bf16[20,32,128]{2,1,0:T(8,128)(2,1)S(1)} %copy-done.1), channel_id=1, source_target_pairs={{0,1},{1,0},{2,3},{3,2},{4,5},{5,4},{6,7},{7,6},{8,9},{9,8},{10,11... | collective-permute-start | bytes 491528 | tf_op jit(solution)/shard_map/ppermute | solution.py:90
  41.1 9.9 %collective-permute-start.22 = (bf16[20,32,128]{2,1,0:T(8,128)(2,1)S(1)}, bf16[20,32,128]{2,1,0:T(8,128)(2,1)S(1)}, u32[]{:S(2)}, u32[]{:S(2)}) collective-permute-start(bf16[20,32,128]{2,1,0:T(8,128)(2,1)S(1)} %collective-permute-done.20.refs_5_), channel_id=1, source_target_pairs={{0,2},{1,3},{2,0},{3,1},{4,6},{5,7},{6,4},{7,5},{8,10},{9,11},{10,... | collective-permute-start | bytes 491528 | tf_op jit(solution)/shard_map/ppermute | solution.py:90
  42.6 12.3 %collective-permute-start.21 = (bf16[20,32,128]{2,1,0:T(8,128)(2,1)S(1)}, bf16[20,32,128]{2,1,0:T(8,128)(2,1)S(1)}, u32[]{:S(2)}, u32[]{:S(2)}) collective-permute-start(bf16[20,32,128]{2,1,0:T(8,128)(2,1)S(1)} %collective-permute-done.20.refs_5_), channel_id=1, source_target_pairs={{0,1},{1,0},{2,3},{3,2},{4,5},{5,4},{6,7},{7,6},{8,9},{9,8},{10,11... | collective-permute-start | bytes 491528 | tf_op jit(solution)/shard_map/ppermute | solution.py:90
  42.7 8.6 %collective-permute-start.26 = (bf16[20,32,128]{2,1,0:T(8,128)(2,1)S(1)}, bf16[20,32,128]{2,1,0:T(8,128)(2,1)S(1)}, u32[]{:S(2)}, u32[]{:S(2)}) collective-permute-start(bf16[20,32,128]{2,1,0:T(8,128)(2,1)S(1)} %collective-permute-done.24.refs_9_), channel_id=1, source_target_pairs={{0,2},{1,3},{2,0},{3,1},{4,6},{5,7},{6,4},{7,5},{8,10},{9,11},{10,... | collective-permute-start | bytes 491528 | tf_op jit(solution)/shard_map/ppermute | solution.py:90
  45.2 10.2 %collective-permute-start.25 = (bf16[20,32,128]{2,1,0:T(8,128)(2,1)S(1)}, bf16[20,32,128]{2,1,0:T(8,128)(2,1)S(1)}, u32[]{:S(2)}, u32[]{:S(2)}) collective-permute-start(bf16[20,32,128]{2,1,0:T(8,128)(2,1)S(1)} %collective-permute-done.24.refs_9_), channel_id=1, source_target_pairs={{0,1},{1,0},{2,3},{3,2},{4,5},{5,4},{6,7},{7,6},{8,9},{9,8},{10,11... | collective-permute-start | bytes 491528 | tf_op jit(solution)/shard_map/ppermute | solution.py:90
  45.3 8.2 %collective-permute-start.30 = (bf16[20,32,128]{2,1,0:T(8,128)(2,1)S(1)}, bf16[20,32,128]{2,1,0:T(8,128)(2,1)S(1)}, u32[]{:S(2)}, u32[]{:S(2)}) collective-permute-start(bf16[20,32,128]{2,1,0:T(8,128)(2,1)S(1)} %collective-permute-done.28.refs_13_), channel_id=1, source_target_pairs={{0,2},{1,3},{2,0},{3,1},{4,6},{5,7},{6,4},{7,5},{8,10},{9,11},{10,... | collective-permute-start | bytes 491528 | tf_op jit(solution)/shard_map/ppermute | solution.py:90
  51.0 10.9 %collective-permute-start.29 = (bf16[20,32,128]{2,1,0:T(8,128)(2,1)S(1)}, bf16[20,32,128]{2,1,0:T(8,128)(2,1)}, u32[]{:S(2)}, u32[]{:S(2)}) collective-permute-start(bf16[20,32,128]{2,1,0:T(8,128)(2,1)S(1)} %collective-permute-done.28.refs_13_), channel_id=1, source_target_pairs={{0,1},{1,0},{2,3},{3,2},{4,5},{5,4},{6,7},{7,6},{8,9},{9,8},{10,11... | collective-permute-start | bytes 491528 | tf_op jit(solution)/shard_map/ppermute | solution.py:90
  51.4 10.6 %collective-permute-start.19 = (bf16[20,32,128]{2,1,0:T(8,128)(2,1)S(1)}, bf16[20,32,128]{2,1,0:T(8,128)(2,1)}, u32[]{:S(2)}, u32[]{:S(2)}) collective-permute-start(bf16[20,32,128]{2,1,0:T(8,128)(2,1)S(1)} %collective-permute-done.18.refs_3_), channel_id=1, source_target_pairs={{0,1},{1,0},{2,3},{3,2},{4,5},{5,4},{6,7},{7,6},{8,9},{9,8},{10,11... | collective-permute-start | bytes 491528 | tf_op jit(solution)/shard_map/ppermute | solution.py:90
  53.4 9.0 %collective-permute-start.10 = (bf16[20,32,128]{2,1,0:T(8,128)(2,1)S(1)}, bf16[20,32,128]{2,1,0:T(8,128)(2,1)}, u32[]{:S(2)}, u32[]{:S(2)}) collective-permute-start(bf16[20,32,128]{2,1,0:T(8,128)(2,1)S(1)} %collective-permute-done.8.refs_9_), channel_id=1, source_target_pairs={{0,2},{1,3},{2,0},{3,1},{4,6},{5,7},{6,4},{7,5},{8,10},{9,11},{10,... | collective-permute-start | bytes 491528 | tf_op jit(solution)/shard_map/ppermute | solution.py:90
  55.0 9.2 %collective-permute-start.14 = (bf16[20,32,128]{2,1,0:T(8,128)(2,1)S(1)}, bf16[20,32,128]{2,1,0:T(8,128)(2,1)}, u32[]{:S(2)}, u32[]{:S(2)}) collective-permute-start(bf16[20,32,128]{2,1,0:T(8,128)(2,1)S(1)} %collective-permute-done.12.refs_13_), channel_id=1, source_target_pairs={{0,2},{1,3},{2,0},{3,1},{4,6},{5,7},{6,4},{7,5},{8,10},{9,11},{10,... | collective-permute-start | bytes 491528 | tf_op jit(solution)/shard_map/ppermute | solution.py:90
  55.5 10.7 %collective-permute-start.6 = (bf16[20,32,128]{2,1,0:T(8,128)(2,1)}, bf16[20,32,128]{2,1,0:T(8,128)(2,1)}, u32[]{:S(2)}, u32[]{:S(2)}) collective-permute-start(bf16[20,32,128]{2,1,0:T(8,128)(2,1)} %collective-permute-done.4.refs_5_), channel_id=1, source_target_pairs={{0,2},{1,3},{2,0},{3,1},{4,6},{5,7},{6,4},{7,5},{8,10},{9,11},{10,... | collective-permute-start | bytes 491528 | tf_op jit(solution)/shard_map/ppermute | solution.py:90
  62.0 4.8 %collective-permute-start.5 = (bf16[20,32,128]{2,1,0:T(8,128)(2,1)}, bf16[20,32,128]{2,1,0:T(8,128)(2,1)S(1)}, u32[]{:S(2)}, u32[]{:S(2)}) collective-permute-start(bf16[20,32,128]{2,1,0:T(8,128)(2,1)} %collective-permute-done.4.refs_5_), channel_id=1, source_target_pairs={{0,1},{1,0},{2,3},{3,2},{4,5},{5,4},{6,7},{7,6},{8,9},{9,8},{10,11... | collective-permute-start | bytes 491528 | tf_op jit(solution)/shard_map/ppermute | solution.py:90
  62.5 4.4 %collective-permute-start.23 = (bf16[20,32,128]{2,1,0:T(8,128)(2,1)}, bf16[20,32,128]{2,1,0:T(8,128)(2,1)S(1)}, u32[]{:S(2)}, u32[]{:S(2)}) collective-permute-start(bf16[20,32,128]{2,1,0:T(8,128)(2,1)} %copy-done.7), channel_id=1, source_target_pairs={{0,1},{1,0},{2,3},{3,2},{4,5},{5,4},{6,7},{7,6},{8,9},{9,8},{10,11... | collective-permute-start | bytes 491528 | tf_op jit(solution)/shard_map/ppermute | solution.py:90
  66.2 31.0 %collective-permute-start.9 = (bf16[20,32,128]{2,1,0:T(8,128)(2,1)S(1)}, bf16[20,32,128]{2,1,0:T(8,128)(2,1)S(1)}, u32[]{:S(2)}, u32[]{:S(2)}) collective-permute-start(bf16[20,32,128]{2,1,0:T(8,128)(2,1)S(1)} %collective-permute-done.8.refs_9_), channel_id=1, source_target_pairs={{0,1},{1,0},{2,3},{3,2},{4,5},{5,4},{6,7},{7,6},{8,9},{9,8},{10,11... | collective-permute-start | bytes 491528 | tf_op jit(solution)/shard_map/ppermute | solution.py:90
  66.8 30.5 %collective-permute-start.3 = (bf16[20,32,128]{2,1,0:T(8,128)(2,1)S(1)}, bf16[20,32,128]{2,1,0:T(8,128)(2,1)S(1)}, u32[]{:S(2)}, u32[]{:S(2)}) collective-permute-start(bf16[20,32,128]{2,1,0:T(8,128)(2,1)S(1)} %collective-permute-done.2.refs_3_), channel_id=1, source_target_pairs={{0,1},{1,0},{2,3},{3,2},{4,5},{5,4},{6,7},{7,6},{8,9},{9,8},{10,11... | collective-permute-start | bytes 491528 | tf_op jit(solution)/shard_map/ppermute | solution.py:90
  66.8 30.4 %collective-permute-start.11 = (bf16[20,32,128]{2,1,0:T(8,128)(2,1)}, bf16[20,32,128]{2,1,0:T(8,128)(2,1)S(1)}, u32[]{:S(2)}, u32[]{:S(2)}) collective-permute-start(bf16[20,32,128]{2,1,0:T(8,128)(2,1)} %collective-permute-done.10.refs_11_), channel_id=1, source_target_pairs={{0,1},{1,0},{2,3},{3,2},{4,5},{5,4},{6,7},{7,6},{8,9},{9,8},{10,11... | collective-permute-start | bytes 491528 | tf_op jit(solution)/shard_map/ppermute | solution.py:90
  67.3 30.0 %collective-permute-start.15 = (bf16[20,32,128]{2,1,0:T(8,128)(2,1)}, bf16[20,32,128]{2,1,0:T(8,128)(2,1)S(1)}, u32[]{:S(2)}, u32[]{:S(2)}) collective-permute-start(bf16[20,32,128]{2,1,0:T(8,128)(2,1)} %collective-permute-done.14.refs_15_), channel_id=1, source_target_pairs={{0,1},{1,0},{2,3},{3,2},{4,5},{5,4},{6,7},{7,6},{8,9},{9,8},{10,11... | collective-permute-start | bytes 491528 | tf_op jit(solution)/shard_map/ppermute | solution.py:90
  67.8 29.5 %collective-permute-start.7 = (bf16[20,32,128]{2,1,0:T(8,128)(2,1)}, bf16[20,32,128]{2,1,0:T(8,128)(2,1)S(1)}, u32[]{:S(2)}, u32[]{:S(2)}) collective-permute-start(bf16[20,32,128]{2,1,0:T(8,128)(2,1)} %collective-permute-done.6.refs_7_), channel_id=1, source_target_pairs={{0,1},{1,0},{2,3},{3,2},{4,5},{5,4},{6,7},{7,6},{8,9},{9,8},{10,11... | collective-permute-start | bytes 491528 | tf_op jit(solution)/shard_map/ppermute | solution.py:90
  120.9 5.2 %collective-permute-start.32 = (f32[4,256]{1,0:T(4,128)S(1)}, f32[4,256]{1,0:T(4,128)S(1)}, u32[]{:S(2)}, u32[]{:S(2)}) collective-permute-start(f32[4,256]{1,0:T(4,128)S(1)} %dynamic-slice_bitcast_fusion.2), channel_id=1, source_target_pairs={{0,16},{16,0},{1,17},{17,1},{2,18},{18,2},{3,19},{19,3},{4,20},{20... | collective-permute-start | bytes 12296 | tf_op jit(solution)/shard_map/ppermute | solution.py:311
  131.6 8.2 %collective-permute-start.37 = (bf16[16,8,128]{2,1,0:T(8,128)(2,1)S(1)}, bf16[16,8,128]{2,1,0:T(8,128)(2,1)S(1)}, u32[]{:S(2)}, u32[]{:S(2)}) collective-permute-start(bf16[16,8,128]{2,1,0:T(8,128)(2,1)S(1)} %dynamic-slice_bitcast_fusion.1), channel_id=1, source_target_pairs={{0,16},{16,0},{1,17},{17,1},{2,18},{18,2},{3,19},{19,3},{4,20},{20... | collective-permute-start | bytes 98312 | tf_op jit(solution)/shard_map/ppermute | solution.py:320
  134.6 4.5 %collective-permute-start.36 = (f32[4,256]{1,0:T(4,128)S(1)}, f32[4,256]{1,0:T(4,128)S(1)}, u32[]{:S(2)}, u32[]{:S(2)}) collective-permute-start(f32[4,256]{1,0:T(4,128)S(1)} %add.68), channel_id=1, source_target_pairs={{0,8},{1,9},{2,10},{3,11},{4,12},{5,13},{6,14},{7,15},{8,0},{9,1},... | collective-permute-start | bytes 12296 | tf_op jit(solution)/shard_map/ppermute | solution.py:90
  (28 other events, 211.9 us)

commit v3 on v2

--- a/solution.py
+++ b/solution.py
@@ -111,47 +111,81 @@
         unit[NQ:] = basis[2 * x + wave].reshape(4, 32, TILE_A)
 
 
-def score_kernel(wave, info, *refs):
+def prepare_kernel(info, own, other, query, block, block_t, grads, query_grads):
+    x = info[0]
+    for layer in range(LAYERS):
+        for c in range(block.shape[1]):
+            cols = slice(c * TILE_A, (c + 1) * TILE_A)
+            tile = block[layer, c]
+            mine = jnp.dot(own[layer, :, cols], tile, preferred_element_type=jnp.float32)
+            came = jnp.dot(other[layer, :, cols], tile, preferred_element_type=jnp.float32)
+            first = jnp.where(x == 0, mine, came).reshape(NQ, 1, 8, TILE_A)
+            second = jnp.where(x == 0, came, mine).reshape(NQ, 1, 8, TILE_A)
+            rows = jnp.concatenate([first, second], axis=1).reshape(TOKENS, TILE_A)
+            grads[layer, :, cols] = rows.astype(BF)
+            query_grads[layer, cols, :] = across(block_t[layer, c], query[layer, :, cols]).astype(BF)
+
+
+def across(left, right):
+    return lax.dot_general(
+        left, right, (((1,), (1,)), ((), ())), preferred_element_type=jnp.float32
+    )
+
+
+def score_kernel(base, count, info, *refs):
     units = refs[:NQ]
     grads, query_grads, codes, eigen, before, totals, own_rows = refs[NQ : NQ + 7]
     held, turned_rows, train_t, query_t, eig, scaled0, scaled1, weights, acc = refs[NQ + 7 : NQ + 16]
     unit_sems, eig_sems = refs[NQ + 16 :]
     scaled = (scaled0, scaled1)
     me = info[0]
-    copies = [
-        pltpu.make_async_copy(units[d], held.at[me ^ d], unit_sems.at[d]) for d in range(NQ)
-    ]
+    start = base % NQ
+    wave = base // NQ
+    copies = []
+    for d in range(NQ):
+        unit, which = units[d]
+        source = unit if which is None else unit.at[which]
+        into = held.at[me ^ d]
+        copies.append(
+            pltpu.make_async_copy(
+                source.at[pl.ds(start, count)], into.at[pl.ds(0, count)], unit_sems.at[d]
+            )
+        )
+        copies.append(
+            pltpu.make_async_copy(
+                source.at[pl.ds(NQ, 4)], into.at[pl.ds(NQ, 4)], unit_sems.at[NQ + d]
+            )
+        )
     for copy in copies:
         copy.start()
 
     def eig_copy(n):
-        tile = info[1 + wave * NQ + n]
+        tile = info[1 + base + n]
         cols = pl.ds(pl.multiple_of((tile % 32) * TILE_A, TILE_A), TILE_A)
         return pltpu.make_async_copy(eigen.at[tile // 32, :, cols], eig.at[n], eig_sems.at[n])
 
-    for n in range(NQ):
+    for n in range(count):
         eig_copy(n).start()
     acc[...] = jnp.zeros_like(acc)
     for copy in copies:
         copy.wait()
 
-    @pl.loop(0, NQ)
-    def _(n):
-        basis = held[n, NQ:].reshape(TILE_A, TILE_A)
+    def rotate(n):
+        basis = held[start + n, NQ:].reshape(TILE_A, TILE_A)
+        basis_t = basis.astype(jnp.float32).T.astype(BF)
         tile = held[:, n]
         train = tile[:, :16].reshape(TOKENS, TILE_A)
         query = tile[:, 16:].reshape(TOKENS, TILE_A)
-        turned = jnp.dot(train, basis, preferred_element_type=jnp.float32)
-        turned_rows[...] = turned.astype(BF)
-        own_rows[n] = turned_rows[pl.ds(pl.multiple_of(me * 16, 16), 16), :]
-        train_t[n] = turned.T.astype(BF)
-        query_t[n] = jnp.dot(query, basis, preferred_element_type=jnp.float32).T.astype(BF)
+        mine = held[me, n, :16]
+        own_rows[n] = jnp.dot(mine, basis, preferred_element_type=jnp.float32).astype(BF)
+        train_t[n] = across(basis_t, train).astype(BF)
+        query_t[n] = across(basis_t, query).astype(BF)
 
     def weigh(n, k):
         weights[k] = 1.0 / (eig[n].T + damping)
 
     def gram(n, k):
-        layer = info[1 + wave * NQ + n] // 32
+        layer = info[1 + base + n] // 32
         code = codes[...]
         rows = train_t[n]
         zero = jnp.zeros_like(rows)
@@ -166,7 +200,7 @@
                 scaled[k][h * 512 : (h + 1) * 512, cols] = part.astype(BF).reshape(512, 256)
 
     def project(n, k):
-        layer = info[1 + wave * NQ + n] // 32
+        layer = info[1 + base + n] // 32
         query = query_t[n].astype(jnp.float32)
         for h in range(2):
             part = jnp.dot(
@@ -177,78 +211,76 @@
             part = part.reshape(4, TILE_A, TOKENS) * query[None]
             acc[4 * h : 4 * h + 4] += jnp.sum(part.reshape(4, TILE_A // 8, 8, TOKENS), axis=1)
 
+    rotate(0)
+    rotate(1)
     eig_copy(0).wait()
     weigh(0, 0)
     eig_copy(1).wait()
     weigh(1, 1)
     gram(0, 0)
 
-    @pl.loop(0, NQ - 2, step=2)
+    @pl.loop(0, count - 2, step=2)
     def _(n):
         eig_copy(n + 2).wait()
         eig_copy(n + 3).wait()
         gram(n + 1, 1)
+        rotate(n + 2)
         project(n, 0)
         weigh(n + 2, 0)
         gram(n + 2, 0)
+        rotate(n + 3)
         project(n + 1, 1)
         weigh(n + 3, 1)
 
-    gram(NQ - 1, 1)
-    project(NQ - 2, 0)
-    project(NQ - 1, 1)
+    gram(count - 1, 1)
+    project(count - 2, 0)
+    project(count - 1, 1)
     totals[...] = before[...] + jnp.sum(acc[...], axis=1)
 
 
 VMEM = pl.BlockSpec(memory_space=pltpu.VMEM)
 SMEM = pl.BlockSpec(memory_space=pltpu.SMEM)
-ANY = pl.BlockSpec(memory_space=pl.ANY)
-
-
-def score_wave(wave, info, units, grads, query_grads, codes, eigenvalues, before):
+HBM = pl.BlockSpec(memory_space=pltpu.HBM)
+
+
+def score_tiles(base, count, info, arrays, places, grads, query_grads, codes, eigenvalues, before):
     width = grads.shape[2]
 
-    def kernel(*refs):
-        score_kernel(wave, *refs)
+    def kernel(info_ref, *refs):
+        held = refs[: len(arrays)]
+        units = [(held[a], which) for a, which in places]
+        score_kernel(base, count, info_ref, *units, *refs[len(arrays) :])
 
     return pl.pallas_call(
         kernel,
-        in_specs=[SMEM] + [ANY] * NQ + [VMEM, VMEM, VMEM, ANY, VMEM],
+        in_specs=[SMEM] + [HBM] * len(arrays) + [VMEM, VMEM, VMEM, HBM, VMEM],
         out_specs=[VMEM, VMEM],
         out_shape=[
             jax.ShapeDtypeStruct((GROUPS, TOKENS), jnp.float32),
-            jax.ShapeDtypeStruct((NQ, 16, TILE_A), BF),
+            jax.ShapeDtypeStruct((count, 16, TILE_A), BF),
         ],
         scratch_shapes=[
             pltpu.VMEM((NQ, UNIT, 32, TILE_A), BF),
             pltpu.VMEM((TOKENS, TILE_A), BF),
-            pltpu.VMEM((NQ, TILE_A, TOKENS), BF),
-            pltpu.VMEM((NQ, TILE_A, TOKENS), BF),
-            pltpu.VMEM((NQ, width, TILE_A), jnp.float32),
+            pltpu.VMEM((count, TILE_A, TOKENS), BF),
+            pltpu.VMEM((count, TILE_A, TOKENS), BF),
+            pltpu.VMEM((count, width, TILE_A), jnp.float32),
             pltpu.VMEM((GROUPS * TILE_A, width), BF),
             pltpu.VMEM((GROUPS * TILE_A, width), BF),
             pltpu.VMEM((2, TILE_A, width), jnp.float32),
             pltpu.VMEM((GROUPS, 8, TOKENS), jnp.float32),
-            pltpu.SemaphoreType.DMA((NQ,)),
-            pltpu.SemaphoreType.DMA((NQ,)),
+            pltpu.SemaphoreType.DMA((2 * NQ,)),
+            pltpu.SemaphoreType.DMA((count,)),
         ],
-        compiler_params=pltpu.CompilerParams(vmem_limit_bytes=40 * 1024 * 1024),
+        compiler_params=pltpu.CompilerParams(vmem_limit_bytes=62 * 1024 * 1024),
         cost_estimate=pl.CostEstimate(
-            flops=20 * 10**9, bytes_accessed=10 * 10**6, transcendentals=0
+            flops=count * 10**9, bytes_accessed=count * 10**6 // 2, transcendentals=0
         ),
-    )(info, *units, grads, query_grads, codes, eigenvalues, before)
-
-
-def gather_units(unit):
-    units = [None] * NQ
-    units[0] = unit
-    for d in (4, 12, 8):
-        units[d] = hop(unit, d)
-    for d in (0, 4, 12, 8):
-        units[d ^ 2] = hop(units[d], 2)
-    for d in (0, 2, 4, 6, 12, 14, 8, 10):
-        units[d ^ 1] = hop(units[d], 1)
-    return units
+    )(info, *arrays, grads, query_grads, codes, eigenvalues, before)
+
+
+def after(value, *others):
+    return lax.optimization_barrier((value, *others))[0]
 
 
 def paired_body(
@@ -269,41 +301,69 @@
     tile_of = jnp.sum(jnp.where(slot_list[None, :] == ids[:, None], ids[None, :], 0), axis=1)
     mine = lax.dynamic_index_in_dim(tile_of.reshape(NQ, 2, WAVES), x, 1, False)
     mine = mine.T.reshape(WAVES * NQ)
+    side = x.reshape(1).astype(jnp.int32)
 
     packed = pl.pallas_call(
         pack_kernel,
         in_specs=[SMEM, VMEM, VMEM, VMEM, VMEM],
         out_specs=[VMEM] * WAVES,
         out_shape=[jax.ShapeDtypeStruct((UNIT, 32, TILE_A), BF)] * WAVES,
-    )(
-        jnp.concatenate([x.reshape(1).astype(jnp.int32), mine]),
-        train_inputs,
-        train_other,
-        query_inputs,
-        input_basis,
-    )
-    waves = [gather_units(unit) for unit in packed]
-
+    )(jnp.concatenate([side, mine]), train_inputs, train_other, query_inputs, input_basis)
+
+    units = [None] * NQ
+    units[0] = packed[0]
+    for d in (4, 12, 8):
+        units[d] = hop(packed[0], d)
+    for d in (0, 4, 12, 8):
+        units[d ^ 2] = hop(units[d], 2)
+    for d in (0, 2, 4, 6, 12, 14, 8, 10):
+        units[d ^ 1] = hop(units[d], 1)
+    places0 = [(d, None) for d in range(NQ)]
+
+    ids_other = lax.ppermute(sequence_ids, "parts", SWAP)
+    out_other = lax.ppermute(after(train_outgrads, packed[0]), "parts", SWAP)
+    id_pair = jnp.where(
+        x == 0, jnp.stack([sequence_ids, ids_other]), jnp.stack([ids_other, sequence_ids])
+    )
+    id_pair = id_pair + SEQS * jnp.arange(2, dtype=jnp.int32)[:, None]
+    codes = id_pair.reshape(2, NQ, 8).transpose(1, 0, 2).reshape(1, TOKENS)
     slab = train_outgrads.shape[2]
-    id_block = jnp.broadcast_to(sequence_ids.astype(BF)[None, :, None], (LAYERS, 128, TILE_A))
-    sent = jnp.concatenate([train_outgrads, id_block], axis=2)
-    other = lax.ppermute(sent, "parts", SWAP)
-    both = jnp.stack(
-        [jnp.where(x == 0, sent, other), jnp.where(x == 0, other, sent)], axis=0
-    ).reshape(2, LAYERS, NQ, 8, slab + TILE_A)
-    both = both.transpose(1, 2, 0, 3, 4).reshape(LAYERS, TOKENS, slab + TILE_A)
-    part_of = (jnp.arange(TOKENS, dtype=jnp.int32) // 8) % 2
-    codes = (both[0, :, slab].astype(jnp.int32) + SEQS * part_of).reshape(1, TOKENS)
-    grads_rot = rotate_blocks(both[:, :, :slab], output_basis, TILE_S)
-    query_rot = rotate_blocks(query_outgrads, output_basis, TILE_S).transpose(0, 2, 1)
+    pairs = output_basis.reshape(LAYERS, slab // TILE_A, 2, TILE_S, TILE_S)
+    blank = jnp.zeros_like(pairs[:, :, 0])
+    block = jnp.concatenate(
+        [
+            jnp.concatenate([pairs[:, :, 0], blank], axis=3),
+            jnp.concatenate([blank, pairs[:, :, 1]], axis=3),
+        ],
+        axis=2,
+    )
+    grads, query_grads = pl.pallas_call(
+        prepare_kernel,
+        in_specs=[SMEM] + [VMEM] * 5,
+        out_specs=[VMEM, VMEM],
+        out_shape=[
+            jax.ShapeDtypeStruct((LAYERS, TOKENS, slab), BF),
+            jax.ShapeDtypeStruct((LAYERS, slab, TOKENS), BF),
+        ],
+    )(side, train_outgrads, out_other, query_outgrads, block, block.transpose(0, 1, 3, 2))
 
     info = jnp.concatenate([me.reshape(1).astype(jnp.int32), mine])
-    totals = jnp.zeros((GROUPS, TOKENS), jnp.float32)
-    own_rows = [None] * WAVES
-    for wave in range(WAVES):
-        totals, own_rows[wave] = score_wave(
-            wave, info, waves[wave], grads_rot, query_rot, codes, eigenvalues, totals
-        )
+    zero = jnp.zeros((GROUPS, TOKENS), jnp.float32)
+    common = (grads, query_grads, codes, eigenvalues)
+    part0, rows0 = score_tiles(0, 8, info, units, places0, *common, zero)
+
+    second = after(packed[1], units[8])
+    along = [second] + [hop(second, d) for d in (4, 12, 8)]
+    line = jnp.stack(lax.optimization_barrier((*along, part0))[:4])
+    beside = hop(line, 2)
+    part1, rows1 = score_tiles(8, 8, info, units, places0, *common, part0)
+    beside = after(beside, part1)
+    line_core, beside_core = hop(line, 1), hop(beside, 1)
+    order = {0: 0, 4: 1, 12: 2, 8: 3}
+    places1 = [((d & 2) // 2 + 2 * (d & 1), order[d & 12]) for d in range(NQ)]
+    totals, rows2 = score_tiles(
+        16, 16, info, [line, beside, line_core, beside_core], places1, *common, part1
+    )
 
     halves = totals.reshape(2, SEQS, TOKENS)
     keep = lax.dynamic_index_in_dim(halves, x, 0, False)
@@ -314,8 +374,8 @@
     scores = jnp.sum(total.reshape(SEQS, QUERIES, QLEN), axis=2).T
 
     slots = [None] * 4
-    for wave in range(WAVES):
-        pair = own_rows[wave].reshape(NQ, 2, 8, TILE_A)
+    for wave, rows in enumerate((jnp.concatenate([rows0, rows1], axis=0), rows2)):
+        pair = rows.reshape(NQ, 2, 8, TILE_A)
         kept = lax.dynamic_index_in_dim(pair, x, 1, False)
         came = lax.ppermute(lax.dynamic_index_in_dim(pair, 1 - x, 1, False), "parts", SWAP)
         slots[wave] = jnp.where(x == 0, kept, came)

time: 142 us -> 124 us (0.87)
  starting transfers between devices: 43.3 us -> 26.5 us
  waiting for transfers between devices: 23.7 us -> 30.1 us
  local copies, waits for them, and re-layouts: 13.8 us -> 8.93 us
  Pallas kernels: 49.8 us -> 53.4 us
  other arithmetic: 6.97 us -> 4.08 us
  matrix products: 2.88 us -> 0 us
    ppermute x34 -> x25, starting transfers between devices: 32.1 us -> 18.8 us  [hop(): return lax.ppermute(value, 'query', [(i, i ^ bits) for i in range(NQ)])]
    unnamed x43 -> x44, local copies, waits for them, and re-layouts: 7.42 us -> 1.71 us
    ppermute x34 -> x25, waiting for transfers between devices: 19.9 us -> 24.6 us  [hop(): return lax.ppermute(value, 'query', [(i, i ^ bits) for i in range(NQ)])]
    pallas_call x2 -> x4, Pallas kernels: 47.4 us -> 51.1 us  [the longest x3 47.7 us: score_tiles(): pl.pallas_call(kernel, in_specs=[SMEM] + [HBM] * len(arrays) + [VMEM, VME...]
    ppermute x1, starting transfers between devices: 3.67 us -> 0.54 us  [paired_body(): total = keep + lax.ppermute(give, 'parts', SWAP)]
    dot_general x2 -> x0, matrix products: 2.88 us -> none  [rotate_blocks(): jnp.einsum('lrbi,lbij->lrbj', blocks, shaped, preferred_element_type=jnp....]
    slice x2 -> x1, local copies, waits for them, and re-layouts: 3.22 us -> 1.05 us  [paired_body(): pairs[:, :, 0]]
    ppermute x2, starting transfers between devices: 3.11 us -> 1.15 us  [paired_body(): lax.ppermute(lax.dynamic_index_in_dim(pair, 1 - x, 1, False), 'parts', SWAP)]
  transfers between devices with their start and end apart: 39 -> 31, of which waited for: 15 -> 13; matrix products, arithmetic and copies ran while one was open for 11% -> 7% of each run, Pallas kernels for 17% -> 23%
where the time goes in v3:
time: 124 us
  Pallas kernels  53.4 us (43%)
  waiting for transfers between devices  30.1 us (24%)
  starting transfers between devices  26.5 us (21%)
  local copies, waits for them, and re-layouts  8.93 us (7%)
  other arithmetic  4.08 us (3%)
    pallas_call x3, Pallas kernels, score_tiles(): pl.pallas_call(kernel, in_specs=[SMEM] + [HBM] * len(arrays) + [VMEM, VME...  47.7 us
    ppermute x25, waiting for transfers between devices, hop(): return lax.ppermute(value, 'query', [(i, i ^ bits) for i in range(NQ)])  24.6 us
    ppermute x25, starting transfers between devices, hop(): return lax.ppermute(value, 'query', [(i, i ^ bits) for i in range(NQ)])  18.8 us
    pallas_call x1, Pallas kernels, paired_body(): pl.pallas_call(prepare_kernel, in_specs=[SMEM] + [VMEM] * 5, out_specs=[V...  3.31 us
    ppermute x1, waiting for transfers between devices, paired_body(): total = keep + lax.ppermute(give, 'parts', SWAP)  3.06 us
    ppermute x1, starting transfers between devices, paired_body(): train_other = lax.ppermute(train_inputs, 'parts', SWAP)  3 us
  transfers between devices with their start and end apart: 31, of which 13 were waited for; matrix products, arithmetic and copies ran while one was open for 7% of the time, Pallas kernels for 23%

profile of v3, /device:TPU:0, one launch (start us, length us, event | category | flops | bytes accessed | tf_op | source)
XLA Modules:
  0.0 123.9 jit_solution(9347380496412538246)
XLA Ops:
  0.6 3.0 %collective-permute-start = (bf16[2,8,4096]{2,1,0:T(8,128)(2,1)}, bf16[2,8,4096]{2,1,0:T(8,128)(2,1)S(1)}, u32[]{:S(2)}, u32[]{:S(2)}) collective-permute-start(bf16[2,8,4096]{2,1,0:T(8,128)(2,1)} %own.2), channel_id=1, source_target_pairs={{0,16},{16,0},{1,17},{17,1},{2,18},{18,2},{3,19},{19,3},{4,20},{20... | collective-permute-start | bytes 393224 | tf_op jit(solution)/shard_map/ppermute | solution.py:299
  5.4 2.0 %collective-permute-done.other = bf16[2,8,4096]{2,1,0:T(8,128)(2,1)S(1)} collective-permute-done((bf16[2,8,4096]{2,1,0:T(8,128)(2,1)}, bf16[2,8,4096]{2,1,0:T(8,128)(2,1)S(1)}, u32[]{:S(2)}, u32[]{:S(2)}) %collective-permute-start) | collective-permute-done | bytes 131104 | tf_op jit(solution)/shard_map/ppermute | solution.py:299
  8.0 2.4 %shard_map.104 = (bf16[20,32,128]{2,1,0:T(8,128)(2,1)}, bf16[20,32,128]{2,1,0:T(8,128)(2,1)}) custom-call(s32[33]{0:T(128)} %get-tuple-element.44.info, bf16[2,8,4096]{2,1,0:T(8,128)(2,1)} %own.2, bf16[2,8,4096]{2,1,0:T(8,128)(2,1)} %copy-done.3, bf16[2,16,4096]{2,1,0:T(8,128)(2,1)} %query.2, bf16[4,128,128]{2,1,0:T(8,128)(2,1)} %basis.1), custom_call_target="tpu_custom_call" | custom-call | tf_op jit(solution)/shard_map/pallas_call | solution.py:306
  10.4 2.8 %collective-permute-start.1 = (bf16[20,32,128]{2,1,0:T(8,128)(2,1)}, bf16[20,32,128]{2,1,0:T(8,128)(2,1)S(1)}, u32[]{:S(2)}, u32[]{:S(2)}) collective-permute-start(bf16[20,32,128]{2,1,0:T(8,128)(2,1)} %get-tuple-element.20.refs_0_), channel_id=1, source_target_pairs={{0,8},{1,9},{2,10},{3,11},{4,12},{5,13},{6,14},{7,15},{8,0},{9,1},... | collective-permute-start | bytes 491528 | tf_op jit(solution)/shard_map/ppermute | solution.py:90
  13.2 1.6 %collective-permute-start.8 = (bf16[20,32,128]{2,1,0:T(8,128)(2,1)}, bf16[20,32,128]{2,1,0:T(8,128)(2,1)S(1)}, u32[]{:S(2)}, u32[]{:S(2)}) collective-permute-start(bf16[20,32,128]{2,1,0:T(8,128)(2,1)} %get-tuple-element.20.refs_0_), channel_id=1, source_target_pairs={{0,4},{1,5},{2,6},{3,7},{4,0},{5,1},{6,2},{7,3},{8,12},{9,13},{10,... | collective-permute-start | bytes 491528 | tf_op jit(solution)/shard_map/ppermute | solution.py:90
  14.8 1.5 %collective-permute-start.20 = (s32[128]{0:T(128)}, s32[128]{0:T(128)S(1)}, u32[]{:S(2)}, u32[]{:S(2)}) collective-permute-start(s32[128]{0:T(128)} %param.11), channel_id=1, source_target_pairs={{0,16},{16,0},{1,17},{17,1},{2,18},{18,2},{3,19},{19,3},{4,20},{20... | collective-permute-start | bytes 1544 | tf_op jit(solution)/shard_map/ppermute | solution.py:323
  16.5 1.5 %collective-permute-start.6 = (bf16[20,32,128]{2,1,0:T(8,128)(2,1)}, bf16[20,32,128]{2,1,0:T(8,128)(2,1)S(1)}, u32[]{:S(2)}, u32[]{:S(2)}) collective-permute-start(bf16[20,32,128]{2,1,0:T(8,128)(2,1)} %get-tuple-element.20.refs_0_), channel_id=1, source_target_pairs={{0,2},{1,3},{2,0},{3,1},{4,6},{5,7},{6,4},{7,5},{8,10},{9,11},{10,... | collective-permute-start | bytes 491528 | tf_op jit(solution)/shard_map/ppermute | solution.py:90
  18.5 6.5 %collective-permute-done.1.refs_8_ = bf16[20,32,128]{2,1,0:T(8,128)(2,1)S(1)} collective-permute-done((bf16[20,32,128]{2,1,0:T(8,128)(2,1)}, bf16[20,32,128]{2,1,0:T(8,128)(2,1)S(1)}, u32[]{:S(2)}, u32[]{:S(2)}) %collective-permute-start.1) | collective-permute-done | bytes 163872 | tf_op jit(solution)/shard_map/ppermute | solution.py:90
  25.0 1.5 %collective-permute-start.19 = (bf16[2,128,768]{2,1,0:T(8,128)(2,1)}, bf16[2,128,768]{2,1,0:T(8,128)(2,1)S(1)}, u32[]{:S(2)}, u32[]{:S(2)}) collective-permute-start(bf16[2,128,768]{2,1,0:T(8,128)(2,1)} %own.3), channel_id=1, source_target_pairs={{0,16},{16,0},{1,17},{17,1},{2,18},{18,2},{3,19},{19,3},{4,20},{20... | collective-permute-start | bytes 1179656 | tf_op jit(solution)/shard_map/ppermute | solution.py:324
  26.5 1.5 %collective-permute-start.13 = (bf16[20,32,128]{2,1,0:T(8,128)(2,1)S(1)}, bf16[20,32,128]{2,1,0:T(8,128)(2,1)S(1)}, u32[]{:S(2)}, u32[]{:S(2)}) collective-permute-start(bf16[20,32,128]{2,1,0:T(8,128)(2,1)S(1)} %collective-permute-done.1.refs_8_), channel_id=1, source_target_pairs={{0,2},{1,3},{2,0},{3,1},{4,6},{5,7},{6,4},{7,5},{8,10},{9,11},{10,... | collective-permute-start | bytes 491528 | tf_op jit(solution)/shard_map/ppermute | solution.py:90
  28.0 1.0 fusion.10
  30.2 1.6 %collective-permute-done.13.refs_10_ = bf16[20,32,128]{2,1,0:T(8,128)(2,1)S(1)} collective-permute-done((bf16[20,32,128]{2,1,0:T(8,128)(2,1)S(1)}, bf16[20,32,128]{2,1,0:T(8,128)(2,1)S(1)}, u32[]{:S(2)}, u32[]{:S(2)}) %collective-permute-start.13) | collective-permute-done | bytes 163872 | tf_op jit(solution)/shard_map/ppermute | solution.py:90
  31.8 1.7 %collective-permute-start.10 = (bf16[20,32,128]{2,1,0:T(8,128)(2,1)S(1)}, bf16[20,32,128]{2,1,0:T(8,128)(2,1)}, u32[]{:S(2)}, u32[]{:S(2)}) collective-permute-start(bf16[20,32,128]{2,1,0:T(8,128)(2,1)S(1)} %collective-permute-done.8.refs_4_), channel_id=1, source_target_pairs={{0,2},{1,3},{2,0},{3,1},{4,6},{5,7},{6,4},{7,5},{8,10},{9,11},{10,... | collective-permute-start | bytes 491528 | tf_op jit(solution)/shard_map/ppermute | solution.py:90
  33.5 1.0 fusion.9
  35.2 1.0 copy.25.block
  36.3 3.5 %collective-permute-done.10.refs_6_ = bf16[20,32,128]{2,1,0:T(8,128)(2,1)} collective-permute-done((bf16[20,32,128]{2,1,0:T(8,128)(2,1)S(1)}, bf16[20,32,128]{2,1,0:T(8,128)(2,1)}, u32[]{:S(2)}, u32[]{:S(2)}) %collective-permute-start.10) | collective-permute-done | bytes 163872 | tf_op jit(solution)/shard_map/ppermute | solution.py:90
  41.6 3.3 %shard_map.105 = (bf16[2,256,768]{2,1,0:T(8,128)(2,1)}, bf16[2,768,256]{2,1,0:T(8,128)(2,1)}) custom-call(s32[1]{0:T(128)} %bitcast.3.info, bf16[2,128,768]{2,1,0:T(8,128)(2,1)} %own.3, bf16[2,128,768]{2,1,0:T(8,128)(2,1)} %copy-done.1, bf16[2,256,768]{2,1,0:T(8,128)(2,1)} %query.3, bf16[2,6,128,128]{3,2,1,0:T(8,128)(2,1)} %copy.25.block, ...), custom_call_target="tpu_custom_call" | custom-call | tf_op jit(solution)/shard_map/pallas_call | solution.py:340
  45.0 2.7 %collective-permute-start.3 = (bf16[20,32,128]{2,1,0:T(8,128)(2,1)}, bf16[20,32,128]{2,1,0:T(8,128)(2,1)S(1)}, u32[]{:S(2)}, u32[]{:S(2)}) collective-permute-start(bf16[20,32,128]{2,1,0:T(8,128)(2,1)} %get-tuple-element.26), channel_id=1, source_target_pairs={{0,12},{1,13},{2,14},{3,15},{4,8},{5,9},{6,10},{7,11},{8,4},{9,5},... | collective-permute-start | bytes 491528 | tf_op jit(solution)/shard_map/ppermute | solution.py:90
  49.8 12.7 %shard_map.106 = (f32[8,256]{1,0:T(8,128)}, bf16[8,16,128]{2,1,0:T(8,128)(2,1)}) custom-call(s32[33]{0:T(128)} %get-tuple-element.45.info_ref, bf16[20,32,128]{2,1,0:T(8,128)(2,1)} %get-tuple-element.20.refs_0_, bf16[20,32,128]{2,1,0:T(8,128)(2,1)} %copy-done.12, bf16[20,32,128]{2,1,0:T(8,128)(2,1)} %copy-done.11, bf16[20,32,128]{2,1,0:T(8,128)(2,1)} %copy-done.18, ...), custom_call_target="tpu_custom_call" | custom-call | flops 8000000000 | bytes 4000000 | tf_op jit(solution)/shard_map/pallas_call | solution.py:254
  62.6 0.9 collective-permute-done.4
  63.6 0.8 collective-permute-start.21
  64.4 13.0 %shard_map.107 = (f32[8,256]{1,0:T(8,128)}, bf16[8,16,128]{2,1,0:T(8,128)(2,1)}) custom-call(s32[33]{0:T(128)} %get-tuple-element.45.info_ref, bf16[20,32,128]{2,1,0:T(8,128)(2,1)} %get-tuple-element.20.refs_0_, bf16[20,32,128]{2,1,0:T(8,128)(2,1)} %copy-done.12, bf16[20,32,128]{2,1,0:T(8,128)(2,1)} %copy-done.11, bf16[20,32,128]{2,1,0:T(8,128)(2,1)} %copy-done.18, ...), custom_call_target="tpu_custom_call" | custom-call | flops 8000000000 | bytes 4000000 | tf_op jit(solution)/shard_map/pallas_call | solution.py:254
  77.4 2.3 %collective-permute-done.21.refs_1_ = bf16[4,20,32,128]{3,2,1,0:T(8,128)(2,1)S(1)} collective-permute-done((bf16[4,20,32,128]{3,2,1,0:T(8,128)(2,1)S(1)}, bf16[4,20,32,128]{3,2,1,0:T(8,128)(2,1)S(1)}, u32[]{:S(2)}, u32[]{:S(2)}) %collective-permute-start.21) | collective-permute-done | bytes 655392 | tf_op jit(solution)/shard_map/ppermute | solution.py:90
  79.7 2.2 %collective-permute-done.23.refs_3_ = bf16[4,20,32,128]{3,2,1,0:T(8,128)(2,1)} collective-permute-done((bf16[4,20,32,128]{3,2,1,0:T(8,128)(2,1)S(1)}, bf16[4,20,32,128]{3,2,1,0:T(8,128)(2,1)}, u32[]{:S(2)}, u32[]{:S(2)}) %collective-permute-start.23) | collective-permute-done | bytes 655392 | tf_op jit(solution)/shard_map/ppermute | solution.py:90
  81.9 22.0 %shard_map.108 = (f32[8,256]{1,0:T(8,128)}, bf16[16,16,128]{2,1,0:T(8,128)(2,1)}) custom-call(s32[33]{0:T(128)} %get-tuple-element.45.info_ref, bf16[4,20,32,128]{3,2,1,0:T(8,128)(2,1)} %copy-done, bf16[4,20,32,128]{3,2,1,0:T(8,128)(2,1)} %copy-done.7, bf16[4,20,32,128]{3,2,1,0:T(8,128)(2,1)} %collective-permute-done.22.refs_2_, ...), custom_call_target="tpu_custom_call" | custom-call | flops 16000000000 | bytes 8000000 | tf_op jit(solution)/shard_map/pallas_call | solution.py:254
  105.1 3.1 %collective-permute-done.24 = f32[4,256]{1,0:T(4,128)S(1)} collective-permute-done((f32[4,256]{1,0:T(4,128)S(1)}, f32[4,256]{1,0:T(4,128)S(1)}, u32[]{:S(2)}, u32[]{:S(2)}) %collective-permute-start.24) | collective-permute-done | bytes 4128 | tf_op jit(solution)/shard_map/ppermute | solution.py:371
  108.2 1.1 collective-permute-done.25
  110.7 2.2 %collective-permute-done.26 = f32[4,256]{1,0:T(4,128)S(1)} collective-permute-done((f32[4,256]{1,0:T(4,128)S(1)}, f32[4,256]{1,0:T(4,128)S(1)}, u32[]{:S(2)}, u32[]{:S(2)}) %collective-permute-start.26) | collective-permute-done | bytes 4128 | tf_op jit(solution)/shard_map/ppermute | solution.py:90
  114.9 1.6 %collective-permute-done.27 = f32[4,256]{1,0:T(4,128)S(1)} collective-permute-done((f32[4,256]{1,0:T(4,128)S(1)}, f32[4,256]{1,0:T(4,128)S(1)}, u32[]{:S(2)}, u32[]{:S(2)}) %collective-permute-start.27) | collective-permute-done | bytes 4128 | tf_op jit(solution)/shard_map/ppermute | solution.py:90
  116.6 1.9 %collective-permute-start.28 = (f32[4,256]{1,0:T(4,128)S(1)}, f32[4,256]{1,0:T(4,128)S(1)}, u32[]{:S(2)}, u32[]{:S(2)}) collective-permute-start(f32[4,256]{1,0:T(4,128)S(1)} %add.50), channel_id=1, source_target_pairs={{0,8},{1,9},{2,10},{3,11},{4,12},{5,13},{6,14},{7,15},{8,0},{9,1},... | collective-permute-start | bytes 12296 | tf_op jit(solution)/shard_map/ppermute | solution.py:90
  118.5 2.6 %collective-permute-done.28 = f32[4,256]{1,0:T(4,128)S(1)} collective-permute-done((f32[4,256]{1,0:T(4,128)S(1)}, f32[4,256]{1,0:T(4,128)S(1)}, u32[]{:S(2)}, u32[]{:S(2)}) %collective-permute-start.28) | collective-permute-done | bytes 4128 | tf_op jit(solution)/shard_map/ppermute | solution.py:90
  122.7 1.3 %gather_fusion = bf16[64,8,128]{2,1,0:T(8,128)(2,1)} fusion(bf16[64,8,128]{2,1,0:T(8,128)(2,1)S(1)} %bitcast.64, s32[1024]{0:T(1024)S(1)} %pad_clamp_fusion), kind=kCustom, calls=%fused_computation | custom fusion | bytes 262400 | tf_op jit(solution)/shard_map/jit(_take)/gather | solution.py:384
  (113 shorter events, 15.2 us)
Async XLA Ops:
  0.6 6.7 %collective-permute-start = (bf16[2,8,4096]{2,1,0:T(8,128)(2,1)}, bf16[2,8,4096]{2,1,0:T(8,128)(2,1)S(1)}, u32[]{:S(2)}, u32[]{:S(2)}) collective-permute-start(bf16[2,8,4096]{2,1,0:T(8,128)(2,1)} %own.2), channel_id=1, source_target_pairs={{0,16},{16,0},{1,17},{17,1},{2,18},{18,2},{3,19},{19,3},{4,20},{20... | collective-permute-start | bytes 393224 | tf_op jit(solution)/shard_map/ppermute | solution.py:299
  10.4 53.1 %copy-start.2 = (bf16[20,32,128]{2,1,0:T(8,128)(2,1)S(1)}, bf16[20,32,128]{2,1,0:T(8,128)(2,1)}, u32[]{:S(2)}) copy-start(bf16[20,32,128]{2,1,0:T(8,128)(2,1)} %get-tuple-element.26) | copy-start | bytes 491524
  10.4 14.6 %collective-permute-start.1 = (bf16[20,32,128]{2,1,0:T(8,128)(2,1)}, bf16[20,32,128]{2,1,0:T(8,128)(2,1)S(1)}, u32[]{:S(2)}, u32[]{:S(2)}) collective-permute-start(bf16[20,32,128]{2,1,0:T(8,128)(2,1)} %get-tuple-element.20.refs_0_), channel_id=1, source_target_pairs={{0,8},{1,9},{2,10},{3,11},{4,12},{5,13},{6,14},{7,15},{8,0},{9,1},... | collective-permute-start | bytes 491528 | tf_op jit(solution)/shard_map/ppermute | solution.py:90
  13.2 13.3 %collective-permute-start.8 = (bf16[20,32,128]{2,1,0:T(8,128)(2,1)}, bf16[20,32,128]{2,1,0:T(8,128)(2,1)S(1)}, u32[]{:S(2)}, u32[]{:S(2)}) collective-permute-start(bf16[20,32,128]{2,1,0:T(8,128)(2,1)} %get-tuple-element.20.refs_0_), channel_id=1, source_target_pairs={{0,4},{1,5},{2,6},{3,7},{4,0},{5,1},{6,2},{7,3},{8,12},{9,13},{10,... | collective-permute-start | bytes 491528 | tf_op jit(solution)/shard_map/ppermute | solution.py:90
  14.8 3.7 %collective-permute-start.20 = (s32[128]{0:T(128)}, s32[128]{0:T(128)S(1)}, u32[]{:S(2)}, u32[]{:S(2)}) collective-permute-start(s32[128]{0:T(128)} %param.11), channel_id=1, source_target_pairs={{0,16},{16,0},{1,17},{17,1},{2,18},{18,2},{3,19},{19,3},{4,20},{20... | collective-permute-start | bytes 1544 | tf_op jit(solution)/shard_map/ppermute | solution.py:323
  16.3 13.1 %collective-permute-start.15 = (bf16[20,32,128]{2,1,0:T(8,128)(2,1)}, bf16[20,32,128]{2,1,0:T(8,128)(2,1)S(1)}, u32[]{:S(2)}, u32[]{:S(2)}) collective-permute-start(bf16[20,32,128]{2,1,0:T(8,128)(2,1)} %get-tuple-element.20.refs_0_), channel_id=1, source_target_pairs={{0,12},{1,13},{2,14},{3,15},{4,8},{5,9},{6,10},{7,11},{8,4},{9,5},... | collective-permute-start | bytes 491528 | tf_op jit(solution)/shard_map/ppermute | solution.py:90
  16.5 13.0 %collective-permute-start.6 = (bf16[20,32,128]{2,1,0:T(8,128)(2,1)}, bf16[20,32,128]{2,1,0:T(8,128)(2,1)S(1)}, u32[]{:S(2)}, u32[]{:S(2)}) collective-permute-start(bf16[20,32,128]{2,1,0:T(8,128)(2,1)} %get-tuple-element.20.refs_0_), channel_id=1, source_target_pairs={{0,2},{1,3},{2,0},{3,1},{4,6},{5,7},{6,4},{7,5},{8,10},{9,11},{10,... | collective-permute-start | bytes 491528 | tf_op jit(solution)/shard_map/ppermute | solution.py:90
  18.5 11.6 %collective-permute-start.5 = (bf16[20,32,128]{2,1,0:T(8,128)(2,1)}, bf16[20,32,128]{2,1,0:T(8,128)(2,1)S(1)}, u32[]{:S(2)}, u32[]{:S(2)}) collective-permute-start(bf16[20,32,128]{2,1,0:T(8,128)(2,1)} %get-tuple-element.20.refs_0_), channel_id=1, source_target_pairs={{0,1},{1,0},{2,3},{3,2},{4,5},{5,4},{6,7},{7,6},{8,9},{9,8},{10,11... | collective-permute-start | bytes 491528 | tf_op jit(solution)/shard_map/ppermute | solution.py:90
  25.0 15.8 %collective-permute-start.19 = (bf16[2,128,768]{2,1,0:T(8,128)(2,1)}, bf16[2,128,768]{2,1,0:T(8,128)(2,1)S(1)}, u32[]{:S(2)}, u32[]{:S(2)}) collective-permute-start(bf16[2,128,768]{2,1,0:T(8,128)(2,1)} %own.3), channel_id=1, source_target_pairs={{0,16},{16,0},{1,17},{17,1},{2,18},{18,2},{3,19},{19,3},{4,20},{20... | collective-permute-start | bytes 1179656 | tf_op jit(solution)/shard_map/ppermute | solution.py:324
  26.5 5.3 %collective-permute-start.13 = (bf16[20,32,128]{2,1,0:T(8,128)(2,1)S(1)}, bf16[20,32,128]{2,1,0:T(8,128)(2,1)S(1)}, u32[]{:S(2)}, u32[]{:S(2)}) collective-permute-start(bf16[20,32,128]{2,1,0:T(8,128)(2,1)S(1)} %collective-permute-done.1.refs_8_), channel_id=1, source_target_pairs={{0,2},{1,3},{2,0},{3,1},{4,6},{5,7},{6,4},{7,5},{8,10},{9,11},{10,... | collective-permute-start | bytes 491528 | tf_op jit(solution)/shard_map/ppermute | solution.py:90
  29.4 10.8 %collective-permute-start.12 = (bf16[20,32,128]{2,1,0:T(8,128)(2,1)S(1)}, bf16[20,32,128]{2,1,0:T(8,128)(2,1)S(1)}, u32[]{:S(2)}, u32[]{:S(2)}) collective-permute-start(bf16[20,32,128]{2,1,0:T(8,128)(2,1)S(1)} %collective-permute-done.1.refs_8_), channel_id=1, source_target_pairs={{0,1},{1,0},{2,3},{3,2},{4,5},{5,4},{6,7},{7,6},{8,9},{9,8},{10,11... | collective-permute-start | bytes 491528 | tf_op jit(solution)/shard_map/ppermute | solution.py:90
  29.5 10.2 %collective-permute-start.17 = (bf16[20,32,128]{2,1,0:T(8,128)(2,1)S(1)}, bf16[20,32,128]{2,1,0:T(8,128)(2,1)S(1)}, u32[]{:S(2)}, u32[]{:S(2)}) collective-permute-start(bf16[20,32,128]{2,1,0:T(8,128)(2,1)S(1)} %collective-permute-done.15.refs_12_), channel_id=1, source_target_pairs={{0,2},{1,3},{2,0},{3,1},{4,6},{5,7},{6,4},{7,5},{8,10},{9,11},{10,... | collective-permute-start | bytes 491528 | tf_op jit(solution)/shard_map/ppermute | solution.py:90
  30.1 10.3 %collective-permute-start.16 = (bf16[20,32,128]{2,1,0:T(8,128)(2,1)S(1)}, bf16[20,32,128]{2,1,0:T(8,128)(2,1)S(1)}, u32[]{:S(2)}, u32[]{:S(2)}) collective-permute-start(bf16[20,32,128]{2,1,0:T(8,128)(2,1)S(1)} %collective-permute-done.15.refs_12_), channel_id=1, source_target_pairs={{0,1},{1,0},{2,3},{3,2},{4,5},{5,4},{6,7},{7,6},{8,9},{9,8},{10,11... | collective-permute-start | bytes 491528 | tf_op jit(solution)/shard_map/ppermute | solution.py:90
  31.8 7.9 %collective-permute-start.10 = (bf16[20,32,128]{2,1,0:T(8,128)(2,1)S(1)}, bf16[20,32,128]{2,1,0:T(8,128)(2,1)}, u32[]{:S(2)}, u32[]{:S(2)}) collective-permute-start(bf16[20,32,128]{2,1,0:T(8,128)(2,1)S(1)} %collective-permute-done.8.refs_4_), channel_id=1, source_target_pairs={{0,2},{1,3},{2,0},{3,1},{4,6},{5,7},{6,4},{7,5},{8,10},{9,11},{10,... | collective-permute-start | bytes 491528 | tf_op jit(solution)/shard_map/ppermute | solution.py:90
  39.7 5.2 %collective-permute-start.9 = (bf16[20,32,128]{2,1,0:T(8,128)(2,1)S(1)}, bf16[20,32,128]{2,1,0:T(8,128)(2,1)S(1)}, u32[]{:S(2)}, u32[]{:S(2)}) collective-permute-start(bf16[20,32,128]{2,1,0:T(8,128)(2,1)S(1)} %collective-permute-done.8.refs_4_), channel_id=1, source_target_pairs={{0,1},{1,0},{2,3},{3,2},{4,5},{5,4},{6,7},{7,6},{8,9},{9,8},{10,11... | collective-permute-start | bytes 491528 | tf_op jit(solution)/shard_map/ppermute | solution.py:90
  39.7 5.2 %collective-permute-start.7 = (bf16[20,32,128]{2,1,0:T(8,128)(2,1)S(1)}, bf16[20,32,128]{2,1,0:T(8,128)(2,1)S(1)}, u32[]{:S(2)}, u32[]{:S(2)}) collective-permute-start(bf16[20,32,128]{2,1,0:T(8,128)(2,1)S(1)} %collective-permute-done.6.refs_2_), channel_id=1, source_target_pairs={{0,1},{1,0},{2,3},{3,2},{4,5},{5,4},{6,7},{7,6},{8,9},{9,8},{10,11... | collective-permute-start | bytes 491528 | tf_op jit(solution)/shard_map/ppermute | solution.py:90
  40.3 7.4 %collective-permute-start.14 = (bf16[20,32,128]{2,1,0:T(8,128)(2,1)S(1)}, bf16[20,32,128]{2,1,0:T(8,128)(2,1)}, u32[]{:S(2)}, u32[]{:S(2)}) collective-permute-start(bf16[20,32,128]{2,1,0:T(8,128)(2,1)S(1)} %collective-permute-done.13.refs_10_), channel_id=1, source_target_pairs={{0,1},{1,0},{2,3},{3,2},{4,5},{5,4},{6,7},{7,6},{8,9},{9,8},{10,11... | collective-permute-start | bytes 491528 | tf_op jit(solution)/shard_map/ppermute | solution.py:90
  40.4 8.1 %collective-permute-start.11 = (bf16[20,32,128]{2,1,0:T(8,128)(2,1)}, bf16[20,32,128]{2,1,0:T(8,128)(2,1)S(1)}, u32[]{:S(2)}, u32[]{:S(2)}) collective-permute-start(bf16[20,32,128]{2,1,0:T(8,128)(2,1)} %collective-permute-done.10.refs_6_), channel_id=1, source_target_pairs={{0,1},{1,0},{2,3},{3,2},{4,5},{5,4},{6,7},{7,6},{8,9},{9,8},{10,11... | collective-permute-start | bytes 491528 | tf_op jit(solution)/shard_map/ppermute | solution.py:90
  40.8 7.7 %collective-permute-start.18 = (bf16[20,32,128]{2,1,0:T(8,128)(2,1)S(1)}, bf16[20,32,128]{2,1,0:T(8,128)(2,1)S(1)}, u32[]{:S(2)}, u32[]{:S(2)}) collective-permute-start(bf16[20,32,128]{2,1,0:T(8,128)(2,1)S(1)} %collective-permute-done.17.refs_14_), channel_id=1, source_target_pairs={{0,1},{1,0},{2,3},{3,2},{4,5},{5,4},{6,7},{7,6},{8,9},{9,8},{10,11... | collective-permute-start | bytes 491528 | tf_op jit(solution)/shard_map/ppermute | solution.py:90
  44.9 17.6 %collective-permute-start.2 = (bf16[20,32,128]{2,1,0:T(8,128)(2,1)}, bf16[20,32,128]{2,1,0:T(8,128)(2,1)S(1)}, u32[]{:S(2)}, u32[]{:S(2)}) collective-permute-start(bf16[20,32,128]{2,1,0:T(8,128)(2,1)} %get-tuple-element.26), channel_id=1, source_target_pairs={{0,4},{1,5},{2,6},{3,7},{4,0},{5,1},{6,2},{7,3},{8,12},{9,13},{10,... | collective-permute-start | bytes 491528 | tf_op jit(solution)/shard_map/ppermute | solution.py:90
  45.0 17.6 %collective-permute-start.3 = (bf16[20,32,128]{2,1,0:T(8,128)(2,1)}, bf16[20,32,128]{2,1,0:T(8,128)(2,1)S(1)}, u32[]{:S(2)}, u32[]{:S(2)}) collective-permute-start(bf16[20,32,128]{2,1,0:T(8,128)(2,1)} %get-tuple-element.26), channel_id=1, source_target_pairs={{0,12},{1,13},{2,14},{3,15},{4,8},{5,9},{6,10},{7,11},{8,4},{9,5},... | collective-permute-start | bytes 491528 | tf_op jit(solution)/shard_map/ppermute | solution.py:90
  47.7 15.8 %collective-permute-start.4 = (bf16[20,32,128]{2,1,0:T(8,128)(2,1)}, bf16[20,32,128]{2,1,0:T(8,128)(2,1)S(1)}, u32[]{:S(2)}, u32[]{:S(2)}) collective-permute-start(bf16[20,32,128]{2,1,0:T(8,128)(2,1)} %get-tuple-element.26), channel_id=1, source_target_pairs={{0,8},{1,9},{2,10},{3,11},{4,12},{5,13},{6,14},{7,15},{8,0},{9,1},... | collective-permute-start | bytes 491528 | tf_op jit(solution)/shard_map/ppermute | solution.py:90
  63.6 16.1 %collective-permute-start.21 = (bf16[4,20,32,128]{3,2,1,0:T(8,128)(2,1)S(1)}, bf16[4,20,32,128]{3,2,1,0:T(8,128)(2,1)S(1)}, u32[]{:S(2)}, u32[]{:S(2)}) collective-permute-start(bf16[4,20,32,128]{3,2,1,0:T(8,128)(2,1)S(1)} %pad_maximum_fusion.refs_0_), channel_id=1, source_target_pairs={{0,2},{1,3},{2,0},{3,1},{4,6},{5,7},{6,4},{7,5},{8,10},{9,11},{10,... | collective-permute-start | bytes 1966088 | tf_op jit(solution)/shard_map/ppermute | solution.py:90
  64.4 15.3 %collective-permute-start.22 = (bf16[4,20,32,128]{3,2,1,0:T(8,128)(2,1)S(1)}, bf16[4,20,32,128]{3,2,1,0:T(8,128)(2,1)}, u32[]{:S(2)}, u32[]{:S(2)}) collective-permute-start(bf16[4,20,32,128]{3,2,1,0:T(8,128)(2,1)S(1)} %pad_maximum_fusion.refs_0_), channel_id=1, source_target_pairs={{0,1},{1,0},{2,3},{3,2},{4,5},{5,4},{6,7},{7,6},{8,9},{9,8},{10,11... | collective-permute-start | bytes 1966088 | tf_op jit(solution)/shard_map/ppermute | solution.py:90
  79.6 2.2 %collective-permute-start.23 = (bf16[4,20,32,128]{3,2,1,0:T(8,128)(2,1)S(1)}, bf16[4,20,32,128]{3,2,1,0:T(8,128)(2,1)}, u32[]{:S(2)}, u32[]{:S(2)}) collective-permute-start(bf16[4,20,32,128]{3,2,1,0:T(8,128)(2,1)S(1)} %collective-permute-done.21.refs_1_), channel_id=1, source_target_pairs={{0,1},{1,0},{2,3},{3,2},{4,5},{5,4},{6,7},{7,6},{8,9},{9,8},{10,11... | collective-permute-start | bytes 1966088 | tf_op jit(solution)/shard_map/ppermute | solution.py:90
  104.6 3.6 %collective-permute-start.24 = (f32[4,256]{1,0:T(4,128)S(1)}, f32[4,256]{1,0:T(4,128)S(1)}, u32[]{:S(2)}, u32[]{:S(2)}) collective-permute-start(f32[4,256]{1,0:T(4,128)S(1)} %dynamic-slice_bitcast_fusion.2), channel_id=1, source_target_pairs={{0,16},{16,0},{1,17},{17,1},{2,18},{18,2},{3,19},{19,3},{4,20},{20... | collective-permute-start | bytes 12296 | tf_op jit(solution)/shard_map/ppermute | solution.py:371
  108.2 1.2 collective-permute-start.25
  109.4 3.6 %collective-permute-start.26 = (f32[4,256]{1,0:T(4,128)S(1)}, f32[4,256]{1,0:T(4,128)S(1)}, u32[]{:S(2)}, u32[]{:S(2)}) collective-permute-start(f32[4,256]{1,0:T(4,128)S(1)} %add.48), channel_id=1, source_target_pairs={{0,2},{1,3},{2,0},{3,1},{4,6},{5,7},{6,4},{7,5},{8,10},{9,11},{10,... | collective-permute-start | bytes 12296 | tf_op jit(solution)/shard_map/ppermute | solution.py:90
  110.1 8.3 %collective-permute-start.29 = (bf16[16,8,128]{2,1,0:T(8,128)(2,1)S(1)}, bf16[16,8,128]{2,1,0:T(8,128)(2,1)S(1)}, u32[]{:S(2)}, u32[]{:S(2)}) collective-permute-start(bf16[16,8,128]{2,1,0:T(8,128)(2,1)S(1)} %dynamic-slice_bitcast_fusion.1), channel_id=1, source_target_pairs={{0,16},{16,0},{1,17},{17,1},{2,18},{18,2},{3,19},{19,3},{4,20},{20... | collective-permute-start | bytes 98312 | tf_op jit(solution)/shard_map/ppermute | solution.py:380
  113.0 3.6 %collective-permute-start.27 = (f32[4,256]{1,0:T(4,128)S(1)}, f32[4,256]{1,0:T(4,128)S(1)}, u32[]{:S(2)}, u32[]{:S(2)}) collective-permute-start(f32[4,256]{1,0:T(4,128)S(1)} %add.49), channel_id=1, source_target_pairs={{0,4},{1,5},{2,6},{3,7},{4,0},{5,1},{6,2},{7,3},{8,12},{9,13},{10,... | collective-permute-start | bytes 12296 | tf_op jit(solution)/shard_map/ppermute | solution.py:90
  114.4 7.5 %collective-permute-start.30 = (bf16[16,8,128]{2,1,0:T(8,128)(2,1)S(1)}, bf16[16,8,128]{2,1,0:T(8,128)(2,1)S(1)}, u32[]{:S(2)}, u32[]{:S(2)}) collective-permute-start(bf16[16,8,128]{2,1,0:T(8,128)(2,1)S(1)} %dynamic-slice_bitcast_fusion), channel_id=1, source_target_pairs={{0,16},{16,0},{1,17},{17,1},{2,18},{18,2},{3,19},{19,3},{4,20},{20... | collective-permute-start | bytes 98312 | tf_op jit(solution)/shard_map/ppermute | solution.py:380
  116.6 4.5 %collective-permute-start.28 = (f32[4,256]{1,0:T(4,128)S(1)}, f32[4,256]{1,0:T(4,128)S(1)}, u32[]{:S(2)}, u32[]{:S(2)}) collective-permute-start(f32[4,256]{1,0:T(4,128)S(1)} %add.50), channel_id=1, source_target_pairs={{0,8},{1,9},{2,10},{3,11},{4,12},{5,13},{6,14},{7,15},{8,0},{9,1},... | collective-permute-start | bytes 12296 | tf_op jit(solution)/shard_map/ppermute | solution.py:90
  (20 other events, 265.1 us)

commit v4 on v3

--- a/solution.py
+++ b/solution.py
@@ -132,54 +132,47 @@
     )
 
 
-def score_kernel(base, count, info, *refs):
+def score_kernel(base, count, last, info, *refs):
     units = refs[:NQ]
-    grads, query_grads, codes, eigen, before, totals, own_rows = refs[NQ : NQ + 7]
-    held, turned_rows, train_t, query_t, eig, scaled0, scaled1, weights, acc = refs[NQ + 7 : NQ + 16]
-    unit_sems, eig_sems = refs[NQ + 16 :]
+    grads, query_grads, codes, eigen, before = refs[NQ : NQ + 5]
+    outs = refs[NQ + 5 : NQ + (9 if last else 8)]
+    rows_kept, rows_given = outs[-2:]
+    bases, train, query, train_t, query_t, eig, scaled0, scaled1, weights, acc, sems = refs[
+        NQ + 5 + len(outs) :
+    ]
     scaled = (scaled0, scaled1)
     me = info[0]
+    x = info[1 + WAVES * NQ]
     start = base % NQ
-    wave = base // NQ
-    copies = []
-    for d in range(NQ):
+
+    def piece(d, index):
         unit, which = units[d]
-        source = unit if which is None else unit.at[which]
-        into = held.at[me ^ d]
-        copies.append(
-            pltpu.make_async_copy(
-                source.at[pl.ds(start, count)], into.at[pl.ds(0, count)], unit_sems.at[d]
-            )
-        )
-        copies.append(
-            pltpu.make_async_copy(
-                source.at[pl.ds(NQ, 4)], into.at[pl.ds(NQ, 4)], unit_sems.at[NQ + d]
-            )
-        )
-    for copy in copies:
-        copy.start()
+        return unit[index] if which is None else unit[which, index]
 
     def eig_copy(n):
         tile = info[1 + base + n]
         cols = pl.ds(pl.multiple_of((tile % 32) * TILE_A, TILE_A), TILE_A)
-        return pltpu.make_async_copy(eigen.at[tile // 32, :, cols], eig.at[n], eig_sems.at[n])
+        return pltpu.make_async_copy(eigen.at[tile // 32, :, cols], eig.at[n], sems.at[n])
 
     for n in range(count):
         eig_copy(n).start()
     acc[...] = jnp.zeros_like(acc)
-    for copy in copies:
-        copy.wait()
+    for d in range(NQ):
+        bases[me ^ d] = piece(d, slice(NQ, NQ + 4))
 
     def rotate(n):
-        basis = held[start + n, NQ:].reshape(TILE_A, TILE_A)
+        basis = bases[start + n].reshape(TILE_A, TILE_A)
         basis_t = basis.astype(jnp.float32).T.astype(BF)
-        tile = held[:, n]
-        train = tile[:, :16].reshape(TOKENS, TILE_A)
-        query = tile[:, 16:].reshape(TOKENS, TILE_A)
-        mine = held[me, n, :16]
-        own_rows[n] = jnp.dot(mine, basis, preferred_element_type=jnp.float32).astype(BF)
-        train_t[n] = across(basis_t, train).astype(BF)
-        query_t[n] = across(basis_t, query).astype(BF)
+        for d in range(NQ):
+            rows = piece(d, start + n)
+            place = pl.ds(pl.multiple_of((me ^ d) * 16, 16), 16)
+            train[place, :] = rows[:16]
+            query[place, :] = rows[16:]
+        own = jnp.dot(piece(0, start + n)[:16], basis, preferred_element_type=jnp.float32)
+        rows_kept[n] = jnp.where(x == 0, own[:8], own[8:]).astype(BF)
+        rows_given[n] = jnp.where(x == 0, own[8:], own[:8]).astype(BF)
+        train_t[n] = across(basis_t, train[...]).astype(BF)
+        query_t[n] = across(basis_t, query[...]).astype(BF)
 
     def weigh(n, k):
         weights[k] = 1.0 / (eig[n].T + damping)
@@ -235,7 +228,12 @@
     gram(count - 1, 1)
     project(count - 2, 0)
     project(count - 1, 1)
-    totals[...] = before[...] + jnp.sum(acc[...], axis=1)
+    total = before[...] + jnp.sum(acc[...], axis=1)
+    if last:
+        outs[0][...] = jnp.where(x == 0, total[:SEQS], total[SEQS:])
+        outs[1][...] = jnp.where(x == 0, total[SEQS:], total[:SEQS])
+    else:
+        outs[0][...] = total
 
 
 VMEM = pl.BlockSpec(memory_space=pltpu.VMEM)
@@ -243,24 +241,28 @@
 HBM = pl.BlockSpec(memory_space=pltpu.HBM)
 
 
-def score_tiles(base, count, info, arrays, places, grads, query_grads, codes, eigenvalues, before):
+def score_tiles(base, count, last, info, arrays, places, grads, query_grads, codes, eigenvalues, before):
     width = grads.shape[2]
 
     def kernel(info_ref, *refs):
         held = refs[: len(arrays)]
         units = [(held[a], which) for a, which in places]
-        score_kernel(base, count, info_ref, *units, *refs[len(arrays) :])
-
+        score_kernel(base, count, last, info_ref, *units, *refs[len(arrays) :])
+
+    sums = (
+        [jax.ShapeDtypeStruct((SEQS, TOKENS), jnp.float32)] * 2
+        if last
+        else [jax.ShapeDtypeStruct((GROUPS, TOKENS), jnp.float32)]
+    )
+    rows = [jax.ShapeDtypeStruct((count, 8, TILE_A), BF)] * 2
     return pl.pallas_call(
         kernel,
-        in_specs=[SMEM] + [HBM] * len(arrays) + [VMEM, VMEM, VMEM, HBM, VMEM],
-        out_specs=[VMEM, VMEM],
-        out_shape=[
-            jax.ShapeDtypeStruct((GROUPS, TOKENS), jnp.float32),
-            jax.ShapeDtypeStruct((count, 16, TILE_A), BF),
-        ],
+        in_specs=[SMEM] + [VMEM] * len(arrays) + [VMEM, VMEM, VMEM, HBM, VMEM],
+        out_specs=[VMEM] * len(sums + rows),
+        out_shape=sums + rows,
         scratch_shapes=[
-            pltpu.VMEM((NQ, UNIT, 32, TILE_A), BF),
+            pltpu.VMEM((NQ, 4, 32, TILE_A), BF),
+            pltpu.VMEM((TOKENS, TILE_A), BF),
             pltpu.VMEM((TOKENS, TILE_A), BF),
             pltpu.VMEM((count, TILE_A, TOKENS), BF),
             pltpu.VMEM((count, TILE_A, TOKENS), BF),
@@ -269,14 +271,25 @@
             pltpu.VMEM((GROUPS * TILE_A, width), BF),
             pltpu.VMEM((2, TILE_A, width), jnp.float32),
             pltpu.VMEM((GROUPS, 8, TOKENS), jnp.float32),
-            pltpu.SemaphoreType.DMA((2 * NQ,)),
             pltpu.SemaphoreType.DMA((count,)),
         ],
-        compiler_params=pltpu.CompilerParams(vmem_limit_bytes=62 * 1024 * 1024),
+        compiler_params=pltpu.CompilerParams(vmem_limit_bytes=42 * 1024 * 1024),
         cost_estimate=pl.CostEstimate(
             flops=count * 10**9, bytes_accessed=count * 10**6 // 2, transcendentals=0
         ),
     )(info, *arrays, grads, query_grads, codes, eigenvalues, before)
+
+
+def unpack_kernel(tiles, kept0, came0, kept1, came1, out):
+    for half, pair in enumerate(((kept0, kept1), (came0, came1))):
+        for wave in range(WAVES):
+            source = pair[wave]
+
+            @pl.loop(0, NQ)
+            def _(owner):
+                tile = tiles[half * WAVES * NQ + wave * NQ + owner]
+                cols = pl.ds(pl.multiple_of((tile % 32) * TILE_A, TILE_A), TILE_A)
+                out[tile // 32, :, cols] = source[owner]
 
 
 def after(value, *others):
@@ -299,8 +312,9 @@
     train_other = lax.ppermute(train_inputs, "parts", SWAP)
     ids = jnp.arange(64, dtype=jnp.int32)
     tile_of = jnp.sum(jnp.where(slot_list[None, :] == ids[:, None], ids[None, :], 0), axis=1)
-    mine = lax.dynamic_index_in_dim(tile_of.reshape(NQ, 2, WAVES), x, 1, False)
-    mine = mine.T.reshape(WAVES * NQ)
+    by_half = tile_of.reshape(NQ, 2, WAVES).transpose(1, 2, 0).reshape(2, WAVES * NQ)
+    mine = jnp.where(x == 0, by_half[0], by_half[1])
+    theirs = jnp.where(x == 0, by_half[1], by_half[0])
     side = x.reshape(1).astype(jnp.int32)
 
     packed = pl.pallas_call(
@@ -310,18 +324,8 @@
         out_shape=[jax.ShapeDtypeStruct((UNIT, 32, TILE_A), BF)] * WAVES,
     )(jnp.concatenate([side, mine]), train_inputs, train_other, query_inputs, input_basis)
 
-    units = [None] * NQ
-    units[0] = packed[0]
-    for d in (4, 12, 8):
-        units[d] = hop(packed[0], d)
-    for d in (0, 4, 12, 8):
-        units[d ^ 2] = hop(units[d], 2)
-    for d in (0, 2, 4, 6, 12, 14, 8, 10):
-        units[d ^ 1] = hop(units[d], 1)
-    places0 = [(d, None) for d in range(NQ)]
-
     ids_other = lax.ppermute(sequence_ids, "parts", SWAP)
-    out_other = lax.ppermute(after(train_outgrads, packed[0]), "parts", SWAP)
+    out_other = lax.ppermute(after(train_outgrads, train_other), "parts", SWAP)
     id_pair = jnp.where(
         x == 0, jnp.stack([sequence_ids, ids_other]), jnp.stack([ids_other, sequence_ids])
     )
@@ -347,44 +351,57 @@
         ],
     )(side, train_outgrads, out_other, query_outgrads, block, block.transpose(0, 1, 3, 2))
 
-    info = jnp.concatenate([me.reshape(1).astype(jnp.int32), mine])
+    units = [None] * NQ
+    units[0] = packed[0]
+    for d in (4, 12, 8):
+        units[d] = hop(packed[0], d)
+    for d in (0, 4, 12):
+        units[d ^ 2] = hop(units[d], 2)
+    units[10] = hop(after(units[8], grads), 2)
+    for d in (0, 2, 4, 6, 12, 14, 8, 10):
+        units[d ^ 1] = hop(units[d], 1)
+    places0 = [(d, None) for d in range(NQ)]
+
+    info = jnp.concatenate([me.reshape(1).astype(jnp.int32), mine, side])
     zero = jnp.zeros((GROUPS, TOKENS), jnp.float32)
     common = (grads, query_grads, codes, eigenvalues)
-    part0, rows0 = score_tiles(0, 8, info, units, places0, *common, zero)
+    part0, kept_a, given_a = score_tiles(0, 8, False, info, units, places0, *common, zero)
 
     second = after(packed[1], units[8])
-    along = [second] + [hop(second, d) for d in (4, 12, 8)]
-    line = jnp.stack(lax.optimization_barrier((*along, part0))[:4])
+    along = [hop(second, d) for d in (4, 12, 8)]
+    near = hop(second, 2)
+    *along, near, _ = lax.optimization_barrier((*along, near, part0))
+    line = jnp.stack(along)
     beside = hop(line, 2)
-    part1, rows1 = score_tiles(8, 8, info, units, places0, *common, part0)
+    part1, kept_b, given_b = score_tiles(8, 8, False, info, units, places0, *common, part0)
     beside = after(beside, part1)
-    line_core, beside_core = hop(line, 1), hop(beside, 1)
-    order = {0: 0, 4: 1, 12: 2, 8: 3}
-    places1 = [((d & 2) // 2 + 2 * (d & 1), order[d & 12]) for d in range(NQ)]
-    totals, rows2 = score_tiles(
-        16, 16, info, [line, beside, line_core, beside_core], places1, *common, part1
-    )
-
-    halves = totals.reshape(2, SEQS, TOKENS)
-    keep = lax.dynamic_index_in_dim(halves, x, 0, False)
-    give = lax.dynamic_index_in_dim(halves, 1 - x, 0, False)
+    arrays = [second, near, line, beside]
+    arrays = arrays + [hop(array, 1) for array in arrays]
+    order = {4: 0, 12: 1, 8: 2}
+    places1 = []
+    for d in range(NQ):
+        across_y = (d & 2) // 2 + 4 * (d & 1)
+        far = d & 12
+        places1.append((across_y + 2, order[far]) if far else (across_y, None))
+    kept0 = jnp.concatenate([kept_a, kept_b], axis=0)
+    came0 = lax.ppermute(jnp.concatenate([given_a, given_b], axis=0), "parts", SWAP)
+    keep, give, kept1, given1 = score_tiles(
+        16, 16, True, info, arrays, places1, *common, after(part1, came0)
+    )
+
     total = keep + lax.ppermute(give, "parts", SWAP)
-    for bits in (1, 2, 4, 8):
+    came1 = lax.ppermute(given1, "parts", SWAP)
+    rotated_out = pl.pallas_call(
+        unpack_kernel,
+        in_specs=[SMEM] + [VMEM] * 4,
+        out_specs=VMEM,
+        out_shape=jax.ShapeDtypeStruct(train_inputs.shape, BF),
+    )(jnp.concatenate([mine, theirs]), kept0, came0, kept1, came1)
+    for bits in (1, 2, 4):
         total = total + hop(total, bits)
+    total = after(total, rotated_out)
+    total = total + hop(total, 8)
     scores = jnp.sum(total.reshape(SEQS, QUERIES, QLEN), axis=2).T
-
-    slots = [None] * 4
-    for wave, rows in enumerate((jnp.concatenate([rows0, rows1], axis=0), rows2)):
-        pair = rows.reshape(NQ, 2, 8, TILE_A)
-        kept = lax.dynamic_index_in_dim(pair, x, 1, False)
-        came = lax.ppermute(lax.dynamic_index_in_dim(pair, 1 - x, 1, False), "parts", SWAP)
-        slots[wave] = jnp.where(x == 0, kept, came)
-        slots[2 + wave] = jnp.where(x == 0, came, kept)
-    by_slot = jnp.stack(slots, axis=1).reshape(64, 8, TILE_A)
-    ordered = jnp.take(by_slot, slot_list, axis=0, mode="clip")
-    rotated_out = (
-        ordered.reshape(LAYERS, 32, 8, TILE_A).transpose(0, 2, 1, 3).reshape(LAYERS, 8, D)
-    )
     return (scores, rotated_out)
 
 

time: 124 us -> 122 us (0.984)
  Pallas kernels: 53.4 us -> 45.3 us
  starting transfers between devices: 26.5 us -> 29.3 us
  waiting for transfers between devices: 30.1 us -> 32.6 us
    pallas_call x3 -> x4, Pallas kernels: 47.7 us -> 39.6 us  [the longest x3 37.3 us: score_tiles(): pl.pallas_call(kernel, in_specs=[SMEM] + [VMEM] * len(arrays) + [VMEM, VM...]
    unnamed x44 -> x20, local copies, waits for them, and re-layouts: 1.71 us -> 5.35 us
    ppermute x3, waiting for transfers between devices: 0.01 us -> 3.45 us  [the longest x1 3.44 us: paired_body(): lax.ppermute(jnp.concatenate([given_a, given_b], axis=0), 'parts', SWAP)]
    ppermute x25 -> x28, starting transfers between devices: 18.8 us -> 21.7 us  [hop(): return lax.ppermute(value, 'query', [(i, i ^ bits) for i in range(NQ)])]
    gather x1 -> x0, local copies, waits for them, and re-layouts: 1.28 us -> none  [paired_body(): ordered = jnp.take(by_slot, slot_list, axis=0, mode='clip')]
    concatenate x0 -> x4, other arithmetic: none -> 1.27 us  [the longest x1 0.6 us: paired_body(): kept0 = jnp.concatenate([kept_a, kept_b], axis=0)]
    ppermute x25 -> x28, waiting for transfers between devices: 24.6 us -> 24.1 us  [hop(): return lax.ppermute(value, 'query', [(i, i ^ bits) for i in range(NQ)])]
  transfers between devices with their start and end apart: 31 -> 34, of which waited for: 13 -> 13; matrix products, arithmetic and copies ran while one was open for 7% -> 6% of each run, Pallas kernels for 23% -> 19%
where the time goes in v4:
time: 122 us; the launch traced here: 121 us
  Pallas kernels  45.3 us (37%)
  waiting for transfers between devices  32.6 us (27%)
  starting transfers between devices  29.3 us (24%)
  local copies, waits for them, and re-layouts  8.79 us (7%)
  other arithmetic  4.45 us (4%)
    pallas_call x3, Pallas kernels, score_tiles(): pl.pallas_call(kernel, in_specs=[SMEM] + [VMEM] * len(arrays) + [VMEM, VM...  37.3 us
    ppermute x28, waiting for transfers between devices, hop(): return lax.ppermute(value, 'query', [(i, i ^ bits) for i in range(NQ)])  24.1 us
    ppermute x28, starting transfers between devices, hop(): return lax.ppermute(value, 'query', [(i, i ^ bits) for i in range(NQ)])  21.7 us
    unnamed x20, local copies, waits for them, and re-layouts  5.35 us
    ppermute x1, waiting for transfers between devices, paired_body(): lax.ppermute(jnp.concatenate([given_a, given_b], axis=0), 'parts', SWAP)  3.44 us
    pallas_call x1, Pallas kernels, paired_body(): pl.pallas_call(prepare_kernel, in_specs=[SMEM] + [VMEM] * 5, out_specs=[V...  3.31 us
    ppermute x1, waiting for transfers between devices, paired_body(): total = keep + lax.ppermute(give, 'parts', SWAP)  3.14 us
    ppermute x1, starting transfers between devices, paired_body(): train_other = lax.ppermute(train_inputs, 'parts', SWAP)  3 us
  transfers between devices with their start and end apart: 34, of which 13 were waited for; matrix products, arithmetic and copies ran while one was open for 6% of the time, Pallas kernels for 19%

profile of v4, /device:TPU:0, one launch (start us, length us, event | category | flops | bytes accessed | tf_op | source)
XLA Modules:
  0.0 121.3 jit_solution(3848259563120485326)
XLA Ops:
  0.6 3.0 %collective-permute-start = (bf16[2,8,4096]{2,1,0:T(8,128)(2,1)}, bf16[2,8,4096]{2,1,0:T(8,128)(2,1)S(1)}, u32[]{:S(2)}, u32[]{:S(2)}) collective-permute-start(bf16[2,8,4096]{2,1,0:T(8,128)(2,1)} %own.2), channel_id=1, source_target_pairs={{0,16},{16,0},{1,17},{17,1},{2,18},{18,2},{3,19},{19,3},{4,20},{20... | collective-permute-start | bytes 393224 | tf_op jit(solution)/shard_map/ppermute | solution.py:312
  5.4 2.0 %collective-permute-done.other = bf16[2,8,4096]{2,1,0:T(8,128)(2,1)S(1)} collective-permute-done((bf16[2,8,4096]{2,1,0:T(8,128)(2,1)}, bf16[2,8,4096]{2,1,0:T(8,128)(2,1)S(1)}, u32[]{:S(2)}, u32[]{:S(2)}) %collective-permute-start) | collective-permute-done | bytes 131104 | tf_op jit(solution)/shard_map/ppermute | solution.py:312
  8.0 2.4 %shard_map.104 = (bf16[20,32,128]{2,1,0:T(8,128)(2,1)}, bf16[20,32,128]{2,1,0:T(8,128)(2,1)}) custom-call(s32[33]{0:T(128)} %pad_add_fusion.1.info, bf16[2,8,4096]{2,1,0:T(8,128)(2,1)} %own.2, bf16[2,8,4096]{2,1,0:T(8,128)(2,1)} %copy-done.6, bf16[2,16,4096]{2,1,0:T(8,128)(2,1)} %query.2, bf16[4,128,128]{2,1,0:T(8,128)(2,1)} %basis.1), custom_call_target="tpu_custom_call" | custom-call | tf_op jit(solution)/shard_map/pallas_call | solution.py:320
  10.4 2.8 %collective-permute-start.1 = (bf16[20,32,128]{2,1,0:T(8,128)(2,1)}, bf16[20,32,128]{2,1,0:T(8,128)(2,1)S(1)}, u32[]{:S(2)}, u32[]{:S(2)}) collective-permute-start(bf16[20,32,128]{2,1,0:T(8,128)(2,1)} %get-tuple-element.27.refs_0_), channel_id=1, source_target_pairs={{0,8},{1,9},{2,10},{3,11},{4,12},{5,13},{6,14},{7,15},{8,0},{9,1},... | collective-permute-start | bytes 491528 | tf_op jit(solution)/shard_map/ppermute | solution.py:90
  13.2 1.5 %collective-permute-start.14 = (bf16[2,128,768]{2,1,0:T(8,128)(2,1)}, bf16[2,128,768]{2,1,0:T(8,128)(2,1)S(1)}, u32[]{:S(2)}, u32[]{:S(2)}) collective-permute-start(bf16[2,128,768]{2,1,0:T(8,128)(2,1)} %own.3), channel_id=1, source_target_pairs={{0,16},{16,0},{1,17},{17,1},{2,18},{18,2},{3,19},{19,3},{4,20},{20... | collective-permute-start | bytes 1179656 | tf_op jit(solution)/shard_map/ppermute | solution.py:328
  14.7 1.6 %collective-permute-start.9 = (bf16[20,32,128]{2,1,0:T(8,128)(2,1)}, bf16[20,32,128]{2,1,0:T(8,128)(2,1)S(1)}, u32[]{:S(2)}, u32[]{:S(2)}) collective-permute-start(bf16[20,32,128]{2,1,0:T(8,128)(2,1)} %get-tuple-element.27.refs_0_), channel_id=1, source_target_pairs={{0,4},{1,5},{2,6},{3,7},{4,0},{5,1},{6,2},{7,3},{8,12},{9,13},{10,... | collective-permute-start | bytes 491528 | tf_op jit(solution)/shard_map/ppermute | solution.py:90
  16.5 1.5 %collective-permute-start.7 = (bf16[20,32,128]{2,1,0:T(8,128)(2,1)}, bf16[20,32,128]{2,1,0:T(8,128)(2,1)S(1)}, u32[]{:S(2)}, u32[]{:S(2)}) collective-permute-start(bf16[20,32,128]{2,1,0:T(8,128)(2,1)} %get-tuple-element.27.refs_0_), channel_id=1, source_target_pairs={{0,2},{1,3},{2,0},{3,1},{4,6},{5,7},{6,4},{7,5},{8,10},{9,11},{10,... | collective-permute-start | bytes 491528 | tf_op jit(solution)/shard_map/ppermute | solution.py:90
  18.0 7.0 %collective-permute-done.1.refs_8_ = bf16[20,32,128]{2,1,0:T(8,128)(2,1)S(1)} collective-permute-done((bf16[20,32,128]{2,1,0:T(8,128)(2,1)}, bf16[20,32,128]{2,1,0:T(8,128)(2,1)S(1)}, u32[]{:S(2)}, u32[]{:S(2)}) %collective-permute-start.1) | collective-permute-done | bytes 163872 | tf_op jit(solution)/shard_map/ppermute | solution.py:90
  25.0 1.1 fusion.6
  26.4 1.5 %collective-permute-start.21 = (s32[128]{0:T(128)}, s32[128]{0:T(128)S(1)}, u32[]{:S(2)}, u32[]{:S(2)}) collective-permute-start(s32[128]{0:T(128)} %param.11), channel_id=1, source_target_pairs={{0,16},{16,0},{1,17},{17,1},{2,18},{18,2},{3,19},{19,3},{4,20},{20... | collective-permute-start | bytes 1544 | tf_op jit(solution)/shard_map/ppermute | solution.py:327
  29.8 3.3 %shard_map.105 = (bf16[2,256,768]{2,1,0:T(8,128)(2,1)}, bf16[2,768,256]{2,1,0:T(8,128)(2,1)}) custom-call(s32[1]{0:T(128)} %bitcast.2.info, bf16[2,128,768]{2,1,0:T(8,128)(2,1)} %own.3, bf16[2,128,768]{2,1,0:T(8,128)(2,1)} %copy-done.5, bf16[2,256,768]{2,1,0:T(8,128)(2,1)} %query.3, bf16[2,6,128,128]{3,2,1,0:T(8,128)(2,1)} %copy.24.block, ...), custom_call_target="tpu_custom_call" | custom-call | tf_op jit(solution)/shard_map/pallas_call | solution.py:344
  33.4 1.5 %collective-permute-start.11 = (bf16[20,32,128]{2,1,0:T(8,128)(2,1)S(1)}, bf16[20,32,128]{2,1,0:T(8,128)(2,1)S(1)}, u32[]{:S(2)}, u32[]{:S(2)}) collective-permute-start(bf16[20,32,128]{2,1,0:T(8,128)(2,1)S(1)} %collective-permute-done.9.refs_4_), channel_id=1, source_target_pairs={{0,2},{1,3},{2,0},{3,1},{4,6},{5,7},{6,4},{7,5},{8,10},{9,11},{10,... | collective-permute-start | bytes 491528 | tf_op jit(solution)/shard_map/ppermute | solution.py:90
  35.5 1.5 %collective-permute-start.15 = (bf16[20,32,128]{2,1,0:T(8,128)(2,1)S(1)}, bf16[20,32,128]{2,1,0:T(8,128)(2,1)S(1)}, u32[]{:S(2)}, u32[]{:S(2)}) collective-permute-start(bf16[20,32,128]{2,1,0:T(8,128)(2,1)S(1)} %collective-permute-done.1.refs_8_), channel_id=1, source_target_pairs={{0,2},{1,3},{2,0},{3,1},{4,6},{5,7},{6,4},{7,5},{8,10},{9,11},{10,... | collective-permute-start | bytes 491528 | tf_op jit(solution)/shard_map/ppermute | solution.py:90
  37.9 2.5 %collective-permute-done.11.refs_6_ = bf16[20,32,128]{2,1,0:T(8,128)(2,1)S(1)} collective-permute-done((bf16[20,32,128]{2,1,0:T(8,128)(2,1)S(1)}, bf16[20,32,128]{2,1,0:T(8,128)(2,1)S(1)}, u32[]{:S(2)}, u32[]{:S(2)}) %collective-permute-start.11) | collective-permute-done | bytes 163872 | tf_op jit(solution)/shard_map/ppermute | solution.py:90
  40.4 3.5 %collective-permute-done.19.refs_14_ = bf16[20,32,128]{2,1,0:T(8,128)(2,1)S(1)} collective-permute-done((bf16[20,32,128]{2,1,0:T(8,128)(2,1)S(1)}, bf16[20,32,128]{2,1,0:T(8,128)(2,1)S(1)}, u32[]{:S(2)}, u32[]{:S(2)}) %collective-permute-start.19) | collective-permute-done | bytes 163872 | tf_op jit(solution)/shard_map/ppermute | solution.py:90
  44.5 2.3 %collective-permute-done.15.refs_10_ = bf16[20,32,128]{2,1,0:T(8,128)(2,1)S(1)} collective-permute-done((bf16[20,32,128]{2,1,0:T(8,128)(2,1)S(1)}, bf16[20,32,128]{2,1,0:T(8,128)(2,1)S(1)}, u32[]{:S(2)}, u32[]{:S(2)}) %collective-permute-start.15) | collective-permute-done | bytes 163872 | tf_op jit(solution)/shard_map/ppermute | solution.py:90
  47.1 2.7 %collective-permute-start.3 = (bf16[20,32,128]{2,1,0:T(8,128)(2,1)}, bf16[20,32,128]{2,1,0:T(8,128)(2,1)S(1)}, u32[]{:S(2)}, u32[]{:S(2)}) collective-permute-start(bf16[20,32,128]{2,1,0:T(8,128)(2,1)} %get-tuple-element.28.refs_0_), channel_id=1, source_target_pairs={{0,12},{1,13},{2,14},{3,15},{4,8},{5,9},{6,10},{7,11},{8,4},{9,5},... | collective-permute-start | bytes 491528 | tf_op jit(solution)/shard_map/ppermute | solution.py:90
  50.6 1.5 %collective-permute-start.5 = (bf16[20,32,128]{2,1,0:T(8,128)(2,1)}, bf16[20,32,128]{2,1,0:T(8,128)(2,1)S(1)}, u32[]{:S(2)}, u32[]{:S(2)}) collective-permute-start(bf16[20,32,128]{2,1,0:T(8,128)(2,1)} %get-tuple-element.28.refs_0_), channel_id=1, source_target_pairs={{0,2},{1,3},{2,0},{3,1},{4,6},{5,7},{6,4},{7,5},{8,10},{9,11},{10,... | collective-permute-start | bytes 491528 | tf_op jit(solution)/shard_map/ppermute | solution.py:90
  52.1 1.1 copy-done.1
  53.2 1.1 copy-done.2
  55.3 9.7 %shard_map.106 = (f32[8,256]{1,0:T(8,128)S(1)}, bf16[8,8,128]{2,1,0:T(8,128)(2,1)S(1)}, bf16[8,8,128]{2,1,0:T(8,128)(2,1)S(1)}) custom-call(s32[34]{0:T(128)S(1)} %pad_add_fusion.info_ref, bf16[20,32,128]{2,1,0:T(8,128)(2,1)S(1)} %copy-done.4, bf16[20,32,128]{2,1,0:T(8,128)(2,1)S(1)} %collective-permute-done.6.refs_1_, ...), custom_call_target="tpu_custom_call" | custom-call | flops 8000000000 | bytes 4000000 | tf_op jit(solution)/shard_map/pallas_call | solution.py:258
  65.7 1.6 %collective-permute-start.22 = (bf16[3,20,32,128]{3,2,1,0:T(8,128)(2,1)S(1)}, bf16[3,20,32,128]{3,2,1,0:T(8,128)(2,1)S(1)}, u32[]{:S(2)}, u32[]{:S(2)}) collective-permute-start(bf16[3,20,32,128]{3,2,1,0:T(8,128)(2,1)S(1)} %pad_maximum_fusion.refs_2_), channel_id=1, source_target_pairs={{0,2},{1,3},{2,0},{3,1},{4,6},{5,7},{6,4},{7,5},{8,10},{9,11},{10,... | collective-permute-start | bytes 1474568 | tf_op jit(solution)/shard_map/ppermute | solution.py:90
  67.3 9.9 %shard_map.107 = (f32[8,256]{1,0:T(8,128)S(1)}, bf16[8,8,128]{2,1,0:T(8,128)(2,1)S(1)}, bf16[8,8,128]{2,1,0:T(8,128)(2,1)S(1)}) custom-call(s32[34]{0:T(128)S(1)} %pad_add_fusion.info_ref, bf16[20,32,128]{2,1,0:T(8,128)(2,1)S(1)} %copy-done.4, bf16[20,32,128]{2,1,0:T(8,128)(2,1)S(1)} %collective-permute-done.6.refs_1_, ...), custom_call_target="tpu_custom_call" | custom-call | flops 8000000000 | bytes 4000000 | tf_op jit(solution)/shard_map/pallas_call | solution.py:258
  77.2 1.1 collective-permute-done.22.refs_3_
  79.4 3.4 %collective-permute-done.27.came0 = bf16[16,8,128]{2,1,0:T(8,128)(2,1)S(1)} collective-permute-done((bf16[16,8,128]{2,1,0:T(8,128)(2,1)S(1)}, bf16[16,8,128]{2,1,0:T(8,128)(2,1)S(1)}, u32[]{:S(2)}, u32[]{:S(2)}) %collective-permute-start.27) | collective-permute-done | bytes 32800 | tf_op jit(solution)/shard_map/ppermute | solution.py:387
  82.9 17.6 %shard_map.108 = (f32[4,256]{1,0:T(4,128)S(1)}, f32[4,256]{1,0:T(4,128)S(1)}, bf16[16,8,128]{2,1,0:T(8,128)(2,1)S(1)}, bf16[16,8,128]{2,1,0:T(8,128)(2,1)S(1)}) custom-call(s32[34]{0:T(128)S(1)} %pad_add_fusion.info_ref, bf16[20,32,128]{2,1,0:T(8,128)(2,1)S(1)} %copy-done.3, bf16[20,32,128]{2,1,0:T(8,128)(2,1)S(1)} %collective-permute-done.5.refs_1_, ...), custom_call_target="tpu_custom_call" | custom-call | flops 16000000000 | bytes 8000000 | tf_op jit(solution)/shard_map/pallas_call | solution.py:258
  101.6 3.1 %collective-permute-done.28 = f32[4,256]{1,0:T(4,128)S(1)} collective-permute-done((f32[4,256]{1,0:T(4,128)S(1)}, f32[4,256]{1,0:T(4,128)S(1)}, u32[]{:S(2)}, u32[]{:S(2)}) %collective-permute-start.28) | collective-permute-done | bytes 4128 | tf_op jit(solution)/shard_map/ppermute | solution.py:392
  105.9 1.5 %collective-permute-start.30 = (f32[4,256]{1,0:T(4,128)S(1)}, f32[4,256]{1,0:T(4,128)S(1)}, u32[]{:S(2)}, u32[]{:S(2)}) collective-permute-start(f32[4,256]{1,0:T(4,128)S(1)} %add.31), channel_id=1, source_target_pairs={{0,2},{1,3},{2,0},{3,1},{4,6},{5,7},{6,4},{7,5},{8,10},{9,11},{10,... | collective-permute-start | bytes 12296 | tf_op jit(solution)/shard_map/ppermute | solution.py:90
  110.8 2.4 %collective-permute-done.31 = f32[4,256]{1,0:T(4,128)S(1)} collective-permute-done((f32[4,256]{1,0:T(4,128)S(1)}, f32[4,256]{1,0:T(4,128)S(1)}, u32[]{:S(2)}, u32[]{:S(2)}) %collective-permute-start.31) | collective-permute-done | bytes 4128 | tf_op jit(solution)/shard_map/ppermute | solution.py:90
  113.7 2.3 %shard_map.109 = bf16[2,8,4096]{2,1,0:T(8,128)(2,1)} custom-call(s32[64]{0:T(128)} %pad_add_fusion.2.tiles, bf16[16,8,128]{2,1,0:T(8,128)(2,1)} %pad_maximum_fusion.2.kept0, bf16[16,8,128]{2,1,0:T(8,128)(2,1)} %copy-done.7, bf16[16,8,128]{2,1,0:T(8,128)(2,1)} %copy-done, bf16[16,8,128]{2,1,0:T(8,128)(2,1)} %copy-done.8), custom_call_target="tpu_custom_call" | custom-call | tf_op jit(solution)/shard_map/pallas_call | solution.py:394
  116.0 1.8 %collective-permute-start.33 = (f32[4,256]{1,0:T(4,128)S(1)}, f32[4,256]{1,0:T(4,128)S(1)}, u32[]{:S(2)}, u32[]{:S(2)}) collective-permute-start(f32[4,256]{1,0:T(4,128)S(1)} %add.33), channel_id=1, source_target_pairs={{0,8},{1,9},{2,10},{3,11},{4,12},{5,13},{6,14},{7,15},{8,0},{9,1},... | collective-permute-start | bytes 12296 | tf_op jit(solution)/shard_map/ppermute | solution.py:90
  117.9 2.7 %collective-permute-done.33 = f32[4,256]{1,0:T(4,128)S(1)} collective-permute-done((f32[4,256]{1,0:T(4,128)S(1)}, f32[4,256]{1,0:T(4,128)S(1)}, u32[]{:S(2)}, u32[]{:S(2)}) %collective-permute-start.33) | collective-permute-done | bytes 4128 | tf_op jit(solution)/shard_map/ppermute | solution.py:90
  (92 shorter events, 17.7 us)
Async XLA Ops:
  0.6 6.7 %collective-permute-start = (bf16[2,8,4096]{2,1,0:T(8,128)(2,1)}, bf16[2,8,4096]{2,1,0:T(8,128)(2,1)S(1)}, u32[]{:S(2)}, u32[]{:S(2)}) collective-permute-start(bf16[2,8,4096]{2,1,0:T(8,128)(2,1)} %own.2), channel_id=1, source_target_pairs={{0,16},{16,0},{1,17},{17,1},{2,18},{18,2},{3,19},{19,3},{4,20},{20... | collective-permute-start | bytes 393224 | tf_op jit(solution)/shard_map/ppermute | solution.py:312
  10.4 14.6 %collective-permute-start.1 = (bf16[20,32,128]{2,1,0:T(8,128)(2,1)}, bf16[20,32,128]{2,1,0:T(8,128)(2,1)S(1)}, u32[]{:S(2)}, u32[]{:S(2)}) collective-permute-start(bf16[20,32,128]{2,1,0:T(8,128)(2,1)} %get-tuple-element.27.refs_0_), channel_id=1, source_target_pairs={{0,8},{1,9},{2,10},{3,11},{4,12},{5,13},{6,14},{7,15},{8,0},{9,1},... | collective-permute-start | bytes 491528 | tf_op jit(solution)/shard_map/ppermute | solution.py:90
  13.2 13.2 %collective-permute-start.14 = (bf16[2,128,768]{2,1,0:T(8,128)(2,1)}, bf16[2,128,768]{2,1,0:T(8,128)(2,1)S(1)}, u32[]{:S(2)}, u32[]{:S(2)}) collective-permute-start(bf16[2,128,768]{2,1,0:T(8,128)(2,1)} %own.3), channel_id=1, source_target_pairs={{0,16},{16,0},{1,17},{17,1},{2,18},{18,2},{3,19},{19,3},{4,20},{20... | collective-permute-start | bytes 1179656 | tf_op jit(solution)/shard_map/ppermute | solution.py:328
  14.7 18.7 %collective-permute-start.9 = (bf16[20,32,128]{2,1,0:T(8,128)(2,1)}, bf16[20,32,128]{2,1,0:T(8,128)(2,1)S(1)}, u32[]{:S(2)}, u32[]{:S(2)}) collective-permute-start(bf16[20,32,128]{2,1,0:T(8,128)(2,1)} %get-tuple-element.27.refs_0_), channel_id=1, source_target_pairs={{0,4},{1,5},{2,6},{3,7},{4,0},{5,1},{6,2},{7,3},{8,12},{9,13},{10,... | collective-permute-start | bytes 491528 | tf_op jit(solution)/shard_map/ppermute | solution.py:90
  16.3 18.6 %collective-permute-start.17 = (bf16[20,32,128]{2,1,0:T(8,128)(2,1)}, bf16[20,32,128]{2,1,0:T(8,128)(2,1)S(1)}, u32[]{:S(2)}, u32[]{:S(2)}) collective-permute-start(bf16[20,32,128]{2,1,0:T(8,128)(2,1)} %get-tuple-element.27.refs_0_), channel_id=1, source_target_pairs={{0,12},{1,13},{2,14},{3,15},{4,8},{5,9},{6,10},{7,11},{8,4},{9,5},... | collective-permute-start | bytes 491528 | tf_op jit(solution)/shard_map/ppermute | solution.py:90
  16.5 18.4 %collective-permute-start.7 = (bf16[20,32,128]{2,1,0:T(8,128)(2,1)}, bf16[20,32,128]{2,1,0:T(8,128)(2,1)S(1)}, u32[]{:S(2)}, u32[]{:S(2)}) collective-permute-start(bf16[20,32,128]{2,1,0:T(8,128)(2,1)} %get-tuple-element.27.refs_0_), channel_id=1, source_target_pairs={{0,2},{1,3},{2,0},{3,1},{4,6},{5,7},{6,4},{7,5},{8,10},{9,11},{10,... | collective-permute-start | bytes 491528 | tf_op jit(solution)/shard_map/ppermute | solution.py:90
  25.0 10.5 %collective-permute-start.6 = (bf16[20,32,128]{2,1,0:T(8,128)(2,1)}, bf16[20,32,128]{2,1,0:T(8,128)(2,1)S(1)}, u32[]{:S(2)}, u32[]{:S(2)}) collective-permute-start(bf16[20,32,128]{2,1,0:T(8,128)(2,1)} %get-tuple-element.27.refs_0_), channel_id=1, source_target_pairs={{0,1},{1,0},{2,3},{3,2},{4,5},{5,4},{6,7},{7,6},{8,9},{9,8},{10,11... | collective-permute-start | bytes 491528 | tf_op jit(solution)/shard_map/ppermute | solution.py:90
  26.4 6.7 %collective-permute-start.21 = (s32[128]{0:T(128)}, s32[128]{0:T(128)S(1)}, u32[]{:S(2)}, u32[]{:S(2)}) collective-permute-start(s32[128]{0:T(128)} %param.11), channel_id=1, source_target_pairs={{0,16},{16,0},{1,17},{17,1},{2,18},{18,2},{3,19},{19,3},{4,20},{20... | collective-permute-start | bytes 1544 | tf_op jit(solution)/shard_map/ppermute | solution.py:327
  33.1 10.8 %collective-permute-start.13 = (bf16[20,32,128]{2,1,0:T(8,128)(2,1)S(1)}, bf16[20,32,128]{2,1,0:T(8,128)(2,1)S(1)}, u32[]{:S(2)}, u32[]{:S(2)}) collective-permute-start(bf16[20,32,128]{2,1,0:T(8,128)(2,1)S(1)} %collective-permute-done.1.refs_8_), channel_id=1, source_target_pairs={{0,1},{1,0},{2,3},{3,2},{4,5},{5,4},{6,7},{7,6},{8,9},{9,8},{10,11... | collective-permute-start | bytes 491528 | tf_op jit(solution)/shard_map/ppermute | solution.py:90
  33.4 7.0 %collective-permute-start.11 = (bf16[20,32,128]{2,1,0:T(8,128)(2,1)S(1)}, bf16[20,32,128]{2,1,0:T(8,128)(2,1)S(1)}, u32[]{:S(2)}, u32[]{:S(2)}) collective-permute-start(bf16[20,32,128]{2,1,0:T(8,128)(2,1)S(1)} %collective-permute-done.9.refs_4_), channel_id=1, source_target_pairs={{0,2},{1,3},{2,0},{3,1},{4,6},{5,7},{6,4},{7,5},{8,10},{9,11},{10,... | collective-permute-start | bytes 491528 | tf_op jit(solution)/shard_map/ppermute | solution.py:90
  34.9 9.5 %collective-permute-start.10 = (bf16[20,32,128]{2,1,0:T(8,128)(2,1)S(1)}, bf16[20,32,128]{2,1,0:T(8,128)(2,1)S(1)}, u32[]{:S(2)}, u32[]{:S(2)}) collective-permute-start(bf16[20,32,128]{2,1,0:T(8,128)(2,1)S(1)} %collective-permute-done.9.refs_4_), channel_id=1, source_target_pairs={{0,1},{1,0},{2,3},{3,2},{4,5},{5,4},{6,7},{7,6},{8,9},{9,8},{10,11... | collective-permute-start | bytes 491528 | tf_op jit(solution)/shard_map/ppermute | solution.py:90
  34.9 9.0 %collective-permute-start.19 = (bf16[20,32,128]{2,1,0:T(8,128)(2,1)S(1)}, bf16[20,32,128]{2,1,0:T(8,128)(2,1)S(1)}, u32[]{:S(2)}, u32[]{:S(2)}) collective-permute-start(bf16[20,32,128]{2,1,0:T(8,128)(2,1)S(1)} %collective-permute-done.17.refs_12_), channel_id=1, source_target_pairs={{0,2},{1,3},{2,0},{3,1},{4,6},{5,7},{6,4},{7,5},{8,10},{9,11},{10,... | collective-permute-start | bytes 491528 | tf_op jit(solution)/shard_map/ppermute | solution.py:90
  35.5 11.3 %collective-permute-start.15 = (bf16[20,32,128]{2,1,0:T(8,128)(2,1)S(1)}, bf16[20,32,128]{2,1,0:T(8,128)(2,1)S(1)}, u32[]{:S(2)}, u32[]{:S(2)}) collective-permute-start(bf16[20,32,128]{2,1,0:T(8,128)(2,1)S(1)} %collective-permute-done.1.refs_8_), channel_id=1, source_target_pairs={{0,2},{1,3},{2,0},{3,1},{4,6},{5,7},{6,4},{7,5},{8,10},{9,11},{10,... | collective-permute-start | bytes 491528 | tf_op jit(solution)/shard_map/ppermute | solution.py:90
  40.4 6.6 %collective-permute-start.18 = (bf16[20,32,128]{2,1,0:T(8,128)(2,1)S(1)}, bf16[20,32,128]{2,1,0:T(8,128)(2,1)S(1)}, u32[]{:S(2)}, u32[]{:S(2)}) collective-permute-start(bf16[20,32,128]{2,1,0:T(8,128)(2,1)S(1)} %collective-permute-done.17.refs_12_), channel_id=1, source_target_pairs={{0,1},{1,0},{2,3},{3,2},{4,5},{5,4},{6,7},{7,6},{8,9},{9,8},{10,11... | collective-permute-start | bytes 491528 | tf_op jit(solution)/shard_map/ppermute | solution.py:90
  43.9 5.9 %collective-permute-start.12 = (bf16[20,32,128]{2,1,0:T(8,128)(2,1)S(1)}, bf16[20,32,128]{2,1,0:T(8,128)(2,1)S(1)}, u32[]{:S(2)}, u32[]{:S(2)}) collective-permute-start(bf16[20,32,128]{2,1,0:T(8,128)(2,1)S(1)} %collective-permute-done.11.refs_6_), channel_id=1, source_target_pairs={{0,1},{1,0},{2,3},{3,2},{4,5},{5,4},{6,7},{7,6},{8,9},{9,8},{10,11... | collective-permute-start | bytes 491528 | tf_op jit(solution)/shard_map/ppermute | solution.py:90
  44.4 6.1 %collective-permute-start.20 = (bf16[20,32,128]{2,1,0:T(8,128)(2,1)S(1)}, bf16[20,32,128]{2,1,0:T(8,128)(2,1)S(1)}, u32[]{:S(2)}, u32[]{:S(2)}) collective-permute-start(bf16[20,32,128]{2,1,0:T(8,128)(2,1)S(1)} %collective-permute-done.19.refs_14_), channel_id=1, source_target_pairs={{0,1},{1,0},{2,3},{3,2},{4,5},{5,4},{6,7},{7,6},{8,9},{9,8},{10,11... | collective-permute-start | bytes 491528 | tf_op jit(solution)/shard_map/ppermute | solution.py:90
  46.8 5.3 %collective-permute-start.16 = (bf16[20,32,128]{2,1,0:T(8,128)(2,1)S(1)}, bf16[20,32,128]{2,1,0:T(8,128)(2,1)S(1)}, u32[]{:S(2)}, u32[]{:S(2)}) collective-permute-start(bf16[20,32,128]{2,1,0:T(8,128)(2,1)S(1)} %collective-permute-done.15.refs_10_), channel_id=1, source_target_pairs={{0,1},{1,0},{2,3},{3,2},{4,5},{5,4},{6,7},{7,6},{8,9},{9,8},{10,11... | collective-permute-start | bytes 491528 | tf_op jit(solution)/shard_map/ppermute | solution.py:90
  47.0 18.0 %collective-permute-start.2 = (bf16[20,32,128]{2,1,0:T(8,128)(2,1)}, bf16[20,32,128]{2,1,0:T(8,128)(2,1)S(1)}, u32[]{:S(2)}, u32[]{:S(2)}) collective-permute-start(bf16[20,32,128]{2,1,0:T(8,128)(2,1)} %get-tuple-element.28.refs_0_), channel_id=1, source_target_pairs={{0,4},{1,5},{2,6},{3,7},{4,0},{5,1},{6,2},{7,3},{8,12},{9,13},{10,... | collective-permute-start | bytes 491528 | tf_op jit(solution)/shard_map/ppermute | solution.py:90
  47.1 18.0 %collective-permute-start.3 = (bf16[20,32,128]{2,1,0:T(8,128)(2,1)}, bf16[20,32,128]{2,1,0:T(8,128)(2,1)S(1)}, u32[]{:S(2)}, u32[]{:S(2)}) collective-permute-start(bf16[20,32,128]{2,1,0:T(8,128)(2,1)} %get-tuple-element.28.refs_0_), channel_id=1, source_target_pairs={{0,12},{1,13},{2,14},{3,15},{4,8},{5,9},{6,10},{7,11},{8,4},{9,5},... | collective-permute-start | bytes 491528 | tf_op jit(solution)/shard_map/ppermute | solution.py:90
  49.8 15.8 %collective-permute-start.4 = (bf16[20,32,128]{2,1,0:T(8,128)(2,1)}, bf16[20,32,128]{2,1,0:T(8,128)(2,1)S(1)}, u32[]{:S(2)}, u32[]{:S(2)}) collective-permute-start(bf16[20,32,128]{2,1,0:T(8,128)(2,1)} %get-tuple-element.28.refs_0_), channel_id=1, source_target_pairs={{0,8},{1,9},{2,10},{3,11},{4,12},{5,13},{6,14},{7,15},{8,0},{9,1},... | collective-permute-start | bytes 491528 | tf_op jit(solution)/shard_map/ppermute | solution.py:90
  50.6 15.1 %collective-permute-start.5 = (bf16[20,32,128]{2,1,0:T(8,128)(2,1)}, bf16[20,32,128]{2,1,0:T(8,128)(2,1)S(1)}, u32[]{:S(2)}, u32[]{:S(2)}) collective-permute-start(bf16[20,32,128]{2,1,0:T(8,128)(2,1)} %get-tuple-element.28.refs_0_), channel_id=1, source_target_pairs={{0,2},{1,3},{2,0},{3,1},{4,6},{5,7},{6,4},{7,5},{8,10},{9,11},{10,... | collective-permute-start | bytes 491528 | tf_op jit(solution)/shard_map/ppermute | solution.py:90
  65.7 12.6 %collective-permute-start.22 = (bf16[3,20,32,128]{3,2,1,0:T(8,128)(2,1)S(1)}, bf16[3,20,32,128]{3,2,1,0:T(8,128)(2,1)S(1)}, u32[]{:S(2)}, u32[]{:S(2)}) collective-permute-start(bf16[3,20,32,128]{3,2,1,0:T(8,128)(2,1)S(1)} %pad_maximum_fusion.refs_2_), channel_id=1, source_target_pairs={{0,2},{1,3},{2,0},{3,1},{4,6},{5,7},{6,4},{7,5},{8,10},{9,11},{10,... | collective-permute-start | bytes 1474568 | tf_op jit(solution)/shard_map/ppermute | solution.py:90
  67.3 15.6 %collective-permute-start.25 = (bf16[3,20,32,128]{3,2,1,0:T(8,128)(2,1)S(1)}, bf16[3,20,32,128]{3,2,1,0:T(8,128)(2,1)S(1)}, u32[]{:S(2)}, u32[]{:S(2)}) collective-permute-start(bf16[3,20,32,128]{3,2,1,0:T(8,128)(2,1)S(1)} %pad_maximum_fusion.refs_2_), channel_id=1, source_target_pairs={{0,1},{1,0},{2,3},{3,2},{4,5},{5,4},{6,7},{7,6},{8,9},{9,8},{10,11... | collective-permute-start | bytes 1474568 | tf_op jit(solution)/shard_map/ppermute | solution.py:90
  78.3 4.5 %collective-permute-start.26 = (bf16[3,20,32,128]{3,2,1,0:T(8,128)(2,1)S(1)}, bf16[3,20,32,128]{3,2,1,0:T(8,128)(2,1)S(1)}, u32[]{:S(2)}, u32[]{:S(2)}) collective-permute-start(bf16[3,20,32,128]{3,2,1,0:T(8,128)(2,1)S(1)} %collective-permute-done.22.refs_3_), channel_id=1, source_target_pairs={{0,1},{1,0},{2,3},{3,2},{4,5},{5,4},{6,7},{7,6},{8,9},{9,8},{10,11... | collective-permute-start | bytes 1474568 | tf_op jit(solution)/shard_map/ppermute | solution.py:90
  78.3 4.5 %collective-permute-start.23 = (bf16[20,32,128]{2,1,0:T(8,128)(2,1)S(1)}, bf16[20,32,128]{2,1,0:T(8,128)(2,1)S(1)}, u32[]{:S(2)}, u32[]{:S(2)}) collective-permute-start(bf16[20,32,128]{2,1,0:T(8,128)(2,1)S(1)} %copy-done.3), channel_id=1, source_target_pairs={{0,1},{1,0},{2,3},{3,2},{4,5},{5,4},{6,7},{7,6},{8,9},{9,8},{10,11... | collective-permute-start | bytes 491528 | tf_op jit(solution)/shard_map/ppermute | solution.py:90
  78.8 4.0 %collective-permute-start.24 = (bf16[20,32,128]{2,1,0:T(8,128)(2,1)S(1)}, bf16[20,32,128]{2,1,0:T(8,128)(2,1)S(1)}, u32[]{:S(2)}, u32[]{:S(2)}) collective-permute-start(bf16[20,32,128]{2,1,0:T(8,128)(2,1)S(1)} %collective-permute-done.5.refs_1_), channel_id=1, source_target_pairs={{0,1},{1,0},{2,3},{3,2},{4,5},{5,4},{6,7},{7,6},{8,9},{9,8},{10,11... | collective-permute-start | bytes 491528 | tf_op jit(solution)/shard_map/ppermute | solution.py:90
  78.9 4.0 %collective-permute-start.27 = (bf16[16,8,128]{2,1,0:T(8,128)(2,1)S(1)}, bf16[16,8,128]{2,1,0:T(8,128)(2,1)S(1)}, u32[]{:S(2)}, u32[]{:S(2)}) collective-permute-start(bf16[16,8,128]{2,1,0:T(8,128)(2,1)S(1)} %pad_maximum_fusion.1), channel_id=1, source_target_pairs={{0,16},{16,0},{1,17},{17,1},{2,18},{18,2},{3,19},{19,3},{4,20},{20... | collective-permute-start | bytes 98312 | tf_op jit(solution)/shard_map/ppermute | solution.py:387
  101.1 3.6 %collective-permute-start.28 = (f32[4,256]{1,0:T(4,128)S(1)}, f32[4,256]{1,0:T(4,128)S(1)}, u32[]{:S(2)}, u32[]{:S(2)}) collective-permute-start(f32[4,256]{1,0:T(4,128)S(1)} %get-tuple-element.44), channel_id=1, source_target_pairs={{0,16},{16,0},{1,17},{17,1},{2,18},{18,2},{3,19},{19,3},{4,20},{20... | collective-permute-start | bytes 12296 | tf_op jit(solution)/shard_map/ppermute | solution.py:392
  105.9 3.6 %collective-permute-start.30 = (f32[4,256]{1,0:T(4,128)S(1)}, f32[4,256]{1,0:T(4,128)S(1)}, u32[]{:S(2)}, u32[]{:S(2)}) collective-permute-start(f32[4,256]{1,0:T(4,128)S(1)} %add.31), channel_id=1, source_target_pairs={{0,2},{1,3},{2,0},{3,1},{4,6},{5,7},{6,4},{7,5},{8,10},{9,11},{10,... | collective-permute-start | bytes 12296 | tf_op jit(solution)/shard_map/ppermute | solution.py:90
  108.0 5.1 %collective-permute-start.32 = (bf16[16,8,128]{2,1,0:T(8,128)(2,1)S(1)}, bf16[16,8,128]{2,1,0:T(8,128)(2,1)S(1)}, u32[]{:S(2)}, u32[]{:S(2)}) collective-permute-start(bf16[16,8,128]{2,1,0:T(8,128)(2,1)S(1)} %get-tuple-element.48), channel_id=1, source_target_pairs={{0,16},{16,0},{1,17},{17,1},{2,18},{18,2},{3,19},{19,3},{4,20},{20... | collective-permute-start | bytes 98312 | tf_op jit(solution)/shard_map/ppermute | solution.py:393
  109.5 3.6 %collective-permute-start.31 = (f32[4,256]{1,0:T(4,128)S(1)}, f32[4,256]{1,0:T(4,128)S(1)}, u32[]{:S(2)}, u32[]{:S(2)}) collective-permute-start(f32[4,256]{1,0:T(4,128)S(1)} %add.32), channel_id=1, source_target_pairs={{0,4},{1,5},{2,6},{3,7},{4,0},{5,1},{6,2},{7,3},{8,12},{9,13},{10,... | collective-permute-start | bytes 12296 | tf_op jit(solution)/shard_map/ppermute | solution.py:90
  116.0 4.5 %collective-permute-start.33 = (f32[4,256]{1,0:T(4,128)S(1)}, f32[4,256]{1,0:T(4,128)S(1)}, u32[]{:S(2)}, u32[]{:S(2)}) collective-permute-start(f32[4,256]{1,0:T(4,128)S(1)} %add.33), channel_id=1, source_target_pairs={{0,8},{1,9},{2,10},{3,11},{4,12},{5,13},{6,14},{7,15},{8,0},{9,1},... | collective-permute-start | bytes 12296 | tf_op jit(solution)/shard_map/ppermute | solution.py:90
  (11 other events, 53.5 us)

commit v5 on v4

--- a/solution.py
+++ b/solution.py
@@ -96,8 +96,7 @@
     for wave in range(WAVES):
         unit = units[wave]
 
-        @pl.loop(0, NQ)
-        def _(owner):
+        for owner in range(NQ):
             tile = info[1 + wave * NQ + owner]
             layer = tile // 32
             cols = pl.ds(pl.multiple_of((tile % 32) * TILE_A, TILE_A), TILE_A)
@@ -111,19 +110,23 @@
         unit[NQ:] = basis[2 * x + wave].reshape(4, 32, TILE_A)
 
 
-def prepare_kernel(info, own, other, query, block, block_t, grads, query_grads):
+def prepare_kernel(info, own, other, query, tiles, grads, query_grads):
     x = info[0]
+    blank = jnp.zeros((TILE_S, TILE_S), jnp.float32)
     for layer in range(LAYERS):
-        for c in range(block.shape[1]):
+        for c in range(tiles.shape[1] // 2):
             cols = slice(c * TILE_A, (c + 1) * TILE_A)
-            tile = block[layer, c]
+            upper = jnp.concatenate([tiles[layer, 2 * c].astype(jnp.float32), blank], axis=1)
+            lower = jnp.concatenate([blank, tiles[layer, 2 * c + 1].astype(jnp.float32)], axis=1)
+            block = jnp.concatenate([upper, lower], axis=0)
+            tile = block.astype(BF)
             mine = jnp.dot(own[layer, :, cols], tile, preferred_element_type=jnp.float32)
             came = jnp.dot(other[layer, :, cols], tile, preferred_element_type=jnp.float32)
             first = jnp.where(x == 0, mine, came).reshape(NQ, 1, 8, TILE_A)
             second = jnp.where(x == 0, came, mine).reshape(NQ, 1, 8, TILE_A)
             rows = jnp.concatenate([first, second], axis=1).reshape(TOKENS, TILE_A)
             grads[layer, :, cols] = rows.astype(BF)
-            query_grads[layer, cols, :] = across(block_t[layer, c], query[layer, :, cols]).astype(BF)
+            query_grads[layer, cols, :] = across(block.T.astype(BF), query[layer, :, cols]).astype(BF)
 
 
 def across(left, right):
@@ -275,21 +278,25 @@
         ],
         compiler_params=pltpu.CompilerParams(vmem_limit_bytes=42 * 1024 * 1024),
         cost_estimate=pl.CostEstimate(
-            flops=count * 10**9, bytes_accessed=count * 10**6 // 2, transcendentals=0
+            flops=count * 10**7 if base == 0 else count * 10**9, bytes_accessed=count * 10**6 // 2, transcendentals=0
         ),
     )(info, *arrays, grads, query_grads, codes, eigenvalues, before)
 
 
-def unpack_kernel(tiles, kept0, came0, kept1, came1, out):
-    for half, pair in enumerate(((kept0, kept1), (came0, came1))):
-        for wave in range(WAVES):
-            source = pair[wave]
-
-            @pl.loop(0, NQ)
-            def _(owner):
-                tile = tiles[half * WAVES * NQ + wave * NQ + owner]
-                cols = pl.ds(pl.multiple_of((tile % 32) * TILE_A, TILE_A), TILE_A)
-                out[tile // 32, :, cols] = source[owner]
+def unpack_kernel(tiles, kept_a, kept_b, kept_c, came, out):
+    first = kept_a.shape[0]
+    both = WAVES * NQ
+    for place in range(2 * both):
+        half, n = place // both, place % both
+        if half:
+            rows = came[n]
+        elif n < first:
+            rows = kept_a[n]
+        else:
+            rows = kept_b[n - first] if n < NQ else kept_c[n - NQ]
+        tile = tiles[place]
+        cols = pl.ds(pl.multiple_of((tile % 32) * TILE_A, TILE_A), TILE_A)
+        out[tile // 32, :, cols] = rows
 
 
 def after(value, *others):
@@ -332,32 +339,24 @@
     id_pair = id_pair + SEQS * jnp.arange(2, dtype=jnp.int32)[:, None]
     codes = id_pair.reshape(2, NQ, 8).transpose(1, 0, 2).reshape(1, TOKENS)
     slab = train_outgrads.shape[2]
-    pairs = output_basis.reshape(LAYERS, slab // TILE_A, 2, TILE_S, TILE_S)
-    blank = jnp.zeros_like(pairs[:, :, 0])
-    block = jnp.concatenate(
-        [
-            jnp.concatenate([pairs[:, :, 0], blank], axis=3),
-            jnp.concatenate([blank, pairs[:, :, 1]], axis=3),
-        ],
-        axis=2,
-    )
     grads, query_grads = pl.pallas_call(
         prepare_kernel,
-        in_specs=[SMEM] + [VMEM] * 5,
+        in_specs=[SMEM] + [VMEM] * 4,
         out_specs=[VMEM, VMEM],
         out_shape=[
             jax.ShapeDtypeStruct((LAYERS, TOKENS, slab), BF),
             jax.ShapeDtypeStruct((LAYERS, slab, TOKENS), BF),
         ],
-    )(side, train_outgrads, out_other, query_outgrads, block, block.transpose(0, 1, 3, 2))
+    )(side, train_outgrads, out_other, query_outgrads, output_basis)
 
     units = [None] * NQ
     units[0] = packed[0]
-    for d in (4, 12, 8):
-        units[d] = hop(packed[0], d)
+    units[4] = hop(packed[0], 4)
+    units[12] = hop(packed[0], 12)
+    units[8] = hop(after(packed[0], units[4], units[12]), 8)
     for d in (0, 4, 12):
         units[d ^ 2] = hop(units[d], 2)
-    units[10] = hop(after(units[8], grads), 2)
+    units[10] = hop(after(units[8], grads, units[2], units[6], units[14]), 2)
     for d in (0, 2, 4, 6, 12, 14, 8, 10):
         units[d ^ 1] = hop(units[d], 1)
     places0 = [(d, None) for d in range(NQ)]
@@ -383,20 +382,19 @@
         across_y = (d & 2) // 2 + 4 * (d & 1)
         far = d & 12
         places1.append((across_y + 2, order[far]) if far else (across_y, None))
-    kept0 = jnp.concatenate([kept_a, kept_b], axis=0)
-    came0 = lax.ppermute(jnp.concatenate([given_a, given_b], axis=0), "parts", SWAP)
     keep, give, kept1, given1 = score_tiles(
-        16, 16, True, info, arrays, places1, *common, after(part1, came0)
+        16, 16, True, info, arrays, places1, *common, part1
     )
 
     total = keep + lax.ppermute(give, "parts", SWAP)
-    came1 = lax.ppermute(given1, "parts", SWAP)
+    came = lax.ppermute(jnp.concatenate([given_a, given_b, given1], axis=0), "parts", SWAP)
+    total = after(total, came)
     rotated_out = pl.pallas_call(
         unpack_kernel,
         in_specs=[SMEM] + [VMEM] * 4,
         out_specs=VMEM,
         out_shape=jax.ShapeDtypeStruct(train_inputs.shape, BF),
-    )(jnp.concatenate([mine, theirs]), kept0, came0, kept1, came1)
+    )(jnp.concatenate([mine, theirs]), kept_a, kept_b, kept1, came)
     for bits in (1, 2, 4):
         total = total + hop(total, bits)
     total = after(total, rotated_out)

time: 122 us -> 110 us (0.902)
  waiting for transfers between devices: 32.6 us -> 21.2 us
  starting transfers between devices: 29.3 us -> 33.1 us
  local copies, waits for them, and re-layouts: 8.79 us -> 6.95 us
  other arithmetic: 4.45 us -> 2.9 us
    ppermute x28, waiting for transfers between devices: 24.1 us -> 16.8 us  [hop(): return lax.ppermute(value, 'query', [(i, i ^ bits) for i in range(NQ)])]
    ppermute x2 -> x1, waiting for transfers between devices: 3.45 us -> 0.01 us  [paired_body(): lax.ppermute(jnp.concatenate([given_a, given_b, given1], axis=0), 'parts'...]
    ppermute x28, starting transfers between devices: 21.7 us -> 25 us  [hop(): return lax.ppermute(value, 'query', [(i, i ^ bits) for i in range(NQ)])]
  transfers between devices with their start and end apart: 34 -> 33, of which waited for: 13 -> 13; matrix products, arithmetic and copies ran while one was open for 6% -> 3% of each run, Pallas kernels for 19% -> 23%
where the time goes in v5:
time: 110 us
  Pallas kernels  44.6 us (41%)
  starting transfers between devices  33.1 us (30%)
  waiting for transfers between devices  21.2 us (19%)
  local copies, waits for them, and re-layouts  6.95 us (6%)
  other arithmetic  2.9 us (3%)
    pallas_call x3, Pallas kernels, score_tiles(): pl.pallas_call(kernel, in_specs=[SMEM] + [VMEM] * len(arrays) + [VMEM, VM...  37.3 us
    ppermute x28, starting transfers between devices, hop(): return lax.ppermute(value, 'query', [(i, i ^ bits) for i in range(NQ)])  25 us
    ppermute x28, waiting for transfers between devices, hop(): return lax.ppermute(value, 'query', [(i, i ^ bits) for i in range(NQ)])  16.8 us
    unnamed x20, local copies, waits for them, and re-layouts  5.49 us
    pallas_call x1, Pallas kernels, paired_body(): pl.pallas_call(prepare_kernel, in_specs=[SMEM] + [VMEM] * 4, out_specs=[V...  3.25 us
    ppermute x1, starting transfers between devices, paired_body(): train_other = lax.ppermute(train_inputs, 'parts', SWAP)  3 us
    ppermute x1, waiting for transfers between devices, paired_body(): total = keep + lax.ppermute(give, 'parts', SWAP)  2.37 us
  transfers between devices with their start and end apart: 33, of which 13 were waited for; matrix products, arithmetic and copies ran while one was open for 3% of the time, Pallas kernels for 23%

profile of v5, /device:TPU:0, one launch (start us, length us, event | category | flops | bytes accessed | tf_op | source)
XLA Modules:
  0.0 109.6 jit_solution(5591952640669639852)
XLA Ops:
  0.6 3.0 %collective-permute-start = (bf16[2,8,4096]{2,1,0:T(8,128)(2,1)}, bf16[2,8,4096]{2,1,0:T(8,128)(2,1)S(1)}, u32[]{:S(2)}, u32[]{:S(2)}) collective-permute-start(bf16[2,8,4096]{2,1,0:T(8,128)(2,1)} %own.2), channel_id=1, source_target_pairs={{0,16},{16,0},{1,17},{17,1},{2,18},{18,2},{3,19},{19,3},{4,20},{20... | collective-permute-start | bytes 393224 | tf_op jit(solution)/shard_map/ppermute | solution.py:319
  5.3 2.0 %collective-permute-done.other = bf16[2,8,4096]{2,1,0:T(8,128)(2,1)S(1)} collective-permute-done((bf16[2,8,4096]{2,1,0:T(8,128)(2,1)}, bf16[2,8,4096]{2,1,0:T(8,128)(2,1)S(1)}, u32[]{:S(2)}, u32[]{:S(2)}) %collective-permute-start) | collective-permute-done | bytes 131104 | tf_op jit(solution)/shard_map/ppermute | solution.py:319
  8.0 2.1 %shard_map.104 = (bf16[20,32,128]{2,1,0:T(8,128)(2,1)}, bf16[20,32,128]{2,1,0:T(8,128)(2,1)}) custom-call(s32[33]{0:T(128)} %pad_add_fusion.1.info, bf16[2,8,4096]{2,1,0:T(8,128)(2,1)} %own.2, bf16[2,8,4096]{2,1,0:T(8,128)(2,1)} %copy-done.8, bf16[2,16,4096]{2,1,0:T(8,128)(2,1)} %query.2, bf16[4,128,128]{2,1,0:T(8,128)(2,1)} %basis.1), custom_call_target="tpu_custom_call" | custom-call | tf_op jit(solution)/shard_map/pallas_call | solution.py:327
  10.1 1.8 %collective-permute-start.1 = (bf16[20,32,128]{2,1,0:T(8,128)(2,1)}, bf16[20,32,128]{2,1,0:T(8,128)(2,1)S(1)}, u32[]{:S(2)}, u32[]{:S(2)}) collective-permute-start(bf16[20,32,128]{2,1,0:T(8,128)(2,1)} %get-tuple-element.29.refs_0_), channel_id=1, source_target_pairs={{0,4},{1,5},{2,6},{3,7},{4,0},{5,1},{6,2},{7,3},{8,12},{9,13},{10,... | collective-permute-start | bytes 491528 | tf_op jit(solution)/shard_map/ppermute | solution.py:90
  11.9 2.5 %collective-permute-start.2 = (bf16[20,32,128]{2,1,0:T(8,128)(2,1)}, bf16[20,32,128]{2,1,0:T(8,128)(2,1)S(1)}, u32[]{:S(2)}, u32[]{:S(2)}) collective-permute-start(bf16[20,32,128]{2,1,0:T(8,128)(2,1)} %get-tuple-element.29.refs_0_), channel_id=1, source_target_pairs={{0,12},{1,13},{2,14},{3,15},{4,8},{5,9},{6,10},{7,11},{8,4},{9,5},... | collective-permute-start | bytes 491528 | tf_op jit(solution)/shard_map/ppermute | solution.py:90
  14.4 1.5 %collective-permute-start.15 = (bf16[2,128,768]{2,1,0:T(8,128)(2,1)}, bf16[2,128,768]{2,1,0:T(8,128)(2,1)S(1)}, u32[]{:S(2)}, u32[]{:S(2)}) collective-permute-start(bf16[2,128,768]{2,1,0:T(8,128)(2,1)} %own.3), channel_id=1, source_target_pairs={{0,16},{16,0},{1,17},{17,1},{2,18},{18,2},{3,19},{19,3},{4,20},{20... | collective-permute-start | bytes 1179656 | tf_op jit(solution)/shard_map/ppermute | solution.py:335
  15.9 1.5 %collective-permute-start.9 = (bf16[20,32,128]{2,1,0:T(8,128)(2,1)}, bf16[20,32,128]{2,1,0:T(8,128)(2,1)S(1)}, u32[]{:S(2)}, u32[]{:S(2)}) collective-permute-start(bf16[20,32,128]{2,1,0:T(8,128)(2,1)} %get-tuple-element.29.refs_0_), channel_id=1, source_target_pairs={{0,2},{1,3},{2,0},{3,1},{4,6},{5,7},{6,4},{7,5},{8,10},{9,11},{10,... | collective-permute-start | bytes 491528 | tf_op jit(solution)/shard_map/ppermute | solution.py:90
  17.4 3.8 %collective-permute-done.2.refs_12_ = bf16[20,32,128]{2,1,0:T(8,128)(2,1)S(1)} collective-permute-done((bf16[20,32,128]{2,1,0:T(8,128)(2,1)}, bf16[20,32,128]{2,1,0:T(8,128)(2,1)S(1)}, u32[]{:S(2)}, u32[]{:S(2)}) %collective-permute-start.2) | collective-permute-done | bytes 163872 | tf_op jit(solution)/shard_map/ppermute | solution.py:90
  21.2 3.6 %collective-permute-start.3 = (bf16[20,32,128]{2,1,0:T(8,128)(2,1)}, bf16[20,32,128]{2,1,0:T(8,128)(2,1)S(1)}, u32[]{:S(2)}, u32[]{:S(2)}) collective-permute-start(bf16[20,32,128]{2,1,0:T(8,128)(2,1)} %get-tuple-element.29.refs_0_), channel_id=1, source_target_pairs={{0,8},{1,9},{2,10},{3,11},{4,12},{5,13},{6,14},{7,15},{8,0},{9,1},... | collective-permute-start | bytes 491528 | tf_op jit(solution)/shard_map/ppermute | solution.py:90
  24.8 1.5 %collective-permute-start.12 = (bf16[20,32,128]{2,1,0:T(8,128)(2,1)S(1)}, bf16[20,32,128]{2,1,0:T(8,128)(2,1)S(1)}, u32[]{:S(2)}, u32[]{:S(2)}) collective-permute-start(bf16[20,32,128]{2,1,0:T(8,128)(2,1)S(1)} %collective-permute-done.1.refs_4_), channel_id=1, source_target_pairs={{0,2},{1,3},{2,0},{3,1},{4,6},{5,7},{6,4},{7,5},{8,10},{9,11},{10,... | collective-permute-start | bytes 491528 | tf_op jit(solution)/shard_map/ppermute | solution.py:90
  26.8 2.7 %collective-permute-done.3.refs_8_ = bf16[20,32,128]{2,1,0:T(8,128)(2,1)S(1)} collective-permute-done((bf16[20,32,128]{2,1,0:T(8,128)(2,1)}, bf16[20,32,128]{2,1,0:T(8,128)(2,1)S(1)}, u32[]{:S(2)}, u32[]{:S(2)}) %collective-permute-start.3) | collective-permute-done | bytes 163872 | tf_op jit(solution)/shard_map/ppermute | solution.py:90
  30.1 1.6 %collective-permute-start.21 = (s32[128]{0:T(128)}, s32[128]{0:T(128)S(1)}, u32[]{:S(2)}, u32[]{:S(2)}) collective-permute-start(s32[128]{0:T(128)} %param.11), channel_id=1, source_target_pairs={{0,16},{16,0},{1,17},{17,1},{2,18},{18,2},{3,19},{19,3},{4,20},{20... | collective-permute-start | bytes 1544 | tf_op jit(solution)/shard_map/ppermute | solution.py:334
  31.7 3.3 %shard_map.105 = (bf16[2,256,768]{2,1,0:T(8,128)(2,1)}, bf16[2,768,256]{2,1,0:T(8,128)(2,1)}) custom-call(s32[1]{0:T(128)} %bitcast.2.info, bf16[2,128,768]{2,1,0:T(8,128)(2,1)} %own.3, bf16[2,128,768]{2,1,0:T(8,128)(2,1)} %copy-done.7, bf16[2,256,768]{2,1,0:T(8,128)(2,1)} %query.3, bf16[2,12,64,64]{3,2,1,0:T(8,128)(2,1)} %tiles.1), custom_call_target="tpu_custom_call" | custom-call | tf_op jit(solution)/shard_map/pallas_call | solution.py:342
  36.0 1.5 %collective-permute-start.17 = (bf16[20,32,128]{2,1,0:T(8,128)(2,1)S(1)}, bf16[20,32,128]{2,1,0:T(8,128)(2,1)S(1)}, u32[]{:S(2)}, u32[]{:S(2)}) collective-permute-start(bf16[20,32,128]{2,1,0:T(8,128)(2,1)S(1)} %collective-permute-done.3.refs_8_), channel_id=1, source_target_pairs={{0,2},{1,3},{2,0},{3,1},{4,6},{5,7},{6,4},{7,5},{8,10},{9,11},{10,... | collective-permute-start | bytes 491528 | tf_op jit(solution)/shard_map/ppermute | solution.py:90
  38.5 3.0 %collective-permute-start.5 = (bf16[20,32,128]{2,1,0:T(8,128)(2,1)}, bf16[20,32,128]{2,1,0:T(8,128)(2,1)S(1)}, u32[]{:S(2)}, u32[]{:S(2)}) collective-permute-start(bf16[20,32,128]{2,1,0:T(8,128)(2,1)} %get-tuple-element.30.refs_0_), channel_id=1, source_target_pairs={{0,12},{1,13},{2,14},{3,15},{4,8},{5,9},{6,10},{7,11},{8,4},{9,5},... | collective-permute-start | bytes 491528 | tf_op jit(solution)/shard_map/ppermute | solution.py:90
  42.7 1.2 %collective-permute-done.18.refs_11_ = bf16[20,32,128]{2,1,0:T(8,128)(2,1)S(1)} collective-permute-done((bf16[20,32,128]{2,1,0:T(8,128)(2,1)S(1)}, bf16[20,32,128]{2,1,0:T(8,128)(2,1)S(1)}, u32[]{:S(2)}, u32[]{:S(2)}) %collective-permute-start.18) | collective-permute-done | bytes 163872 | tf_op jit(solution)/shard_map/ppermute | solution.py:90
  43.9 1.1 %copy-done = bf16[2,256,768]{2,1,0:T(8,128)(2,1)S(1)} copy-done((bf16[2,256,768]{2,1,0:T(8,128)(2,1)S(1)}, bf16[2,256,768]{2,1,0:T(8,128)(2,1)}, u32[]{:S(2)}) %copy-start) | copy-done | bytes 786456
  45.0 1.1 %copy-done.1 = bf16[2,768,256]{2,1,0:T(8,128)(2,1)S(1)} copy-done((bf16[2,768,256]{2,1,0:T(8,128)(2,1)S(1)}, bf16[2,768,256]{2,1,0:T(8,128)(2,1)}, u32[]{:S(2)}) %copy-start.1) | copy-done | bytes 786456
  47.1 9.9 %shard_map.106 = (f32[8,256]{1,0:T(8,128)S(1)}, bf16[8,8,128]{2,1,0:T(8,128)(2,1)S(1)}, bf16[8,8,128]{2,1,0:T(8,128)(2,1)S(1)}) custom-call(s32[34]{0:T(128)S(1)} %pad_add_fusion.info_ref, bf16[20,32,128]{2,1,0:T(8,128)(2,1)S(1)} %copy-done.2, bf16[20,32,128]{2,1,0:T(8,128)(2,1)S(1)} %collective-permute-done.8.refs_1_, ...), custom_call_target="tpu_custom_call" | custom-call | flops 80000000 | bytes 4000000 | tf_op jit(solution)/shard_map/pallas_call | solution.py:261
  57.6 1.5 %collective-permute-start.22 = (bf16[3,20,32,128]{3,2,1,0:T(8,128)(2,1)S(1)}, bf16[3,20,32,128]{3,2,1,0:T(8,128)(2,1)S(1)}, u32[]{:S(2)}, u32[]{:S(2)}) collective-permute-start(bf16[3,20,32,128]{3,2,1,0:T(8,128)(2,1)S(1)} %pad_maximum_fusion.refs_2_), channel_id=1, source_target_pairs={{0,2},{1,3},{2,0},{3,1},{4,6},{5,7},{6,4},{7,5},{8,10},{9,11},{10,... | collective-permute-start | bytes 1474568 | tf_op jit(solution)/shard_map/ppermute | solution.py:90
  59.1 9.7 %shard_map.107 = (f32[8,256]{1,0:T(8,128)S(1)}, bf16[8,8,128]{2,1,0:T(8,128)(2,1)S(1)}, bf16[8,8,128]{2,1,0:T(8,128)(2,1)S(1)}) custom-call(s32[34]{0:T(128)S(1)} %pad_add_fusion.info_ref, bf16[20,32,128]{2,1,0:T(8,128)(2,1)S(1)} %copy-done.2, bf16[20,32,128]{2,1,0:T(8,128)(2,1)S(1)} %collective-permute-done.8.refs_1_, ...), custom_call_target="tpu_custom_call" | custom-call | flops 8000000000 | bytes 4000000 | tf_op jit(solution)/shard_map/pallas_call | solution.py:261
  69.5 1.4 %collective-permute-done.22.refs_3_ = bf16[3,20,32,128]{3,2,1,0:T(8,128)(2,1)S(1)} collective-permute-done((bf16[3,20,32,128]{3,2,1,0:T(8,128)(2,1)S(1)}, bf16[3,20,32,128]{3,2,1,0:T(8,128)(2,1)S(1)}, u32[]{:S(2)}, u32[]{:S(2)}) %collective-permute-start.22) | collective-permute-done | bytes 491552 | tf_op jit(solution)/shard_map/ppermute | solution.py:90
  71.4 1.6 %collective-permute-done.23.refs_4_ = bf16[20,32,128]{2,1,0:T(8,128)(2,1)S(1)} collective-permute-done((bf16[20,32,128]{2,1,0:T(8,128)(2,1)S(1)}, bf16[20,32,128]{2,1,0:T(8,128)(2,1)S(1)}, u32[]{:S(2)}, u32[]{:S(2)}) %collective-permute-start.23) | collective-permute-done | bytes 163872 | tf_op jit(solution)/shard_map/ppermute | solution.py:90
  73.2 17.6 %shard_map.108 = (f32[4,256]{1,0:T(4,128)S(1)}, f32[4,256]{1,0:T(4,128)S(1)}, bf16[16,8,128]{2,1,0:T(8,128)(2,1)S(1)}, bf16[16,8,128]{2,1,0:T(8,128)(2,1)S(1)}) custom-call(s32[34]{0:T(128)S(1)} %pad_add_fusion.info_ref, bf16[20,32,128]{2,1,0:T(8,128)(2,1)S(1)} %copy-done.6, bf16[20,32,128]{2,1,0:T(8,128)(2,1)S(1)} %collective-permute-done.7.refs_1_, ...), custom_call_target="tpu_custom_call" | custom-call | flops 16000000000 | bytes 8000000 | tf_op jit(solution)/shard_map/pallas_call | solution.py:261
  92.2 1.2 %collective-permute-start.27 = (f32[4,256]{1,0:T(4,128)S(1)}, f32[4,256]{1,0:T(4,128)S(1)}, u32[]{:S(2)}, u32[]{:S(2)}) collective-permute-start(f32[4,256]{1,0:T(4,128)S(1)} %get-tuple-element.43), channel_id=1, source_target_pairs={{0,16},{16,0},{1,17},{17,1},{2,18},{18,2},{3,19},{19,3},{4,20},{20... | collective-permute-start | bytes 12296 | tf_op jit(solution)/shard_map/ppermute | solution.py:389
  93.5 2.4 %collective-permute-done.27 = f32[4,256]{1,0:T(4,128)S(1)} collective-permute-done((f32[4,256]{1,0:T(4,128)S(1)}, f32[4,256]{1,0:T(4,128)S(1)}, u32[]{:S(2)}, u32[]{:S(2)}) %collective-permute-start.27) | collective-permute-done | bytes 4128 | tf_op jit(solution)/shard_map/ppermute | solution.py:389
  95.9 1.2 %collective-permute-done.29 = f32[4,256]{1,0:T(4,128)S(1)} collective-permute-done((f32[4,256]{1,0:T(4,128)S(1)}, f32[4,256]{1,0:T(4,128)S(1)}, u32[]{:S(2)}, u32[]{:S(2)}) %collective-permute-start.29) | collective-permute-done | bytes 4128 | tf_op jit(solution)/shard_map/ppermute | solution.py:90
  97.1 1.5 %collective-permute-start.30 = (f32[4,256]{1,0:T(4,128)S(1)}, f32[4,256]{1,0:T(4,128)S(1)}, u32[]{:S(2)}, u32[]{:S(2)}) collective-permute-start(f32[4,256]{1,0:T(4,128)S(1)} %add.27), channel_id=1, source_target_pairs={{0,2},{1,3},{2,0},{3,1},{4,6},{5,7},{6,4},{7,5},{8,10},{9,11},{10,... | collective-permute-start | bytes 12296 | tf_op jit(solution)/shard_map/ppermute | solution.py:90
  98.8 1.9 %collective-permute-done.30 = f32[4,256]{1,0:T(4,128)S(1)} collective-permute-done((f32[4,256]{1,0:T(4,128)S(1)}, f32[4,256]{1,0:T(4,128)S(1)}, u32[]{:S(2)}, u32[]{:S(2)}) %collective-permute-start.30) | collective-permute-done | bytes 4128 | tf_op jit(solution)/shard_map/ppermute | solution.py:90
  102.2 2.0 %shard_map.109 = bf16[2,8,4096]{2,1,0:T(8,128)(2,1)} custom-call(s32[64]{0:T(128)} %pad_add_fusion.2.tiles, bf16[8,8,128]{2,1,0:T(8,128)(2,1)} %copy-done.4, bf16[8,8,128]{2,1,0:T(8,128)(2,1)} %copy-done.5, bf16[16,8,128]{2,1,0:T(8,128)(2,1)} %copy-done.3, bf16[32,8,128]{2,1,0:T(8,128)(2,1)} %copy-done.9), custom_call_target="tpu_custom_call" | custom-call | tf_op jit(solution)/shard_map/pallas_call | solution.py:392
  104.3 2.4 %collective-permute-start.32 = (f32[4,256]{1,0:T(4,128)S(1)}, f32[4,256]{1,0:T(4,128)S(1)}, u32[]{:S(2)}, u32[]{:S(2)}) collective-permute-start(f32[4,256]{1,0:T(4,128)S(1)} %add.29), channel_id=1, source_target_pairs={{0,8},{1,9},{2,10},{3,11},{4,12},{5,13},{6,14},{7,15},{8,0},{9,1},... | collective-permute-start | bytes 12296 | tf_op jit(solution)/shard_map/ppermute | solution.py:90
  106.7 2.1 %collective-permute-done.32 = f32[4,256]{1,0:T(4,128)S(1)} collective-permute-done((f32[4,256]{1,0:T(4,128)S(1)}, f32[4,256]{1,0:T(4,128)S(1)}, u32[]{:S(2)}, u32[]{:S(2)}) %collective-permute-start.32) | collective-permute-done | bytes 4128 | tf_op jit(solution)/shard_map/ppermute | solution.py:90
  (86 shorter events, 13.5 us)
Async XLA Ops:
  0.6 6.7 %collective-permute-start = (bf16[2,8,4096]{2,1,0:T(8,128)(2,1)}, bf16[2,8,4096]{2,1,0:T(8,128)(2,1)S(1)}, u32[]{:S(2)}, u32[]{:S(2)}) collective-permute-start(bf16[2,8,4096]{2,1,0:T(8,128)(2,1)} %own.2), channel_id=1, source_target_pairs={{0,16},{16,0},{1,17},{17,1},{2,18},{18,2},{3,19},{19,3},{4,20},{20... | collective-permute-start | bytes 393224 | tf_op jit(solution)/shard_map/ppermute | solution.py:319
  10.1 7.3 %collective-permute-start.1 = (bf16[20,32,128]{2,1,0:T(8,128)(2,1)}, bf16[20,32,128]{2,1,0:T(8,128)(2,1)S(1)}, u32[]{:S(2)}, u32[]{:S(2)}) collective-permute-start(bf16[20,32,128]{2,1,0:T(8,128)(2,1)} %get-tuple-element.29.refs_0_), channel_id=1, source_target_pairs={{0,4},{1,5},{2,6},{3,7},{4,0},{5,1},{6,2},{7,3},{8,12},{9,13},{10,... | collective-permute-start | bytes 491528 | tf_op jit(solution)/shard_map/ppermute | solution.py:90
  11.9 9.3 %collective-permute-start.2 = (bf16[20,32,128]{2,1,0:T(8,128)(2,1)}, bf16[20,32,128]{2,1,0:T(8,128)(2,1)S(1)}, u32[]{:S(2)}, u32[]{:S(2)}) collective-permute-start(bf16[20,32,128]{2,1,0:T(8,128)(2,1)} %get-tuple-element.29.refs_0_), channel_id=1, source_target_pairs={{0,12},{1,13},{2,14},{3,15},{4,8},{5,9},{6,10},{7,11},{8,4},{9,5},... | collective-permute-start | bytes 491528 | tf_op jit(solution)/shard_map/ppermute | solution.py:90
  14.4 15.7 %collective-permute-start.15 = (bf16[2,128,768]{2,1,0:T(8,128)(2,1)}, bf16[2,128,768]{2,1,0:T(8,128)(2,1)S(1)}, u32[]{:S(2)}, u32[]{:S(2)}) collective-permute-start(bf16[2,128,768]{2,1,0:T(8,128)(2,1)} %own.3), channel_id=1, source_target_pairs={{0,16},{16,0},{1,17},{17,1},{2,18},{18,2},{3,19},{19,3},{4,20},{20... | collective-permute-start | bytes 1179656 | tf_op jit(solution)/shard_map/ppermute | solution.py:335
  15.9 10.9 %collective-permute-start.9 = (bf16[20,32,128]{2,1,0:T(8,128)(2,1)}, bf16[20,32,128]{2,1,0:T(8,128)(2,1)S(1)}, u32[]{:S(2)}, u32[]{:S(2)}) collective-permute-start(bf16[20,32,128]{2,1,0:T(8,128)(2,1)} %get-tuple-element.29.refs_0_), channel_id=1, source_target_pairs={{0,2},{1,3},{2,0},{3,1},{4,6},{5,7},{6,4},{7,5},{8,10},{9,11},{10,... | collective-permute-start | bytes 491528 | tf_op jit(solution)/shard_map/ppermute | solution.py:90
  21.2 8.3 %collective-permute-start.3 = (bf16[20,32,128]{2,1,0:T(8,128)(2,1)}, bf16[20,32,128]{2,1,0:T(8,128)(2,1)S(1)}, u32[]{:S(2)}, u32[]{:S(2)}) collective-permute-start(bf16[20,32,128]{2,1,0:T(8,128)(2,1)} %get-tuple-element.29.refs_0_), channel_id=1, source_target_pairs={{0,8},{1,9},{2,10},{3,11},{4,12},{5,13},{6,14},{7,15},{8,0},{9,1},... | collective-permute-start | bytes 491528 | tf_op jit(solution)/shard_map/ppermute | solution.py:90
  24.8 5.3 %collective-permute-start.12 = (bf16[20,32,128]{2,1,0:T(8,128)(2,1)S(1)}, bf16[20,32,128]{2,1,0:T(8,128)(2,1)S(1)}, u32[]{:S(2)}, u32[]{:S(2)}) collective-permute-start(bf16[20,32,128]{2,1,0:T(8,128)(2,1)S(1)} %collective-permute-done.1.refs_4_), channel_id=1, source_target_pairs={{0,2},{1,3},{2,0},{3,1},{4,6},{5,7},{6,4},{7,5},{8,10},{9,11},{10,... | collective-permute-start | bytes 491528 | tf_op jit(solution)/shard_map/ppermute | solution.py:90
  26.3 8.6 %collective-permute-start.16 = (bf16[20,32,128]{2,1,0:T(8,128)(2,1)S(1)}, bf16[20,32,128]{2,1,0:T(8,128)(2,1)S(1)}, u32[]{:S(2)}, u32[]{:S(2)}) collective-permute-start(bf16[20,32,128]{2,1,0:T(8,128)(2,1)S(1)} %collective-permute-done.2.refs_12_), channel_id=1, source_target_pairs={{0,2},{1,3},{2,0},{3,1},{4,6},{5,7},{6,4},{7,5},{8,10},{9,11},{10,... | collective-permute-start | bytes 491528 | tf_op jit(solution)/shard_map/ppermute | solution.py:90
  26.8 8.6 %collective-permute-start.8 = (bf16[20,32,128]{2,1,0:T(8,128)(2,1)}, bf16[20,32,128]{2,1,0:T(8,128)(2,1)S(1)}, u32[]{:S(2)}, u32[]{:S(2)}) collective-permute-start(bf16[20,32,128]{2,1,0:T(8,128)(2,1)} %get-tuple-element.29.refs_0_), channel_id=1, source_target_pairs={{0,1},{1,0},{2,3},{3,2},{4,5},{5,4},{6,7},{7,6},{8,9},{9,8},{10,11... | collective-permute-start | bytes 491528 | tf_op jit(solution)/shard_map/ppermute | solution.py:90
  29.5 6.1 %collective-permute-start.11 = (bf16[20,32,128]{2,1,0:T(8,128)(2,1)S(1)}, bf16[20,32,128]{2,1,0:T(8,128)(2,1)S(1)}, u32[]{:S(2)}, u32[]{:S(2)}) collective-permute-start(bf16[20,32,128]{2,1,0:T(8,128)(2,1)S(1)} %collective-permute-done.1.refs_4_), channel_id=1, source_target_pairs={{0,1},{1,0},{2,3},{3,2},{4,5},{5,4},{6,7},{7,6},{8,9},{9,8},{10,11... | collective-permute-start | bytes 491528 | tf_op jit(solution)/shard_map/ppermute | solution.py:90
  30.1 5.9 %collective-permute-start.19 = (bf16[20,32,128]{2,1,0:T(8,128)(2,1)S(1)}, bf16[20,32,128]{2,1,0:T(8,128)(2,1)S(1)}, u32[]{:S(2)}, u32[]{:S(2)}) collective-permute-start(bf16[20,32,128]{2,1,0:T(8,128)(2,1)S(1)} %collective-permute-done.2.refs_12_), channel_id=1, source_target_pairs={{0,1},{1,0},{2,3},{3,2},{4,5},{5,4},{6,7},{7,6},{8,9},{9,8},{10,11... | collective-permute-start | bytes 491528 | tf_op jit(solution)/shard_map/ppermute | solution.py:90
  30.1 5.0 %collective-permute-start.21 = (s32[128]{0:T(128)}, s32[128]{0:T(128)S(1)}, u32[]{:S(2)}, u32[]{:S(2)}) collective-permute-start(s32[128]{0:T(128)} %param.11), channel_id=1, source_target_pairs={{0,16},{16,0},{1,17},{17,1},{2,18},{18,2},{3,19},{19,3},{4,20},{20... | collective-permute-start | bytes 1544 | tf_op jit(solution)/shard_map/ppermute | solution.py:334
  34.9 3.5 %collective-permute-start.10 = (bf16[20,32,128]{2,1,0:T(8,128)(2,1)S(1)}, bf16[20,32,128]{2,1,0:T(8,128)(2,1)S(1)}, u32[]{:S(2)}, u32[]{:S(2)}) collective-permute-start(bf16[20,32,128]{2,1,0:T(8,128)(2,1)S(1)} %collective-permute-done.9.refs_2_), channel_id=1, source_target_pairs={{0,1},{1,0},{2,3},{3,2},{4,5},{5,4},{6,7},{7,6},{8,9},{9,8},{10,11... | collective-permute-start | bytes 491528 | tf_op jit(solution)/shard_map/ppermute | solution.py:90
  35.1 3.4 %collective-permute-start.14 = (bf16[20,32,128]{2,1,0:T(8,128)(2,1)S(1)}, bf16[20,32,128]{2,1,0:T(8,128)(2,1)S(1)}, u32[]{:S(2)}, u32[]{:S(2)}) collective-permute-start(bf16[20,32,128]{2,1,0:T(8,128)(2,1)S(1)} %collective-permute-done.3.refs_8_), channel_id=1, source_target_pairs={{0,1},{1,0},{2,3},{3,2},{4,5},{5,4},{6,7},{7,6},{8,9},{9,8},{10,11... | collective-permute-start | bytes 491528 | tf_op jit(solution)/shard_map/ppermute | solution.py:90
  35.5 6.0 %collective-permute-start.13 = (bf16[20,32,128]{2,1,0:T(8,128)(2,1)S(1)}, bf16[20,32,128]{2,1,0:T(8,128)(2,1)S(1)}, u32[]{:S(2)}, u32[]{:S(2)}) collective-permute-start(bf16[20,32,128]{2,1,0:T(8,128)(2,1)S(1)} %collective-permute-done.12.refs_6_), channel_id=1, source_target_pairs={{0,1},{1,0},{2,3},{3,2},{4,5},{5,4},{6,7},{7,6},{8,9},{9,8},{10,11... | collective-permute-start | bytes 491528 | tf_op jit(solution)/shard_map/ppermute | solution.py:90
  35.6 6.4 %collective-permute-start.20 = (bf16[20,32,128]{2,1,0:T(8,128)(2,1)S(1)}, bf16[20,32,128]{2,1,0:T(8,128)(2,1)S(1)}, u32[]{:S(2)}, u32[]{:S(2)}) collective-permute-start(bf16[20,32,128]{2,1,0:T(8,128)(2,1)S(1)} %collective-permute-done.16.refs_14_), channel_id=1, source_target_pairs={{0,1},{1,0},{2,3},{3,2},{4,5},{5,4},{6,7},{7,6},{8,9},{9,8},{10,11... | collective-permute-start | bytes 491528 | tf_op jit(solution)/shard_map/ppermute | solution.py:90
  36.0 6.5 %collective-permute-start.17 = (bf16[20,32,128]{2,1,0:T(8,128)(2,1)S(1)}, bf16[20,32,128]{2,1,0:T(8,128)(2,1)S(1)}, u32[]{:S(2)}, u32[]{:S(2)}) collective-permute-start(bf16[20,32,128]{2,1,0:T(8,128)(2,1)S(1)} %collective-permute-done.3.refs_8_), channel_id=1, source_target_pairs={{0,2},{1,3},{2,0},{3,1},{4,6},{5,7},{6,4},{7,5},{8,10},{9,11},{10,... | collective-permute-start | bytes 491528 | tf_op jit(solution)/shard_map/ppermute | solution.py:90
  38.4 18.6 %collective-permute-start.4 = (bf16[20,32,128]{2,1,0:T(8,128)(2,1)}, bf16[20,32,128]{2,1,0:T(8,128)(2,1)S(1)}, u32[]{:S(2)}, u32[]{:S(2)}) collective-permute-start(bf16[20,32,128]{2,1,0:T(8,128)(2,1)} %get-tuple-element.30.refs_0_), channel_id=1, source_target_pairs={{0,4},{1,5},{2,6},{3,7},{4,0},{5,1},{6,2},{7,3},{8,12},{9,13},{10,... | collective-permute-start | bytes 491528 | tf_op jit(solution)/shard_map/ppermute | solution.py:90
  38.5 18.5 %collective-permute-start.5 = (bf16[20,32,128]{2,1,0:T(8,128)(2,1)}, bf16[20,32,128]{2,1,0:T(8,128)(2,1)S(1)}, u32[]{:S(2)}, u32[]{:S(2)}) collective-permute-start(bf16[20,32,128]{2,1,0:T(8,128)(2,1)} %get-tuple-element.30.refs_0_), channel_id=1, source_target_pairs={{0,12},{1,13},{2,14},{3,15},{4,8},{5,9},{6,10},{7,11},{8,4},{9,5},... | collective-permute-start | bytes 491528 | tf_op jit(solution)/shard_map/ppermute | solution.py:90
  41.5 15.5 %collective-permute-start.6 = (bf16[20,32,128]{2,1,0:T(8,128)(2,1)}, bf16[20,32,128]{2,1,0:T(8,128)(2,1)S(1)}, u32[]{:S(2)}, u32[]{:S(2)}) collective-permute-start(bf16[20,32,128]{2,1,0:T(8,128)(2,1)} %get-tuple-element.30.refs_0_), channel_id=1, source_target_pairs={{0,8},{1,9},{2,10},{3,11},{4,12},{5,13},{6,14},{7,15},{8,0},{9,1},... | collective-permute-start | bytes 491528 | tf_op jit(solution)/shard_map/ppermute | solution.py:90
  42.0 15.1 %collective-permute-start.7 = (bf16[20,32,128]{2,1,0:T(8,128)(2,1)}, bf16[20,32,128]{2,1,0:T(8,128)(2,1)S(1)}, u32[]{:S(2)}, u32[]{:S(2)}) collective-permute-start(bf16[20,32,128]{2,1,0:T(8,128)(2,1)} %get-tuple-element.30.refs_0_), channel_id=1, source_target_pairs={{0,2},{1,3},{2,0},{3,1},{4,6},{5,7},{6,4},{7,5},{8,10},{9,11},{10,... | collective-permute-start | bytes 491528 | tf_op jit(solution)/shard_map/ppermute | solution.py:90
  42.5 1.4 %collective-permute-start.18 = (bf16[20,32,128]{2,1,0:T(8,128)(2,1)S(1)}, bf16[20,32,128]{2,1,0:T(8,128)(2,1)S(1)}, u32[]{:S(2)}, u32[]{:S(2)}) collective-permute-start(bf16[20,32,128]{2,1,0:T(8,128)(2,1)S(1)} %collective-permute-done.17.refs_10_), channel_id=1, source_target_pairs={{0,1},{1,0},{2,3},{3,2},{4,5},{5,4},{6,7},{7,6},{8,9},{9,8},{10,11... | collective-permute-start | bytes 491528 | tf_op jit(solution)/shard_map/ppermute | solution.py:90
  57.6 13.3 %collective-permute-start.22 = (bf16[3,20,32,128]{3,2,1,0:T(8,128)(2,1)S(1)}, bf16[3,20,32,128]{3,2,1,0:T(8,128)(2,1)S(1)}, u32[]{:S(2)}, u32[]{:S(2)}) collective-permute-start(bf16[3,20,32,128]{3,2,1,0:T(8,128)(2,1)S(1)} %pad_maximum_fusion.refs_2_), channel_id=1, source_target_pairs={{0,2},{1,3},{2,0},{3,1},{4,6},{5,7},{6,4},{7,5},{8,10},{9,11},{10,... | collective-permute-start | bytes 1474568 | tf_op jit(solution)/shard_map/ppermute | solution.py:90
  59.1 14.1 %collective-permute-start.25 = (bf16[3,20,32,128]{3,2,1,0:T(8,128)(2,1)S(1)}, bf16[3,20,32,128]{3,2,1,0:T(8,128)(2,1)S(1)}, u32[]{:S(2)}, u32[]{:S(2)}) collective-permute-start(bf16[3,20,32,128]{3,2,1,0:T(8,128)(2,1)S(1)} %pad_maximum_fusion.refs_2_), channel_id=1, source_target_pairs={{0,1},{1,0},{2,3},{3,2},{4,5},{5,4},{6,7},{7,6},{8,9},{9,8},{10,11... | collective-permute-start | bytes 1474568 | tf_op jit(solution)/shard_map/ppermute | solution.py:90
  70.9 2.3 %collective-permute-start.26 = (bf16[3,20,32,128]{3,2,1,0:T(8,128)(2,1)S(1)}, bf16[3,20,32,128]{3,2,1,0:T(8,128)(2,1)S(1)}, u32[]{:S(2)}, u32[]{:S(2)}) collective-permute-start(bf16[3,20,32,128]{3,2,1,0:T(8,128)(2,1)S(1)} %collective-permute-done.22.refs_3_), channel_id=1, source_target_pairs={{0,1},{1,0},{2,3},{3,2},{4,5},{5,4},{6,7},{7,6},{8,9},{9,8},{10,11... | collective-permute-start | bytes 1474568 | tf_op jit(solution)/shard_map/ppermute | solution.py:90
  70.9 2.1 %collective-permute-start.23 = (bf16[20,32,128]{2,1,0:T(8,128)(2,1)S(1)}, bf16[20,32,128]{2,1,0:T(8,128)(2,1)S(1)}, u32[]{:S(2)}, u32[]{:S(2)}) collective-permute-start(bf16[20,32,128]{2,1,0:T(8,128)(2,1)S(1)} %copy-done.6), channel_id=1, source_target_pairs={{0,1},{1,0},{2,3},{3,2},{4,5},{5,4},{6,7},{7,6},{8,9},{9,8},{10,11... | collective-permute-start | bytes 491528 | tf_op jit(solution)/shard_map/ppermute | solution.py:90
  71.4 1.8 %collective-permute-start.24 = (bf16[20,32,128]{2,1,0:T(8,128)(2,1)S(1)}, bf16[20,32,128]{2,1,0:T(8,128)(2,1)S(1)}, u32[]{:S(2)}, u32[]{:S(2)}) collective-permute-start(bf16[20,32,128]{2,1,0:T(8,128)(2,1)S(1)} %collective-permute-done.7.refs_1_), channel_id=1, source_target_pairs={{0,1},{1,0},{2,3},{3,2},{4,5},{5,4},{6,7},{7,6},{8,9},{9,8},{10,11... | collective-permute-start | bytes 491528 | tf_op jit(solution)/shard_map/ppermute | solution.py:90
  91.4 4.4 %collective-permute-start.28 = (bf16[32,8,128]{2,1,0:T(8,128)(2,1)S(1)}, bf16[32,8,128]{2,1,0:T(8,128)(2,1)S(1)}, u32[]{:S(2)}, u32[]{:S(2)}) collective-permute-start(bf16[32,8,128]{2,1,0:T(8,128)(2,1)S(1)} %pad_maximum_fusion.1), channel_id=1, source_target_pairs={{0,16},{16,0},{1,17},{17,1},{2,18},{18,2},{3,19},{19,3},{4,20},{20... | collective-permute-start | bytes 196616 | tf_op jit(solution)/shard_map/ppermute | solution.py:390
  92.2 3.6 %collective-permute-start.27 = (f32[4,256]{1,0:T(4,128)S(1)}, f32[4,256]{1,0:T(4,128)S(1)}, u32[]{:S(2)}, u32[]{:S(2)}) collective-permute-start(f32[4,256]{1,0:T(4,128)S(1)} %get-tuple-element.43), channel_id=1, source_target_pairs={{0,16},{16,0},{1,17},{17,1},{2,18},{18,2},{3,19},{19,3},{4,20},{20... | collective-permute-start | bytes 12296 | tf_op jit(solution)/shard_map/ppermute | solution.py:389
  97.1 3.6 %collective-permute-start.30 = (f32[4,256]{1,0:T(4,128)S(1)}, f32[4,256]{1,0:T(4,128)S(1)}, u32[]{:S(2)}, u32[]{:S(2)}) collective-permute-start(f32[4,256]{1,0:T(4,128)S(1)} %add.27), channel_id=1, source_target_pairs={{0,2},{1,3},{2,0},{3,1},{4,6},{5,7},{6,4},{7,5},{8,10},{9,11},{10,... | collective-permute-start | bytes 12296 | tf_op jit(solution)/shard_map/ppermute | solution.py:90
  100.7 3.6 %collective-permute-start.31 = (f32[4,256]{1,0:T(4,128)S(1)}, f32[4,256]{1,0:T(4,128)S(1)}, u32[]{:S(2)}, u32[]{:S(2)}) collective-permute-start(f32[4,256]{1,0:T(4,128)S(1)} %add.28), channel_id=1, source_target_pairs={{0,4},{1,5},{2,6},{3,7},{4,0},{5,1},{6,2},{7,3},{8,12},{9,13},{10,... | collective-permute-start | bytes 12296 | tf_op jit(solution)/shard_map/ppermute | solution.py:90
  104.3 4.5 %collective-permute-start.32 = (f32[4,256]{1,0:T(4,128)S(1)}, f32[4,256]{1,0:T(4,128)S(1)}, u32[]{:S(2)}, u32[]{:S(2)}) collective-permute-start(f32[4,256]{1,0:T(4,128)S(1)} %add.29), channel_id=1, source_target_pairs={{0,8},{1,9},{2,10},{3,11},{4,12},{5,13},{6,14},{7,15},{8,0},{9,1},... | collective-permute-start | bytes 12296 | tf_op jit(solution)/shard_map/ppermute | solution.py:90
  (11 other events, 38.6 us)

commit v6 on v5

--- a/solution.py
+++ b/solution.py
@@ -91,7 +91,7 @@
 
 
 def pack_kernel(info, own, other, query, basis, *units):
-    x = info[0]
+    x = info[1 + WAVES * NQ]
 
     for wave in range(WAVES):
         unit = units[wave]
@@ -111,7 +111,7 @@
 
 
 def prepare_kernel(info, own, other, query, tiles, grads, query_grads):
-    x = info[0]
+    x = info[1 + WAVES * NQ]
     blank = jnp.zeros((TILE_S, TILE_S), jnp.float32)
     for layer in range(LAYERS):
         for c in range(tiles.shape[1] // 2):
@@ -283,7 +283,7 @@
     )(info, *arrays, grads, query_grads, codes, eigenvalues, before)
 
 
-def unpack_kernel(tiles, kept_a, kept_b, kept_c, came, out):
+def unpack_kernel(info, kept_a, kept_b, kept_c, came, out):
     first = kept_a.shape[0]
     both = WAVES * NQ
     for place in range(2 * both):
@@ -294,7 +294,7 @@
             rows = kept_a[n]
         else:
             rows = kept_b[n - first] if n < NQ else kept_c[n - NQ]
-        tile = tiles[place]
+        tile = info[1 + n + (both + 1 if half else 0)]
         cols = pl.ds(pl.multiple_of((tile % 32) * TILE_A, TILE_A), TILE_A)
         out[tile // 32, :, cols] = rows
 
@@ -322,16 +322,17 @@
     by_half = tile_of.reshape(NQ, 2, WAVES).transpose(1, 2, 0).reshape(2, WAVES * NQ)
     mine = jnp.where(x == 0, by_half[0], by_half[1])
     theirs = jnp.where(x == 0, by_half[1], by_half[0])
+    ids_other = lax.ppermute(after(sequence_ids, mine), "parts", SWAP)
     side = x.reshape(1).astype(jnp.int32)
+    info = jnp.concatenate([me.reshape(1).astype(jnp.int32), mine, side, theirs])
 
     packed = pl.pallas_call(
         pack_kernel,
         in_specs=[SMEM, VMEM, VMEM, VMEM, VMEM],
         out_specs=[VMEM] * WAVES,
         out_shape=[jax.ShapeDtypeStruct((UNIT, 32, TILE_A), BF)] * WAVES,
-    )(jnp.concatenate([side, mine]), train_inputs, train_other, query_inputs, input_basis)
-
-    ids_other = lax.ppermute(sequence_ids, "parts", SWAP)
+    )(after(info, ids_other), train_inputs, train_other, query_inputs, input_basis)
+
     out_other = lax.ppermute(after(train_outgrads, train_other), "parts", SWAP)
     id_pair = jnp.where(
         x == 0, jnp.stack([sequence_ids, ids_other]), jnp.stack([ids_other, sequence_ids])
@@ -347,21 +348,21 @@
             jax.ShapeDtypeStruct((LAYERS, TOKENS, slab), BF),
             jax.ShapeDtypeStruct((LAYERS, slab, TOKENS), BF),
         ],
-    )(side, train_outgrads, out_other, query_outgrads, output_basis)
+    )(info, train_outgrads, out_other, query_outgrads, output_basis)
 
     units = [None] * NQ
     units[0] = packed[0]
     units[4] = hop(packed[0], 4)
     units[12] = hop(packed[0], 12)
     units[8] = hop(after(packed[0], units[4], units[12]), 8)
-    for d in (0, 4, 12):
-        units[d ^ 2] = hop(units[d], 2)
-    units[10] = hop(after(units[8], grads, units[2], units[6], units[14]), 2)
+    units[2] = hop(units[0], 2)
+    units[6] = hop(units[4], 2)
+    units[14] = hop(after(units[12], grads), 2)
+    units[10] = hop(after(units[8], units[2], units[6]), 2)
     for d in (0, 2, 4, 6, 12, 14, 8, 10):
         units[d ^ 1] = hop(units[d], 1)
     places0 = [(d, None) for d in range(NQ)]
 
-    info = jnp.concatenate([me.reshape(1).astype(jnp.int32), mine, side])
     zero = jnp.zeros((GROUPS, TOKENS), jnp.float32)
     common = (grads, query_grads, codes, eigenvalues)
     part0, kept_a, given_a = score_tiles(0, 8, False, info, units, places0, *common, zero)
@@ -394,7 +395,7 @@
         in_specs=[SMEM] + [VMEM] * 4,
         out_specs=VMEM,
         out_shape=jax.ShapeDtypeStruct(train_inputs.shape, BF),
-    )(jnp.concatenate([mine, theirs]), kept_a, kept_b, kept1, came)
+    )(info, kept_a, kept_b, kept1, came)
     for bits in (1, 2, 4):
         total = total + hop(total, bits)
     total = after(total, rotated_out)

time: 110 us -> 112 us (1.018)
  waiting for transfers between devices: 21.2 us -> 25.3 us
  starting transfers between devices: 33.1 us -> 30 us
  local copies, waits for them, and re-layouts: 6.95 us -> 8.13 us
    ppermute x28, waiting for transfers between devices: 16.8 us -> 20.1 us  [hop(): return lax.ppermute(value, 'query', [(i, i ^ bits) for i in range(NQ)])]
    ppermute x1, waiting for transfers between devices: 0.01 us -> 2.89 us  [paired_body(): ids_other = lax.ppermute(after(sequence_ids, mine), 'parts', SWAP)]
    ppermute x1, waiting for transfers between devices: 2 us -> 0.01 us  [paired_body(): train_other = lax.ppermute(train_inputs, 'parts', SWAP)]
    ppermute x1, starting transfers between devices: 1.56 us -> 0.02 us  [paired_body(): ids_other = lax.ppermute(after(sequence_ids, mine), 'parts', SWAP)]
    unnamed x20 -> x22, local copies, waits for them, and re-layouts: 5.49 us -> 6.67 us
  transfers between devices with their start and end apart: 33 -> 33, of which waited for: 13 -> 15; matrix products, arithmetic and copies ran while one was open for 3% -> 3% of each run, Pallas kernels for 23% -> 23%
where the time goes in v6:
time: 112 us
  Pallas kernels  45.2 us (40%)
  starting transfers between devices  30 us (27%)
  waiting for transfers between devices  25.3 us (23%)
  local copies, waits for them, and re-layouts  8.13 us (7%)
  other arithmetic  2.21 us (2%)
    pallas_call x3, Pallas kernels, score_tiles(): pl.pallas_call(kernel, in_specs=[SMEM] + [VMEM] * len(arrays) + [VMEM, VM...  37.8 us
    ppermute x28, starting transfers between devices, hop(): return lax.ppermute(value, 'query', [(i, i ^ bits) for i in range(NQ)])  24.2 us
    ppermute x28, waiting for transfers between devices, hop(): return lax.ppermute(value, 'query', [(i, i ^ bits) for i in range(NQ)])  20.1 us
    unnamed x22, local copies, waits for them, and re-layouts  6.67 us
    pallas_call x1, Pallas kernels, paired_body(): pl.pallas_call(prepare_kernel, in_specs=[SMEM] + [VMEM] * 4, out_specs=[V...  3.26 us
    ppermute x1, starting transfers between devices, paired_body(): train_other = lax.ppermute(train_inputs, 'parts', SWAP)  3 us
    ppermute x1, waiting for transfers between devices, paired_body(): ids_other = lax.ppermute(after(sequence_ids, mine), 'parts', SWAP)  2.89 us
    ppermute x1, waiting for transfers between devices, paired_body(): total = keep + lax.ppermute(give, 'parts', SWAP)  2.3 us
  transfers between devices with their start and end apart: 33, of which 15 were waited for; matrix products, arithmetic and copies ran while one was open for 3% of the time, Pallas kernels for 23%

profile of v6, /device:TPU:0, one launch (start us, length us, event | category | flops | bytes accessed | tf_op | source)
XLA Modules:
  0.0 111.7 jit_solution(11603928415756193303)
XLA Ops:
  0.6 3.0 %collective-permute-start.1 = (bf16[2,8,4096]{2,1,0:T(8,128)(2,1)}, bf16[2,8,4096]{2,1,0:T(8,128)(2,1)S(1)}, u32[]{:S(2)}, u32[]{:S(2)}) collective-permute-start(bf16[2,8,4096]{2,1,0:T(8,128)(2,1)} %own.2), channel_id=1, source_target_pairs={{0,16},{16,0},{1,17},{17,1},{2,18},{18,2},{3,19},{19,3},{4,20},{20... | collective-permute-start | bytes 393224 | tf_op jit(solution)/shard_map/ppermute | solution.py:319
  5.5 2.9 %collective-permute-done = s32[128]{0:T(128)S(1)} collective-permute-done((s32[128]{0:T(128)}, s32[128]{0:T(128)S(1)}, u32[]{:S(2)}, u32[]{:S(2)}) %collective-permute-start) | collective-permute-done | bytes 544 | tf_op jit(solution)/shard_map/ppermute | solution.py:325
  9.1 2.1 %shard_map.104 = (bf16[20,32,128]{2,1,0:T(8,128)(2,1)}, bf16[20,32,128]{2,1,0:T(8,128)(2,1)}) custom-call(s32[66]{0:T(128)} %pad_add_fusion.info.info_ref, bf16[2,8,4096]{2,1,0:T(8,128)(2,1)} %own.2, bf16[2,8,4096]{2,1,0:T(8,128)(2,1)} %copy-done.9, bf16[2,16,4096]{2,1,0:T(8,128)(2,1)} %query.2, bf16[4,128,128]{2,1,0:T(8,128)(2,1)} %basis.1), custom_call_target="tpu_custom_call" | custom-call | tf_op jit(solution)/shard_map/pallas_call | solution.py:329
  11.2 1.6 %collective-permute-start.2 = (bf16[20,32,128]{2,1,0:T(8,128)(2,1)}, bf16[20,32,128]{2,1,0:T(8,128)(2,1)S(1)}, u32[]{:S(2)}, u32[]{:S(2)}) collective-permute-start(bf16[20,32,128]{2,1,0:T(8,128)(2,1)} %get-tuple-element.34.refs_0_), channel_id=1, source_target_pairs={{0,4},{1,5},{2,6},{3,7},{4,0},{5,1},{6,2},{7,3},{8,12},{9,13},{10,... | collective-permute-start | bytes 491528 | tf_op jit(solution)/shard_map/ppermute | solution.py:90
  12.7 2.5 %collective-permute-start.3 = (bf16[20,32,128]{2,1,0:T(8,128)(2,1)}, bf16[20,32,128]{2,1,0:T(8,128)(2,1)S(1)}, u32[]{:S(2)}, u32[]{:S(2)}) collective-permute-start(bf16[20,32,128]{2,1,0:T(8,128)(2,1)} %get-tuple-element.34.refs_0_), channel_id=1, source_target_pairs={{0,12},{1,13},{2,14},{3,15},{4,8},{5,9},{6,10},{7,11},{8,4},{9,5},... | collective-permute-start | bytes 491528 | tf_op jit(solution)/shard_map/ppermute | solution.py:90
  16.0 1.5 %collective-permute-start.10 = (bf16[20,32,128]{2,1,0:T(8,128)(2,1)}, bf16[20,32,128]{2,1,0:T(8,128)(2,1)S(1)}, u32[]{:S(2)}, u32[]{:S(2)}) collective-permute-start(bf16[20,32,128]{2,1,0:T(8,128)(2,1)} %get-tuple-element.34.refs_0_), channel_id=1, source_target_pairs={{0,2},{1,3},{2,0},{3,1},{4,6},{5,7},{6,4},{7,5},{8,10},{9,11},{10,... | collective-permute-start | bytes 491528 | tf_op jit(solution)/shard_map/ppermute | solution.py:90
  17.6 4.2 %collective-permute-done.3.refs_12_ = bf16[20,32,128]{2,1,0:T(8,128)(2,1)S(1)} collective-permute-done((bf16[20,32,128]{2,1,0:T(8,128)(2,1)}, bf16[20,32,128]{2,1,0:T(8,128)(2,1)S(1)}, u32[]{:S(2)}, u32[]{:S(2)}) %collective-permute-start.3) | collective-permute-done | bytes 163872 | tf_op jit(solution)/shard_map/ppermute | solution.py:90
  21.8 3.7 %collective-permute-start.4 = (bf16[20,32,128]{2,1,0:T(8,128)(2,1)}, bf16[20,32,128]{2,1,0:T(8,128)(2,1)S(1)}, u32[]{:S(2)}, u32[]{:S(2)}) collective-permute-start(bf16[20,32,128]{2,1,0:T(8,128)(2,1)} %get-tuple-element.34.refs_0_), channel_id=1, source_target_pairs={{0,8},{1,9},{2,10},{3,11},{4,12},{5,13},{6,14},{7,15},{8,0},{9,1},... | collective-permute-start | bytes 491528 | tf_op jit(solution)/shard_map/ppermute | solution.py:90
  25.5 1.5 %collective-permute-start.13 = (bf16[20,32,128]{2,1,0:T(8,128)(2,1)S(1)}, bf16[20,32,128]{2,1,0:T(8,128)(2,1)S(1)}, u32[]{:S(2)}, u32[]{:S(2)}) collective-permute-start(bf16[20,32,128]{2,1,0:T(8,128)(2,1)S(1)} %collective-permute-done.2.refs_4_), channel_id=1, source_target_pairs={{0,2},{1,3},{2,0},{3,1},{4,6},{5,7},{6,4},{7,5},{8,10},{9,11},{10,... | collective-permute-start | bytes 491528 | tf_op jit(solution)/shard_map/ppermute | solution.py:90
  27.5 3.2 %collective-permute-done.4.refs_8_ = bf16[20,32,128]{2,1,0:T(8,128)(2,1)S(1)} collective-permute-done((bf16[20,32,128]{2,1,0:T(8,128)(2,1)}, bf16[20,32,128]{2,1,0:T(8,128)(2,1)S(1)}, u32[]{:S(2)}, u32[]{:S(2)}) %collective-permute-start.4) | collective-permute-done | bytes 163872 | tf_op jit(solution)/shard_map/ppermute | solution.py:90
  30.8 1.5 %collective-permute-start.16 = (bf16[20,32,128]{2,1,0:T(8,128)(2,1)S(1)}, bf16[20,32,128]{2,1,0:T(8,128)(2,1)S(1)}, u32[]{:S(2)}, u32[]{:S(2)}) collective-permute-start(bf16[20,32,128]{2,1,0:T(8,128)(2,1)S(1)} %collective-permute-done.4.refs_8_), channel_id=1, source_target_pairs={{0,2},{1,3},{2,0},{3,1},{4,6},{5,7},{6,4},{7,5},{8,10},{9,11},{10,... | collective-permute-start | bytes 491528 | tf_op jit(solution)/shard_map/ppermute | solution.py:90
  33.1 3.3 %shard_map.105 = (bf16[2,256,768]{2,1,0:T(8,128)(2,1)}, bf16[2,768,256]{2,1,0:T(8,128)(2,1)}) custom-call(s32[66]{0:T(128)} %pad_add_fusion.info.info_ref, bf16[2,128,768]{2,1,0:T(8,128)(2,1)} %own.3, bf16[2,128,768]{2,1,0:T(8,128)(2,1)} %copy-done.8, bf16[2,256,768]{2,1,0:T(8,128)(2,1)} %query.3, bf16[2,12,64,64]{3,2,1,0:T(8,128)(2,1)} %tiles.1), custom_call_target="tpu_custom_call" | custom-call | tf_op jit(solution)/shard_map/pallas_call | solution.py:343
  38.3 2.6 %collective-permute-start.6 = (bf16[20,32,128]{2,1,0:T(8,128)(2,1)}, bf16[20,32,128]{2,1,0:T(8,128)(2,1)S(1)}, u32[]{:S(2)}, u32[]{:S(2)}) collective-permute-start(bf16[20,32,128]{2,1,0:T(8,128)(2,1)} %get-tuple-element.35.refs_0_), channel_id=1, source_target_pairs={{0,12},{1,13},{2,14},{3,15},{4,8},{5,9},{6,10},{7,11},{8,4},{9,5},... | collective-permute-start | bytes 491528 | tf_op jit(solution)/shard_map/ppermute | solution.py:90
  41.8 1.4 %collective-permute-done.20.refs_14_ = bf16[20,32,128]{2,1,0:T(8,128)(2,1)S(1)} collective-permute-done((bf16[20,32,128]{2,1,0:T(8,128)(2,1)S(1)}, bf16[20,32,128]{2,1,0:T(8,128)(2,1)S(1)}, u32[]{:S(2)}, u32[]{:S(2)}) %collective-permute-start.20) | collective-permute-done | bytes 163872 | tf_op jit(solution)/shard_map/ppermute | solution.py:90
  43.8 1.2 %collective-permute-done.21.refs_15_ = bf16[20,32,128]{2,1,0:T(8,128)(2,1)S(1)} collective-permute-done((bf16[20,32,128]{2,1,0:T(8,128)(2,1)S(1)}, bf16[20,32,128]{2,1,0:T(8,128)(2,1)S(1)}, u32[]{:S(2)}, u32[]{:S(2)}) %collective-permute-start.21) | collective-permute-done | bytes 163872 | tf_op jit(solution)/shard_map/ppermute | solution.py:90
  45.1 1.1 %copy-done = bf16[2,256,768]{2,1,0:T(8,128)(2,1)S(1)} copy-done((bf16[2,256,768]{2,1,0:T(8,128)(2,1)S(1)}, bf16[2,256,768]{2,1,0:T(8,128)(2,1)}, u32[]{:S(2)}) %copy-start) | copy-done | bytes 786456
  46.2 1.1 %copy-done.1 = bf16[2,768,256]{2,1,0:T(8,128)(2,1)S(1)} copy-done((bf16[2,768,256]{2,1,0:T(8,128)(2,1)S(1)}, bf16[2,768,256]{2,1,0:T(8,128)(2,1)}, u32[]{:S(2)}) %copy-start.1) | copy-done | bytes 786456
  47.3 0.9 copy-done.2
  48.8 10.0 %shard_map.106 = (f32[8,256]{1,0:T(8,128)S(1)}, bf16[8,8,128]{2,1,0:T(8,128)(2,1)S(1)}, bf16[8,8,128]{2,1,0:T(8,128)(2,1)S(1)}) custom-call(s32[66]{0:T(128)S(1)} %copy-done.6, bf16[20,32,128]{2,1,0:T(8,128)(2,1)S(1)} %copy-done.2, bf16[20,32,128]{2,1,0:T(8,128)(2,1)S(1)} %collective-permute-done.9.refs_1_, ...), custom_call_target="tpu_custom_call" | custom-call | flops 80000000 | bytes 4000000 | tf_op jit(solution)/shard_map/pallas_call | solution.py:261
  59.5 1.5 %collective-permute-start.22 = (bf16[3,20,32,128]{3,2,1,0:T(8,128)(2,1)S(1)}, bf16[3,20,32,128]{3,2,1,0:T(8,128)(2,1)S(1)}, u32[]{:S(2)}, u32[]{:S(2)}) collective-permute-start(bf16[3,20,32,128]{3,2,1,0:T(8,128)(2,1)S(1)} %pad_maximum_fusion.refs_2_), channel_id=1, source_target_pairs={{0,2},{1,3},{2,0},{3,1},{4,6},{5,7},{6,4},{7,5},{8,10},{9,11},{10,... | collective-permute-start | bytes 1474568 | tf_op jit(solution)/shard_map/ppermute | solution.py:90
  61.0 9.9 %shard_map.107 = (f32[8,256]{1,0:T(8,128)S(1)}, bf16[8,8,128]{2,1,0:T(8,128)(2,1)S(1)}, bf16[8,8,128]{2,1,0:T(8,128)(2,1)S(1)}) custom-call(s32[66]{0:T(128)S(1)} %copy-done.6, bf16[20,32,128]{2,1,0:T(8,128)(2,1)S(1)} %copy-done.2, bf16[20,32,128]{2,1,0:T(8,128)(2,1)S(1)} %collective-permute-done.9.refs_1_, ...), custom_call_target="tpu_custom_call" | custom-call | flops 8000000000 | bytes 4000000 | tf_op jit(solution)/shard_map/pallas_call | solution.py:261
  71.5 1.3 %collective-permute-done.22.refs_3_ = bf16[3,20,32,128]{3,2,1,0:T(8,128)(2,1)S(1)} collective-permute-done((bf16[3,20,32,128]{3,2,1,0:T(8,128)(2,1)S(1)}, bf16[3,20,32,128]{3,2,1,0:T(8,128)(2,1)S(1)}, u32[]{:S(2)}, u32[]{:S(2)}) %collective-permute-start.22) | collective-permute-done | bytes 491552 | tf_op jit(solution)/shard_map/ppermute | solution.py:90
  73.3 1.6 %collective-permute-done.23.refs_4_ = bf16[20,32,128]{2,1,0:T(8,128)(2,1)S(1)} collective-permute-done((bf16[20,32,128]{2,1,0:T(8,128)(2,1)S(1)}, bf16[20,32,128]{2,1,0:T(8,128)(2,1)S(1)}, u32[]{:S(2)}, u32[]{:S(2)}) %collective-permute-start.23) | collective-permute-done | bytes 163872 | tf_op jit(solution)/shard_map/ppermute | solution.py:90
  75.1 17.9 %shard_map.108 = (f32[4,256]{1,0:T(4,128)S(1)}, f32[4,256]{1,0:T(4,128)S(1)}, bf16[16,8,128]{2,1,0:T(8,128)(2,1)S(1)}, bf16[16,8,128]{2,1,0:T(8,128)(2,1)S(1)}) custom-call(s32[66]{0:T(128)S(1)} %copy-done.6, bf16[20,32,128]{2,1,0:T(8,128)(2,1)S(1)} %copy-done.7, bf16[20,32,128]{2,1,0:T(8,128)(2,1)S(1)} %collective-permute-done.8.refs_1_, ...), custom_call_target="tpu_custom_call" | custom-call | flops 16000000000 | bytes 8000000 | tf_op jit(solution)/shard_map/pallas_call | solution.py:261
  94.3 1.3 %collective-permute-start.27 = (f32[4,256]{1,0:T(4,128)S(1)}, f32[4,256]{1,0:T(4,128)S(1)}, u32[]{:S(2)}, u32[]{:S(2)}) collective-permute-start(f32[4,256]{1,0:T(4,128)S(1)} %get-tuple-element.49), channel_id=1, source_target_pairs={{0,16},{16,0},{1,17},{17,1},{2,18},{18,2},{3,19},{19,3},{4,20},{20... | collective-permute-start | bytes 12296 | tf_op jit(solution)/shard_map/ppermute | solution.py:390
  95.6 2.3 %collective-permute-done.27 = f32[4,256]{1,0:T(4,128)S(1)} collective-permute-done((f32[4,256]{1,0:T(4,128)S(1)}, f32[4,256]{1,0:T(4,128)S(1)}, u32[]{:S(2)}, u32[]{:S(2)}) %collective-permute-start.27) | collective-permute-done | bytes 4128 | tf_op jit(solution)/shard_map/ppermute | solution.py:390
  98.0 1.2 %collective-permute-done.29 = f32[4,256]{1,0:T(4,128)S(1)} collective-permute-done((f32[4,256]{1,0:T(4,128)S(1)}, f32[4,256]{1,0:T(4,128)S(1)}, u32[]{:S(2)}, u32[]{:S(2)}) %collective-permute-start.29) | collective-permute-done | bytes 4128 | tf_op jit(solution)/shard_map/ppermute | solution.py:90
  99.2 1.5 %collective-permute-start.30 = (f32[4,256]{1,0:T(4,128)S(1)}, f32[4,256]{1,0:T(4,128)S(1)}, u32[]{:S(2)}, u32[]{:S(2)}) collective-permute-start(f32[4,256]{1,0:T(4,128)S(1)} %add.27), channel_id=1, source_target_pairs={{0,2},{1,3},{2,0},{3,1},{4,6},{5,7},{6,4},{7,5},{8,10},{9,11},{10,... | collective-permute-start | bytes 12296 | tf_op jit(solution)/shard_map/ppermute | solution.py:90
  100.7 2.1 %collective-permute-done.30 = f32[4,256]{1,0:T(4,128)S(1)} collective-permute-done((f32[4,256]{1,0:T(4,128)S(1)}, f32[4,256]{1,0:T(4,128)S(1)}, u32[]{:S(2)}, u32[]{:S(2)}) %collective-permute-start.30) | collective-permute-done | bytes 4128 | tf_op jit(solution)/shard_map/ppermute | solution.py:90
  103.5 2.0 %shard_map.109 = bf16[2,8,4096]{2,1,0:T(8,128)(2,1)} custom-call(s32[66]{0:T(128)} %pad_add_fusion.info.info_ref, bf16[8,8,128]{2,1,0:T(8,128)(2,1)} %copy-done.4, bf16[8,8,128]{2,1,0:T(8,128)(2,1)} %copy-done.5, bf16[16,8,128]{2,1,0:T(8,128)(2,1)} %copy-done.3, bf16[32,8,128]{2,1,0:T(8,128)(2,1)} %copy-done.10), custom_call_target="tpu_custom_call" | custom-call | tf_op jit(solution)/shard_map/pallas_call | solution.py:393
  106.4 1.8 %collective-permute-start.32 = (f32[4,256]{1,0:T(4,128)S(1)}, f32[4,256]{1,0:T(4,128)S(1)}, u32[]{:S(2)}, u32[]{:S(2)}) collective-permute-start(f32[4,256]{1,0:T(4,128)S(1)} %add.29), channel_id=1, source_target_pairs={{0,8},{1,9},{2,10},{3,11},{4,12},{5,13},{6,14},{7,15},{8,0},{9,1},... | collective-permute-start | bytes 12296 | tf_op jit(solution)/shard_map/ppermute | solution.py:90
  108.2 2.7 %collective-permute-done.32 = f32[4,256]{1,0:T(4,128)S(1)} collective-permute-done((f32[4,256]{1,0:T(4,128)S(1)}, f32[4,256]{1,0:T(4,128)S(1)}, u32[]{:S(2)}, u32[]{:S(2)}) %collective-permute-start.32) | collective-permute-done | bytes 4128 | tf_op jit(solution)/shard_map/ppermute | solution.py:90
  (86 shorter events, 14.4 us)
Async XLA Ops:
  0.6 7.8 %collective-permute-start.1 = (bf16[2,8,4096]{2,1,0:T(8,128)(2,1)}, bf16[2,8,4096]{2,1,0:T(8,128)(2,1)S(1)}, u32[]{:S(2)}, u32[]{:S(2)}) collective-permute-start(bf16[2,8,4096]{2,1,0:T(8,128)(2,1)} %own.2), channel_id=1, source_target_pairs={{0,16},{16,0},{1,17},{17,1},{2,18},{18,2},{3,19},{19,3},{4,20},{20... | collective-permute-start | bytes 393224 | tf_op jit(solution)/shard_map/ppermute | solution.py:319
  4.7 3.7 %collective-permute-start = (s32[128]{0:T(128)}, s32[128]{0:T(128)S(1)}, u32[]{:S(2)}, u32[]{:S(2)}) collective-permute-start(s32[128]{0:T(128)} %param.11), channel_id=1, source_target_pairs={{0,16},{16,0},{1,17},{17,1},{2,18},{18,2},{3,19},{19,3},{4,20},{20... | collective-permute-start | bytes 1544 | tf_op jit(solution)/shard_map/ppermute | solution.py:325
  11.2 6.4 %collective-permute-start.2 = (bf16[20,32,128]{2,1,0:T(8,128)(2,1)}, bf16[20,32,128]{2,1,0:T(8,128)(2,1)S(1)}, u32[]{:S(2)}, u32[]{:S(2)}) collective-permute-start(bf16[20,32,128]{2,1,0:T(8,128)(2,1)} %get-tuple-element.34.refs_0_), channel_id=1, source_target_pairs={{0,4},{1,5},{2,6},{3,7},{4,0},{5,1},{6,2},{7,3},{8,12},{9,13},{10,... | collective-permute-start | bytes 491528 | tf_op jit(solution)/shard_map/ppermute | solution.py:90
  12.7 9.1 %collective-permute-start.3 = (bf16[20,32,128]{2,1,0:T(8,128)(2,1)}, bf16[20,32,128]{2,1,0:T(8,128)(2,1)S(1)}, u32[]{:S(2)}, u32[]{:S(2)}) collective-permute-start(bf16[20,32,128]{2,1,0:T(8,128)(2,1)} %get-tuple-element.34.refs_0_), channel_id=1, source_target_pairs={{0,12},{1,13},{2,14},{3,15},{4,8},{5,9},{6,10},{7,11},{8,4},{9,5},... | collective-permute-start | bytes 491528 | tf_op jit(solution)/shard_map/ppermute | solution.py:90
  15.2 17.1 %collective-permute-start.19 = (bf16[2,128,768]{2,1,0:T(8,128)(2,1)}, bf16[2,128,768]{2,1,0:T(8,128)(2,1)S(1)}, u32[]{:S(2)}, u32[]{:S(2)}) collective-permute-start(bf16[2,128,768]{2,1,0:T(8,128)(2,1)} %own.3), channel_id=1, source_target_pairs={{0,16},{16,0},{1,17},{17,1},{2,18},{18,2},{3,19},{19,3},{4,20},{20... | collective-permute-start | bytes 1179656 | tf_op jit(solution)/shard_map/ppermute | solution.py:336
  16.0 11.0 %collective-permute-start.10 = (bf16[20,32,128]{2,1,0:T(8,128)(2,1)}, bf16[20,32,128]{2,1,0:T(8,128)(2,1)S(1)}, u32[]{:S(2)}, u32[]{:S(2)}) collective-permute-start(bf16[20,32,128]{2,1,0:T(8,128)(2,1)} %get-tuple-element.34.refs_0_), channel_id=1, source_target_pairs={{0,2},{1,3},{2,0},{3,1},{4,6},{5,7},{6,4},{7,5},{8,10},{9,11},{10,... | collective-permute-start | bytes 491528 | tf_op jit(solution)/shard_map/ppermute | solution.py:90
  21.8 8.9 %collective-permute-start.4 = (bf16[20,32,128]{2,1,0:T(8,128)(2,1)}, bf16[20,32,128]{2,1,0:T(8,128)(2,1)S(1)}, u32[]{:S(2)}, u32[]{:S(2)}) collective-permute-start(bf16[20,32,128]{2,1,0:T(8,128)(2,1)} %get-tuple-element.34.refs_0_), channel_id=1, source_target_pairs={{0,8},{1,9},{2,10},{3,11},{4,12},{5,13},{6,14},{7,15},{8,0},{9,1},... | collective-permute-start | bytes 491528 | tf_op jit(solution)/shard_map/ppermute | solution.py:90
  25.5 5.3 %collective-permute-start.13 = (bf16[20,32,128]{2,1,0:T(8,128)(2,1)S(1)}, bf16[20,32,128]{2,1,0:T(8,128)(2,1)S(1)}, u32[]{:S(2)}, u32[]{:S(2)}) collective-permute-start(bf16[20,32,128]{2,1,0:T(8,128)(2,1)S(1)} %collective-permute-done.2.refs_4_), channel_id=1, source_target_pairs={{0,2},{1,3},{2,0},{3,1},{4,6},{5,7},{6,4},{7,5},{8,10},{9,11},{10,... | collective-permute-start | bytes 491528 | tf_op jit(solution)/shard_map/ppermute | solution.py:90
  27.0 9.3 %collective-permute-start.9 = (bf16[20,32,128]{2,1,0:T(8,128)(2,1)}, bf16[20,32,128]{2,1,0:T(8,128)(2,1)S(1)}, u32[]{:S(2)}, u32[]{:S(2)}) collective-permute-start(bf16[20,32,128]{2,1,0:T(8,128)(2,1)} %get-tuple-element.34.refs_0_), channel_id=1, source_target_pairs={{0,1},{1,0},{2,3},{3,2},{4,5},{5,4},{6,7},{7,6},{8,9},{9,8},{10,11... | collective-permute-start | bytes 491528 | tf_op jit(solution)/shard_map/ppermute | solution.py:90
  27.0 9.5 %collective-permute-start.12 = (bf16[20,32,128]{2,1,0:T(8,128)(2,1)S(1)}, bf16[20,32,128]{2,1,0:T(8,128)(2,1)S(1)}, u32[]{:S(2)}, u32[]{:S(2)}) collective-permute-start(bf16[20,32,128]{2,1,0:T(8,128)(2,1)S(1)} %collective-permute-done.2.refs_4_), channel_id=1, source_target_pairs={{0,1},{1,0},{2,3},{3,2},{4,5},{5,4},{6,7},{7,6},{8,9},{9,8},{10,11... | collective-permute-start | bytes 491528 | tf_op jit(solution)/shard_map/ppermute | solution.py:90
  30.8 6.1 %collective-permute-start.18 = (bf16[20,32,128]{2,1,0:T(8,128)(2,1)S(1)}, bf16[20,32,128]{2,1,0:T(8,128)(2,1)S(1)}, u32[]{:S(2)}, u32[]{:S(2)}) collective-permute-start(bf16[20,32,128]{2,1,0:T(8,128)(2,1)S(1)} %collective-permute-done.3.refs_12_), channel_id=1, source_target_pairs={{0,1},{1,0},{2,3},{3,2},{4,5},{5,4},{6,7},{7,6},{8,9},{9,8},{10,11... | collective-permute-start | bytes 491528 | tf_op jit(solution)/shard_map/ppermute | solution.py:90
  30.8 6.6 %collective-permute-start.16 = (bf16[20,32,128]{2,1,0:T(8,128)(2,1)S(1)}, bf16[20,32,128]{2,1,0:T(8,128)(2,1)S(1)}, u32[]{:S(2)}, u32[]{:S(2)}) collective-permute-start(bf16[20,32,128]{2,1,0:T(8,128)(2,1)S(1)} %collective-permute-done.4.refs_8_), channel_id=1, source_target_pairs={{0,2},{1,3},{2,0},{3,1},{4,6},{5,7},{6,4},{7,5},{8,10},{9,11},{10,... | collective-permute-start | bytes 491528 | tf_op jit(solution)/shard_map/ppermute | solution.py:90
  32.3 5.9 %collective-permute-start.11 = (bf16[20,32,128]{2,1,0:T(8,128)(2,1)S(1)}, bf16[20,32,128]{2,1,0:T(8,128)(2,1)S(1)}, u32[]{:S(2)}, u32[]{:S(2)}) collective-permute-start(bf16[20,32,128]{2,1,0:T(8,128)(2,1)S(1)} %collective-permute-done.10.refs_2_), channel_id=1, source_target_pairs={{0,1},{1,0},{2,3},{3,2},{4,5},{5,4},{6,7},{7,6},{8,9},{9,8},{10,11... | collective-permute-start | bytes 491528 | tf_op jit(solution)/shard_map/ppermute | solution.py:90
  36.3 2.0 %collective-permute-start.15 = (bf16[20,32,128]{2,1,0:T(8,128)(2,1)S(1)}, bf16[20,32,128]{2,1,0:T(8,128)(2,1)S(1)}, u32[]{:S(2)}, u32[]{:S(2)}) collective-permute-start(bf16[20,32,128]{2,1,0:T(8,128)(2,1)S(1)} %collective-permute-done.4.refs_8_), channel_id=1, source_target_pairs={{0,1},{1,0},{2,3},{3,2},{4,5},{5,4},{6,7},{7,6},{8,9},{9,8},{10,11... | collective-permute-start | bytes 491528 | tf_op jit(solution)/shard_map/ppermute | solution.py:90
  36.5 4.4 %collective-permute-start.14 = (bf16[20,32,128]{2,1,0:T(8,128)(2,1)S(1)}, bf16[20,32,128]{2,1,0:T(8,128)(2,1)S(1)}, u32[]{:S(2)}, u32[]{:S(2)}) collective-permute-start(bf16[20,32,128]{2,1,0:T(8,128)(2,1)S(1)} %collective-permute-done.13.refs_6_), channel_id=1, source_target_pairs={{0,1},{1,0},{2,3},{3,2},{4,5},{5,4},{6,7},{7,6},{8,9},{9,8},{10,11... | collective-permute-start | bytes 491528 | tf_op jit(solution)/shard_map/ppermute | solution.py:90
  36.9 6.3 %collective-permute-start.20 = (bf16[20,32,128]{2,1,0:T(8,128)(2,1)S(1)}, bf16[20,32,128]{2,1,0:T(8,128)(2,1)S(1)}, u32[]{:S(2)}, u32[]{:S(2)}) collective-permute-start(bf16[20,32,128]{2,1,0:T(8,128)(2,1)S(1)} %collective-permute-done.3.refs_12_), channel_id=1, source_target_pairs={{0,2},{1,3},{2,0},{3,1},{4,6},{5,7},{6,4},{7,5},{8,10},{9,11},{10,... | collective-permute-start | bytes 491528 | tf_op jit(solution)/shard_map/ppermute | solution.py:90
  37.4 6.3 %collective-permute-start.17 = (bf16[20,32,128]{2,1,0:T(8,128)(2,1)S(1)}, bf16[20,32,128]{2,1,0:T(8,128)(2,1)S(1)}, u32[]{:S(2)}, u32[]{:S(2)}) collective-permute-start(bf16[20,32,128]{2,1,0:T(8,128)(2,1)S(1)} %collective-permute-done.16.refs_10_), channel_id=1, source_target_pairs={{0,1},{1,0},{2,3},{3,2},{4,5},{5,4},{6,7},{7,6},{8,9},{9,8},{10,11... | collective-permute-start | bytes 491528 | tf_op jit(solution)/shard_map/ppermute | solution.py:90
  38.2 20.7 %collective-permute-start.5 = (bf16[20,32,128]{2,1,0:T(8,128)(2,1)}, bf16[20,32,128]{2,1,0:T(8,128)(2,1)S(1)}, u32[]{:S(2)}, u32[]{:S(2)}) collective-permute-start(bf16[20,32,128]{2,1,0:T(8,128)(2,1)} %get-tuple-element.35.refs_0_), channel_id=1, source_target_pairs={{0,4},{1,5},{2,6},{3,7},{4,0},{5,1},{6,2},{7,3},{8,12},{9,13},{10,... | collective-permute-start | bytes 491528 | tf_op jit(solution)/shard_map/ppermute | solution.py:90
  38.3 20.6 %collective-permute-start.6 = (bf16[20,32,128]{2,1,0:T(8,128)(2,1)}, bf16[20,32,128]{2,1,0:T(8,128)(2,1)S(1)}, u32[]{:S(2)}, u32[]{:S(2)}) collective-permute-start(bf16[20,32,128]{2,1,0:T(8,128)(2,1)} %get-tuple-element.35.refs_0_), channel_id=1, source_target_pairs={{0,12},{1,13},{2,14},{3,15},{4,8},{5,9},{6,10},{7,11},{8,4},{9,5},... | collective-permute-start | bytes 491528 | tf_op jit(solution)/shard_map/ppermute | solution.py:90
  40.9 18.0 %collective-permute-start.7 = (bf16[20,32,128]{2,1,0:T(8,128)(2,1)}, bf16[20,32,128]{2,1,0:T(8,128)(2,1)S(1)}, u32[]{:S(2)}, u32[]{:S(2)}) collective-permute-start(bf16[20,32,128]{2,1,0:T(8,128)(2,1)} %get-tuple-element.35.refs_0_), channel_id=1, source_target_pairs={{0,8},{1,9},{2,10},{3,11},{4,12},{5,13},{6,14},{7,15},{8,0},{9,1},... | collective-permute-start | bytes 491528 | tf_op jit(solution)/shard_map/ppermute | solution.py:90
  43.1 15.8 %collective-permute-start.8 = (bf16[20,32,128]{2,1,0:T(8,128)(2,1)}, bf16[20,32,128]{2,1,0:T(8,128)(2,1)S(1)}, u32[]{:S(2)}, u32[]{:S(2)}) collective-permute-start(bf16[20,32,128]{2,1,0:T(8,128)(2,1)} %get-tuple-element.35.refs_0_), channel_id=1, source_target_pairs={{0,2},{1,3},{2,0},{3,1},{4,6},{5,7},{6,4},{7,5},{8,10},{9,11},{10,... | collective-permute-start | bytes 491528 | tf_op jit(solution)/shard_map/ppermute | solution.py:90
  43.7 1.4 %collective-permute-start.21 = (bf16[20,32,128]{2,1,0:T(8,128)(2,1)S(1)}, bf16[20,32,128]{2,1,0:T(8,128)(2,1)S(1)}, u32[]{:S(2)}, u32[]{:S(2)}) collective-permute-start(bf16[20,32,128]{2,1,0:T(8,128)(2,1)S(1)} %collective-permute-done.20.refs_14_), channel_id=1, source_target_pairs={{0,1},{1,0},{2,3},{3,2},{4,5},{5,4},{6,7},{7,6},{8,9},{9,8},{10,11... | collective-permute-start | bytes 491528 | tf_op jit(solution)/shard_map/ppermute | solution.py:90
  59.5 13.3 %collective-permute-start.22 = (bf16[3,20,32,128]{3,2,1,0:T(8,128)(2,1)S(1)}, bf16[3,20,32,128]{3,2,1,0:T(8,128)(2,1)S(1)}, u32[]{:S(2)}, u32[]{:S(2)}) collective-permute-start(bf16[3,20,32,128]{3,2,1,0:T(8,128)(2,1)S(1)} %pad_maximum_fusion.refs_2_), channel_id=1, source_target_pairs={{0,2},{1,3},{2,0},{3,1},{4,6},{5,7},{6,4},{7,5},{8,10},{9,11},{10,... | collective-permute-start | bytes 1474568 | tf_op jit(solution)/shard_map/ppermute | solution.py:90
  61.0 14.1 %collective-permute-start.25 = (bf16[3,20,32,128]{3,2,1,0:T(8,128)(2,1)S(1)}, bf16[3,20,32,128]{3,2,1,0:T(8,128)(2,1)S(1)}, u32[]{:S(2)}, u32[]{:S(2)}) collective-permute-start(bf16[3,20,32,128]{3,2,1,0:T(8,128)(2,1)S(1)} %pad_maximum_fusion.refs_2_), channel_id=1, source_target_pairs={{0,1},{1,0},{2,3},{3,2},{4,5},{5,4},{6,7},{7,6},{8,9},{9,8},{10,11... | collective-permute-start | bytes 1474568 | tf_op jit(solution)/shard_map/ppermute | solution.py:90
  72.8 2.3 %collective-permute-start.26 = (bf16[3,20,32,128]{3,2,1,0:T(8,128)(2,1)S(1)}, bf16[3,20,32,128]{3,2,1,0:T(8,128)(2,1)S(1)}, u32[]{:S(2)}, u32[]{:S(2)}) collective-permute-start(bf16[3,20,32,128]{3,2,1,0:T(8,128)(2,1)S(1)} %collective-permute-done.22.refs_3_), channel_id=1, source_target_pairs={{0,1},{1,0},{2,3},{3,2},{4,5},{5,4},{6,7},{7,6},{8,9},{9,8},{10,11... | collective-permute-start | bytes 1474568 | tf_op jit(solution)/shard_map/ppermute | solution.py:90
  72.8 2.1 %collective-permute-start.23 = (bf16[20,32,128]{2,1,0:T(8,128)(2,1)S(1)}, bf16[20,32,128]{2,1,0:T(8,128)(2,1)S(1)}, u32[]{:S(2)}, u32[]{:S(2)}) collective-permute-start(bf16[20,32,128]{2,1,0:T(8,128)(2,1)S(1)} %copy-done.7), channel_id=1, source_target_pairs={{0,1},{1,0},{2,3},{3,2},{4,5},{5,4},{6,7},{7,6},{8,9},{9,8},{10,11... | collective-permute-start | bytes 491528 | tf_op jit(solution)/shard_map/ppermute | solution.py:90
  73.3 1.8 %collective-permute-start.24 = (bf16[20,32,128]{2,1,0:T(8,128)(2,1)S(1)}, bf16[20,32,128]{2,1,0:T(8,128)(2,1)S(1)}, u32[]{:S(2)}, u32[]{:S(2)}) collective-permute-start(bf16[20,32,128]{2,1,0:T(8,128)(2,1)S(1)} %collective-permute-done.8.refs_1_), channel_id=1, source_target_pairs={{0,1},{1,0},{2,3},{3,2},{4,5},{5,4},{6,7},{7,6},{8,9},{9,8},{10,11... | collective-permute-start | bytes 491528 | tf_op jit(solution)/shard_map/ppermute | solution.py:90
  93.6 4.3 %collective-permute-start.28 = (bf16[32,8,128]{2,1,0:T(8,128)(2,1)S(1)}, bf16[32,8,128]{2,1,0:T(8,128)(2,1)S(1)}, u32[]{:S(2)}, u32[]{:S(2)}) collective-permute-start(bf16[32,8,128]{2,1,0:T(8,128)(2,1)S(1)} %pad_maximum_fusion.1), channel_id=1, source_target_pairs={{0,16},{16,0},{1,17},{17,1},{2,18},{18,2},{3,19},{19,3},{4,20},{20... | collective-permute-start | bytes 196616 | tf_op jit(solution)/shard_map/ppermute | solution.py:391
  94.3 3.6 %collective-permute-start.27 = (f32[4,256]{1,0:T(4,128)S(1)}, f32[4,256]{1,0:T(4,128)S(1)}, u32[]{:S(2)}, u32[]{:S(2)}) collective-permute-start(f32[4,256]{1,0:T(4,128)S(1)} %get-tuple-element.49), channel_id=1, source_target_pairs={{0,16},{16,0},{1,17},{17,1},{2,18},{18,2},{3,19},{19,3},{4,20},{20... | collective-permute-start | bytes 12296 | tf_op jit(solution)/shard_map/ppermute | solution.py:390
  99.2 3.6 %collective-permute-start.30 = (f32[4,256]{1,0:T(4,128)S(1)}, f32[4,256]{1,0:T(4,128)S(1)}, u32[]{:S(2)}, u32[]{:S(2)}) collective-permute-start(f32[4,256]{1,0:T(4,128)S(1)} %add.27), channel_id=1, source_target_pairs={{0,2},{1,3},{2,0},{3,1},{4,6},{5,7},{6,4},{7,5},{8,10},{9,11},{10,... | collective-permute-start | bytes 12296 | tf_op jit(solution)/shard_map/ppermute | solution.py:90
  102.8 3.6 %collective-permute-start.31 = (f32[4,256]{1,0:T(4,128)S(1)}, f32[4,256]{1,0:T(4,128)S(1)}, u32[]{:S(2)}, u32[]{:S(2)}) collective-permute-start(f32[4,256]{1,0:T(4,128)S(1)} %add.28), channel_id=1, source_target_pairs={{0,4},{1,5},{2,6},{3,7},{4,0},{5,1},{6,2},{7,3},{8,12},{9,13},{10,... | collective-permute-start | bytes 12296 | tf_op jit(solution)/shard_map/ppermute | solution.py:90
  106.4 4.5 %collective-permute-start.32 = (f32[4,256]{1,0:T(4,128)S(1)}, f32[4,256]{1,0:T(4,128)S(1)}, u32[]{:S(2)}, u32[]{:S(2)}) collective-permute-start(f32[4,256]{1,0:T(4,128)S(1)} %add.29), channel_id=1, source_target_pairs={{0,8},{1,9},{2,10},{3,11},{4,12},{5,13},{6,14},{7,15},{8,0},{9,1},... | collective-permute-start | bytes 12296 | tf_op jit(solution)/shard_map/ppermute | solution.py:90
  (12 other events, 37.7 us)

commit v7 on v6

--- a/solution.py
+++ b/solution.py
@@ -354,11 +354,11 @@
     units[0] = packed[0]
     units[4] = hop(packed[0], 4)
     units[12] = hop(packed[0], 12)
-    units[8] = hop(after(packed[0], units[4], units[12]), 8)
+    units[8] = hop(after(packed[0], units[4], units[12], grads), 8)
     units[2] = hop(units[0], 2)
     units[6] = hop(units[4], 2)
-    units[14] = hop(after(units[12], grads), 2)
-    units[10] = hop(after(units[8], units[2], units[6]), 2)
+    units[14] = hop(units[12], 2)
+    units[10] = hop(after(units[8], units[2], units[6], units[14]), 2)
     for d in (0, 2, 4, 6, 12, 14, 8, 10):
         units[d ^ 1] = hop(units[d], 1)
     places0 = [(d, None) for d in range(NQ)]

time: 112 us -> 112 us (level)
    ppermute x1, waiting for transfers between devices: 2.89 us -> 0.01 us  [paired_body(): ids_other = lax.ppermute(after(sequence_ids, mine), 'parts', SWAP)]
    ppermute x1, waiting for transfers between devices: 0.01 us -> 2.44 us  [paired_body(): train_other = lax.ppermute(train_inputs, 'parts', SWAP)]
    ppermute x28, starting transfers between devices: 24.2 us -> 22.5 us  [hop(): return lax.ppermute(value, 'query', [(i, i ^ bits) for i in range(NQ)])]
    ppermute x28, waiting for transfers between devices: 20.1 us -> 21.4 us  [hop(): return lax.ppermute(value, 'query', [(i, i ^ bits) for i in range(NQ)])]
  transfers between devices with their start and end apart: 33 -> 33, of which waited for: 15 -> 14; matrix products, arithmetic and copies ran while one was open for 3% -> 3% of each run, Pallas kernels for 23% -> 24%
where the time goes in v7:
time: 112 us; the launch traced here: 111 us
  Pallas kernels  45.2 us (40%)
  starting transfers between devices  29.3 us (26%)
  waiting for transfers between devices  26.1 us (23%)
  local copies, waits for them, and re-layouts  7.65 us (7%)
  other arithmetic  2.21 us (2%)
    pallas_call x3, Pallas kernels, score_tiles(): pl.pallas_call(kernel, in_specs=[SMEM] + [VMEM] * len(arrays) + [VMEM, VM...  37.8 us
    ppermute x28, starting transfers between devices, hop(): return lax.ppermute(value, 'query', [(i, i ^ bits) for i in range(NQ)])  22.5 us
    ppermute x28, waiting for transfers between devices, hop(): return lax.ppermute(value, 'query', [(i, i ^ bits) for i in range(NQ)])  21.4 us
    unnamed x22, local copies, waits for them, and re-layouts  6.2 us
    pallas_call x1, Pallas kernels, paired_body(): pl.pallas_call(prepare_kernel, in_specs=[SMEM] + [VMEM] * 4, out_specs=[V...  3.26 us
    ppermute x1, starting transfers between devices, paired_body(): train_other = lax.ppermute(train_inputs, 'parts', SWAP)  3 us
    ppermute x1, waiting for transfers between devices, paired_body(): train_other = lax.ppermute(train_inputs, 'parts', SWAP)  2.44 us
    ppermute x1, waiting for transfers between devices, paired_body(): total = keep + lax.ppermute(give, 'parts', SWAP)  2.28 us
  transfers between devices with their start and end apart: 33, of which 14 were waited for; matrix products, arithmetic and copies ran while one was open for 3% of the time, Pallas kernels for 24%

profile of v7, /device:TPU:0, one launch (start us, length us, event | category | flops | bytes accessed | tf_op | source)
XLA Modules:
  0.0 111.4 jit_solution(1023075839503771063)
XLA Ops:
  0.6 3.0 %collective-permute-start.1 = (bf16[2,8,4096]{2,1,0:T(8,128)(2,1)}, bf16[2,8,4096]{2,1,0:T(8,128)(2,1)S(1)}, u32[]{:S(2)}, u32[]{:S(2)}) collective-permute-start(bf16[2,8,4096]{2,1,0:T(8,128)(2,1)} %own.2), channel_id=1, source_target_pairs={{0,16},{16,0},{1,17},{17,1},{2,18},{18,2},{3,19},{19,3},{4,20},{20... | collective-permute-start | bytes 393224 | tf_op jit(solution)/shard_map/ppermute | solution.py:319
  4.9 2.4 %collective-permute-done.1.other = bf16[2,8,4096]{2,1,0:T(8,128)(2,1)S(1)} collective-permute-done((bf16[2,8,4096]{2,1,0:T(8,128)(2,1)}, bf16[2,8,4096]{2,1,0:T(8,128)(2,1)S(1)}, u32[]{:S(2)}, u32[]{:S(2)}) %collective-permute-start.1) | collective-permute-done | bytes 131104 | tf_op jit(solution)/shard_map/ppermute | solution.py:319
  7.4 1.7 %collective-permute-start.4 = (bf16[2,128,768]{2,1,0:T(8,128)(2,1)}, bf16[2,128,768]{2,1,0:T(8,128)(2,1)S(1)}, u32[]{:S(2)}, u32[]{:S(2)}) collective-permute-start(bf16[2,128,768]{2,1,0:T(8,128)(2,1)} %own.3), channel_id=1, source_target_pairs={{0,16},{16,0},{1,17},{17,1},{2,18},{18,2},{3,19},{19,3},{4,20},{20... | collective-permute-start | bytes 1179656 | tf_op jit(solution)/shard_map/ppermute | solution.py:336
  9.7 2.1 %shard_map.104 = (bf16[20,32,128]{2,1,0:T(8,128)(2,1)}, bf16[20,32,128]{2,1,0:T(8,128)(2,1)}) custom-call(s32[66]{0:T(128)} %pad_add_fusion.info.info_ref, bf16[2,8,4096]{2,1,0:T(8,128)(2,1)} %own.2, bf16[2,8,4096]{2,1,0:T(8,128)(2,1)} %copy-done.9, bf16[2,16,4096]{2,1,0:T(8,128)(2,1)} %query.2, bf16[4,128,128]{2,1,0:T(8,128)(2,1)} %basis.1), custom_call_target="tpu_custom_call" | custom-call | tf_op jit(solution)/shard_map/pallas_call | solution.py:329
  11.8 1.6 %collective-permute-start.2 = (bf16[20,32,128]{2,1,0:T(8,128)(2,1)}, bf16[20,32,128]{2,1,0:T(8,128)(2,1)S(1)}, u32[]{:S(2)}, u32[]{:S(2)}) collective-permute-start(bf16[20,32,128]{2,1,0:T(8,128)(2,1)} %get-tuple-element.35.refs_0_), channel_id=1, source_target_pairs={{0,4},{1,5},{2,6},{3,7},{4,0},{5,1},{6,2},{7,3},{8,12},{9,13},{10,... | collective-permute-start | bytes 491528 | tf_op jit(solution)/shard_map/ppermute | solution.py:90
  13.4 2.5 %collective-permute-start.3 = (bf16[20,32,128]{2,1,0:T(8,128)(2,1)}, bf16[20,32,128]{2,1,0:T(8,128)(2,1)S(1)}, u32[]{:S(2)}, u32[]{:S(2)}) collective-permute-start(bf16[20,32,128]{2,1,0:T(8,128)(2,1)} %get-tuple-element.35.refs_0_), channel_id=1, source_target_pairs={{0,12},{1,13},{2,14},{3,15},{4,8},{5,9},{6,10},{7,11},{8,4},{9,5},... | collective-permute-start | bytes 491528 | tf_op jit(solution)/shard_map/ppermute | solution.py:90
  15.9 1.5 %collective-permute-start.11 = (bf16[20,32,128]{2,1,0:T(8,128)(2,1)}, bf16[20,32,128]{2,1,0:T(8,128)(2,1)S(1)}, u32[]{:S(2)}, u32[]{:S(2)}) collective-permute-start(bf16[20,32,128]{2,1,0:T(8,128)(2,1)} %get-tuple-element.35.refs_0_), channel_id=1, source_target_pairs={{0,2},{1,3},{2,0},{3,1},{4,6},{5,7},{6,4},{7,5},{8,10},{9,11},{10,... | collective-permute-start | bytes 491528 | tf_op jit(solution)/shard_map/ppermute | solution.py:90
  18.2 1.5 %collective-permute-start.14 = (bf16[20,32,128]{2,1,0:T(8,128)(2,1)S(1)}, bf16[20,32,128]{2,1,0:T(8,128)(2,1)S(1)}, u32[]{:S(2)}, u32[]{:S(2)}) collective-permute-start(bf16[20,32,128]{2,1,0:T(8,128)(2,1)S(1)} %collective-permute-done.2.refs_4_), channel_id=1, source_target_pairs={{0,2},{1,3},{2,0},{3,1},{4,6},{5,7},{6,4},{7,5},{8,10},{9,11},{10,... | collective-permute-start | bytes 491528 | tf_op jit(solution)/shard_map/ppermute | solution.py:90
  19.7 2.7 %collective-permute-done.3.refs_12_ = bf16[20,32,128]{2,1,0:T(8,128)(2,1)S(1)} collective-permute-done((bf16[20,32,128]{2,1,0:T(8,128)(2,1)}, bf16[20,32,128]{2,1,0:T(8,128)(2,1)S(1)}, u32[]{:S(2)}, u32[]{:S(2)}) %collective-permute-start.3) | collective-permute-done | bytes 163872 | tf_op jit(solution)/shard_map/ppermute | solution.py:90
  22.4 1.5 %collective-permute-start.17 = (bf16[20,32,128]{2,1,0:T(8,128)(2,1)S(1)}, bf16[20,32,128]{2,1,0:T(8,128)(2,1)S(1)}, u32[]{:S(2)}, u32[]{:S(2)}) collective-permute-start(bf16[20,32,128]{2,1,0:T(8,128)(2,1)S(1)} %collective-permute-done.3.refs_12_), channel_id=1, source_target_pairs={{0,2},{1,3},{2,0},{3,1},{4,6},{5,7},{6,4},{7,5},{8,10},{9,11},{10,... | collective-permute-start | bytes 491528 | tf_op jit(solution)/shard_map/ppermute | solution.py:90
  24.7 3.3 %shard_map.105 = (bf16[2,256,768]{2,1,0:T(8,128)(2,1)}, bf16[2,768,256]{2,1,0:T(8,128)(2,1)}) custom-call(s32[66]{0:T(128)} %pad_add_fusion.info.info_ref, bf16[2,128,768]{2,1,0:T(8,128)(2,1)} %own.3, bf16[2,128,768]{2,1,0:T(8,128)(2,1)} %copy-done.8, bf16[2,256,768]{2,1,0:T(8,128)(2,1)} %query.3, bf16[2,12,64,64]{3,2,1,0:T(8,128)(2,1)} %tiles.1), custom_call_target="tpu_custom_call" | custom-call | tf_op jit(solution)/shard_map/pallas_call | solution.py:343
  28.0 1.8 %collective-permute-start.5 = (bf16[20,32,128]{2,1,0:T(8,128)(2,1)}, bf16[20,32,128]{2,1,0:T(8,128)(2,1)S(1)}, u32[]{:S(2)}, u32[]{:S(2)}) collective-permute-start(bf16[20,32,128]{2,1,0:T(8,128)(2,1)} %get-tuple-element.35.refs_0_), channel_id=1, source_target_pairs={{0,8},{1,9},{2,10},{3,11},{4,12},{5,13},{6,14},{7,15},{8,0},{9,1},... | collective-permute-start | bytes 491528 | tf_op jit(solution)/shard_map/ppermute | solution.py:90
  30.8 5.4 %collective-permute-done.5.refs_8_ = bf16[20,32,128]{2,1,0:T(8,128)(2,1)S(1)} collective-permute-done((bf16[20,32,128]{2,1,0:T(8,128)(2,1)}, bf16[20,32,128]{2,1,0:T(8,128)(2,1)S(1)}, u32[]{:S(2)}, u32[]{:S(2)}) %collective-permute-start.5) | collective-permute-done | bytes 163872 | tf_op jit(solution)/shard_map/ppermute | solution.py:90
  38.1 2.7 %collective-permute-start.7 = (bf16[20,32,128]{2,1,0:T(8,128)(2,1)}, bf16[20,32,128]{2,1,0:T(8,128)(2,1)S(1)}, u32[]{:S(2)}, u32[]{:S(2)}) collective-permute-start(bf16[20,32,128]{2,1,0:T(8,128)(2,1)} %get-tuple-element.36.refs_0_), channel_id=1, source_target_pairs={{0,12},{1,13},{2,14},{3,15},{4,8},{5,9},{6,10},{7,11},{8,4},{9,5},... | collective-permute-start | bytes 491528 | tf_op jit(solution)/shard_map/ppermute | solution.py:90
  41.6 1.3 %collective-permute-done.18.refs_10_ = bf16[20,32,128]{2,1,0:T(8,128)(2,1)S(1)} collective-permute-done((bf16[20,32,128]{2,1,0:T(8,128)(2,1)S(1)}, bf16[20,32,128]{2,1,0:T(8,128)(2,1)S(1)}, u32[]{:S(2)}, u32[]{:S(2)}) %collective-permute-start.18) | collective-permute-done | bytes 163872 | tf_op jit(solution)/shard_map/ppermute | solution.py:90
  43.5 1.2 %collective-permute-done.19.refs_11_ = bf16[20,32,128]{2,1,0:T(8,128)(2,1)S(1)} collective-permute-done((bf16[20,32,128]{2,1,0:T(8,128)(2,1)S(1)}, bf16[20,32,128]{2,1,0:T(8,128)(2,1)S(1)}, u32[]{:S(2)}, u32[]{:S(2)}) %collective-permute-start.19) | collective-permute-done | bytes 163872 | tf_op jit(solution)/shard_map/ppermute | solution.py:90
  44.8 1.1 %copy-done = bf16[2,256,768]{2,1,0:T(8,128)(2,1)S(1)} copy-done((bf16[2,256,768]{2,1,0:T(8,128)(2,1)S(1)}, bf16[2,256,768]{2,1,0:T(8,128)(2,1)}, u32[]{:S(2)}) %copy-start) | copy-done | bytes 786456
  45.9 1.1 %copy-done.1 = bf16[2,768,256]{2,1,0:T(8,128)(2,1)S(1)} copy-done((bf16[2,768,256]{2,1,0:T(8,128)(2,1)S(1)}, bf16[2,768,256]{2,1,0:T(8,128)(2,1)}, u32[]{:S(2)}) %copy-start.1) | copy-done | bytes 786456
  48.5 10.0 %shard_map.106 = (f32[8,256]{1,0:T(8,128)S(1)}, bf16[8,8,128]{2,1,0:T(8,128)(2,1)S(1)}, bf16[8,8,128]{2,1,0:T(8,128)(2,1)S(1)}) custom-call(s32[66]{0:T(128)S(1)} %copy-done.6, bf16[20,32,128]{2,1,0:T(8,128)(2,1)S(1)} %copy-done.2, bf16[20,32,128]{2,1,0:T(8,128)(2,1)S(1)} %collective-permute-done.10.refs_1_, ...), custom_call_target="tpu_custom_call" | custom-call | flops 80000000 | bytes 4000000 | tf_op jit(solution)/shard_map/pallas_call | solution.py:261
  59.2 1.5 %collective-permute-start.22 = (bf16[3,20,32,128]{3,2,1,0:T(8,128)(2,1)S(1)}, bf16[3,20,32,128]{3,2,1,0:T(8,128)(2,1)S(1)}, u32[]{:S(2)}, u32[]{:S(2)}) collective-permute-start(bf16[3,20,32,128]{3,2,1,0:T(8,128)(2,1)S(1)} %pad_maximum_fusion.refs_2_), channel_id=1, source_target_pairs={{0,2},{1,3},{2,0},{3,1},{4,6},{5,7},{6,4},{7,5},{8,10},{9,11},{10,... | collective-permute-start | bytes 1474568 | tf_op jit(solution)/shard_map/ppermute | solution.py:90
  60.7 9.9 %shard_map.107 = (f32[8,256]{1,0:T(8,128)S(1)}, bf16[8,8,128]{2,1,0:T(8,128)(2,1)S(1)}, bf16[8,8,128]{2,1,0:T(8,128)(2,1)S(1)}) custom-call(s32[66]{0:T(128)S(1)} %copy-done.6, bf16[20,32,128]{2,1,0:T(8,128)(2,1)S(1)} %copy-done.2, bf16[20,32,128]{2,1,0:T(8,128)(2,1)S(1)} %collective-permute-done.10.refs_1_, ...), custom_call_target="tpu_custom_call" | custom-call | flops 8000000000 | bytes 4000000 | tf_op jit(solution)/shard_map/pallas_call | solution.py:261
  71.2 1.3 %collective-permute-done.22.refs_3_ = bf16[3,20,32,128]{3,2,1,0:T(8,128)(2,1)S(1)} collective-permute-done((bf16[3,20,32,128]{3,2,1,0:T(8,128)(2,1)S(1)}, bf16[3,20,32,128]{3,2,1,0:T(8,128)(2,1)S(1)}, u32[]{:S(2)}, u32[]{:S(2)}) %collective-permute-start.22) | collective-permute-done | bytes 491552 | tf_op jit(solution)/shard_map/ppermute | solution.py:90
  73.0 1.6 %collective-permute-done.23.refs_4_ = bf16[20,32,128]{2,1,0:T(8,128)(2,1)S(1)} collective-permute-done((bf16[20,32,128]{2,1,0:T(8,128)(2,1)S(1)}, bf16[20,32,128]{2,1,0:T(8,128)(2,1)S(1)}, u32[]{:S(2)}, u32[]{:S(2)}) %collective-permute-start.23) | collective-permute-done | bytes 163872 | tf_op jit(solution)/shard_map/ppermute | solution.py:90
  74.8 17.9 %shard_map.108 = (f32[4,256]{1,0:T(4,128)S(1)}, f32[4,256]{1,0:T(4,128)S(1)}, bf16[16,8,128]{2,1,0:T(8,128)(2,1)S(1)}, bf16[16,8,128]{2,1,0:T(8,128)(2,1)S(1)}) custom-call(s32[66]{0:T(128)S(1)} %copy-done.6, bf16[20,32,128]{2,1,0:T(8,128)(2,1)S(1)} %copy-done.7, bf16[20,32,128]{2,1,0:T(8,128)(2,1)S(1)} %collective-permute-done.9.refs_1_, ...), custom_call_target="tpu_custom_call" | custom-call | flops 16000000000 | bytes 8000000 | tf_op jit(solution)/shard_map/pallas_call | solution.py:261
  93.9 1.5 %collective-permute-start.27 = (f32[4,256]{1,0:T(4,128)S(1)}, f32[4,256]{1,0:T(4,128)S(1)}, u32[]{:S(2)}, u32[]{:S(2)}) collective-permute-start(f32[4,256]{1,0:T(4,128)S(1)} %get-tuple-element.47), channel_id=1, source_target_pairs={{0,16},{16,0},{1,17},{17,1},{2,18},{18,2},{3,19},{19,3},{4,20},{20... | collective-permute-start | bytes 12296 | tf_op jit(solution)/shard_map/ppermute | solution.py:390
  95.3 2.3 %collective-permute-done.27 = f32[4,256]{1,0:T(4,128)S(1)} collective-permute-done((f32[4,256]{1,0:T(4,128)S(1)}, f32[4,256]{1,0:T(4,128)S(1)}, u32[]{:S(2)}, u32[]{:S(2)}) %collective-permute-start.27) | collective-permute-done | bytes 4128 | tf_op jit(solution)/shard_map/ppermute | solution.py:390
  97.7 1.2 %collective-permute-done.29 = f32[4,256]{1,0:T(4,128)S(1)} collective-permute-done((f32[4,256]{1,0:T(4,128)S(1)}, f32[4,256]{1,0:T(4,128)S(1)}, u32[]{:S(2)}, u32[]{:S(2)}) %collective-permute-start.29) | collective-permute-done | bytes 4128 | tf_op jit(solution)/shard_map/ppermute | solution.py:90
  98.9 1.5 %collective-permute-start.30 = (f32[4,256]{1,0:T(4,128)S(1)}, f32[4,256]{1,0:T(4,128)S(1)}, u32[]{:S(2)}, u32[]{:S(2)}) collective-permute-start(f32[4,256]{1,0:T(4,128)S(1)} %add.27), channel_id=1, source_target_pairs={{0,2},{1,3},{2,0},{3,1},{4,6},{5,7},{6,4},{7,5},{8,10},{9,11},{10,... | collective-permute-start | bytes 12296 | tf_op jit(solution)/shard_map/ppermute | solution.py:90
  100.4 2.1 %collective-permute-done.30 = f32[4,256]{1,0:T(4,128)S(1)} collective-permute-done((f32[4,256]{1,0:T(4,128)S(1)}, f32[4,256]{1,0:T(4,128)S(1)}, u32[]{:S(2)}, u32[]{:S(2)}) %collective-permute-start.30) | collective-permute-done | bytes 4128 | tf_op jit(solution)/shard_map/ppermute | solution.py:90
  103.2 2.0 %shard_map.109 = bf16[2,8,4096]{2,1,0:T(8,128)(2,1)} custom-call(s32[66]{0:T(128)} %pad_add_fusion.info.info_ref, bf16[8,8,128]{2,1,0:T(8,128)(2,1)} %copy-done.4, bf16[8,8,128]{2,1,0:T(8,128)(2,1)} %copy-done.5, bf16[16,8,128]{2,1,0:T(8,128)(2,1)} %copy-done.3, bf16[32,8,128]{2,1,0:T(8,128)(2,1)} %copy-done.10), custom_call_target="tpu_custom_call" | custom-call | tf_op jit(solution)/shard_map/pallas_call | solution.py:393
  106.1 1.7 %collective-permute-start.32 = (f32[4,256]{1,0:T(4,128)S(1)}, f32[4,256]{1,0:T(4,128)S(1)}, u32[]{:S(2)}, u32[]{:S(2)}) collective-permute-start(f32[4,256]{1,0:T(4,128)S(1)} %add.29), channel_id=1, source_target_pairs={{0,8},{1,9},{2,10},{3,11},{4,12},{5,13},{6,14},{7,15},{8,0},{9,1},... | collective-permute-start | bytes 12296 | tf_op jit(solution)/shard_map/ppermute | solution.py:90
  107.8 2.8 %collective-permute-done.32 = f32[4,256]{1,0:T(4,128)S(1)} collective-permute-done((f32[4,256]{1,0:T(4,128)S(1)}, f32[4,256]{1,0:T(4,128)S(1)}, u32[]{:S(2)}, u32[]{:S(2)}) %collective-permute-start.32) | collective-permute-done | bytes 4128 | tf_op jit(solution)/shard_map/ppermute | solution.py:90
  (86 shorter events, 14.8 us)
Async XLA Ops:
  0.6 6.7 %collective-permute-start.1 = (bf16[2,8,4096]{2,1,0:T(8,128)(2,1)}, bf16[2,8,4096]{2,1,0:T(8,128)(2,1)S(1)}, u32[]{:S(2)}, u32[]{:S(2)}) collective-permute-start(bf16[2,8,4096]{2,1,0:T(8,128)(2,1)} %own.2), channel_id=1, source_target_pairs={{0,16},{16,0},{1,17},{17,1},{2,18},{18,2},{3,19},{19,3},{4,20},{20... | collective-permute-start | bytes 393224 | tf_op jit(solution)/shard_map/ppermute | solution.py:319
  4.7 5.0 %collective-permute-start = (s32[128]{0:T(128)}, s32[128]{0:T(128)S(1)}, u32[]{:S(2)}, u32[]{:S(2)}) collective-permute-start(s32[128]{0:T(128)} %param.11), channel_id=1, source_target_pairs={{0,16},{16,0},{1,17},{17,1},{2,18},{18,2},{3,19},{19,3},{4,20},{20... | collective-permute-start | bytes 1544 | tf_op jit(solution)/shard_map/ppermute | solution.py:325
  7.4 16.6 %collective-permute-start.4 = (bf16[2,128,768]{2,1,0:T(8,128)(2,1)}, bf16[2,128,768]{2,1,0:T(8,128)(2,1)S(1)}, u32[]{:S(2)}, u32[]{:S(2)}) collective-permute-start(bf16[2,128,768]{2,1,0:T(8,128)(2,1)} %own.3), channel_id=1, source_target_pairs={{0,16},{16,0},{1,17},{17,1},{2,18},{18,2},{3,19},{19,3},{4,20},{20... | collective-permute-start | bytes 1179656 | tf_op jit(solution)/shard_map/ppermute | solution.py:336
  11.8 6.4 %collective-permute-start.2 = (bf16[20,32,128]{2,1,0:T(8,128)(2,1)}, bf16[20,32,128]{2,1,0:T(8,128)(2,1)S(1)}, u32[]{:S(2)}, u32[]{:S(2)}) collective-permute-start(bf16[20,32,128]{2,1,0:T(8,128)(2,1)} %get-tuple-element.35.refs_0_), channel_id=1, source_target_pairs={{0,4},{1,5},{2,6},{3,7},{4,0},{5,1},{6,2},{7,3},{8,12},{9,13},{10,... | collective-permute-start | bytes 491528 | tf_op jit(solution)/shard_map/ppermute | solution.py:90
  13.4 9.1 %collective-permute-start.3 = (bf16[20,32,128]{2,1,0:T(8,128)(2,1)}, bf16[20,32,128]{2,1,0:T(8,128)(2,1)S(1)}, u32[]{:S(2)}, u32[]{:S(2)}) collective-permute-start(bf16[20,32,128]{2,1,0:T(8,128)(2,1)} %get-tuple-element.35.refs_0_), channel_id=1, source_target_pairs={{0,12},{1,13},{2,14},{3,15},{4,8},{5,9},{6,10},{7,11},{8,4},{9,5},... | collective-permute-start | bytes 491528 | tf_op jit(solution)/shard_map/ppermute | solution.py:90
  15.9 13.9 %collective-permute-start.11 = (bf16[20,32,128]{2,1,0:T(8,128)(2,1)}, bf16[20,32,128]{2,1,0:T(8,128)(2,1)S(1)}, u32[]{:S(2)}, u32[]{:S(2)}) collective-permute-start(bf16[20,32,128]{2,1,0:T(8,128)(2,1)} %get-tuple-element.35.refs_0_), channel_id=1, source_target_pairs={{0,2},{1,3},{2,0},{3,1},{4,6},{5,7},{6,4},{7,5},{8,10},{9,11},{10,... | collective-permute-start | bytes 491528 | tf_op jit(solution)/shard_map/ppermute | solution.py:90
  18.2 12.0 %collective-permute-start.14 = (bf16[20,32,128]{2,1,0:T(8,128)(2,1)S(1)}, bf16[20,32,128]{2,1,0:T(8,128)(2,1)S(1)}, u32[]{:S(2)}, u32[]{:S(2)}) collective-permute-start(bf16[20,32,128]{2,1,0:T(8,128)(2,1)S(1)} %collective-permute-done.2.refs_4_), channel_id=1, source_target_pairs={{0,2},{1,3},{2,0},{3,1},{4,6},{5,7},{6,4},{7,5},{8,10},{9,11},{10,... | collective-permute-start | bytes 491528 | tf_op jit(solution)/shard_map/ppermute | solution.py:90
  22.4 7.9 %collective-permute-start.17 = (bf16[20,32,128]{2,1,0:T(8,128)(2,1)S(1)}, bf16[20,32,128]{2,1,0:T(8,128)(2,1)S(1)}, u32[]{:S(2)}, u32[]{:S(2)}) collective-permute-start(bf16[20,32,128]{2,1,0:T(8,128)(2,1)S(1)} %collective-permute-done.3.refs_12_), channel_id=1, source_target_pairs={{0,2},{1,3},{2,0},{3,1},{4,6},{5,7},{6,4},{7,5},{8,10},{9,11},{10,... | collective-permute-start | bytes 491528 | tf_op jit(solution)/shard_map/ppermute | solution.py:90
  28.0 8.2 %collective-permute-start.5 = (bf16[20,32,128]{2,1,0:T(8,128)(2,1)}, bf16[20,32,128]{2,1,0:T(8,128)(2,1)S(1)}, u32[]{:S(2)}, u32[]{:S(2)}) collective-permute-start(bf16[20,32,128]{2,1,0:T(8,128)(2,1)} %get-tuple-element.35.refs_0_), channel_id=1, source_target_pairs={{0,8},{1,9},{2,10},{3,11},{4,12},{5,13},{6,14},{7,15},{8,0},{9,1},... | collective-permute-start | bytes 491528 | tf_op jit(solution)/shard_map/ppermute | solution.py:90
  29.7 6.4 %collective-permute-start.10 = (bf16[20,32,128]{2,1,0:T(8,128)(2,1)}, bf16[20,32,128]{2,1,0:T(8,128)(2,1)S(1)}, u32[]{:S(2)}, u32[]{:S(2)}) collective-permute-start(bf16[20,32,128]{2,1,0:T(8,128)(2,1)} %get-tuple-element.35.refs_0_), channel_id=1, source_target_pairs={{0,1},{1,0},{2,3},{3,2},{4,5},{5,4},{6,7},{7,6},{8,9},{9,8},{10,11... | collective-permute-start | bytes 491528 | tf_op jit(solution)/shard_map/ppermute | solution.py:90
  29.7 6.9 %collective-permute-start.13 = (bf16[20,32,128]{2,1,0:T(8,128)(2,1)S(1)}, bf16[20,32,128]{2,1,0:T(8,128)(2,1)S(1)}, u32[]{:S(2)}, u32[]{:S(2)}) collective-permute-start(bf16[20,32,128]{2,1,0:T(8,128)(2,1)S(1)} %collective-permute-done.2.refs_4_), channel_id=1, source_target_pairs={{0,1},{1,0},{2,3},{3,2},{4,5},{5,4},{6,7},{7,6},{8,9},{9,8},{10,11... | collective-permute-start | bytes 491528 | tf_op jit(solution)/shard_map/ppermute | solution.py:90
  30.2 6.9 %collective-permute-start.20 = (bf16[20,32,128]{2,1,0:T(8,128)(2,1)S(1)}, bf16[20,32,128]{2,1,0:T(8,128)(2,1)S(1)}, u32[]{:S(2)}, u32[]{:S(2)}) collective-permute-start(bf16[20,32,128]{2,1,0:T(8,128)(2,1)S(1)} %collective-permute-done.3.refs_12_), channel_id=1, source_target_pairs={{0,1},{1,0},{2,3},{3,2},{4,5},{5,4},{6,7},{7,6},{8,9},{9,8},{10,11... | collective-permute-start | bytes 491528 | tf_op jit(solution)/shard_map/ppermute | solution.py:90
  30.3 7.7 %collective-permute-start.12 = (bf16[20,32,128]{2,1,0:T(8,128)(2,1)S(1)}, bf16[20,32,128]{2,1,0:T(8,128)(2,1)S(1)}, u32[]{:S(2)}, u32[]{:S(2)}) collective-permute-start(bf16[20,32,128]{2,1,0:T(8,128)(2,1)S(1)} %collective-permute-done.11.refs_2_), channel_id=1, source_target_pairs={{0,1},{1,0},{2,3},{3,2},{4,5},{5,4},{6,7},{7,6},{8,9},{9,8},{10,11... | collective-permute-start | bytes 491528 | tf_op jit(solution)/shard_map/ppermute | solution.py:90
  36.2 2.0 %collective-permute-start.15 = (bf16[20,32,128]{2,1,0:T(8,128)(2,1)S(1)}, bf16[20,32,128]{2,1,0:T(8,128)(2,1)S(1)}, u32[]{:S(2)}, u32[]{:S(2)}) collective-permute-start(bf16[20,32,128]{2,1,0:T(8,128)(2,1)S(1)} %collective-permute-done.14.refs_6_), channel_id=1, source_target_pairs={{0,1},{1,0},{2,3},{3,2},{4,5},{5,4},{6,7},{7,6},{8,9},{9,8},{10,11... | collective-permute-start | bytes 491528 | tf_op jit(solution)/shard_map/ppermute | solution.py:90
  36.2 4.7 %collective-permute-start.21 = (bf16[20,32,128]{2,1,0:T(8,128)(2,1)S(1)}, bf16[20,32,128]{2,1,0:T(8,128)(2,1)S(1)}, u32[]{:S(2)}, u32[]{:S(2)}) collective-permute-start(bf16[20,32,128]{2,1,0:T(8,128)(2,1)S(1)} %collective-permute-done.17.refs_14_), channel_id=1, source_target_pairs={{0,1},{1,0},{2,3},{3,2},{4,5},{5,4},{6,7},{7,6},{8,9},{9,8},{10,11... | collective-permute-start | bytes 491528 | tf_op jit(solution)/shard_map/ppermute | solution.py:90
  36.7 6.2 %collective-permute-start.18 = (bf16[20,32,128]{2,1,0:T(8,128)(2,1)S(1)}, bf16[20,32,128]{2,1,0:T(8,128)(2,1)S(1)}, u32[]{:S(2)}, u32[]{:S(2)}) collective-permute-start(bf16[20,32,128]{2,1,0:T(8,128)(2,1)S(1)} %collective-permute-done.5.refs_8_), channel_id=1, source_target_pairs={{0,2},{1,3},{2,0},{3,1},{4,6},{5,7},{6,4},{7,5},{8,10},{9,11},{10,... | collective-permute-start | bytes 491528 | tf_op jit(solution)/shard_map/ppermute | solution.py:90
  37.2 6.2 %collective-permute-start.16 = (bf16[20,32,128]{2,1,0:T(8,128)(2,1)S(1)}, bf16[20,32,128]{2,1,0:T(8,128)(2,1)S(1)}, u32[]{:S(2)}, u32[]{:S(2)}) collective-permute-start(bf16[20,32,128]{2,1,0:T(8,128)(2,1)S(1)} %collective-permute-done.5.refs_8_), channel_id=1, source_target_pairs={{0,1},{1,0},{2,3},{3,2},{4,5},{5,4},{6,7},{7,6},{8,9},{9,8},{10,11... | collective-permute-start | bytes 491528 | tf_op jit(solution)/shard_map/ppermute | solution.py:90
  38.0 20.6 %collective-permute-start.6 = (bf16[20,32,128]{2,1,0:T(8,128)(2,1)}, bf16[20,32,128]{2,1,0:T(8,128)(2,1)S(1)}, u32[]{:S(2)}, u32[]{:S(2)}) collective-permute-start(bf16[20,32,128]{2,1,0:T(8,128)(2,1)} %get-tuple-element.36.refs_0_), channel_id=1, source_target_pairs={{0,4},{1,5},{2,6},{3,7},{4,0},{5,1},{6,2},{7,3},{8,12},{9,13},{10,... | collective-permute-start | bytes 491528 | tf_op jit(solution)/shard_map/ppermute | solution.py:90
  38.1 20.5 %collective-permute-start.7 = (bf16[20,32,128]{2,1,0:T(8,128)(2,1)}, bf16[20,32,128]{2,1,0:T(8,128)(2,1)S(1)}, u32[]{:S(2)}, u32[]{:S(2)}) collective-permute-start(bf16[20,32,128]{2,1,0:T(8,128)(2,1)} %get-tuple-element.36.refs_0_), channel_id=1, source_target_pairs={{0,12},{1,13},{2,14},{3,15},{4,8},{5,9},{6,10},{7,11},{8,4},{9,5},... | collective-permute-start | bytes 491528 | tf_op jit(solution)/shard_map/ppermute | solution.py:90
  40.8 17.8 %collective-permute-start.8 = (bf16[20,32,128]{2,1,0:T(8,128)(2,1)}, bf16[20,32,128]{2,1,0:T(8,128)(2,1)S(1)}, u32[]{:S(2)}, u32[]{:S(2)}) collective-permute-start(bf16[20,32,128]{2,1,0:T(8,128)(2,1)} %get-tuple-element.36.refs_0_), channel_id=1, source_target_pairs={{0,8},{1,9},{2,10},{3,11},{4,12},{5,13},{6,14},{7,15},{8,0},{9,1},... | collective-permute-start | bytes 491528 | tf_op jit(solution)/shard_map/ppermute | solution.py:90
  42.8 15.8 %collective-permute-start.9 = (bf16[20,32,128]{2,1,0:T(8,128)(2,1)}, bf16[20,32,128]{2,1,0:T(8,128)(2,1)S(1)}, u32[]{:S(2)}, u32[]{:S(2)}) collective-permute-start(bf16[20,32,128]{2,1,0:T(8,128)(2,1)} %get-tuple-element.36.refs_0_), channel_id=1, source_target_pairs={{0,2},{1,3},{2,0},{3,1},{4,6},{5,7},{6,4},{7,5},{8,10},{9,11},{10,... | collective-permute-start | bytes 491528 | tf_op jit(solution)/shard_map/ppermute | solution.py:90
  43.4 1.4 %collective-permute-start.19 = (bf16[20,32,128]{2,1,0:T(8,128)(2,1)S(1)}, bf16[20,32,128]{2,1,0:T(8,128)(2,1)S(1)}, u32[]{:S(2)}, u32[]{:S(2)}) collective-permute-start(bf16[20,32,128]{2,1,0:T(8,128)(2,1)S(1)} %collective-permute-done.18.refs_10_), channel_id=1, source_target_pairs={{0,1},{1,0},{2,3},{3,2},{4,5},{5,4},{6,7},{7,6},{8,9},{9,8},{10,11... | collective-permute-start | bytes 491528 | tf_op jit(solution)/shard_map/ppermute | solution.py:90
  59.2 13.3 %collective-permute-start.22 = (bf16[3,20,32,128]{3,2,1,0:T(8,128)(2,1)S(1)}, bf16[3,20,32,128]{3,2,1,0:T(8,128)(2,1)S(1)}, u32[]{:S(2)}, u32[]{:S(2)}) collective-permute-start(bf16[3,20,32,128]{3,2,1,0:T(8,128)(2,1)S(1)} %pad_maximum_fusion.refs_2_), channel_id=1, source_target_pairs={{0,2},{1,3},{2,0},{3,1},{4,6},{5,7},{6,4},{7,5},{8,10},{9,11},{10,... | collective-permute-start | bytes 1474568 | tf_op jit(solution)/shard_map/ppermute | solution.py:90
  60.7 14.1 %collective-permute-start.25 = (bf16[3,20,32,128]{3,2,1,0:T(8,128)(2,1)S(1)}, bf16[3,20,32,128]{3,2,1,0:T(8,128)(2,1)S(1)}, u32[]{:S(2)}, u32[]{:S(2)}) collective-permute-start(bf16[3,20,32,128]{3,2,1,0:T(8,128)(2,1)S(1)} %pad_maximum_fusion.refs_2_), channel_id=1, source_target_pairs={{0,1},{1,0},{2,3},{3,2},{4,5},{5,4},{6,7},{7,6},{8,9},{9,8},{10,11... | collective-permute-start | bytes 1474568 | tf_op jit(solution)/shard_map/ppermute | solution.py:90
  72.5 2.3 %collective-permute-start.26 = (bf16[3,20,32,128]{3,2,1,0:T(8,128)(2,1)S(1)}, bf16[3,20,32,128]{3,2,1,0:T(8,128)(2,1)S(1)}, u32[]{:S(2)}, u32[]{:S(2)}) collective-permute-start(bf16[3,20,32,128]{3,2,1,0:T(8,128)(2,1)S(1)} %collective-permute-done.22.refs_3_), channel_id=1, source_target_pairs={{0,1},{1,0},{2,3},{3,2},{4,5},{5,4},{6,7},{7,6},{8,9},{9,8},{10,11... | collective-permute-start | bytes 1474568 | tf_op jit(solution)/shard_map/ppermute | solution.py:90
  72.5 2.1 %collective-permute-start.23 = (bf16[20,32,128]{2,1,0:T(8,128)(2,1)S(1)}, bf16[20,32,128]{2,1,0:T(8,128)(2,1)S(1)}, u32[]{:S(2)}, u32[]{:S(2)}) collective-permute-start(bf16[20,32,128]{2,1,0:T(8,128)(2,1)S(1)} %copy-done.7), channel_id=1, source_target_pairs={{0,1},{1,0},{2,3},{3,2},{4,5},{5,4},{6,7},{7,6},{8,9},{9,8},{10,11... | collective-permute-start | bytes 491528 | tf_op jit(solution)/shard_map/ppermute | solution.py:90
  73.0 1.8 %collective-permute-start.24 = (bf16[20,32,128]{2,1,0:T(8,128)(2,1)S(1)}, bf16[20,32,128]{2,1,0:T(8,128)(2,1)S(1)}, u32[]{:S(2)}, u32[]{:S(2)}) collective-permute-start(bf16[20,32,128]{2,1,0:T(8,128)(2,1)S(1)} %collective-permute-done.9.refs_1_), channel_id=1, source_target_pairs={{0,1},{1,0},{2,3},{3,2},{4,5},{5,4},{6,7},{7,6},{8,9},{9,8},{10,11... | collective-permute-start | bytes 491528 | tf_op jit(solution)/shard_map/ppermute | solution.py:90
  93.3 4.3 %collective-permute-start.28 = (bf16[32,8,128]{2,1,0:T(8,128)(2,1)S(1)}, bf16[32,8,128]{2,1,0:T(8,128)(2,1)S(1)}, u32[]{:S(2)}, u32[]{:S(2)}) collective-permute-start(bf16[32,8,128]{2,1,0:T(8,128)(2,1)S(1)} %pad_maximum_fusion.1), channel_id=1, source_target_pairs={{0,16},{16,0},{1,17},{17,1},{2,18},{18,2},{3,19},{19,3},{4,20},{20... | collective-permute-start | bytes 196616 | tf_op jit(solution)/shard_map/ppermute | solution.py:391
  93.9 3.8 %collective-permute-start.27 = (f32[4,256]{1,0:T(4,128)S(1)}, f32[4,256]{1,0:T(4,128)S(1)}, u32[]{:S(2)}, u32[]{:S(2)}) collective-permute-start(f32[4,256]{1,0:T(4,128)S(1)} %get-tuple-element.47), channel_id=1, source_target_pairs={{0,16},{16,0},{1,17},{17,1},{2,18},{18,2},{3,19},{19,3},{4,20},{20... | collective-permute-start | bytes 12296 | tf_op jit(solution)/shard_map/ppermute | solution.py:390
  98.9 3.6 %collective-permute-start.30 = (f32[4,256]{1,0:T(4,128)S(1)}, f32[4,256]{1,0:T(4,128)S(1)}, u32[]{:S(2)}, u32[]{:S(2)}) collective-permute-start(f32[4,256]{1,0:T(4,128)S(1)} %add.27), channel_id=1, source_target_pairs={{0,2},{1,3},{2,0},{3,1},{4,6},{5,7},{6,4},{7,5},{8,10},{9,11},{10,... | collective-permute-start | bytes 12296 | tf_op jit(solution)/shard_map/ppermute | solution.py:90
  102.5 3.6 %collective-permute-start.31 = (f32[4,256]{1,0:T(4,128)S(1)}, f32[4,256]{1,0:T(4,128)S(1)}, u32[]{:S(2)}, u32[]{:S(2)}) collective-permute-start(f32[4,256]{1,0:T(4,128)S(1)} %add.28), channel_id=1, source_target_pairs={{0,4},{1,5},{2,6},{3,7},{4,0},{5,1},{6,2},{7,3},{8,12},{9,13},{10,... | collective-permute-start | bytes 12296 | tf_op jit(solution)/shard_map/ppermute | solution.py:90
  106.1 4.5 %collective-permute-start.32 = (f32[4,256]{1,0:T(4,128)S(1)}, f32[4,256]{1,0:T(4,128)S(1)}, u32[]{:S(2)}, u32[]{:S(2)}) collective-permute-start(f32[4,256]{1,0:T(4,128)S(1)} %add.29), channel_id=1, source_target_pairs={{0,8},{1,9},{2,10},{3,11},{4,12},{5,13},{6,14},{7,15},{8,0},{9,1},... | collective-permute-start | bytes 12296 | tf_op jit(solution)/shard_map/ppermute | solution.py:90
  (12 other events, 39.4 us)

commit v8 on v7

--- a/solution.py
+++ b/solution.py
@@ -331,6 +331,7 @@
         in_specs=[SMEM, VMEM, VMEM, VMEM, VMEM],
         out_specs=[VMEM] * WAVES,
         out_shape=[jax.ShapeDtypeStruct((UNIT, 32, TILE_A), BF)] * WAVES,
+        compiler_params=pltpu.CompilerParams(vmem_limit_bytes=8 * 1024 * 1024),
     )(after(info, ids_other), train_inputs, train_other, query_inputs, input_basis)
 
     out_other = lax.ppermute(after(train_outgrads, train_other), "parts", SWAP)
@@ -348,6 +349,7 @@
             jax.ShapeDtypeStruct((LAYERS, TOKENS, slab), BF),
             jax.ShapeDtypeStruct((LAYERS, slab, TOKENS), BF),
         ],
+        compiler_params=pltpu.CompilerParams(vmem_limit_bytes=16 * 1024 * 1024),
     )(info, train_outgrads, out_other, query_outgrads, output_basis)
 
     units = [None] * NQ
@@ -395,6 +397,7 @@
         in_specs=[SMEM] + [VMEM] * 4,
         out_specs=VMEM,
         out_shape=jax.ShapeDtypeStruct(train_inputs.shape, BF),
+        compiler_params=pltpu.CompilerParams(vmem_limit_bytes=8 * 1024 * 1024),
     )(info, kept_a, kept_b, kept1, came)
     for bits in (1, 2, 4):
         total = total + hop(total, bits)

time: 112 us -> 112 us (level)
  Pallas kernels: 45.2 us -> 42.6 us
  local copies, waits for them, and re-layouts: 7.65 us -> 9.94 us
  waiting for transfers between devices: 26.1 us -> 24.7 us
  other arithmetic: 2.21 us -> 3.53 us
    pallas_call x1, Pallas kernels: 3.26 us -> 1.2 us  [paired_body(): pl.pallas_call(prepare_kernel, in_specs=[SMEM] + [VMEM] * 4, out_specs=[V...]
    ppermute x28, waiting for transfers between devices: 21.4 us -> 19.9 us  [hop(): return lax.ppermute(value, 'query', [(i, i ^ bits) for i in range(NQ)])]
    pallas_call x1, Pallas kernels: 2.11 us -> 0.81 us  [paired_body(): pl.pallas_call(pack_kernel, in_specs=[SMEM, VMEM, VMEM, VMEM, VMEM], out_...]
    another operation x2, local copies, waits for them, and re-layouts: 0.81 us -> 2.09 us  [paired_body(): jnp.stack([sequence_ids, ids_other])]
    pallas_call x3, Pallas kernels: 37.8 us -> 39 us  [score_tiles(): pl.pallas_call(kernel, in_specs=[SMEM] + [VMEM] * len(arrays) + [VMEM, VM...]
    unnamed x22 -> x16, local copies, waits for them, and re-layouts: 6.2 us -> 5.89 us
  transfers between devices with their start and end apart: 33 -> 33, of which waited for: 14 -> 14; matrix products, arithmetic and copies ran while one was open for 3% -> 5% of each run, Pallas kernels for 24% -> 22%
where the time goes in v8:
time: 112 us
  Pallas kernels  42.6 us (38%)
  starting transfers between devices  30.2 us (27%)
  waiting for transfers between devices  24.7 us (22%)
  local copies, waits for them, and re-layouts  9.94 us (9%)
  other arithmetic  3.53 us (3%)
    pallas_call x3, Pallas kernels, score_tiles(): pl.pallas_call(kernel, in_specs=[SMEM] + [VMEM] * len(arrays) + [VMEM, VM...  39 us
    ppermute x28, starting transfers between devices, hop(): return lax.ppermute(value, 'query', [(i, i ^ bits) for i in range(NQ)])  23.3 us
    ppermute x28, waiting for transfers between devices, hop(): return lax.ppermute(value, 'query', [(i, i ^ bits) for i in range(NQ)])  19.9 us
    unnamed x16, local copies, waits for them, and re-layouts  5.89 us
    ppermute x1, starting transfers between devices, paired_body(): train_other = lax.ppermute(train_inputs, 'parts', SWAP)  3 us
    ppermute x1, waiting for transfers between devices, paired_body(): train_other = lax.ppermute(train_inputs, 'parts', SWAP)  2.44 us
    ppermute x1, waiting for transfers between devices, paired_body(): total = keep + lax.ppermute(give, 'parts', SWAP)  2.28 us
  transfers between devices with their start and end apart: 33, of which 14 were waited for; matrix products, arithmetic and copies ran while one was open for 5% of the time, Pallas kernels for 22%

profile of v8, /device:TPU:0, one launch (start us, length us, event | category | flops | bytes accessed | tf_op | source)
XLA Modules:
  0.0 111.7 jit_solution(9320713456656216079)
XLA Ops:
  0.6 3.0 %collective-permute-start.1 = (bf16[2,8,4096]{2,1,0:T(8,128)(2,1)}, bf16[2,8,4096]{2,1,0:T(8,128)(2,1)S(1)}, u32[]{:S(2)}, u32[]{:S(2)}) collective-permute-start(bf16[2,8,4096]{2,1,0:T(8,128)(2,1)} %own.2), channel_id=1, source_target_pairs={{0,16},{16,0},{1,17},{17,1},{2,18},{18,2},{3,19},{19,3},{4,20},{20... | collective-permute-start | bytes 393224 | tf_op jit(solution)/shard_map/ppermute | solution.py:319
  4.9 2.4 %collective-permute-done.1.other = bf16[2,8,4096]{2,1,0:T(8,128)(2,1)S(1)} collective-permute-done((bf16[2,8,4096]{2,1,0:T(8,128)(2,1)}, bf16[2,8,4096]{2,1,0:T(8,128)(2,1)S(1)}, u32[]{:S(2)}, u32[]{:S(2)}) %collective-permute-start.1) | collective-permute-done | bytes 131104 | tf_op jit(solution)/shard_map/ppermute | solution.py:319
  7.3 1.7 %collective-permute-start.4 = (bf16[2,128,768]{2,1,0:T(8,128)(2,1)}, bf16[2,128,768]{2,1,0:T(8,128)(2,1)S(1)}, u32[]{:S(2)}, u32[]{:S(2)}) collective-permute-start(bf16[2,128,768]{2,1,0:T(8,128)(2,1)} %own.3), channel_id=1, source_target_pairs={{0,16},{16,0},{1,17},{17,1},{2,18},{18,2},{3,19},{19,3},{4,20},{20... | collective-permute-start | bytes 1179656 | tf_op jit(solution)/shard_map/ppermute | solution.py:337
  12.8 1.6 %collective-permute-start.2 = (bf16[20,32,128]{2,1,0:T(8,128)(2,1)S(1)}, bf16[20,32,128]{2,1,0:T(8,128)(2,1)S(1)}, u32[]{:S(2)}, u32[]{:S(2)}) collective-permute-start(bf16[20,32,128]{2,1,0:T(8,128)(2,1)S(1)} %get-tuple-element.35.refs_0_), channel_id=1, source_target_pairs={{0,4},{1,5},{2,6},{3,7},{4,0},{5,1},{6,2},{7,3},{8,12},{9,13},{10,... | collective-permute-start | bytes 491528 | tf_op jit(solution)/shard_map/ppermute | solution.py:90
  14.4 2.5 %collective-permute-start.3 = (bf16[20,32,128]{2,1,0:T(8,128)(2,1)S(1)}, bf16[20,32,128]{2,1,0:T(8,128)(2,1)S(1)}, u32[]{:S(2)}, u32[]{:S(2)}) collective-permute-start(bf16[20,32,128]{2,1,0:T(8,128)(2,1)S(1)} %get-tuple-element.35.refs_0_), channel_id=1, source_target_pairs={{0,12},{1,13},{2,14},{3,15},{4,8},{5,9},{6,10},{7,11},{8,4},{9,5},... | collective-permute-start | bytes 491528 | tf_op jit(solution)/shard_map/ppermute | solution.py:90
  16.9 1.5 %collective-permute-start.11 = (bf16[20,32,128]{2,1,0:T(8,128)(2,1)S(1)}, bf16[20,32,128]{2,1,0:T(8,128)(2,1)S(1)}, u32[]{:S(2)}, u32[]{:S(2)}) collective-permute-start(bf16[20,32,128]{2,1,0:T(8,128)(2,1)S(1)} %get-tuple-element.35.refs_0_), channel_id=1, source_target_pairs={{0,2},{1,3},{2,0},{3,1},{4,6},{5,7},{6,4},{7,5},{8,10},{9,11},{10,... | collective-permute-start | bytes 491528 | tf_op jit(solution)/shard_map/ppermute | solution.py:90
  19.0 1.5 %collective-permute-start.14 = (bf16[20,32,128]{2,1,0:T(8,128)(2,1)S(1)}, bf16[20,32,128]{2,1,0:T(8,128)(2,1)S(1)}, u32[]{:S(2)}, u32[]{:S(2)}) collective-permute-start(bf16[20,32,128]{2,1,0:T(8,128)(2,1)S(1)} %collective-permute-done.2.refs_4_), channel_id=1, source_target_pairs={{0,2},{1,3},{2,0},{3,1},{4,6},{5,7},{6,4},{7,5},{8,10},{9,11},{10,... | collective-permute-start | bytes 491528 | tf_op jit(solution)/shard_map/ppermute | solution.py:90
  20.5 2.7 %collective-permute-done.3.refs_12_ = bf16[20,32,128]{2,1,0:T(8,128)(2,1)S(1)} collective-permute-done((bf16[20,32,128]{2,1,0:T(8,128)(2,1)S(1)}, bf16[20,32,128]{2,1,0:T(8,128)(2,1)S(1)}, u32[]{:S(2)}, u32[]{:S(2)}) %collective-permute-start.3) | collective-permute-done | bytes 163872 | tf_op jit(solution)/shard_map/ppermute | solution.py:90
  23.2 1.5 %collective-permute-start.17 = (bf16[20,32,128]{2,1,0:T(8,128)(2,1)S(1)}, bf16[20,32,128]{2,1,0:T(8,128)(2,1)S(1)}, u32[]{:S(2)}, u32[]{:S(2)}) collective-permute-start(bf16[20,32,128]{2,1,0:T(8,128)(2,1)S(1)} %collective-permute-done.3.refs_12_), channel_id=1, source_target_pairs={{0,2},{1,3},{2,0},{3,1},{4,6},{5,7},{6,4},{7,5},{8,10},{9,11},{10,... | collective-permute-start | bytes 491528 | tf_op jit(solution)/shard_map/ppermute | solution.py:90
  24.8 1.1 %copy-done = bf16[2,256,768]{2,1,0:T(8,128)(2,1)S(1)} copy-done((bf16[2,256,768]{2,1,0:T(8,128)(2,1)S(1)}, bf16[2,256,768]{2,1,0:T(8,128)(2,1)}, u32[]{:S(2)}) %copy-start) | copy-done | bytes 786456
  27.9 1.2 %shard_map.105 = (bf16[2,256,768]{2,1,0:T(8,128)(2,1)S(1)}, bf16[2,768,256]{2,1,0:T(8,128)(2,1)S(1)}) custom-call(s32[66]{0:T(128)S(1)} %pad_add_fusion.info.info_ref, bf16[2,128,768]{2,1,0:T(8,128)(2,1)S(1)} %copy-done.1, bf16[2,128,768]{2,1,0:T(8,128)(2,1)S(1)} %collective-permute-done.4.other, bf16[2,256,768]{2,1,0:T(8,128)(2,1)S(1)} %copy-done, ...), custom_call_target="tpu_custom_call" | custom-call | tf_op jit(solution)/shard_map/pallas_call | solution.py:344
  29.1 1.8 %collective-permute-start.5 = (bf16[20,32,128]{2,1,0:T(8,128)(2,1)S(1)}, bf16[20,32,128]{2,1,0:T(8,128)(2,1)S(1)}, u32[]{:S(2)}, u32[]{:S(2)}) collective-permute-start(bf16[20,32,128]{2,1,0:T(8,128)(2,1)S(1)} %get-tuple-element.35.refs_0_), channel_id=1, source_target_pairs={{0,8},{1,9},{2,10},{3,11},{4,12},{5,13},{6,14},{7,15},{8,0},{9,1},... | collective-permute-start | bytes 491528 | tf_op jit(solution)/shard_map/ppermute | solution.py:90
  32.0 5.2 %collective-permute-done.5.refs_8_ = bf16[20,32,128]{2,1,0:T(8,128)(2,1)S(1)} collective-permute-done((bf16[20,32,128]{2,1,0:T(8,128)(2,1)S(1)}, bf16[20,32,128]{2,1,0:T(8,128)(2,1)S(1)}, u32[]{:S(2)}, u32[]{:S(2)}) %collective-permute-start.5) | collective-permute-done | bytes 163872 | tf_op jit(solution)/shard_map/ppermute | solution.py:90
  38.9 1.4 %stack.27 = s32[1,16,8]{2,1,0:T(8,128)} reshape(s32[128]{0:T(128)} %collective-permute-done) | data formatting | bytes 1024 | tf_op jit(solution)/shard_map/stack | solution.py:339
  40.3 2.7 %collective-permute-start.7 = (bf16[20,32,128]{2,1,0:T(8,128)(2,1)}, bf16[20,32,128]{2,1,0:T(8,128)(2,1)}, u32[]{:S(2)}, u32[]{:S(2)}) collective-permute-start(bf16[20,32,128]{2,1,0:T(8,128)(2,1)} %copy-done.6), channel_id=1, source_target_pairs={{0,12},{1,13},{2,14},{3,15},{4,8},{5,9},{6,10},{7,11},{8,4},{9,5},... | collective-permute-start | bytes 491528 | tf_op jit(solution)/shard_map/ppermute | solution.py:90
  43.9 1.4 %collective-permute-start.9 = (bf16[20,32,128]{2,1,0:T(8,128)(2,1)}, bf16[20,32,128]{2,1,0:T(8,128)(2,1)}, u32[]{:S(2)}, u32[]{:S(2)}) collective-permute-start(bf16[20,32,128]{2,1,0:T(8,128)(2,1)} %copy-done.6), channel_id=1, source_target_pairs={{0,2},{1,3},{2,0},{3,1},{4,6},{5,7},{6,4},{7,5},{8,10},{9,11},{10,... | collective-permute-start | bytes 491528 | tf_op jit(solution)/shard_map/ppermute | solution.py:90
  47.6 10.6 %shard_map.106 = (f32[8,256]{1,0:T(8,128)S(1)}, bf16[8,8,128]{2,1,0:T(8,128)(2,1)S(1)}, bf16[8,8,128]{2,1,0:T(8,128)(2,1)S(1)}) custom-call(s32[66]{0:T(128)S(1)} %pad_add_fusion.info.info_ref, bf16[20,32,128]{2,1,0:T(8,128)(2,1)S(1)} %get-tuple-element.35.refs_0_, bf16[20,32,128]{2,1,0:T(8,128)(2,1)S(1)} %collective-permute-done.10.refs_1_, ...), custom_call_target="tpu_custom_call" | custom-call | flops 80000000 | bytes 4000000 | tf_op jit(solution)/shard_map/pallas_call | solution.py:261
  59.0 1.1 %pad_maximum_fusion.refs_2_ = bf16[3,20,32,128]{3,2,1,0:T(8,128)(2,1)S(1)} fusion(bf16[1,20,32,128]{3,2,1,0:T(8,128)(2,1)} %bitcast.6, bf16[1,20,32,128]{3,2,1,0:T(8,128)(2,1)} %bitcast.5, bf16[1,20,32,128]{3,2,1,0:T(8,128)(2,1)} %bitcast.4), kind=kLoop, calls=%fused_computation | loop fusion | flops 491520 | bytes 983040 | tf_op jit(solution)/shard_map/stack | solution.py:376
  60.1 1.5 %collective-permute-start.22 = (bf16[3,20,32,128]{3,2,1,0:T(8,128)(2,1)S(1)}, bf16[3,20,32,128]{3,2,1,0:T(8,128)(2,1)S(1)}, u32[]{:S(2)}, u32[]{:S(2)}) collective-permute-start(bf16[3,20,32,128]{3,2,1,0:T(8,128)(2,1)S(1)} %pad_maximum_fusion.refs_2_), channel_id=1, source_target_pairs={{0,2},{1,3},{2,0},{3,1},{4,6},{5,7},{6,4},{7,5},{8,10},{9,11},{10,... | collective-permute-start | bytes 1474568 | tf_op jit(solution)/shard_map/ppermute | solution.py:90
  61.6 10.4 %shard_map.107 = (f32[8,256]{1,0:T(8,128)S(1)}, bf16[8,8,128]{2,1,0:T(8,128)(2,1)S(1)}, bf16[8,8,128]{2,1,0:T(8,128)(2,1)S(1)}) custom-call(s32[66]{0:T(128)S(1)} %pad_add_fusion.info.info_ref, bf16[20,32,128]{2,1,0:T(8,128)(2,1)S(1)} %get-tuple-element.35.refs_0_, bf16[20,32,128]{2,1,0:T(8,128)(2,1)S(1)} %collective-permute-done.10.refs_1_, ...), custom_call_target="tpu_custom_call" | custom-call | flops 8000000000 | bytes 4000000 | tf_op jit(solution)/shard_map/pallas_call | solution.py:261
  72.0 1.1 collective-permute-done.22.refs_3_
  73.6 1.8 %collective-permute-done.23.refs_4_ = bf16[20,32,128]{2,1,0:T(8,128)(2,1)S(1)} collective-permute-done((bf16[20,32,128]{2,1,0:T(8,128)(2,1)S(1)}, bf16[20,32,128]{2,1,0:T(8,128)(2,1)S(1)}, u32[]{:S(2)}, u32[]{:S(2)}) %collective-permute-start.23) | collective-permute-done | bytes 163872 | tf_op jit(solution)/shard_map/ppermute | solution.py:90
  75.6 18.0 %shard_map.108 = (f32[4,256]{1,0:T(4,128)S(1)}, f32[4,256]{1,0:T(4,128)S(1)}, bf16[16,8,128]{2,1,0:T(8,128)(2,1)S(1)}, bf16[16,8,128]{2,1,0:T(8,128)(2,1)S(1)}) custom-call(s32[66]{0:T(128)S(1)} %pad_add_fusion.info.info_ref, bf16[20,32,128]{2,1,0:T(8,128)(2,1)S(1)} %copy-done.7, bf16[20,32,128]{2,1,0:T(8,128)(2,1)} %collective-permute-done.9.refs_1_, ...), custom_call_target="tpu_custom_call" | custom-call | flops 16000000000 | bytes 8000000 | tf_op jit(solution)/shard_map/pallas_call | solution.py:261
  94.3 1.5 %collective-permute-start.27 = (f32[4,256]{1,0:T(4,128)S(1)}, f32[4,256]{1,0:T(4,128)S(1)}, u32[]{:S(2)}, u32[]{:S(2)}) collective-permute-start(f32[4,256]{1,0:T(4,128)S(1)} %get-tuple-element.47), channel_id=1, source_target_pairs={{0,16},{16,0},{1,17},{17,1},{2,18},{18,2},{3,19},{19,3},{4,20},{20... | collective-permute-start | bytes 12296 | tf_op jit(solution)/shard_map/ppermute | solution.py:392
  95.8 2.3 %collective-permute-done.27 = f32[4,256]{1,0:T(4,128)S(1)} collective-permute-done((f32[4,256]{1,0:T(4,128)S(1)}, f32[4,256]{1,0:T(4,128)S(1)}, u32[]{:S(2)}, u32[]{:S(2)}) %collective-permute-start.27) | collective-permute-done | bytes 4128 | tf_op jit(solution)/shard_map/ppermute | solution.py:392
  98.1 1.2 %collective-permute-done.29 = f32[4,256]{1,0:T(4,128)S(1)} collective-permute-done((f32[4,256]{1,0:T(4,128)S(1)}, f32[4,256]{1,0:T(4,128)S(1)}, u32[]{:S(2)}, u32[]{:S(2)}) %collective-permute-start.29) | collective-permute-done | bytes 4128 | tf_op jit(solution)/shard_map/ppermute | solution.py:90
  99.3 1.1 collective-permute-start.30
  100.3 2.6 %collective-permute-done.30 = f32[4,256]{1,0:T(4,128)S(1)} collective-permute-done((f32[4,256]{1,0:T(4,128)S(1)}, f32[4,256]{1,0:T(4,128)S(1)}, u32[]{:S(2)}, u32[]{:S(2)}) %collective-permute-start.30) | collective-permute-done | bytes 4128 | tf_op jit(solution)/shard_map/ppermute | solution.py:90
  103.8 1.6 %shard_map.109 = bf16[2,8,4096]{2,1,0:T(8,128)(2,1)} custom-call(s32[66]{0:T(128)S(1)} %pad_add_fusion.info.info_ref, bf16[8,8,128]{2,1,0:T(8,128)(2,1)S(1)} %get-tuple-element.52.kept_a, bf16[8,8,128]{2,1,0:T(8,128)(2,1)S(1)} %get-tuple-element.53.kept_b, bf16[16,8,128]{2,1,0:T(8,128)(2,1)S(1)} %get-tuple-element.54.kept_c, ...), custom_call_target="tpu_custom_call" | custom-call | tf_op jit(solution)/shard_map/pallas_call | solution.py:395
  105.5 1.0 collective-permute-done.31
  106.5 1.8 %collective-permute-start.32 = (f32[4,256]{1,0:T(4,128)S(1)}, f32[4,256]{1,0:T(4,128)S(1)}, u32[]{:S(2)}, u32[]{:S(2)}) collective-permute-start(f32[4,256]{1,0:T(4,128)S(1)} %add.29), channel_id=1, source_target_pairs={{0,8},{1,9},{2,10},{3,11},{4,12},{5,13},{6,14},{7,15},{8,0},{9,1},... | collective-permute-start | bytes 12296 | tf_op jit(solution)/shard_map/ppermute | solution.py:90
  108.3 2.7 %collective-permute-done.32 = f32[4,256]{1,0:T(4,128)S(1)} collective-permute-done((f32[4,256]{1,0:T(4,128)S(1)}, f32[4,256]{1,0:T(4,128)S(1)}, u32[]{:S(2)}, u32[]{:S(2)}) %collective-permute-start.32) | collective-permute-done | bytes 4128 | tf_op jit(solution)/shard_map/ppermute | solution.py:90
  (80 shorter events, 17.3 us)
Async XLA Ops:
  0.6 6.7 %collective-permute-start.1 = (bf16[2,8,4096]{2,1,0:T(8,128)(2,1)}, bf16[2,8,4096]{2,1,0:T(8,128)(2,1)S(1)}, u32[]{:S(2)}, u32[]{:S(2)}) collective-permute-start(bf16[2,8,4096]{2,1,0:T(8,128)(2,1)} %own.2), channel_id=1, source_target_pairs={{0,16},{16,0},{1,17},{17,1},{2,18},{18,2},{3,19},{19,3},{4,20},{20... | collective-permute-start | bytes 393224 | tf_op jit(solution)/shard_map/ppermute | solution.py:319
  4.7 4.4 %collective-permute-start = (s32[128]{0:T(128)}, s32[128]{0:T(128)}, u32[]{:S(2)}, u32[]{:S(2)}) collective-permute-start(s32[128]{0:T(128)} %param.11), channel_id=1, source_target_pairs={{0,16},{16,0},{1,17},{17,1},{2,18},{18,2},{3,19},{19,3},{4,20},{20... | collective-permute-start | bytes 1544 | tf_op jit(solution)/shard_map/ppermute | solution.py:325
  7.3 17.4 %collective-permute-start.4 = (bf16[2,128,768]{2,1,0:T(8,128)(2,1)}, bf16[2,128,768]{2,1,0:T(8,128)(2,1)S(1)}, u32[]{:S(2)}, u32[]{:S(2)}) collective-permute-start(bf16[2,128,768]{2,1,0:T(8,128)(2,1)} %own.3), channel_id=1, source_target_pairs={{0,16},{16,0},{1,17},{17,1},{2,18},{18,2},{3,19},{19,3},{4,20},{20... | collective-permute-start | bytes 1179656 | tf_op jit(solution)/shard_map/ppermute | solution.py:337
  12.8 6.2 %collective-permute-start.2 = (bf16[20,32,128]{2,1,0:T(8,128)(2,1)S(1)}, bf16[20,32,128]{2,1,0:T(8,128)(2,1)S(1)}, u32[]{:S(2)}, u32[]{:S(2)}) collective-permute-start(bf16[20,32,128]{2,1,0:T(8,128)(2,1)S(1)} %get-tuple-element.35.refs_0_), channel_id=1, source_target_pairs={{0,4},{1,5},{2,6},{3,7},{4,0},{5,1},{6,2},{7,3},{8,12},{9,13},{10,... | collective-permute-start | bytes 491528 | tf_op jit(solution)/shard_map/ppermute | solution.py:90
  14.4 8.8 %collective-permute-start.3 = (bf16[20,32,128]{2,1,0:T(8,128)(2,1)S(1)}, bf16[20,32,128]{2,1,0:T(8,128)(2,1)S(1)}, u32[]{:S(2)}, u32[]{:S(2)}) collective-permute-start(bf16[20,32,128]{2,1,0:T(8,128)(2,1)S(1)} %get-tuple-element.35.refs_0_), channel_id=1, source_target_pairs={{0,12},{1,13},{2,14},{3,15},{4,8},{5,9},{6,10},{7,11},{8,4},{9,5},... | collective-permute-start | bytes 491528 | tf_op jit(solution)/shard_map/ppermute | solution.py:90
  16.9 14.1 %collective-permute-start.11 = (bf16[20,32,128]{2,1,0:T(8,128)(2,1)S(1)}, bf16[20,32,128]{2,1,0:T(8,128)(2,1)S(1)}, u32[]{:S(2)}, u32[]{:S(2)}) collective-permute-start(bf16[20,32,128]{2,1,0:T(8,128)(2,1)S(1)} %get-tuple-element.35.refs_0_), channel_id=1, source_target_pairs={{0,2},{1,3},{2,0},{3,1},{4,6},{5,7},{6,4},{7,5},{8,10},{9,11},{10,... | collective-permute-start | bytes 491528 | tf_op jit(solution)/shard_map/ppermute | solution.py:90
  19.0 12.4 %collective-permute-start.14 = (bf16[20,32,128]{2,1,0:T(8,128)(2,1)S(1)}, bf16[20,32,128]{2,1,0:T(8,128)(2,1)S(1)}, u32[]{:S(2)}, u32[]{:S(2)}) collective-permute-start(bf16[20,32,128]{2,1,0:T(8,128)(2,1)S(1)} %collective-permute-done.2.refs_4_), channel_id=1, source_target_pairs={{0,2},{1,3},{2,0},{3,1},{4,6},{5,7},{6,4},{7,5},{8,10},{9,11},{10,... | collective-permute-start | bytes 491528 | tf_op jit(solution)/shard_map/ppermute | solution.py:90
  23.2 8.3 %collective-permute-start.17 = (bf16[20,32,128]{2,1,0:T(8,128)(2,1)S(1)}, bf16[20,32,128]{2,1,0:T(8,128)(2,1)S(1)}, u32[]{:S(2)}, u32[]{:S(2)}) collective-permute-start(bf16[20,32,128]{2,1,0:T(8,128)(2,1)S(1)} %collective-permute-done.3.refs_12_), channel_id=1, source_target_pairs={{0,2},{1,3},{2,0},{3,1},{4,6},{5,7},{6,4},{7,5},{8,10},{9,11},{10,... | collective-permute-start | bytes 491528 | tf_op jit(solution)/shard_map/ppermute | solution.py:90
  29.1 8.0 %collective-permute-start.5 = (bf16[20,32,128]{2,1,0:T(8,128)(2,1)S(1)}, bf16[20,32,128]{2,1,0:T(8,128)(2,1)S(1)}, u32[]{:S(2)}, u32[]{:S(2)}) collective-permute-start(bf16[20,32,128]{2,1,0:T(8,128)(2,1)S(1)} %get-tuple-element.35.refs_0_), channel_id=1, source_target_pairs={{0,8},{1,9},{2,10},{3,11},{4,12},{5,13},{6,14},{7,15},{8,0},{9,1},... | collective-permute-start | bytes 491528 | tf_op jit(solution)/shard_map/ppermute | solution.py:90
  30.9 6.2 %collective-permute-start.10 = (bf16[20,32,128]{2,1,0:T(8,128)(2,1)S(1)}, bf16[20,32,128]{2,1,0:T(8,128)(2,1)S(1)}, u32[]{:S(2)}, u32[]{:S(2)}) collective-permute-start(bf16[20,32,128]{2,1,0:T(8,128)(2,1)S(1)} %get-tuple-element.35.refs_0_), channel_id=1, source_target_pairs={{0,1},{1,0},{2,3},{3,2},{4,5},{5,4},{6,7},{7,6},{8,9},{9,8},{10,11... | collective-permute-start | bytes 491528 | tf_op jit(solution)/shard_map/ppermute | solution.py:90
  30.9 6.7 %collective-permute-start.13 = (bf16[20,32,128]{2,1,0:T(8,128)(2,1)S(1)}, bf16[20,32,128]{2,1,0:T(8,128)(2,1)S(1)}, u32[]{:S(2)}, u32[]{:S(2)}) collective-permute-start(bf16[20,32,128]{2,1,0:T(8,128)(2,1)S(1)} %collective-permute-done.2.refs_4_), channel_id=1, source_target_pairs={{0,1},{1,0},{2,3},{3,2},{4,5},{5,4},{6,7},{7,6},{8,9},{9,8},{10,11... | collective-permute-start | bytes 491528 | tf_op jit(solution)/shard_map/ppermute | solution.py:90
  31.4 6.7 %collective-permute-start.20 = (bf16[20,32,128]{2,1,0:T(8,128)(2,1)S(1)}, bf16[20,32,128]{2,1,0:T(8,128)(2,1)S(1)}, u32[]{:S(2)}, u32[]{:S(2)}) collective-permute-start(bf16[20,32,128]{2,1,0:T(8,128)(2,1)S(1)} %collective-permute-done.3.refs_12_), channel_id=1, source_target_pairs={{0,1},{1,0},{2,3},{3,2},{4,5},{5,4},{6,7},{7,6},{8,9},{9,8},{10,11... | collective-permute-start | bytes 491528 | tf_op jit(solution)/shard_map/ppermute | solution.py:90
  31.5 8.8 %collective-permute-start.12 = (bf16[20,32,128]{2,1,0:T(8,128)(2,1)S(1)}, bf16[20,32,128]{2,1,0:T(8,128)(2,1)S(1)}, u32[]{:S(2)}, u32[]{:S(2)}) collective-permute-start(bf16[20,32,128]{2,1,0:T(8,128)(2,1)S(1)} %collective-permute-done.11.refs_2_), channel_id=1, source_target_pairs={{0,1},{1,0},{2,3},{3,2},{4,5},{5,4},{6,7},{7,6},{8,9},{9,8},{10,11... | collective-permute-start | bytes 491528 | tf_op jit(solution)/shard_map/ppermute | solution.py:90
  37.1 3.1 %collective-permute-start.15 = (bf16[20,32,128]{2,1,0:T(8,128)(2,1)S(1)}, bf16[20,32,128]{2,1,0:T(8,128)(2,1)S(1)}, u32[]{:S(2)}, u32[]{:S(2)}) collective-permute-start(bf16[20,32,128]{2,1,0:T(8,128)(2,1)S(1)} %collective-permute-done.14.refs_6_), channel_id=1, source_target_pairs={{0,1},{1,0},{2,3},{3,2},{4,5},{5,4},{6,7},{7,6},{8,9},{9,8},{10,11... | collective-permute-start | bytes 491528 | tf_op jit(solution)/shard_map/ppermute | solution.py:90
  37.1 5.9 %collective-permute-start.21 = (bf16[20,32,128]{2,1,0:T(8,128)(2,1)S(1)}, bf16[20,32,128]{2,1,0:T(8,128)(2,1)}, u32[]{:S(2)}, u32[]{:S(2)}) collective-permute-start(bf16[20,32,128]{2,1,0:T(8,128)(2,1)S(1)} %collective-permute-done.17.refs_14_), channel_id=1, source_target_pairs={{0,1},{1,0},{2,3},{3,2},{4,5},{5,4},{6,7},{7,6},{8,9},{9,8},{10,11... | collective-permute-start | bytes 491528 | tf_op jit(solution)/shard_map/ppermute | solution.py:90
  37.7 6.3 %collective-permute-start.18 = (bf16[20,32,128]{2,1,0:T(8,128)(2,1)S(1)}, bf16[20,32,128]{2,1,0:T(8,128)(2,1)}, u32[]{:S(2)}, u32[]{:S(2)}) collective-permute-start(bf16[20,32,128]{2,1,0:T(8,128)(2,1)S(1)} %collective-permute-done.5.refs_8_), channel_id=1, source_target_pairs={{0,2},{1,3},{2,0},{3,1},{4,6},{5,7},{6,4},{7,5},{8,10},{9,11},{10,... | collective-permute-start | bytes 491528 | tf_op jit(solution)/shard_map/ppermute | solution.py:90
  38.2 7.1 %collective-permute-start.16 = (bf16[20,32,128]{2,1,0:T(8,128)(2,1)S(1)}, bf16[20,32,128]{2,1,0:T(8,128)(2,1)}, u32[]{:S(2)}, u32[]{:S(2)}) collective-permute-start(bf16[20,32,128]{2,1,0:T(8,128)(2,1)S(1)} %collective-permute-done.5.refs_8_), channel_id=1, source_target_pairs={{0,1},{1,0},{2,3},{3,2},{4,5},{5,4},{6,7},{7,6},{8,9},{9,8},{10,11... | collective-permute-start | bytes 491528 | tf_op jit(solution)/shard_map/ppermute | solution.py:90
  40.3 18.0 %collective-permute-start.6 = (bf16[20,32,128]{2,1,0:T(8,128)(2,1)}, bf16[20,32,128]{2,1,0:T(8,128)(2,1)}, u32[]{:S(2)}, u32[]{:S(2)}) collective-permute-start(bf16[20,32,128]{2,1,0:T(8,128)(2,1)} %copy-done.6), channel_id=1, source_target_pairs={{0,4},{1,5},{2,6},{3,7},{4,0},{5,1},{6,2},{7,3},{8,12},{9,13},{10,... | collective-permute-start | bytes 491528 | tf_op jit(solution)/shard_map/ppermute | solution.py:90
  40.3 18.0 %collective-permute-start.7 = (bf16[20,32,128]{2,1,0:T(8,128)(2,1)}, bf16[20,32,128]{2,1,0:T(8,128)(2,1)}, u32[]{:S(2)}, u32[]{:S(2)}) collective-permute-start(bf16[20,32,128]{2,1,0:T(8,128)(2,1)} %copy-done.6), channel_id=1, source_target_pairs={{0,12},{1,13},{2,14},{3,15},{4,8},{5,9},{6,10},{7,11},{8,4},{9,5},... | collective-permute-start | bytes 491528 | tf_op jit(solution)/shard_map/ppermute | solution.py:90
  43.0 16.0 %collective-permute-start.8 = (bf16[20,32,128]{2,1,0:T(8,128)(2,1)}, bf16[20,32,128]{2,1,0:T(8,128)(2,1)}, u32[]{:S(2)}, u32[]{:S(2)}) collective-permute-start(bf16[20,32,128]{2,1,0:T(8,128)(2,1)} %copy-done.6), channel_id=1, source_target_pairs={{0,8},{1,9},{2,10},{3,11},{4,12},{5,13},{6,14},{7,15},{8,0},{9,1},... | collective-permute-start | bytes 491528 | tf_op jit(solution)/shard_map/ppermute | solution.py:90
  43.9 15.0 %collective-permute-start.9 = (bf16[20,32,128]{2,1,0:T(8,128)(2,1)}, bf16[20,32,128]{2,1,0:T(8,128)(2,1)}, u32[]{:S(2)}, u32[]{:S(2)}) collective-permute-start(bf16[20,32,128]{2,1,0:T(8,128)(2,1)} %copy-done.6), channel_id=1, source_target_pairs={{0,2},{1,3},{2,0},{3,1},{4,6},{5,7},{6,4},{7,5},{8,10},{9,11},{10,... | collective-permute-start | bytes 491528 | tf_op jit(solution)/shard_map/ppermute | solution.py:90
  45.3 2.3 %collective-permute-start.19 = (bf16[20,32,128]{2,1,0:T(8,128)(2,1)}, bf16[20,32,128]{2,1,0:T(8,128)(2,1)}, u32[]{:S(2)}, u32[]{:S(2)}) collective-permute-start(bf16[20,32,128]{2,1,0:T(8,128)(2,1)} %collective-permute-done.18.refs_10_), channel_id=1, source_target_pairs={{0,1},{1,0},{2,3},{3,2},{4,5},{5,4},{6,7},{7,6},{8,9},{9,8},{10,11... | collective-permute-start | bytes 491528 | tf_op jit(solution)/shard_map/ppermute | solution.py:90
  60.1 13.0 %collective-permute-start.22 = (bf16[3,20,32,128]{3,2,1,0:T(8,128)(2,1)S(1)}, bf16[3,20,32,128]{3,2,1,0:T(8,128)(2,1)S(1)}, u32[]{:S(2)}, u32[]{:S(2)}) collective-permute-start(bf16[3,20,32,128]{3,2,1,0:T(8,128)(2,1)S(1)} %pad_maximum_fusion.refs_2_), channel_id=1, source_target_pairs={{0,2},{1,3},{2,0},{3,1},{4,6},{5,7},{6,4},{7,5},{8,10},{9,11},{10,... | collective-permute-start | bytes 1474568 | tf_op jit(solution)/shard_map/ppermute | solution.py:90
  61.6 14.0 %collective-permute-start.25 = (bf16[3,20,32,128]{3,2,1,0:T(8,128)(2,1)S(1)}, bf16[3,20,32,128]{3,2,1,0:T(8,128)(2,1)S(1)}, u32[]{:S(2)}, u32[]{:S(2)}) collective-permute-start(bf16[3,20,32,128]{3,2,1,0:T(8,128)(2,1)S(1)} %pad_maximum_fusion.refs_2_), channel_id=1, source_target_pairs={{0,1},{1,0},{2,3},{3,2},{4,5},{5,4},{6,7},{7,6},{8,9},{9,8},{10,11... | collective-permute-start | bytes 1474568 | tf_op jit(solution)/shard_map/ppermute | solution.py:90
  73.1 2.5 %collective-permute-start.26 = (bf16[3,20,32,128]{3,2,1,0:T(8,128)(2,1)S(1)}, bf16[3,20,32,128]{3,2,1,0:T(8,128)(2,1)S(1)}, u32[]{:S(2)}, u32[]{:S(2)}) collective-permute-start(bf16[3,20,32,128]{3,2,1,0:T(8,128)(2,1)S(1)} %collective-permute-done.22.refs_3_), channel_id=1, source_target_pairs={{0,1},{1,0},{2,3},{3,2},{4,5},{5,4},{6,7},{7,6},{8,9},{9,8},{10,11... | collective-permute-start | bytes 1474568 | tf_op jit(solution)/shard_map/ppermute | solution.py:90
  73.1 2.3 %collective-permute-start.23 = (bf16[20,32,128]{2,1,0:T(8,128)(2,1)S(1)}, bf16[20,32,128]{2,1,0:T(8,128)(2,1)S(1)}, u32[]{:S(2)}, u32[]{:S(2)}) collective-permute-start(bf16[20,32,128]{2,1,0:T(8,128)(2,1)S(1)} %copy-done.7), channel_id=1, source_target_pairs={{0,1},{1,0},{2,3},{3,2},{4,5},{5,4},{6,7},{7,6},{8,9},{9,8},{10,11... | collective-permute-start | bytes 491528 | tf_op jit(solution)/shard_map/ppermute | solution.py:90
  73.6 2.0 %collective-permute-start.24 = (bf16[20,32,128]{2,1,0:T(8,128)(2,1)}, bf16[20,32,128]{2,1,0:T(8,128)(2,1)S(1)}, u32[]{:S(2)}, u32[]{:S(2)}) collective-permute-start(bf16[20,32,128]{2,1,0:T(8,128)(2,1)} %collective-permute-done.9.refs_1_), channel_id=1, source_target_pairs={{0,1},{1,0},{2,3},{3,2},{4,5},{5,4},{6,7},{7,6},{8,9},{9,8},{10,11... | collective-permute-start | bytes 491528 | tf_op jit(solution)/shard_map/ppermute | solution.py:90
  93.7 4.4 %collective-permute-start.28 = (bf16[32,8,128]{2,1,0:T(8,128)(2,1)S(1)}, bf16[32,8,128]{2,1,0:T(8,128)(2,1)S(1)}, u32[]{:S(2)}, u32[]{:S(2)}) collective-permute-start(bf16[32,8,128]{2,1,0:T(8,128)(2,1)S(1)} %pad_maximum_fusion.1), channel_id=1, source_target_pairs={{0,16},{16,0},{1,17},{17,1},{2,18},{18,2},{3,19},{19,3},{4,20},{20... | collective-permute-start | bytes 196616 | tf_op jit(solution)/shard_map/ppermute | solution.py:393
  94.3 3.8 %collective-permute-start.27 = (f32[4,256]{1,0:T(4,128)S(1)}, f32[4,256]{1,0:T(4,128)S(1)}, u32[]{:S(2)}, u32[]{:S(2)}) collective-permute-start(f32[4,256]{1,0:T(4,128)S(1)} %get-tuple-element.47), channel_id=1, source_target_pairs={{0,16},{16,0},{1,17},{17,1},{2,18},{18,2},{3,19},{19,3},{4,20},{20... | collective-permute-start | bytes 12296 | tf_op jit(solution)/shard_map/ppermute | solution.py:392
  99.3 3.6 %collective-permute-start.30 = (f32[4,256]{1,0:T(4,128)S(1)}, f32[4,256]{1,0:T(4,128)S(1)}, u32[]{:S(2)}, u32[]{:S(2)}) collective-permute-start(f32[4,256]{1,0:T(4,128)S(1)} %add.27), channel_id=1, source_target_pairs={{0,2},{1,3},{2,0},{3,1},{4,6},{5,7},{6,4},{7,5},{8,10},{9,11},{10,... | collective-permute-start | bytes 12296 | tf_op jit(solution)/shard_map/ppermute | solution.py:90
  102.9 3.6 %collective-permute-start.31 = (f32[4,256]{1,0:T(4,128)S(1)}, f32[4,256]{1,0:T(4,128)S(1)}, u32[]{:S(2)}, u32[]{:S(2)}) collective-permute-start(f32[4,256]{1,0:T(4,128)S(1)} %add.28), channel_id=1, source_target_pairs={{0,4},{1,5},{2,6},{3,7},{4,0},{5,1},{6,2},{7,3},{8,12},{9,13},{10,... | collective-permute-start | bytes 12296 | tf_op jit(solution)/shard_map/ppermute | solution.py:90
  106.5 4.5 %collective-permute-start.32 = (f32[4,256]{1,0:T(4,128)S(1)}, f32[4,256]{1,0:T(4,128)S(1)}, u32[]{:S(2)}, u32[]{:S(2)}) collective-permute-start(f32[4,256]{1,0:T(4,128)S(1)} %add.29), channel_id=1, source_target_pairs={{0,8},{1,9},{2,10},{3,11},{4,12},{5,13},{6,14},{7,15},{8,0},{9,1},... | collective-permute-start | bytes 12296 | tf_op jit(solution)/shard_map/ppermute | solution.py:90
  (9 other events, 44.6 us)

commit v9 on v8

--- a/solution.py
+++ b/solution.py
@@ -110,23 +110,45 @@
         unit[NQ:] = basis[2 * x + wave].reshape(4, 32, TILE_A)
 
 
-def prepare_kernel(info, own, other, query, tiles, grads, query_grads):
-    x = info[1 + WAVES * NQ]
+def diagonal(tiles, layer, c):
     blank = jnp.zeros((TILE_S, TILE_S), jnp.float32)
+    upper = jnp.concatenate([tiles[layer, 2 * c].astype(jnp.float32), blank], axis=1)
+    lower = jnp.concatenate([blank, tiles[layer, 2 * c + 1].astype(jnp.float32)], axis=1)
+    return jnp.concatenate([upper, lower], axis=0)
+
+
+def query_kernel(query, tiles, query_grads):
     for layer in range(LAYERS):
         for c in range(tiles.shape[1] // 2):
             cols = slice(c * TILE_A, (c + 1) * TILE_A)
-            upper = jnp.concatenate([tiles[layer, 2 * c].astype(jnp.float32), blank], axis=1)
-            lower = jnp.concatenate([blank, tiles[layer, 2 * c + 1].astype(jnp.float32)], axis=1)
-            block = jnp.concatenate([upper, lower], axis=0)
-            tile = block.astype(BF)
+            block_t = diagonal(tiles, layer, c).T.astype(BF)
+            query_grads[layer, cols, :] = across(block_t, query[layer, :, cols]).astype(BF)
+
+
+def train_kernel(info, own, other, ids, ids_other, tiles, grads, codes):
+    x = info[1 + WAVES * NQ]
+    for layer in range(LAYERS):
+        for c in range(tiles.shape[1] // 2):
+            cols = slice(c * TILE_A, (c + 1) * TILE_A)
+            tile = diagonal(tiles, layer, c).astype(BF)
             mine = jnp.dot(own[layer, :, cols], tile, preferred_element_type=jnp.float32)
             came = jnp.dot(other[layer, :, cols], tile, preferred_element_type=jnp.float32)
             first = jnp.where(x == 0, mine, came).reshape(NQ, 1, 8, TILE_A)
             second = jnp.where(x == 0, came, mine).reshape(NQ, 1, 8, TILE_A)
             rows = jnp.concatenate([first, second], axis=1).reshape(TOKENS, TILE_A)
             grads[layer, :, cols] = rows.astype(BF)
-            query_grads[layer, cols, :] = across(block.T.astype(BF), query[layer, :, cols]).astype(BF)
+    half = TOKENS // 2
+    row = lax.broadcasted_iota(jnp.int32, (half, TOKENS), 0)
+    col = lax.broadcasted_iota(jnp.int32, (half, TOKENS), 1)
+    hit = row == (col >> 4) * 8 + (col & 7)
+    part = (col >> 3) & 1
+    own_f, other_f = ids[...].astype(jnp.float32), ids_other[...].astype(jnp.float32)
+    mine = jnp.where(hit & (part == x), 1.0, 0.0)
+    came = jnp.where(hit & (part != x), 1.0, 0.0)
+    placed = jnp.dot(
+        jnp.broadcast_to(own_f, (8, half)), mine, preferred_element_type=jnp.float32
+    ) + jnp.dot(jnp.broadcast_to(other_f, (8, half)), came, preferred_element_type=jnp.float32)
+    codes[...] = (placed[:1] + 0.5).astype(jnp.int32) + SEQS * part[:1]
 
 
 def across(left, right):
@@ -322,7 +344,8 @@
     by_half = tile_of.reshape(NQ, 2, WAVES).transpose(1, 2, 0).reshape(2, WAVES * NQ)
     mine = jnp.where(x == 0, by_half[0], by_half[1])
     theirs = jnp.where(x == 0, by_half[1], by_half[0])
-    ids_other = lax.ppermute(after(sequence_ids, mine), "parts", SWAP)
+    ids = sequence_ids.reshape(1, sequence_ids.shape[0])
+    ids_other = lax.ppermute(after(ids, mine), "parts", SWAP)
     side = x.reshape(1).astype(jnp.int32)
     info = jnp.concatenate([me.reshape(1).astype(jnp.int32), mine, side, theirs])
 
@@ -335,32 +358,35 @@
     )(after(info, ids_other), train_inputs, train_other, query_inputs, input_basis)
 
     out_other = lax.ppermute(after(train_outgrads, train_other), "parts", SWAP)
-    id_pair = jnp.where(
-        x == 0, jnp.stack([sequence_ids, ids_other]), jnp.stack([ids_other, sequence_ids])
-    )
-    id_pair = id_pair + SEQS * jnp.arange(2, dtype=jnp.int32)[:, None]
-    codes = id_pair.reshape(2, NQ, 8).transpose(1, 0, 2).reshape(1, TOKENS)
     slab = train_outgrads.shape[2]
-    grads, query_grads = pl.pallas_call(
-        prepare_kernel,
-        in_specs=[SMEM] + [VMEM] * 4,
+    little = pltpu.CompilerParams(vmem_limit_bytes=16 * 1024 * 1024)
+    query_grads = pl.pallas_call(
+        query_kernel,
+        in_specs=[VMEM] * 2,
+        out_specs=VMEM,
+        out_shape=jax.ShapeDtypeStruct((LAYERS, slab, TOKENS), BF),
+        compiler_params=little,
+    )(query_outgrads, output_basis)
+    grads, codes = pl.pallas_call(
+        train_kernel,
+        in_specs=[SMEM] + [VMEM] * 5,
         out_specs=[VMEM, VMEM],
         out_shape=[
             jax.ShapeDtypeStruct((LAYERS, TOKENS, slab), BF),
-            jax.ShapeDtypeStruct((LAYERS, slab, TOKENS), BF),
+            jax.ShapeDtypeStruct((1, TOKENS), jnp.int32),
         ],
-        compiler_params=pltpu.CompilerParams(vmem_limit_bytes=16 * 1024 * 1024),
-    )(info, train_outgrads, out_other, query_outgrads, output_basis)
+        compiler_params=little,
+    )(info, train_outgrads, out_other, ids, ids_other, output_basis)
 
     units = [None] * NQ
     units[0] = packed[0]
     units[4] = hop(packed[0], 4)
     units[12] = hop(packed[0], 12)
-    units[8] = hop(after(packed[0], units[4], units[12], grads), 8)
+    units[8] = hop(after(packed[0], units[4], units[12], query_grads), 8)
     units[2] = hop(units[0], 2)
     units[6] = hop(units[4], 2)
     units[14] = hop(units[12], 2)
-    units[10] = hop(after(units[8], units[2], units[6], units[14]), 2)
+    units[10] = hop(after(units[8], grads, units[2], units[6], units[14]), 2)
     for d in (0, 2, 4, 6, 12, 14, 8, 10):
         units[d ^ 1] = hop(units[d], 1)
     places0 = [(d, None) for d in range(NQ)]

time: 112 us -> 112 us (level)
  waiting for transfers between devices: 24.7 us -> 29 us
  other arithmetic: 3.53 us -> 1.61 us
  local copies, waits for them, and re-layouts: 9.94 us -> 8.07 us
    ppermute x28, waiting for transfers between devices: 19.9 us -> 24.3 us  [hop(): return lax.ppermute(value, 'query', [(i, i ^ bits) for i in range(NQ)])]
    another operation x2 -> x0, local copies, waits for them, and re-layouts: 2.09 us -> none  [paired_body(): jnp.stack([sequence_ids, ids_other])]
    unnamed x16, local copies, waits for them, and re-layouts: 5.89 us -> 7.53 us
  transfers between devices with their start and end apart: 33 -> 33, of which waited for: 14 -> 13; matrix products, arithmetic and copies ran while one was open for 5% -> 1% of each run, Pallas kernels for 22% -> 22%
where the time goes in v9:
time: 112 us
  Pallas kernels  42.2 us (38%)
  starting transfers between devices  30.3 us (27%)
  waiting for transfers between devices  29 us (26%)
  local copies, waits for them, and re-layouts  8.07 us (7%)
  other arithmetic  1.61 us (1%)
    pallas_call x3, Pallas kernels, score_tiles(): pl.pallas_call(kernel, in_specs=[SMEM] + [VMEM] * len(arrays) + [VMEM, VM...  38.2 us
    ppermute x28, waiting for transfers between devices, hop(): return lax.ppermute(value, 'query', [(i, i ^ bits) for i in range(NQ)])  24.3 us
    ppermute x28, starting transfers between devices, hop(): return lax.ppermute(value, 'query', [(i, i ^ bits) for i in range(NQ)])  23.4 us
    unnamed x16, local copies, waits for them, and re-layouts  7.53 us
    ppermute x1, starting transfers between devices, paired_body(): train_other = lax.ppermute(train_inputs, 'parts', SWAP)  3 us
    ppermute x1, waiting for transfers between devices, paired_body(): train_other = lax.ppermute(train_inputs, 'parts', SWAP)  2.44 us
    ppermute x1, waiting for transfers between devices, paired_body(): total = keep + lax.ppermute(give, 'parts', SWAP)  2.28 us
  transfers between devices with their start and end apart: 33, of which 13 were waited for; matrix products, arithmetic and copies ran while one was open for 1% of the time, Pallas kernels for 22%

profile of v9, /device:TPU:0, one launch (start us, length us, event | category | flops | bytes accessed | tf_op | source)
XLA Modules:
  0.0 112.0 jit_solution(12887729097678924208)
XLA Ops:
  0.6 3.0 %collective-permute-start.1 = (bf16[2,8,4096]{2,1,0:T(8,128)(2,1)}, bf16[2,8,4096]{2,1,0:T(8,128)(2,1)S(1)}, u32[]{:S(2)}, u32[]{:S(2)}) collective-permute-start(bf16[2,8,4096]{2,1,0:T(8,128)(2,1)} %own.2), channel_id=1, source_target_pairs={{0,16},{16,0},{1,17},{17,1},{2,18},{18,2},{3,19},{19,3},{4,20},{20... | collective-permute-start | bytes 393224 | tf_op jit(solution)/shard_map/ppermute | solution.py:341
  4.9 2.4 %collective-permute-done.1.other = bf16[2,8,4096]{2,1,0:T(8,128)(2,1)S(1)} collective-permute-done((bf16[2,8,4096]{2,1,0:T(8,128)(2,1)}, bf16[2,8,4096]{2,1,0:T(8,128)(2,1)S(1)}, u32[]{:S(2)}, u32[]{:S(2)}) %collective-permute-start.1) | collective-permute-done | bytes 131104 | tf_op jit(solution)/shard_map/ppermute | solution.py:341
  7.3 1.7 %collective-permute-start.16 = (bf16[2,128,768]{2,1,0:T(8,128)(2,1)}, bf16[2,128,768]{2,1,0:T(8,128)(2,1)S(1)}, u32[]{:S(2)}, u32[]{:S(2)}) collective-permute-start(bf16[2,128,768]{2,1,0:T(8,128)(2,1)} %own.3), channel_id=1, source_target_pairs={{0,16},{16,0},{1,17},{17,1},{2,18},{18,2},{3,19},{19,3},{4,20},{20... | collective-permute-start | bytes 1179656 | tf_op jit(solution)/shard_map/ppermute | solution.py:360
  12.7 1.6 %collective-permute-start.2 = (bf16[20,32,128]{2,1,0:T(8,128)(2,1)S(1)}, bf16[20,32,128]{2,1,0:T(8,128)(2,1)S(1)}, u32[]{:S(2)}, u32[]{:S(2)}) collective-permute-start(bf16[20,32,128]{2,1,0:T(8,128)(2,1)S(1)} %get-tuple-element.33.refs_0_), channel_id=1, source_target_pairs={{0,4},{1,5},{2,6},{3,7},{4,0},{5,1},{6,2},{7,3},{8,12},{9,13},{10,... | collective-permute-start | bytes 491528 | tf_op jit(solution)/shard_map/ppermute | solution.py:90
  14.4 2.5 %collective-permute-start.3 = (bf16[20,32,128]{2,1,0:T(8,128)(2,1)S(1)}, bf16[20,32,128]{2,1,0:T(8,128)(2,1)S(1)}, u32[]{:S(2)}, u32[]{:S(2)}) collective-permute-start(bf16[20,32,128]{2,1,0:T(8,128)(2,1)S(1)} %get-tuple-element.33.refs_0_), channel_id=1, source_target_pairs={{0,12},{1,13},{2,14},{3,15},{4,8},{5,9},{6,10},{7,11},{8,4},{9,5},... | collective-permute-start | bytes 491528 | tf_op jit(solution)/shard_map/ppermute | solution.py:90
  16.9 1.0 copy-done
  17.9 1.1 %copy-done.2 = bf16[2,256,768]{2,1,0:T(8,128)(2,1)S(1)} copy-done((bf16[2,256,768]{2,1,0:T(8,128)(2,1)S(1)}, bf16[2,256,768]{2,1,0:T(8,128)(2,1)}, u32[]{:S(2)}) %copy-start.2) | copy-done | bytes 786456
  19.6 1.6 %collective-permute-start.10 = (bf16[20,32,128]{2,1,0:T(8,128)(2,1)S(1)}, bf16[20,32,128]{2,1,0:T(8,128)(2,1)S(1)}, u32[]{:S(2)}, u32[]{:S(2)}) collective-permute-start(bf16[20,32,128]{2,1,0:T(8,128)(2,1)S(1)} %get-tuple-element.33.refs_0_), channel_id=1, source_target_pairs={{0,2},{1,3},{2,0},{3,1},{4,6},{5,7},{6,4},{7,5},{8,10},{9,11},{10,... | collective-permute-start | bytes 491528 | tf_op jit(solution)/shard_map/ppermute | solution.py:90
  21.1 2.1 %collective-permute-done.3.refs_12_ = bf16[20,32,128]{2,1,0:T(8,128)(2,1)S(1)} collective-permute-done((bf16[20,32,128]{2,1,0:T(8,128)(2,1)S(1)}, bf16[20,32,128]{2,1,0:T(8,128)(2,1)S(1)}, u32[]{:S(2)}, u32[]{:S(2)}) %collective-permute-start.3) | collective-permute-done | bytes 163872 | tf_op jit(solution)/shard_map/ppermute | solution.py:90
  23.2 3.9 %collective-permute-start.4 = (bf16[20,32,128]{2,1,0:T(8,128)(2,1)S(1)}, bf16[20,32,128]{2,1,0:T(8,128)(2,1)S(1)}, u32[]{:S(2)}, u32[]{:S(2)}) collective-permute-start(bf16[20,32,128]{2,1,0:T(8,128)(2,1)S(1)} %get-tuple-element.33.refs_0_), channel_id=1, source_target_pairs={{0,8},{1,9},{2,10},{3,11},{4,12},{5,13},{6,14},{7,15},{8,0},{9,1},... | collective-permute-start | bytes 491528 | tf_op jit(solution)/shard_map/ppermute | solution.py:90
  27.1 1.5 %collective-permute-start.13 = (bf16[20,32,128]{2,1,0:T(8,128)(2,1)S(1)}, bf16[20,32,128]{2,1,0:T(8,128)(2,1)S(1)}, u32[]{:S(2)}, u32[]{:S(2)}) collective-permute-start(bf16[20,32,128]{2,1,0:T(8,128)(2,1)S(1)} %collective-permute-done.2.refs_4_), channel_id=1, source_target_pairs={{0,2},{1,3},{2,0},{3,1},{4,6},{5,7},{6,4},{7,5},{8,10},{9,11},{10,... | collective-permute-start | bytes 491528 | tf_op jit(solution)/shard_map/ppermute | solution.py:90
  29.2 3.0 %collective-permute-done.4.refs_8_ = bf16[20,32,128]{2,1,0:T(8,128)(2,1)S(1)} collective-permute-done((bf16[20,32,128]{2,1,0:T(8,128)(2,1)S(1)}, bf16[20,32,128]{2,1,0:T(8,128)(2,1)S(1)}, u32[]{:S(2)}, u32[]{:S(2)}) %collective-permute-start.4) | collective-permute-done | bytes 163872 | tf_op jit(solution)/shard_map/ppermute | solution.py:90
  33.7 1.0 copy-done.3
  36.3 1.6 %collective-permute-start.18 = (bf16[20,32,128]{2,1,0:T(8,128)(2,1)S(1)}, bf16[20,32,128]{2,1,0:T(8,128)(2,1)S(1)}, u32[]{:S(2)}, u32[]{:S(2)}) collective-permute-start(bf16[20,32,128]{2,1,0:T(8,128)(2,1)S(1)} %collective-permute-done.4.refs_8_), channel_id=1, source_target_pairs={{0,2},{1,3},{2,0},{3,1},{4,6},{5,7},{6,4},{7,5},{8,10},{9,11},{10,... | collective-permute-start | bytes 491528 | tf_op jit(solution)/shard_map/ppermute | solution.py:90
  39.0 3.6 %collective-permute-done.18.refs_10_ = bf16[20,32,128]{2,1,0:T(8,128)(2,1)S(1)} collective-permute-done((bf16[20,32,128]{2,1,0:T(8,128)(2,1)S(1)}, bf16[20,32,128]{2,1,0:T(8,128)(2,1)S(1)}, u32[]{:S(2)}, u32[]{:S(2)}) %collective-permute-start.18) | collective-permute-done | bytes 163872 | tf_op jit(solution)/shard_map/ppermute | solution.py:90
  42.5 2.6 %collective-permute-start.6 = (bf16[20,32,128]{2,1,0:T(8,128)(2,1)S(1)}, bf16[20,32,128]{2,1,0:T(8,128)(2,1)S(1)}, u32[]{:S(2)}, u32[]{:S(2)}) collective-permute-start(bf16[20,32,128]{2,1,0:T(8,128)(2,1)S(1)} %get-tuple-element.34.refs_0_), channel_id=1, source_target_pairs={{0,12},{1,13},{2,14},{3,15},{4,8},{5,9},{6,10},{7,11},{8,4},{9,5},... | collective-permute-start | bytes 491528 | tf_op jit(solution)/shard_map/ppermute | solution.py:90
  46.0 1.5 %collective-permute-start.8 = (bf16[20,32,128]{2,1,0:T(8,128)(2,1)S(1)}, bf16[20,32,128]{2,1,0:T(8,128)(2,1)S(1)}, u32[]{:S(2)}, u32[]{:S(2)}) collective-permute-start(bf16[20,32,128]{2,1,0:T(8,128)(2,1)S(1)} %get-tuple-element.34.refs_0_), channel_id=1, source_target_pairs={{0,2},{1,3},{2,0},{3,1},{4,6},{5,7},{6,4},{7,5},{8,10},{9,11},{10,... | collective-permute-start | bytes 491528 | tf_op jit(solution)/shard_map/ppermute | solution.py:90
  47.5 10.2 %shard_map.107 = (f32[8,256]{1,0:T(8,128)S(1)}, bf16[8,8,128]{2,1,0:T(8,128)(2,1)S(1)}, bf16[8,8,128]{2,1,0:T(8,128)(2,1)S(1)}) custom-call(s32[66]{0:T(128)S(1)} %pad_add_fusion.info.info_ref, bf16[20,32,128]{2,1,0:T(8,128)(2,1)S(1)} %get-tuple-element.33.refs_0_, bf16[20,32,128]{2,1,0:T(8,128)(2,1)S(1)} %collective-permute-done.9.refs_1_, ...), custom_call_target="tpu_custom_call" | custom-call | flops 80000000 | bytes 4000000 | tf_op jit(solution)/shard_map/pallas_call | solution.py:283
  57.7 3.1 %collective-permute-done.7 = bf16[20,32,128]{2,1,0:T(8,128)(2,1)S(1)} collective-permute-done((bf16[20,32,128]{2,1,0:T(8,128)(2,1)S(1)}, bf16[20,32,128]{2,1,0:T(8,128)(2,1)S(1)}, u32[]{:S(2)}, u32[]{:S(2)}) %collective-permute-start.7) | collective-permute-done | bytes 163872 | tf_op jit(solution)/shard_map/ppermute | solution.py:90
  60.9 1.6 %collective-permute-start.22 = (bf16[3,20,32,128]{3,2,1,0:T(8,128)(2,1)S(1)}, bf16[3,20,32,128]{3,2,1,0:T(8,128)(2,1)S(1)}, u32[]{:S(2)}, u32[]{:S(2)}) collective-permute-start(bf16[3,20,32,128]{3,2,1,0:T(8,128)(2,1)S(1)} %pad_maximum_fusion.refs_2_), channel_id=1, source_target_pairs={{0,2},{1,3},{2,0},{3,1},{4,6},{5,7},{6,4},{7,5},{8,10},{9,11},{10,... | collective-permute-start | bytes 1474568 | tf_op jit(solution)/shard_map/ppermute | solution.py:90
  62.5 10.0 %shard_map.108 = (f32[8,256]{1,0:T(8,128)S(1)}, bf16[8,8,128]{2,1,0:T(8,128)(2,1)S(1)}, bf16[8,8,128]{2,1,0:T(8,128)(2,1)S(1)}) custom-call(s32[66]{0:T(128)S(1)} %pad_add_fusion.info.info_ref, bf16[20,32,128]{2,1,0:T(8,128)(2,1)S(1)} %get-tuple-element.33.refs_0_, bf16[20,32,128]{2,1,0:T(8,128)(2,1)S(1)} %collective-permute-done.9.refs_1_, ...), custom_call_target="tpu_custom_call" | custom-call | flops 8000000000 | bytes 4000000 | tf_op jit(solution)/shard_map/pallas_call | solution.py:283
  72.5 1.0 collective-permute-done.22.refs_3_
  74.0 1.6 %collective-permute-done.23.refs_4_ = bf16[20,32,128]{2,1,0:T(8,128)(2,1)S(1)} collective-permute-done((bf16[20,32,128]{2,1,0:T(8,128)(2,1)S(1)}, bf16[20,32,128]{2,1,0:T(8,128)(2,1)S(1)}, u32[]{:S(2)}, u32[]{:S(2)}) %collective-permute-start.23) | collective-permute-done | bytes 163872 | tf_op jit(solution)/shard_map/ppermute | solution.py:90
  75.9 18.1 %shard_map.109 = (f32[4,256]{1,0:T(4,128)S(1)}, f32[4,256]{1,0:T(4,128)S(1)}, bf16[16,8,128]{2,1,0:T(8,128)(2,1)S(1)}, bf16[16,8,128]{2,1,0:T(8,128)(2,1)S(1)}) custom-call(s32[66]{0:T(128)S(1)} %pad_add_fusion.info.info_ref, bf16[20,32,128]{2,1,0:T(8,128)(2,1)S(1)} %get-tuple-element.34.refs_0_, bf16[20,32,128]{2,1,0:T(8,128)(2,1)S(1)} %collective-permute-done.8.refs_1_, ...), custom_call_target="tpu_custom_call" | custom-call | flops 16000000000 | bytes 8000000 | tf_op jit(solution)/shard_map/pallas_call | solution.py:283
  94.6 1.5 %collective-permute-start.27 = (f32[4,256]{1,0:T(4,128)S(1)}, f32[4,256]{1,0:T(4,128)S(1)}, u32[]{:S(2)}, u32[]{:S(2)}) collective-permute-start(f32[4,256]{1,0:T(4,128)S(1)} %get-tuple-element.47), channel_id=1, source_target_pairs={{0,16},{16,0},{1,17},{17,1},{2,18},{18,2},{3,19},{19,3},{4,20},{20... | collective-permute-start | bytes 12296 | tf_op jit(solution)/shard_map/ppermute | solution.py:418
  96.1 2.3 %collective-permute-done.27 = f32[4,256]{1,0:T(4,128)S(1)} collective-permute-done((f32[4,256]{1,0:T(4,128)S(1)}, f32[4,256]{1,0:T(4,128)S(1)}, u32[]{:S(2)}, u32[]{:S(2)}) %collective-permute-start.27) | collective-permute-done | bytes 4128 | tf_op jit(solution)/shard_map/ppermute | solution.py:418
  98.4 1.2 %collective-permute-done.29 = f32[4,256]{1,0:T(4,128)S(1)} collective-permute-done((f32[4,256]{1,0:T(4,128)S(1)}, f32[4,256]{1,0:T(4,128)S(1)}, u32[]{:S(2)}, u32[]{:S(2)}) %collective-permute-start.29) | collective-permute-done | bytes 4128 | tf_op jit(solution)/shard_map/ppermute | solution.py:90
  99.6 1.5 %collective-permute-start.30 = (f32[4,256]{1,0:T(4,128)S(1)}, f32[4,256]{1,0:T(4,128)S(1)}, u32[]{:S(2)}, u32[]{:S(2)}) collective-permute-start(f32[4,256]{1,0:T(4,128)S(1)} %add.16), channel_id=1, source_target_pairs={{0,2},{1,3},{2,0},{3,1},{4,6},{5,7},{6,4},{7,5},{8,10},{9,11},{10,... | collective-permute-start | bytes 12296 | tf_op jit(solution)/shard_map/ppermute | solution.py:90
  101.1 2.1 %collective-permute-done.30 = f32[4,256]{1,0:T(4,128)S(1)} collective-permute-done((f32[4,256]{1,0:T(4,128)S(1)}, f32[4,256]{1,0:T(4,128)S(1)}, u32[]{:S(2)}, u32[]{:S(2)}) %collective-permute-start.30) | collective-permute-done | bytes 4128 | tf_op jit(solution)/shard_map/ppermute | solution.py:90
  103.2 1.6 %shard_map.110 = bf16[2,8,4096]{2,1,0:T(8,128)(2,1)} custom-call(s32[66]{0:T(128)S(1)} %pad_add_fusion.info.info_ref, bf16[8,8,128]{2,1,0:T(8,128)(2,1)S(1)} %get-tuple-element.52.kept_a, bf16[8,8,128]{2,1,0:T(8,128)(2,1)S(1)} %get-tuple-element.53.kept_b, bf16[16,8,128]{2,1,0:T(8,128)(2,1)S(1)} %get-tuple-element.54.kept_c, ...), custom_call_target="tpu_custom_call" | custom-call | tf_op jit(solution)/shard_map/pallas_call | solution.py:421
  104.8 2.0 %collective-permute-done.31 = f32[4,256]{1,0:T(4,128)S(1)} collective-permute-done((f32[4,256]{1,0:T(4,128)S(1)}, f32[4,256]{1,0:T(4,128)S(1)}, u32[]{:S(2)}, u32[]{:S(2)}) %collective-permute-start.31) | collective-permute-done | bytes 4128 | tf_op jit(solution)/shard_map/ppermute | solution.py:90
  106.8 4.4 %collective-permute-done.32 = f32[4,256]{1,0:T(4,128)S(1)} collective-permute-done((f32[4,256]{1,0:T(4,128)S(1)}, f32[4,256]{1,0:T(4,128)S(1)}, u32[]{:S(2)}, u32[]{:S(2)}) %collective-permute-start.32) | collective-permute-done | bytes 4128 | tf_op jit(solution)/shard_map/ppermute | solution.py:90
  (75 shorter events, 13.3 us)
Async XLA Ops:
  0.6 6.7 %collective-permute-start.1 = (bf16[2,8,4096]{2,1,0:T(8,128)(2,1)}, bf16[2,8,4096]{2,1,0:T(8,128)(2,1)S(1)}, u32[]{:S(2)}, u32[]{:S(2)}) collective-permute-start(bf16[2,8,4096]{2,1,0:T(8,128)(2,1)} %own.2), channel_id=1, source_target_pairs={{0,16},{16,0},{1,17},{17,1},{2,18},{18,2},{3,19},{19,3},{4,20},{20... | collective-permute-start | bytes 393224 | tf_op jit(solution)/shard_map/ppermute | solution.py:341
  4.7 4.4 %collective-permute-start = (s32[1,128]{1,0:T(1,128)}, s32[1,128]{1,0:T(1,128)S(1)}, u32[]{:S(2)}, u32[]{:S(2)}) collective-permute-start(s32[1,128]{1,0:T(1,128)} %bitcast.8), channel_id=1, source_target_pairs={{0,16},{16,0},{1,17},{17,1},{2,18},{18,2},{3,19},{19,3},{4,20},{20... | collective-permute-start | bytes 1544 | tf_op jit(solution)/shard_map/ppermute | solution.py:348
  7.3 24.8 %collective-permute-start.16 = (bf16[2,128,768]{2,1,0:T(8,128)(2,1)}, bf16[2,128,768]{2,1,0:T(8,128)(2,1)S(1)}, u32[]{:S(2)}, u32[]{:S(2)}) collective-permute-start(bf16[2,128,768]{2,1,0:T(8,128)(2,1)} %own.3), channel_id=1, source_target_pairs={{0,16},{16,0},{1,17},{17,1},{2,18},{18,2},{3,19},{19,3},{4,20},{20... | collective-permute-start | bytes 1179656 | tf_op jit(solution)/shard_map/ppermute | solution.py:360
  12.7 8.4 %collective-permute-start.2 = (bf16[20,32,128]{2,1,0:T(8,128)(2,1)S(1)}, bf16[20,32,128]{2,1,0:T(8,128)(2,1)S(1)}, u32[]{:S(2)}, u32[]{:S(2)}) collective-permute-start(bf16[20,32,128]{2,1,0:T(8,128)(2,1)S(1)} %get-tuple-element.33.refs_0_), channel_id=1, source_target_pairs={{0,4},{1,5},{2,6},{3,7},{4,0},{5,1},{6,2},{7,3},{8,12},{9,13},{10,... | collective-permute-start | bytes 491528 | tf_op jit(solution)/shard_map/ppermute | solution.py:90
  14.4 8.8 %collective-permute-start.3 = (bf16[20,32,128]{2,1,0:T(8,128)(2,1)S(1)}, bf16[20,32,128]{2,1,0:T(8,128)(2,1)S(1)}, u32[]{:S(2)}, u32[]{:S(2)}) collective-permute-start(bf16[20,32,128]{2,1,0:T(8,128)(2,1)S(1)} %get-tuple-element.33.refs_0_), channel_id=1, source_target_pairs={{0,12},{1,13},{2,14},{3,15},{4,8},{5,9},{6,10},{7,11},{8,4},{9,5},... | collective-permute-start | bytes 491528 | tf_op jit(solution)/shard_map/ppermute | solution.py:90
  19.6 9.6 %collective-permute-start.10 = (bf16[20,32,128]{2,1,0:T(8,128)(2,1)S(1)}, bf16[20,32,128]{2,1,0:T(8,128)(2,1)S(1)}, u32[]{:S(2)}, u32[]{:S(2)}) collective-permute-start(bf16[20,32,128]{2,1,0:T(8,128)(2,1)S(1)} %get-tuple-element.33.refs_0_), channel_id=1, source_target_pairs={{0,2},{1,3},{2,0},{3,1},{4,6},{5,7},{6,4},{7,5},{8,10},{9,11},{10,... | collective-permute-start | bytes 491528 | tf_op jit(solution)/shard_map/ppermute | solution.py:90
  23.2 8.9 %collective-permute-start.4 = (bf16[20,32,128]{2,1,0:T(8,128)(2,1)S(1)}, bf16[20,32,128]{2,1,0:T(8,128)(2,1)S(1)}, u32[]{:S(2)}, u32[]{:S(2)}) collective-permute-start(bf16[20,32,128]{2,1,0:T(8,128)(2,1)S(1)} %get-tuple-element.33.refs_0_), channel_id=1, source_target_pairs={{0,8},{1,9},{2,10},{3,11},{4,12},{5,13},{6,14},{7,15},{8,0},{9,1},... | collective-permute-start | bytes 491528 | tf_op jit(solution)/shard_map/ppermute | solution.py:90
  27.1 9.2 %collective-permute-start.13 = (bf16[20,32,128]{2,1,0:T(8,128)(2,1)S(1)}, bf16[20,32,128]{2,1,0:T(8,128)(2,1)S(1)}, u32[]{:S(2)}, u32[]{:S(2)}) collective-permute-start(bf16[20,32,128]{2,1,0:T(8,128)(2,1)S(1)} %collective-permute-done.2.refs_4_), channel_id=1, source_target_pairs={{0,2},{1,3},{2,0},{3,1},{4,6},{5,7},{6,4},{7,5},{8,10},{9,11},{10,... | collective-permute-start | bytes 491528 | tf_op jit(solution)/shard_map/ppermute | solution.py:90
  28.6 7.7 %collective-permute-start.17 = (bf16[20,32,128]{2,1,0:T(8,128)(2,1)S(1)}, bf16[20,32,128]{2,1,0:T(8,128)(2,1)S(1)}, u32[]{:S(2)}, u32[]{:S(2)}) collective-permute-start(bf16[20,32,128]{2,1,0:T(8,128)(2,1)S(1)} %collective-permute-done.3.refs_12_), channel_id=1, source_target_pairs={{0,2},{1,3},{2,0},{3,1},{4,6},{5,7},{6,4},{7,5},{8,10},{9,11},{10,... | collective-permute-start | bytes 491528 | tf_op jit(solution)/shard_map/ppermute | solution.py:90
  29.1 8.8 %collective-permute-start.9 = (bf16[20,32,128]{2,1,0:T(8,128)(2,1)S(1)}, bf16[20,32,128]{2,1,0:T(8,128)(2,1)S(1)}, u32[]{:S(2)}, u32[]{:S(2)}) collective-permute-start(bf16[20,32,128]{2,1,0:T(8,128)(2,1)S(1)} %get-tuple-element.33.refs_0_), channel_id=1, source_target_pairs={{0,1},{1,0},{2,3},{3,2},{4,5},{5,4},{6,7},{7,6},{8,9},{9,8},{10,11... | collective-permute-start | bytes 491528 | tf_op jit(solution)/shard_map/ppermute | solution.py:90
  32.2 6.3 %collective-permute-start.12 = (bf16[20,32,128]{2,1,0:T(8,128)(2,1)S(1)}, bf16[20,32,128]{2,1,0:T(8,128)(2,1)S(1)}, u32[]{:S(2)}, u32[]{:S(2)}) collective-permute-start(bf16[20,32,128]{2,1,0:T(8,128)(2,1)S(1)} %collective-permute-done.2.refs_4_), channel_id=1, source_target_pairs={{0,1},{1,0},{2,3},{3,2},{4,5},{5,4},{6,7},{7,6},{8,9},{9,8},{10,11... | collective-permute-start | bytes 491528 | tf_op jit(solution)/shard_map/ppermute | solution.py:90
  32.2 6.3 %collective-permute-start.20 = (bf16[20,32,128]{2,1,0:T(8,128)(2,1)S(1)}, bf16[20,32,128]{2,1,0:T(8,128)(2,1)S(1)}, u32[]{:S(2)}, u32[]{:S(2)}) collective-permute-start(bf16[20,32,128]{2,1,0:T(8,128)(2,1)S(1)} %collective-permute-done.3.refs_12_), channel_id=1, source_target_pairs={{0,1},{1,0},{2,3},{3,2},{4,5},{5,4},{6,7},{7,6},{8,9},{9,8},{10,11... | collective-permute-start | bytes 491528 | tf_op jit(solution)/shard_map/ppermute | solution.py:90
  36.3 6.2 %collective-permute-start.18 = (bf16[20,32,128]{2,1,0:T(8,128)(2,1)S(1)}, bf16[20,32,128]{2,1,0:T(8,128)(2,1)S(1)}, u32[]{:S(2)}, u32[]{:S(2)}) collective-permute-start(bf16[20,32,128]{2,1,0:T(8,128)(2,1)S(1)} %collective-permute-done.4.refs_8_), channel_id=1, source_target_pairs={{0,2},{1,3},{2,0},{3,1},{4,6},{5,7},{6,4},{7,5},{8,10},{9,11},{10,... | collective-permute-start | bytes 491528 | tf_op jit(solution)/shard_map/ppermute | solution.py:90
  37.9 4.6 %collective-permute-start.11 = (bf16[20,32,128]{2,1,0:T(8,128)(2,1)S(1)}, bf16[20,32,128]{2,1,0:T(8,128)(2,1)S(1)}, u32[]{:S(2)}, u32[]{:S(2)}) collective-permute-start(bf16[20,32,128]{2,1,0:T(8,128)(2,1)S(1)} %collective-permute-done.10.refs_2_), channel_id=1, source_target_pairs={{0,1},{1,0},{2,3},{3,2},{4,5},{5,4},{6,7},{7,6},{8,9},{9,8},{10,11... | collective-permute-start | bytes 491528 | tf_op jit(solution)/shard_map/ppermute | solution.py:90
  37.9 4.6 %collective-permute-start.15 = (bf16[20,32,128]{2,1,0:T(8,128)(2,1)S(1)}, bf16[20,32,128]{2,1,0:T(8,128)(2,1)S(1)}, u32[]{:S(2)}, u32[]{:S(2)}) collective-permute-start(bf16[20,32,128]{2,1,0:T(8,128)(2,1)S(1)} %collective-permute-done.4.refs_8_), channel_id=1, source_target_pairs={{0,1},{1,0},{2,3},{3,2},{4,5},{5,4},{6,7},{7,6},{8,9},{9,8},{10,11... | collective-permute-start | bytes 491528 | tf_op jit(solution)/shard_map/ppermute | solution.py:90
  38.4 6.7 %collective-permute-start.14 = (bf16[20,32,128]{2,1,0:T(8,128)(2,1)S(1)}, bf16[20,32,128]{2,1,0:T(8,128)(2,1)S(1)}, u32[]{:S(2)}, u32[]{:S(2)}) collective-permute-start(bf16[20,32,128]{2,1,0:T(8,128)(2,1)S(1)} %collective-permute-done.13.refs_6_), channel_id=1, source_target_pairs={{0,1},{1,0},{2,3},{3,2},{4,5},{5,4},{6,7},{7,6},{8,9},{9,8},{10,11... | collective-permute-start | bytes 491528 | tf_op jit(solution)/shard_map/ppermute | solution.py:90
  38.5 7.5 %collective-permute-start.21 = (bf16[20,32,128]{2,1,0:T(8,128)(2,1)S(1)}, bf16[20,32,128]{2,1,0:T(8,128)(2,1)S(1)}, u32[]{:S(2)}, u32[]{:S(2)}) collective-permute-start(bf16[20,32,128]{2,1,0:T(8,128)(2,1)S(1)} %collective-permute-done.17.refs_14_), channel_id=1, source_target_pairs={{0,1},{1,0},{2,3},{3,2},{4,5},{5,4},{6,7},{7,6},{8,9},{9,8},{10,11... | collective-permute-start | bytes 491528 | tf_op jit(solution)/shard_map/ppermute | solution.py:90
  42.5 5.0 %collective-permute-start.19 = (bf16[20,32,128]{2,1,0:T(8,128)(2,1)S(1)}, bf16[20,32,128]{2,1,0:T(8,128)(2,1)S(1)}, u32[]{:S(2)}, u32[]{:S(2)}) collective-permute-start(bf16[20,32,128]{2,1,0:T(8,128)(2,1)S(1)} %collective-permute-done.18.refs_10_), channel_id=1, source_target_pairs={{0,1},{1,0},{2,3},{3,2},{4,5},{5,4},{6,7},{7,6},{8,9},{9,8},{10,11... | collective-permute-start | bytes 491528 | tf_op jit(solution)/shard_map/ppermute | solution.py:90
  42.5 15.2 %collective-permute-start.5 = (bf16[20,32,128]{2,1,0:T(8,128)(2,1)S(1)}, bf16[20,32,128]{2,1,0:T(8,128)(2,1)S(1)}, u32[]{:S(2)}, u32[]{:S(2)}) collective-permute-start(bf16[20,32,128]{2,1,0:T(8,128)(2,1)S(1)} %get-tuple-element.34.refs_0_), channel_id=1, source_target_pairs={{0,4},{1,5},{2,6},{3,7},{4,0},{5,1},{6,2},{7,3},{8,12},{9,13},{10,... | collective-permute-start | bytes 491528 | tf_op jit(solution)/shard_map/ppermute | solution.py:90
  42.5 15.2 %collective-permute-start.6 = (bf16[20,32,128]{2,1,0:T(8,128)(2,1)S(1)}, bf16[20,32,128]{2,1,0:T(8,128)(2,1)S(1)}, u32[]{:S(2)}, u32[]{:S(2)}) collective-permute-start(bf16[20,32,128]{2,1,0:T(8,128)(2,1)S(1)} %get-tuple-element.34.refs_0_), channel_id=1, source_target_pairs={{0,12},{1,13},{2,14},{3,15},{4,8},{5,9},{6,10},{7,11},{8,4},{9,5},... | collective-permute-start | bytes 491528 | tf_op jit(solution)/shard_map/ppermute | solution.py:90
  45.2 15.7 %collective-permute-start.7 = (bf16[20,32,128]{2,1,0:T(8,128)(2,1)S(1)}, bf16[20,32,128]{2,1,0:T(8,128)(2,1)S(1)}, u32[]{:S(2)}, u32[]{:S(2)}) collective-permute-start(bf16[20,32,128]{2,1,0:T(8,128)(2,1)S(1)} %get-tuple-element.34.refs_0_), channel_id=1, source_target_pairs={{0,8},{1,9},{2,10},{3,11},{4,12},{5,13},{6,14},{7,15},{8,0},{9,1},... | collective-permute-start | bytes 491528 | tf_op jit(solution)/shard_map/ppermute | solution.py:90
  46.0 14.8 %collective-permute-start.8 = (bf16[20,32,128]{2,1,0:T(8,128)(2,1)S(1)}, bf16[20,32,128]{2,1,0:T(8,128)(2,1)S(1)}, u32[]{:S(2)}, u32[]{:S(2)}) collective-permute-start(bf16[20,32,128]{2,1,0:T(8,128)(2,1)S(1)} %get-tuple-element.34.refs_0_), channel_id=1, source_target_pairs={{0,2},{1,3},{2,0},{3,1},{4,6},{5,7},{6,4},{7,5},{8,10},{9,11},{10,... | collective-permute-start | bytes 491528 | tf_op jit(solution)/shard_map/ppermute | solution.py:90
  60.9 12.6 %collective-permute-start.22 = (bf16[3,20,32,128]{3,2,1,0:T(8,128)(2,1)S(1)}, bf16[3,20,32,128]{3,2,1,0:T(8,128)(2,1)S(1)}, u32[]{:S(2)}, u32[]{:S(2)}) collective-permute-start(bf16[3,20,32,128]{3,2,1,0:T(8,128)(2,1)S(1)} %pad_maximum_fusion.refs_2_), channel_id=1, source_target_pairs={{0,2},{1,3},{2,0},{3,1},{4,6},{5,7},{6,4},{7,5},{8,10},{9,11},{10,... | collective-permute-start | bytes 1474568 | tf_op jit(solution)/shard_map/ppermute | solution.py:90
  62.5 13.4 %collective-permute-start.25 = (bf16[3,20,32,128]{3,2,1,0:T(8,128)(2,1)S(1)}, bf16[3,20,32,128]{3,2,1,0:T(8,128)(2,1)S(1)}, u32[]{:S(2)}, u32[]{:S(2)}) collective-permute-start(bf16[3,20,32,128]{3,2,1,0:T(8,128)(2,1)S(1)} %pad_maximum_fusion.refs_2_), channel_id=1, source_target_pairs={{0,1},{1,0},{2,3},{3,2},{4,5},{5,4},{6,7},{7,6},{8,9},{9,8},{10,11... | collective-permute-start | bytes 1474568 | tf_op jit(solution)/shard_map/ppermute | solution.py:90
  73.5 2.3 %collective-permute-start.26 = (bf16[3,20,32,128]{3,2,1,0:T(8,128)(2,1)S(1)}, bf16[3,20,32,128]{3,2,1,0:T(8,128)(2,1)S(1)}, u32[]{:S(2)}, u32[]{:S(2)}) collective-permute-start(bf16[3,20,32,128]{3,2,1,0:T(8,128)(2,1)S(1)} %collective-permute-done.22.refs_3_), channel_id=1, source_target_pairs={{0,1},{1,0},{2,3},{3,2},{4,5},{5,4},{6,7},{7,6},{8,9},{9,8},{10,11... | collective-permute-start | bytes 1474568 | tf_op jit(solution)/shard_map/ppermute | solution.py:90
  73.5 2.1 %collective-permute-start.23 = (bf16[20,32,128]{2,1,0:T(8,128)(2,1)S(1)}, bf16[20,32,128]{2,1,0:T(8,128)(2,1)S(1)}, u32[]{:S(2)}, u32[]{:S(2)}) collective-permute-start(bf16[20,32,128]{2,1,0:T(8,128)(2,1)S(1)} %get-tuple-element.34.refs_0_), channel_id=1, source_target_pairs={{0,1},{1,0},{2,3},{3,2},{4,5},{5,4},{6,7},{7,6},{8,9},{9,8},{10,11... | collective-permute-start | bytes 491528 | tf_op jit(solution)/shard_map/ppermute | solution.py:90
  74.0 1.8 %collective-permute-start.24 = (bf16[20,32,128]{2,1,0:T(8,128)(2,1)S(1)}, bf16[20,32,128]{2,1,0:T(8,128)(2,1)S(1)}, u32[]{:S(2)}, u32[]{:S(2)}) collective-permute-start(bf16[20,32,128]{2,1,0:T(8,128)(2,1)S(1)} %collective-permute-done.8.refs_1_), channel_id=1, source_target_pairs={{0,1},{1,0},{2,3},{3,2},{4,5},{5,4},{6,7},{7,6},{8,9},{9,8},{10,11... | collective-permute-start | bytes 491528 | tf_op jit(solution)/shard_map/ppermute | solution.py:90
  94.0 4.4 %collective-permute-start.28 = (bf16[32,8,128]{2,1,0:T(8,128)(2,1)S(1)}, bf16[32,8,128]{2,1,0:T(8,128)(2,1)S(1)}, u32[]{:S(2)}, u32[]{:S(2)}) collective-permute-start(bf16[32,8,128]{2,1,0:T(8,128)(2,1)S(1)} %pad_maximum_fusion.1), channel_id=1, source_target_pairs={{0,16},{16,0},{1,17},{17,1},{2,18},{18,2},{3,19},{19,3},{4,20},{20... | collective-permute-start | bytes 196616 | tf_op jit(solution)/shard_map/ppermute | solution.py:419
  94.6 3.8 %collective-permute-start.27 = (f32[4,256]{1,0:T(4,128)S(1)}, f32[4,256]{1,0:T(4,128)S(1)}, u32[]{:S(2)}, u32[]{:S(2)}) collective-permute-start(f32[4,256]{1,0:T(4,128)S(1)} %get-tuple-element.47), channel_id=1, source_target_pairs={{0,16},{16,0},{1,17},{17,1},{2,18},{18,2},{3,19},{19,3},{4,20},{20... | collective-permute-start | bytes 12296 | tf_op jit(solution)/shard_map/ppermute | solution.py:418
  99.6 3.6 %collective-permute-start.30 = (f32[4,256]{1,0:T(4,128)S(1)}, f32[4,256]{1,0:T(4,128)S(1)}, u32[]{:S(2)}, u32[]{:S(2)}) collective-permute-start(f32[4,256]{1,0:T(4,128)S(1)} %add.16), channel_id=1, source_target_pairs={{0,2},{1,3},{2,0},{3,1},{4,6},{5,7},{6,4},{7,5},{8,10},{9,11},{10,... | collective-permute-start | bytes 12296 | tf_op jit(solution)/shard_map/ppermute | solution.py:90
  103.2 3.6 %collective-permute-start.31 = (f32[4,256]{1,0:T(4,128)S(1)}, f32[4,256]{1,0:T(4,128)S(1)}, u32[]{:S(2)}, u32[]{:S(2)}) collective-permute-start(f32[4,256]{1,0:T(4,128)S(1)} %add.17), channel_id=1, source_target_pairs={{0,4},{1,5},{2,6},{3,7},{4,0},{5,1},{6,2},{7,3},{8,12},{9,13},{10,... | collective-permute-start | bytes 12296 | tf_op jit(solution)/shard_map/ppermute | solution.py:90
  106.8 4.5 %collective-permute-start.32 = (f32[4,256]{1,0:T(4,128)S(1)}, f32[4,256]{1,0:T(4,128)S(1)}, u32[]{:S(2)}, u32[]{:S(2)}) collective-permute-start(f32[4,256]{1,0:T(4,128)S(1)} %add.18), channel_id=1, source_target_pairs={{0,8},{1,9},{2,10},{3,11},{4,12},{5,13},{6,14},{7,15},{8,0},{9,1},... | collective-permute-start | bytes 12296 | tf_op jit(solution)/shard_map/ppermute | solution.py:90
  (9 other events, 8.7 us)

commit v10 on v9

--- a/solution.py
+++ b/solution.py
@@ -357,7 +357,7 @@
         compiler_params=pltpu.CompilerParams(vmem_limit_bytes=8 * 1024 * 1024),
     )(after(info, ids_other), train_inputs, train_other, query_inputs, input_basis)
 
-    out_other = lax.ppermute(after(train_outgrads, train_other), "parts", SWAP)
+    out_other = lax.ppermute(after(train_outgrads, packed[0]), "parts", SWAP)
     slab = train_outgrads.shape[2]
     little = pltpu.CompilerParams(vmem_limit_bytes=16 * 1024 * 1024)
     query_grads = pl.pallas_call(
@@ -385,10 +385,11 @@
     units[8] = hop(after(packed[0], units[4], units[12], query_grads), 8)
     units[2] = hop(units[0], 2)
     units[6] = hop(units[4], 2)
-    units[14] = hop(units[12], 2)
-    units[10] = hop(after(units[8], grads, units[2], units[6], units[14]), 2)
-    for d in (0, 2, 4, 6, 12, 14, 8, 10):
+    units[14] = hop(after(units[12], out_other), 2)
+    units[10] = hop(after(units[8], units[2], units[6], units[14]), 2)
+    for d in (0, 2, 4, 6, 12, 8, 10):
         units[d ^ 1] = hop(units[d], 1)
+    units[15] = hop(after(units[14], grads), 1)
     places0 = [(d, None) for d in range(NQ)]
 
     zero = jnp.zeros((GROUPS, TOKENS), jnp.float32)

time: 112 us -> 110 us (0.982)
  starting transfers between devices: 30.3 us -> 26 us
  waiting for transfers between devices: 29 us -> 31.2 us
    ppermute x1, waiting for transfers between devices: 0.01 us -> 3.41 us  [paired_body(): ids_other = lax.ppermute(after(ids, mine), 'parts', SWAP)]
    ppermute x28, starting transfers between devices: 23.4 us -> 20.1 us  [hop(): return lax.ppermute(value, 'query', [(i, i ^ bits) for i in range(NQ)])]
    ppermute x1, waiting for transfers between devices: 2.44 us -> 0.01 us  [paired_body(): train_other = lax.ppermute(train_inputs, 'parts', SWAP)]
  transfers between devices with their start and end apart: 33 -> 33, of which waited for: 13 -> 15; matrix products, arithmetic and copies ran while one was open for 1% -> 1% of each run, Pallas kernels for 22% -> 21%
where the time goes in v10:
time: 110 us
  Pallas kernels  42.2 us (38%)
  waiting for transfers between devices  31.2 us (28%)
  starting transfers between devices  26 us (24%)
  local copies, waits for them, and re-layouts  8.07 us (7%)
  other arithmetic  1.61 us (1%)
    pallas_call x3, Pallas kernels, score_tiles(): pl.pallas_call(kernel, in_specs=[SMEM] + [VMEM] * len(arrays) + [VMEM, VM...  38.2 us
    ppermute x28, waiting for transfers between devices, hop(): return lax.ppermute(value, 'query', [(i, i ^ bits) for i in range(NQ)])  25.3 us
    ppermute x28, starting transfers between devices, hop(): return lax.ppermute(value, 'query', [(i, i ^ bits) for i in range(NQ)])  20.1 us
    unnamed x16, local copies, waits for them, and re-layouts  7.53 us
    ppermute x1, waiting for transfers between devices, paired_body(): ids_other = lax.ppermute(after(ids, mine), 'parts', SWAP)  3.41 us
    ppermute x1, starting transfers between devices, paired_body(): train_other = lax.ppermute(train_inputs, 'parts', SWAP)  3 us
    ppermute x1, waiting for transfers between devices, paired_body(): total = keep + lax.ppermute(give, 'parts', SWAP)  2.49 us
  transfers between devices with their start and end apart: 33, of which 15 were waited for; matrix products, arithmetic and copies ran while one was open for 1% of the time, Pallas kernels for 21%

profile of v10, /device:TPU:0, one launch (start us, length us, event | category | flops | bytes accessed | tf_op | source)
XLA Modules:
  0.0 109.9 jit_solution(9484300701792768521)
XLA Ops:
  0.6 3.0 %collective-permute-start.1 = (bf16[2,8,4096]{2,1,0:T(8,128)(2,1)}, bf16[2,8,4096]{2,1,0:T(8,128)(2,1)S(1)}, u32[]{:S(2)}, u32[]{:S(2)}) collective-permute-start(bf16[2,8,4096]{2,1,0:T(8,128)(2,1)} %own.2), channel_id=1, source_target_pairs={{0,16},{16,0},{1,17},{17,1},{2,18},{18,2},{3,19},{19,3},{4,20},{20... | collective-permute-start | bytes 393224 | tf_op jit(solution)/shard_map/ppermute | solution.py:341
  5.0 3.4 %collective-permute-done.ids_other = s32[1,128]{1,0:T(1,128)S(1)} collective-permute-done((s32[1,128]{1,0:T(1,128)}, s32[1,128]{1,0:T(1,128)S(1)}, u32[]{:S(2)}, u32[]{:S(2)}) %collective-permute-start) | collective-permute-done | bytes 544 | tf_op jit(solution)/shard_map/ppermute | solution.py:348
  12.8 1.6 %collective-permute-start.2 = (bf16[20,32,128]{2,1,0:T(8,128)(2,1)S(1)}, bf16[20,32,128]{2,1,0:T(8,128)(2,1)S(1)}, u32[]{:S(2)}, u32[]{:S(2)}) collective-permute-start(bf16[20,32,128]{2,1,0:T(8,128)(2,1)S(1)} %get-tuple-element.35.refs_0_), channel_id=1, source_target_pairs={{0,4},{1,5},{2,6},{3,7},{4,0},{5,1},{6,2},{7,3},{8,12},{9,13},{10,... | collective-permute-start | bytes 491528 | tf_op jit(solution)/shard_map/ppermute | solution.py:90
  14.4 2.5 %collective-permute-start.3 = (bf16[20,32,128]{2,1,0:T(8,128)(2,1)S(1)}, bf16[20,32,128]{2,1,0:T(8,128)(2,1)S(1)}, u32[]{:S(2)}, u32[]{:S(2)}) collective-permute-start(bf16[20,32,128]{2,1,0:T(8,128)(2,1)S(1)} %get-tuple-element.35.refs_0_), channel_id=1, source_target_pairs={{0,12},{1,13},{2,14},{3,15},{4,8},{5,9},{6,10},{7,11},{8,4},{9,5},... | collective-permute-start | bytes 491528 | tf_op jit(solution)/shard_map/ppermute | solution.py:90
  16.8 1.0 copy-done
  17.8 1.1 %copy-done.2 = bf16[2,256,768]{2,1,0:T(8,128)(2,1)S(1)} copy-done((bf16[2,256,768]{2,1,0:T(8,128)(2,1)S(1)}, bf16[2,256,768]{2,1,0:T(8,128)(2,1)}, u32[]{:S(2)}) %copy-start.2) | copy-done | bytes 786456
  19.5 1.6 %collective-permute-start.10 = (bf16[20,32,128]{2,1,0:T(8,128)(2,1)S(1)}, bf16[20,32,128]{2,1,0:T(8,128)(2,1)S(1)}, u32[]{:S(2)}, u32[]{:S(2)}) collective-permute-start(bf16[20,32,128]{2,1,0:T(8,128)(2,1)S(1)} %get-tuple-element.35.refs_0_), channel_id=1, source_target_pairs={{0,2},{1,3},{2,0},{3,1},{4,6},{5,7},{6,4},{7,5},{8,10},{9,11},{10,... | collective-permute-start | bytes 491528 | tf_op jit(solution)/shard_map/ppermute | solution.py:90
  21.1 2.0 %collective-permute-done.3.refs_12_ = bf16[20,32,128]{2,1,0:T(8,128)(2,1)S(1)} collective-permute-done((bf16[20,32,128]{2,1,0:T(8,128)(2,1)S(1)}, bf16[20,32,128]{2,1,0:T(8,128)(2,1)S(1)}, u32[]{:S(2)}, u32[]{:S(2)}) %collective-permute-start.3) | collective-permute-done | bytes 163872 | tf_op jit(solution)/shard_map/ppermute | solution.py:90
  23.2 3.8 %collective-permute-start.4 = (bf16[20,32,128]{2,1,0:T(8,128)(2,1)S(1)}, bf16[20,32,128]{2,1,0:T(8,128)(2,1)S(1)}, u32[]{:S(2)}, u32[]{:S(2)}) collective-permute-start(bf16[20,32,128]{2,1,0:T(8,128)(2,1)S(1)} %get-tuple-element.35.refs_0_), channel_id=1, source_target_pairs={{0,8},{1,9},{2,10},{3,11},{4,12},{5,13},{6,14},{7,15},{8,0},{9,1},... | collective-permute-start | bytes 491528 | tf_op jit(solution)/shard_map/ppermute | solution.py:90
  26.9 1.5 %collective-permute-start.13 = (bf16[20,32,128]{2,1,0:T(8,128)(2,1)S(1)}, bf16[20,32,128]{2,1,0:T(8,128)(2,1)S(1)}, u32[]{:S(2)}, u32[]{:S(2)}) collective-permute-start(bf16[20,32,128]{2,1,0:T(8,128)(2,1)S(1)} %collective-permute-done.2.refs_4_), channel_id=1, source_target_pairs={{0,2},{1,3},{2,0},{3,1},{4,6},{5,7},{6,4},{7,5},{8,10},{9,11},{10,... | collective-permute-start | bytes 491528 | tf_op jit(solution)/shard_map/ppermute | solution.py:90
  29.5 2.5 %collective-permute-done.4.refs_8_ = bf16[20,32,128]{2,1,0:T(8,128)(2,1)S(1)} collective-permute-done((bf16[20,32,128]{2,1,0:T(8,128)(2,1)S(1)}, bf16[20,32,128]{2,1,0:T(8,128)(2,1)S(1)}, u32[]{:S(2)}, u32[]{:S(2)}) %collective-permute-start.4) | collective-permute-done | bytes 163872 | tf_op jit(solution)/shard_map/ppermute | solution.py:90
  32.3 1.8 %collective-permute-done.17.refs_14_ = bf16[20,32,128]{2,1,0:T(8,128)(2,1)S(1)} collective-permute-done((bf16[20,32,128]{2,1,0:T(8,128)(2,1)S(1)}, bf16[20,32,128]{2,1,0:T(8,128)(2,1)S(1)}, u32[]{:S(2)}, u32[]{:S(2)}) %collective-permute-start.17) | collective-permute-done | bytes 163872 | tf_op jit(solution)/shard_map/ppermute | solution.py:90
  34.0 1.5 %collective-permute-start.18 = (bf16[20,32,128]{2,1,0:T(8,128)(2,1)S(1)}, bf16[20,32,128]{2,1,0:T(8,128)(2,1)S(1)}, u32[]{:S(2)}, u32[]{:S(2)}) collective-permute-start(bf16[20,32,128]{2,1,0:T(8,128)(2,1)S(1)} %collective-permute-done.4.refs_8_), channel_id=1, source_target_pairs={{0,2},{1,3},{2,0},{3,1},{4,6},{5,7},{6,4},{7,5},{8,10},{9,11},{10,... | collective-permute-start | bytes 491528 | tf_op jit(solution)/shard_map/ppermute | solution.py:90
  35.5 1.0 copy-done.1
  36.5 1.0 copy-done.3
  38.2 1.0 shard_map.106
  40.8 1.1 collective-permute-start.6
  41.8 2.0 %collective-permute-start.7 = (bf16[20,32,128]{2,1,0:T(8,128)(2,1)S(1)}, bf16[20,32,128]{2,1,0:T(8,128)(2,1)S(1)}, u32[]{:S(2)}, u32[]{:S(2)}) collective-permute-start(bf16[20,32,128]{2,1,0:T(8,128)(2,1)S(1)} %get-tuple-element.36.refs_0_), channel_id=1, source_target_pairs={{0,8},{1,9},{2,10},{3,11},{4,12},{5,13},{6,14},{7,15},{8,0},{9,1},... | collective-permute-start | bytes 491528 | tf_op jit(solution)/shard_map/ppermute | solution.py:90
  44.4 10.2 %shard_map.107 = (f32[8,256]{1,0:T(8,128)S(1)}, bf16[8,8,128]{2,1,0:T(8,128)(2,1)S(1)}, bf16[8,8,128]{2,1,0:T(8,128)(2,1)S(1)}) custom-call(s32[66]{0:T(128)S(1)} %pad_add_fusion.info.info_ref, bf16[20,32,128]{2,1,0:T(8,128)(2,1)S(1)} %get-tuple-element.35.refs_0_, bf16[20,32,128]{2,1,0:T(8,128)(2,1)S(1)} %collective-permute-done.9.refs_1_, ...), custom_call_target="tpu_custom_call" | custom-call | flops 80000000 | bytes 4000000 | tf_op jit(solution)/shard_map/pallas_call | solution.py:283
  54.6 4.0 %collective-permute-done.7 = bf16[20,32,128]{2,1,0:T(8,128)(2,1)S(1)} collective-permute-done((bf16[20,32,128]{2,1,0:T(8,128)(2,1)S(1)}, bf16[20,32,128]{2,1,0:T(8,128)(2,1)S(1)}, u32[]{:S(2)}, u32[]{:S(2)}) %collective-permute-start.7) | collective-permute-done | bytes 163872 | tf_op jit(solution)/shard_map/ppermute | solution.py:90
  59.3 10.0 %shard_map.108 = (f32[8,256]{1,0:T(8,128)S(1)}, bf16[8,8,128]{2,1,0:T(8,128)(2,1)S(1)}, bf16[8,8,128]{2,1,0:T(8,128)(2,1)S(1)}) custom-call(s32[66]{0:T(128)S(1)} %pad_add_fusion.info.info_ref, bf16[20,32,128]{2,1,0:T(8,128)(2,1)S(1)} %get-tuple-element.35.refs_0_, bf16[20,32,128]{2,1,0:T(8,128)(2,1)S(1)} %collective-permute-done.9.refs_1_, ...), custom_call_target="tpu_custom_call" | custom-call | flops 8000000000 | bytes 4000000 | tf_op jit(solution)/shard_map/pallas_call | solution.py:283
  69.3 1.9 %collective-permute-done.22.refs_3_ = bf16[3,20,32,128]{3,2,1,0:T(8,128)(2,1)S(1)} collective-permute-done((bf16[3,20,32,128]{3,2,1,0:T(8,128)(2,1)S(1)}, bf16[3,20,32,128]{3,2,1,0:T(8,128)(2,1)S(1)}, u32[]{:S(2)}, u32[]{:S(2)}) %collective-permute-start.22) | collective-permute-done | bytes 491552 | tf_op jit(solution)/shard_map/ppermute | solution.py:90
  71.7 1.6 %collective-permute-done.23.refs_4_ = bf16[20,32,128]{2,1,0:T(8,128)(2,1)S(1)} collective-permute-done((bf16[20,32,128]{2,1,0:T(8,128)(2,1)S(1)}, bf16[20,32,128]{2,1,0:T(8,128)(2,1)S(1)}, u32[]{:S(2)}, u32[]{:S(2)}) %collective-permute-start.23) | collective-permute-done | bytes 163872 | tf_op jit(solution)/shard_map/ppermute | solution.py:90
  73.5 18.1 %shard_map.109 = (f32[4,256]{1,0:T(4,128)S(1)}, f32[4,256]{1,0:T(4,128)S(1)}, bf16[16,8,128]{2,1,0:T(8,128)(2,1)S(1)}, bf16[16,8,128]{2,1,0:T(8,128)(2,1)S(1)}) custom-call(s32[66]{0:T(128)S(1)} %pad_add_fusion.info.info_ref, bf16[20,32,128]{2,1,0:T(8,128)(2,1)S(1)} %get-tuple-element.36.refs_0_, bf16[20,32,128]{2,1,0:T(8,128)(2,1)S(1)} %collective-permute-done.8.refs_1_, ...), custom_call_target="tpu_custom_call" | custom-call | flops 16000000000 | bytes 8000000 | tf_op jit(solution)/shard_map/pallas_call | solution.py:283
  91.7 1.0 collective-permute-start.28
  92.6 1.1 %collective-permute-start.27 = (f32[4,256]{1,0:T(4,128)S(1)}, f32[4,256]{1,0:T(4,128)S(1)}, u32[]{:S(2)}, u32[]{:S(2)}) collective-permute-start(f32[4,256]{1,0:T(4,128)S(1)} %get-tuple-element.51), channel_id=1, source_target_pairs={{0,16},{16,0},{1,17},{17,1},{2,18},{18,2},{3,19},{19,3},{4,20},{20... | collective-permute-start | bytes 12296 | tf_op jit(solution)/shard_map/ppermute | solution.py:419
  93.8 2.5 %collective-permute-done.27 = f32[4,256]{1,0:T(4,128)S(1)} collective-permute-done((f32[4,256]{1,0:T(4,128)S(1)}, f32[4,256]{1,0:T(4,128)S(1)}, u32[]{:S(2)}, u32[]{:S(2)}) %collective-permute-start.27) | collective-permute-done | bytes 4128 | tf_op jit(solution)/shard_map/ppermute | solution.py:419
  96.3 1.2 %collective-permute-done.29 = f32[4,256]{1,0:T(4,128)S(1)} collective-permute-done((f32[4,256]{1,0:T(4,128)S(1)}, f32[4,256]{1,0:T(4,128)S(1)}, u32[]{:S(2)}, u32[]{:S(2)}) %collective-permute-start.29) | collective-permute-done | bytes 4128 | tf_op jit(solution)/shard_map/ppermute | solution.py:90
  98.0 3.0 %collective-permute-done.30 = f32[4,256]{1,0:T(4,128)S(1)} collective-permute-done((f32[4,256]{1,0:T(4,128)S(1)}, f32[4,256]{1,0:T(4,128)S(1)}, u32[]{:S(2)}, u32[]{:S(2)}) %collective-permute-start.30) | collective-permute-done | bytes 4128 | tf_op jit(solution)/shard_map/ppermute | solution.py:90
  101.0 1.6 %shard_map.110 = bf16[2,8,4096]{2,1,0:T(8,128)(2,1)} custom-call(s32[66]{0:T(128)S(1)} %pad_add_fusion.info.info_ref, bf16[8,8,128]{2,1,0:T(8,128)(2,1)S(1)} %get-tuple-element.56.kept_a, bf16[8,8,128]{2,1,0:T(8,128)(2,1)S(1)} %get-tuple-element.57.kept_b, bf16[16,8,128]{2,1,0:T(8,128)(2,1)S(1)} %get-tuple-element.58.kept_c, ...), custom_call_target="tpu_custom_call" | custom-call | tf_op jit(solution)/shard_map/pallas_call | solution.py:422
  102.7 2.0 %collective-permute-done.31 = f32[4,256]{1,0:T(4,128)S(1)} collective-permute-done((f32[4,256]{1,0:T(4,128)S(1)}, f32[4,256]{1,0:T(4,128)S(1)}, u32[]{:S(2)}, u32[]{:S(2)}) %collective-permute-start.31) | collective-permute-done | bytes 4128 | tf_op jit(solution)/shard_map/ppermute | solution.py:90
  104.7 4.4 %collective-permute-done.32 = f32[4,256]{1,0:T(4,128)S(1)} collective-permute-done((f32[4,256]{1,0:T(4,128)S(1)}, f32[4,256]{1,0:T(4,128)S(1)}, u32[]{:S(2)}, u32[]{:S(2)}) %collective-permute-start.32) | collective-permute-done | bytes 4128 | tf_op jit(solution)/shard_map/ppermute | solution.py:90
  (75 shorter events, 13.3 us)
Async XLA Ops:
  0.6 7.8 %collective-permute-start.1 = (bf16[2,8,4096]{2,1,0:T(8,128)(2,1)}, bf16[2,8,4096]{2,1,0:T(8,128)(2,1)S(1)}, u32[]{:S(2)}, u32[]{:S(2)}) collective-permute-start(bf16[2,8,4096]{2,1,0:T(8,128)(2,1)} %own.2), channel_id=1, source_target_pairs={{0,16},{16,0},{1,17},{17,1},{2,18},{18,2},{3,19},{19,3},{4,20},{20... | collective-permute-start | bytes 393224 | tf_op jit(solution)/shard_map/ppermute | solution.py:341
  4.7 3.7 %collective-permute-start = (s32[1,128]{1,0:T(1,128)}, s32[1,128]{1,0:T(1,128)S(1)}, u32[]{:S(2)}, u32[]{:S(2)}) collective-permute-start(s32[1,128]{1,0:T(1,128)} %bitcast.8), channel_id=1, source_target_pairs={{0,16},{16,0},{1,17},{17,1},{2,18},{18,2},{3,19},{19,3},{4,20},{20... | collective-permute-start | bytes 1544 | tf_op jit(solution)/shard_map/ppermute | solution.py:348
  12.0 16.5 %collective-permute-start.16 = (bf16[2,128,768]{2,1,0:T(8,128)(2,1)}, bf16[2,128,768]{2,1,0:T(8,128)(2,1)S(1)}, u32[]{:S(2)}, u32[]{:S(2)}) collective-permute-start(bf16[2,128,768]{2,1,0:T(8,128)(2,1)} %own.3), channel_id=1, source_target_pairs={{0,16},{16,0},{1,17},{17,1},{2,18},{18,2},{3,19},{19,3},{4,20},{20... | collective-permute-start | bytes 1179656 | tf_op jit(solution)/shard_map/ppermute | solution.py:360
  12.8 8.3 %collective-permute-start.2 = (bf16[20,32,128]{2,1,0:T(8,128)(2,1)S(1)}, bf16[20,32,128]{2,1,0:T(8,128)(2,1)S(1)}, u32[]{:S(2)}, u32[]{:S(2)}) collective-permute-start(bf16[20,32,128]{2,1,0:T(8,128)(2,1)S(1)} %get-tuple-element.35.refs_0_), channel_id=1, source_target_pairs={{0,4},{1,5},{2,6},{3,7},{4,0},{5,1},{6,2},{7,3},{8,12},{9,13},{10,... | collective-permute-start | bytes 491528 | tf_op jit(solution)/shard_map/ppermute | solution.py:90
  14.4 8.8 %collective-permute-start.3 = (bf16[20,32,128]{2,1,0:T(8,128)(2,1)S(1)}, bf16[20,32,128]{2,1,0:T(8,128)(2,1)S(1)}, u32[]{:S(2)}, u32[]{:S(2)}) collective-permute-start(bf16[20,32,128]{2,1,0:T(8,128)(2,1)S(1)} %get-tuple-element.35.refs_0_), channel_id=1, source_target_pairs={{0,12},{1,13},{2,14},{3,15},{4,8},{5,9},{6,10},{7,11},{8,4},{9,5},... | collective-permute-start | bytes 491528 | tf_op jit(solution)/shard_map/ppermute | solution.py:90
  19.5 9.4 %collective-permute-start.10 = (bf16[20,32,128]{2,1,0:T(8,128)(2,1)S(1)}, bf16[20,32,128]{2,1,0:T(8,128)(2,1)S(1)}, u32[]{:S(2)}, u32[]{:S(2)}) collective-permute-start(bf16[20,32,128]{2,1,0:T(8,128)(2,1)S(1)} %get-tuple-element.35.refs_0_), channel_id=1, source_target_pairs={{0,2},{1,3},{2,0},{3,1},{4,6},{5,7},{6,4},{7,5},{8,10},{9,11},{10,... | collective-permute-start | bytes 491528 | tf_op jit(solution)/shard_map/ppermute | solution.py:90
  23.2 8.8 %collective-permute-start.4 = (bf16[20,32,128]{2,1,0:T(8,128)(2,1)S(1)}, bf16[20,32,128]{2,1,0:T(8,128)(2,1)S(1)}, u32[]{:S(2)}, u32[]{:S(2)}) collective-permute-start(bf16[20,32,128]{2,1,0:T(8,128)(2,1)S(1)} %get-tuple-element.35.refs_0_), channel_id=1, source_target_pairs={{0,8},{1,9},{2,10},{3,11},{4,12},{5,13},{6,14},{7,15},{8,0},{9,1},... | collective-permute-start | bytes 491528 | tf_op jit(solution)/shard_map/ppermute | solution.py:90
  26.9 5.3 %collective-permute-start.13 = (bf16[20,32,128]{2,1,0:T(8,128)(2,1)S(1)}, bf16[20,32,128]{2,1,0:T(8,128)(2,1)S(1)}, u32[]{:S(2)}, u32[]{:S(2)}) collective-permute-start(bf16[20,32,128]{2,1,0:T(8,128)(2,1)S(1)} %collective-permute-done.2.refs_4_), channel_id=1, source_target_pairs={{0,2},{1,3},{2,0},{3,1},{4,6},{5,7},{6,4},{7,5},{8,10},{9,11},{10,... | collective-permute-start | bytes 491528 | tf_op jit(solution)/shard_map/ppermute | solution.py:90
  28.5 5.6 %collective-permute-start.17 = (bf16[20,32,128]{2,1,0:T(8,128)(2,1)S(1)}, bf16[20,32,128]{2,1,0:T(8,128)(2,1)S(1)}, u32[]{:S(2)}, u32[]{:S(2)}) collective-permute-start(bf16[20,32,128]{2,1,0:T(8,128)(2,1)S(1)} %collective-permute-done.3.refs_12_), channel_id=1, source_target_pairs={{0,2},{1,3},{2,0},{3,1},{4,6},{5,7},{6,4},{7,5},{8,10},{9,11},{10,... | collective-permute-start | bytes 491528 | tf_op jit(solution)/shard_map/ppermute | solution.py:90
  29.0 10.2 %collective-permute-start.9 = (bf16[20,32,128]{2,1,0:T(8,128)(2,1)S(1)}, bf16[20,32,128]{2,1,0:T(8,128)(2,1)S(1)}, u32[]{:S(2)}, u32[]{:S(2)}) collective-permute-start(bf16[20,32,128]{2,1,0:T(8,128)(2,1)S(1)} %get-tuple-element.35.refs_0_), channel_id=1, source_target_pairs={{0,1},{1,0},{2,3},{3,2},{4,5},{5,4},{6,7},{7,6},{8,9},{9,8},{10,11... | collective-permute-start | bytes 491528 | tf_op jit(solution)/shard_map/ppermute | solution.py:90
  29.0 10.8 %collective-permute-start.12 = (bf16[20,32,128]{2,1,0:T(8,128)(2,1)S(1)}, bf16[20,32,128]{2,1,0:T(8,128)(2,1)S(1)}, u32[]{:S(2)}, u32[]{:S(2)}) collective-permute-start(bf16[20,32,128]{2,1,0:T(8,128)(2,1)S(1)} %collective-permute-done.2.refs_4_), channel_id=1, source_target_pairs={{0,1},{1,0},{2,3},{3,2},{4,5},{5,4},{6,7},{7,6},{8,9},{9,8},{10,11... | collective-permute-start | bytes 491528 | tf_op jit(solution)/shard_map/ppermute | solution.py:90
  32.0 7.9 %collective-permute-start.20 = (bf16[20,32,128]{2,1,0:T(8,128)(2,1)S(1)}, bf16[20,32,128]{2,1,0:T(8,128)(2,1)S(1)}, u32[]{:S(2)}, u32[]{:S(2)}) collective-permute-start(bf16[20,32,128]{2,1,0:T(8,128)(2,1)S(1)} %collective-permute-done.3.refs_12_), channel_id=1, source_target_pairs={{0,1},{1,0},{2,3},{3,2},{4,5},{5,4},{6,7},{7,6},{8,9},{9,8},{10,11... | collective-permute-start | bytes 491528 | tf_op jit(solution)/shard_map/ppermute | solution.py:90
  34.0 6.3 %collective-permute-start.18 = (bf16[20,32,128]{2,1,0:T(8,128)(2,1)S(1)}, bf16[20,32,128]{2,1,0:T(8,128)(2,1)S(1)}, u32[]{:S(2)}, u32[]{:S(2)}) collective-permute-start(bf16[20,32,128]{2,1,0:T(8,128)(2,1)S(1)} %collective-permute-done.4.refs_8_), channel_id=1, source_target_pairs={{0,2},{1,3},{2,0},{3,1},{4,6},{5,7},{6,4},{7,5},{8,10},{9,11},{10,... | collective-permute-start | bytes 491528 | tf_op jit(solution)/shard_map/ppermute | solution.py:90
  35.5 4.8 %collective-permute-start.11 = (bf16[20,32,128]{2,1,0:T(8,128)(2,1)S(1)}, bf16[20,32,128]{2,1,0:T(8,128)(2,1)S(1)}, u32[]{:S(2)}, u32[]{:S(2)}) collective-permute-start(bf16[20,32,128]{2,1,0:T(8,128)(2,1)S(1)} %collective-permute-done.10.refs_2_), channel_id=1, source_target_pairs={{0,1},{1,0},{2,3},{3,2},{4,5},{5,4},{6,7},{7,6},{8,9},{9,8},{10,11... | collective-permute-start | bytes 491528 | tf_op jit(solution)/shard_map/ppermute | solution.py:90
  39.2 1.6 %collective-permute-start.15 = (bf16[20,32,128]{2,1,0:T(8,128)(2,1)S(1)}, bf16[20,32,128]{2,1,0:T(8,128)(2,1)S(1)}, u32[]{:S(2)}, u32[]{:S(2)}) collective-permute-start(bf16[20,32,128]{2,1,0:T(8,128)(2,1)S(1)} %collective-permute-done.4.refs_8_), channel_id=1, source_target_pairs={{0,1},{1,0},{2,3},{3,2},{4,5},{5,4},{6,7},{7,6},{8,9},{9,8},{10,11... | collective-permute-start | bytes 491528 | tf_op jit(solution)/shard_map/ppermute | solution.py:90
  39.7 2.1 %collective-permute-start.14 = (bf16[20,32,128]{2,1,0:T(8,128)(2,1)S(1)}, bf16[20,32,128]{2,1,0:T(8,128)(2,1)S(1)}, u32[]{:S(2)}, u32[]{:S(2)}) collective-permute-start(bf16[20,32,128]{2,1,0:T(8,128)(2,1)S(1)} %collective-permute-done.13.refs_6_), channel_id=1, source_target_pairs={{0,1},{1,0},{2,3},{3,2},{4,5},{5,4},{6,7},{7,6},{8,9},{9,8},{10,11... | collective-permute-start | bytes 491528 | tf_op jit(solution)/shard_map/ppermute | solution.py:90
  39.8 4.0 %collective-permute-start.21 = (bf16[20,32,128]{2,1,0:T(8,128)(2,1)S(1)}, bf16[20,32,128]{2,1,0:T(8,128)(2,1)S(1)}, u32[]{:S(2)}, u32[]{:S(2)}) collective-permute-start(bf16[20,32,128]{2,1,0:T(8,128)(2,1)S(1)} %collective-permute-done.17.refs_14_), channel_id=1, source_target_pairs={{0,1},{1,0},{2,3},{3,2},{4,5},{5,4},{6,7},{7,6},{8,9},{9,8},{10,11... | collective-permute-start | bytes 491528 | tf_op jit(solution)/shard_map/ppermute | solution.py:90
  40.3 4.1 %collective-permute-start.19 = (bf16[20,32,128]{2,1,0:T(8,128)(2,1)S(1)}, bf16[20,32,128]{2,1,0:T(8,128)(2,1)S(1)}, u32[]{:S(2)}, u32[]{:S(2)}) collective-permute-start(bf16[20,32,128]{2,1,0:T(8,128)(2,1)S(1)} %collective-permute-done.18.refs_10_), channel_id=1, source_target_pairs={{0,1},{1,0},{2,3},{3,2},{4,5},{5,4},{6,7},{7,6},{8,9},{9,8},{10,11... | collective-permute-start | bytes 491528 | tf_op jit(solution)/shard_map/ppermute | solution.py:90
  40.4 14.2 %collective-permute-start.5 = (bf16[20,32,128]{2,1,0:T(8,128)(2,1)S(1)}, bf16[20,32,128]{2,1,0:T(8,128)(2,1)S(1)}, u32[]{:S(2)}, u32[]{:S(2)}) collective-permute-start(bf16[20,32,128]{2,1,0:T(8,128)(2,1)S(1)} %get-tuple-element.36.refs_0_), channel_id=1, source_target_pairs={{0,4},{1,5},{2,6},{3,7},{4,0},{5,1},{6,2},{7,3},{8,12},{9,13},{10,... | collective-permute-start | bytes 491528 | tf_op jit(solution)/shard_map/ppermute | solution.py:90
  40.8 13.8 %collective-permute-start.6 = (bf16[20,32,128]{2,1,0:T(8,128)(2,1)S(1)}, bf16[20,32,128]{2,1,0:T(8,128)(2,1)S(1)}, u32[]{:S(2)}, u32[]{:S(2)}) collective-permute-start(bf16[20,32,128]{2,1,0:T(8,128)(2,1)S(1)} %get-tuple-element.36.refs_0_), channel_id=1, source_target_pairs={{0,12},{1,13},{2,14},{3,15},{4,8},{5,9},{6,10},{7,11},{8,4},{9,5},... | collective-permute-start | bytes 491528 | tf_op jit(solution)/shard_map/ppermute | solution.py:90
  41.8 16.8 %collective-permute-start.7 = (bf16[20,32,128]{2,1,0:T(8,128)(2,1)S(1)}, bf16[20,32,128]{2,1,0:T(8,128)(2,1)S(1)}, u32[]{:S(2)}, u32[]{:S(2)}) collective-permute-start(bf16[20,32,128]{2,1,0:T(8,128)(2,1)S(1)} %get-tuple-element.36.refs_0_), channel_id=1, source_target_pairs={{0,8},{1,9},{2,10},{3,11},{4,12},{5,13},{6,14},{7,15},{8,0},{9,1},... | collective-permute-start | bytes 491528 | tf_op jit(solution)/shard_map/ppermute | solution.py:90
  43.9 14.8 %collective-permute-start.8 = (bf16[20,32,128]{2,1,0:T(8,128)(2,1)S(1)}, bf16[20,32,128]{2,1,0:T(8,128)(2,1)S(1)}, u32[]{:S(2)}, u32[]{:S(2)}) collective-permute-start(bf16[20,32,128]{2,1,0:T(8,128)(2,1)S(1)} %get-tuple-element.36.refs_0_), channel_id=1, source_target_pairs={{0,2},{1,3},{2,0},{3,1},{4,6},{5,7},{6,4},{7,5},{8,10},{9,11},{10,... | collective-permute-start | bytes 491528 | tf_op jit(solution)/shard_map/ppermute | solution.py:90
  58.7 12.5 %collective-permute-start.22 = (bf16[3,20,32,128]{3,2,1,0:T(8,128)(2,1)S(1)}, bf16[3,20,32,128]{3,2,1,0:T(8,128)(2,1)S(1)}, u32[]{:S(2)}, u32[]{:S(2)}) collective-permute-start(bf16[3,20,32,128]{3,2,1,0:T(8,128)(2,1)S(1)} %pad_maximum_fusion.refs_2_), channel_id=1, source_target_pairs={{0,2},{1,3},{2,0},{3,1},{4,6},{5,7},{6,4},{7,5},{8,10},{9,11},{10,... | collective-permute-start | bytes 1474568 | tf_op jit(solution)/shard_map/ppermute | solution.py:90
  59.3 14.2 %collective-permute-start.25 = (bf16[3,20,32,128]{3,2,1,0:T(8,128)(2,1)S(1)}, bf16[3,20,32,128]{3,2,1,0:T(8,128)(2,1)S(1)}, u32[]{:S(2)}, u32[]{:S(2)}) collective-permute-start(bf16[3,20,32,128]{3,2,1,0:T(8,128)(2,1)S(1)} %pad_maximum_fusion.refs_2_), channel_id=1, source_target_pairs={{0,1},{1,0},{2,3},{3,2},{4,5},{5,4},{6,7},{7,6},{8,9},{9,8},{10,11... | collective-permute-start | bytes 1474568 | tf_op jit(solution)/shard_map/ppermute | solution.py:90
  71.2 2.3 %collective-permute-start.26 = (bf16[3,20,32,128]{3,2,1,0:T(8,128)(2,1)S(1)}, bf16[3,20,32,128]{3,2,1,0:T(8,128)(2,1)S(1)}, u32[]{:S(2)}, u32[]{:S(2)}) collective-permute-start(bf16[3,20,32,128]{3,2,1,0:T(8,128)(2,1)S(1)} %collective-permute-done.22.refs_3_), channel_id=1, source_target_pairs={{0,1},{1,0},{2,3},{3,2},{4,5},{5,4},{6,7},{7,6},{8,9},{9,8},{10,11... | collective-permute-start | bytes 1474568 | tf_op jit(solution)/shard_map/ppermute | solution.py:90
  71.2 2.1 %collective-permute-start.23 = (bf16[20,32,128]{2,1,0:T(8,128)(2,1)S(1)}, bf16[20,32,128]{2,1,0:T(8,128)(2,1)S(1)}, u32[]{:S(2)}, u32[]{:S(2)}) collective-permute-start(bf16[20,32,128]{2,1,0:T(8,128)(2,1)S(1)} %get-tuple-element.36.refs_0_), channel_id=1, source_target_pairs={{0,1},{1,0},{2,3},{3,2},{4,5},{5,4},{6,7},{7,6},{8,9},{9,8},{10,11... | collective-permute-start | bytes 491528 | tf_op jit(solution)/shard_map/ppermute | solution.py:90
  71.7 1.8 %collective-permute-start.24 = (bf16[20,32,128]{2,1,0:T(8,128)(2,1)S(1)}, bf16[20,32,128]{2,1,0:T(8,128)(2,1)S(1)}, u32[]{:S(2)}, u32[]{:S(2)}) collective-permute-start(bf16[20,32,128]{2,1,0:T(8,128)(2,1)S(1)} %collective-permute-done.8.refs_1_), channel_id=1, source_target_pairs={{0,1},{1,0},{2,3},{3,2},{4,5},{5,4},{6,7},{7,6},{8,9},{9,8},{10,11... | collective-permute-start | bytes 491528 | tf_op jit(solution)/shard_map/ppermute | solution.py:90
  91.7 4.6 %collective-permute-start.28 = (bf16[32,8,128]{2,1,0:T(8,128)(2,1)S(1)}, bf16[32,8,128]{2,1,0:T(8,128)(2,1)S(1)}, u32[]{:S(2)}, u32[]{:S(2)}) collective-permute-start(bf16[32,8,128]{2,1,0:T(8,128)(2,1)S(1)} %pad_maximum_fusion.1), channel_id=1, source_target_pairs={{0,16},{16,0},{1,17},{17,1},{2,18},{18,2},{3,19},{19,3},{4,20},{20... | collective-permute-start | bytes 196616 | tf_op jit(solution)/shard_map/ppermute | solution.py:420
  92.6 3.6 %collective-permute-start.27 = (f32[4,256]{1,0:T(4,128)S(1)}, f32[4,256]{1,0:T(4,128)S(1)}, u32[]{:S(2)}, u32[]{:S(2)}) collective-permute-start(f32[4,256]{1,0:T(4,128)S(1)} %get-tuple-element.51), channel_id=1, source_target_pairs={{0,16},{16,0},{1,17},{17,1},{2,18},{18,2},{3,19},{19,3},{4,20},{20... | collective-permute-start | bytes 12296 | tf_op jit(solution)/shard_map/ppermute | solution.py:419
  97.4 3.6 %collective-permute-start.30 = (f32[4,256]{1,0:T(4,128)S(1)}, f32[4,256]{1,0:T(4,128)S(1)}, u32[]{:S(2)}, u32[]{:S(2)}) collective-permute-start(f32[4,256]{1,0:T(4,128)S(1)} %add.16), channel_id=1, source_target_pairs={{0,2},{1,3},{2,0},{3,1},{4,6},{5,7},{6,4},{7,5},{8,10},{9,11},{10,... | collective-permute-start | bytes 12296 | tf_op jit(solution)/shard_map/ppermute | solution.py:90
  101.0 3.6 %collective-permute-start.31 = (f32[4,256]{1,0:T(4,128)S(1)}, f32[4,256]{1,0:T(4,128)S(1)}, u32[]{:S(2)}, u32[]{:S(2)}) collective-permute-start(f32[4,256]{1,0:T(4,128)S(1)} %add.17), channel_id=1, source_target_pairs={{0,4},{1,5},{2,6},{3,7},{4,0},{5,1},{6,2},{7,3},{8,12},{9,13},{10,... | collective-permute-start | bytes 12296 | tf_op jit(solution)/shard_map/ppermute | solution.py:90
  104.6 4.5 %collective-permute-start.32 = (f32[4,256]{1,0:T(4,128)S(1)}, f32[4,256]{1,0:T(4,128)S(1)}, u32[]{:S(2)}, u32[]{:S(2)}) collective-permute-start(f32[4,256]{1,0:T(4,128)S(1)} %add.18), channel_id=1, source_target_pairs={{0,8},{1,9},{2,10},{3,11},{4,12},{5,13},{6,14},{7,15},{8,0},{9,1},... | collective-permute-start | bytes 12296 | tf_op jit(solution)/shard_map/ppermute | solution.py:90
  (9 other events, 8.7 us)

commit v11 on v10

--- a/solution.py
+++ b/solution.py
@@ -345,7 +345,6 @@
     mine = jnp.where(x == 0, by_half[0], by_half[1])
     theirs = jnp.where(x == 0, by_half[1], by_half[0])
     ids = sequence_ids.reshape(1, sequence_ids.shape[0])
-    ids_other = lax.ppermute(after(ids, mine), "parts", SWAP)
     side = x.reshape(1).astype(jnp.int32)
     info = jnp.concatenate([me.reshape(1).astype(jnp.int32), mine, side, theirs])
 
@@ -355,8 +354,14 @@
         out_specs=[VMEM] * WAVES,
         out_shape=[jax.ShapeDtypeStruct((UNIT, 32, TILE_A), BF)] * WAVES,
         compiler_params=pltpu.CompilerParams(vmem_limit_bytes=8 * 1024 * 1024),
-    )(after(info, ids_other), train_inputs, train_other, query_inputs, input_basis)
-
+    )(info, train_inputs, train_other, query_inputs, input_basis)
+
+    units = [None] * NQ
+    units[0] = packed[0]
+    units[4] = hop(packed[0], 4)
+    units[12] = hop(packed[0], 12)
+
+    ids_other = lax.ppermute(after(ids, units[12]), "parts", SWAP)
     out_other = lax.ppermute(after(train_outgrads, packed[0]), "parts", SWAP)
     slab = train_outgrads.shape[2]
     little = pltpu.CompilerParams(vmem_limit_bytes=16 * 1024 * 1024)
@@ -378,10 +383,6 @@
         compiler_params=little,
     )(info, train_outgrads, out_other, ids, ids_other, output_basis)
 
-    units = [None] * NQ
-    units[0] = packed[0]
-    units[4] = hop(packed[0], 4)
-    units[12] = hop(packed[0], 12)
     units[8] = hop(after(packed[0], units[4], units[12], query_grads), 8)
     units[2] = hop(units[0], 2)
     units[6] = hop(units[4], 2)

time: 110 us -> 112 us (1.018)
  waiting for transfers between devices: 31.2 us -> 34.7 us
  starting transfers between devices: 26 us -> 24.3 us
    ppermute x28, starting transfers between devices: 20.1 us -> 16.9 us  [hop(): return lax.ppermute(value, 'query', [(i, i ^ bits) for i in range(NQ)])]
    ppermute x1, waiting for transfers between devices: 0.01 us -> 2.38 us  [paired_body(): train_other = lax.ppermute(train_inputs, 'parts', SWAP)]
    ppermute x28, waiting for transfers between devices: 25.3 us -> 26.9 us  [hop(): return lax.ppermute(value, 'query', [(i, i ^ bits) for i in range(NQ)])]
  transfers between devices with their start and end apart: 33 -> 33, of which waited for: 15 -> 14; matrix products, arithmetic and copies ran while one was open for 1% -> 1% of each run, Pallas kernels for 21% -> 21%
where the time goes in v11:
time: 112 us
  Pallas kernels  42.2 us (38%)
  waiting for transfers between devices  34.7 us (31%)
  starting transfers between devices  24.3 us (22%)
  local copies, waits for them, and re-layouts  8.07 us (7%)
  other arithmetic  1.61 us (1%)
    pallas_call x3, Pallas kernels, score_tiles(): pl.pallas_call(kernel, in_specs=[SMEM] + [VMEM] * len(arrays) + [VMEM, VM...  38.2 us
    ppermute x28, waiting for transfers between devices, hop(): return lax.ppermute(value, 'query', [(i, i ^ bits) for i in range(NQ)])  26.9 us
    ppermute x28, starting transfers between devices, hop(): return lax.ppermute(value, 'query', [(i, i ^ bits) for i in range(NQ)])  16.9 us
    unnamed x16, local copies, waits for them, and re-layouts  7.53 us
    ppermute x1, waiting for transfers between devices, paired_body(): ids_other = lax.ppermute(after(ids, units[12]), 'parts', SWAP)  3.14 us
    ppermute x1, starting transfers between devices, paired_body(): train_other = lax.ppermute(train_inputs, 'parts', SWAP)  3 us
    ppermute x1, waiting for transfers between devices, paired_body(): train_other = lax.ppermute(train_inputs, 'parts', SWAP)  2.38 us
    ppermute x1, waiting for transfers between devices, paired_body(): total = keep + lax.ppermute(give, 'parts', SWAP)  2.28 us
  transfers between devices with their start and end apart: 33, of which 14 were waited for; matrix products, arithmetic and copies ran while one was open for 1% of the time, Pallas kernels for 21%

profile of v11, /device:TPU:0, one launch (start us, length us, event | category | flops | bytes accessed | tf_op | source)
XLA Modules:
  0.0 111.7 jit_solution(10139776059444987943)
XLA Ops:
  0.6 3.0 %collective-permute-start = (bf16[2,8,4096]{2,1,0:T(8,128)(2,1)}, bf16[2,8,4096]{2,1,0:T(8,128)(2,1)S(1)}, u32[]{:S(2)}, u32[]{:S(2)}) collective-permute-start(bf16[2,8,4096]{2,1,0:T(8,128)(2,1)} %own.2), channel_id=1, source_target_pairs={{0,16},{16,0},{1,17},{17,1},{2,18},{18,2},{3,19},{19,3},{4,20},{20... | collective-permute-start | bytes 393224 | tf_op jit(solution)/shard_map/ppermute | solution.py:341
  5.0 2.4 %collective-permute-done.other = bf16[2,8,4096]{2,1,0:T(8,128)(2,1)S(1)} collective-permute-done((bf16[2,8,4096]{2,1,0:T(8,128)(2,1)}, bf16[2,8,4096]{2,1,0:T(8,128)(2,1)S(1)}, u32[]{:S(2)}, u32[]{:S(2)}) %collective-permute-start) | collective-permute-done | bytes 131104 | tf_op jit(solution)/shard_map/ppermute | solution.py:341
  7.3 0.9 copy-done.4
  8.3 0.9 copy-done.5
  10.9 1.8 %collective-permute-start.15 = (bf16[2,128,768]{2,1,0:T(8,128)(2,1)}, bf16[2,128,768]{2,1,0:T(8,128)(2,1)S(1)}, u32[]{:S(2)}, u32[]{:S(2)}) collective-permute-start(bf16[2,128,768]{2,1,0:T(8,128)(2,1)} %own.3), channel_id=1, source_target_pairs={{0,16},{16,0},{1,17},{17,1},{2,18},{18,2},{3,19},{19,3},{4,20},{20... | collective-permute-start | bytes 1179656 | tf_op jit(solution)/shard_map/ppermute | solution.py:365
  12.7 3.6 %collective-permute-start.2 = (bf16[20,32,128]{2,1,0:T(8,128)(2,1)S(1)}, bf16[20,32,128]{2,1,0:T(8,128)(2,1)S(1)}, u32[]{:S(2)}, u32[]{:S(2)}) collective-permute-start(bf16[20,32,128]{2,1,0:T(8,128)(2,1)S(1)} %get-tuple-element.32.refs_0_), channel_id=1, source_target_pairs={{0,12},{1,13},{2,14},{3,15},{4,8},{5,9},{6,10},{7,11},{8,4},{9,5},... | collective-permute-start | bytes 491528 | tf_op jit(solution)/shard_map/ppermute | solution.py:90
  16.3 1.0 copy-done
  17.3 1.1 %copy-done.2 = bf16[2,256,768]{2,1,0:T(8,128)(2,1)S(1)} copy-done((bf16[2,256,768]{2,1,0:T(8,128)(2,1)S(1)}, bf16[2,256,768]{2,1,0:T(8,128)(2,1)}, u32[]{:S(2)}) %copy-start.2) | copy-done | bytes 786456
  19.0 1.6 %collective-permute-start.9 = (bf16[20,32,128]{2,1,0:T(8,128)(2,1)S(1)}, bf16[20,32,128]{2,1,0:T(8,128)(2,1)S(1)}, u32[]{:S(2)}, u32[]{:S(2)}) collective-permute-start(bf16[20,32,128]{2,1,0:T(8,128)(2,1)S(1)} %get-tuple-element.32.refs_0_), channel_id=1, source_target_pairs={{0,2},{1,3},{2,0},{3,1},{4,6},{5,7},{6,4},{7,5},{8,10},{9,11},{10,... | collective-permute-start | bytes 491528 | tf_op jit(solution)/shard_map/ppermute | solution.py:90
  21.2 1.8 %collective-permute-done.1.refs_4_ = bf16[20,32,128]{2,1,0:T(8,128)(2,1)S(1)} collective-permute-done((bf16[20,32,128]{2,1,0:T(8,128)(2,1)S(1)}, bf16[20,32,128]{2,1,0:T(8,128)(2,1)S(1)}, u32[]{:S(2)}, u32[]{:S(2)}) %collective-permute-start.1) | collective-permute-done | bytes 163872 | tf_op jit(solution)/shard_map/ppermute | solution.py:90
  23.5 1.5 %collective-permute-start.12 = (bf16[20,32,128]{2,1,0:T(8,128)(2,1)S(1)}, bf16[20,32,128]{2,1,0:T(8,128)(2,1)S(1)}, u32[]{:S(2)}, u32[]{:S(2)}) collective-permute-start(bf16[20,32,128]{2,1,0:T(8,128)(2,1)S(1)} %collective-permute-done.1.refs_4_), channel_id=1, source_target_pairs={{0,2},{1,3},{2,0},{3,1},{4,6},{5,7},{6,4},{7,5},{8,10},{9,11},{10,... | collective-permute-start | bytes 491528 | tf_op jit(solution)/shard_map/ppermute | solution.py:90
  26.0 6.2 %collective-permute-done.3.refs_8_ = bf16[20,32,128]{2,1,0:T(8,128)(2,1)S(1)} collective-permute-done((bf16[20,32,128]{2,1,0:T(8,128)(2,1)S(1)}, bf16[20,32,128]{2,1,0:T(8,128)(2,1)S(1)}, u32[]{:S(2)}, u32[]{:S(2)}) %collective-permute-start.3) | collective-permute-done | bytes 163872 | tf_op jit(solution)/shard_map/ppermute | solution.py:90
  32.3 1.6 %collective-permute-start.17 = (bf16[20,32,128]{2,1,0:T(8,128)(2,1)S(1)}, bf16[20,32,128]{2,1,0:T(8,128)(2,1)S(1)}, u32[]{:S(2)}, u32[]{:S(2)}) collective-permute-start(bf16[20,32,128]{2,1,0:T(8,128)(2,1)S(1)} %collective-permute-done.3.refs_8_), channel_id=1, source_target_pairs={{0,2},{1,3},{2,0},{3,1},{4,6},{5,7},{6,4},{7,5},{8,10},{9,11},{10,... | collective-permute-start | bytes 491528 | tf_op jit(solution)/shard_map/ppermute | solution.py:90
  34.4 3.1 %collective-permute-done.20.ids_other = s32[1,128]{1,0:T(1,128)S(1)} collective-permute-done((s32[1,128]{1,0:T(1,128)}, s32[1,128]{1,0:T(1,128)S(1)}, u32[]{:S(2)}, u32[]{:S(2)}) %collective-permute-start.20) | collective-permute-done | bytes 544 | tf_op jit(solution)/shard_map/ppermute | solution.py:364
  37.5 1.0 copy-done.1
  38.5 1.0 copy-done.3
  40.2 1.0 shard_map.106
  42.3 1.1 %collective-permute-start.4 = (bf16[20,32,128]{2,1,0:T(8,128)(2,1)S(1)}, bf16[20,32,128]{2,1,0:T(8,128)(2,1)S(1)}, u32[]{:S(2)}, u32[]{:S(2)}) collective-permute-start(bf16[20,32,128]{2,1,0:T(8,128)(2,1)S(1)} %get-tuple-element.33.refs_0_), channel_id=1, source_target_pairs={{0,4},{1,5},{2,6},{3,7},{4,0},{5,1},{6,2},{7,3},{8,12},{9,13},{10,... | collective-permute-start | bytes 491528 | tf_op jit(solution)/shard_map/ppermute | solution.py:90
  43.5 2.0 %collective-permute-start.5 = (bf16[20,32,128]{2,1,0:T(8,128)(2,1)S(1)}, bf16[20,32,128]{2,1,0:T(8,128)(2,1)S(1)}, u32[]{:S(2)}, u32[]{:S(2)}) collective-permute-start(bf16[20,32,128]{2,1,0:T(8,128)(2,1)S(1)} %get-tuple-element.33.refs_0_), channel_id=1, source_target_pairs={{0,12},{1,13},{2,14},{3,15},{4,8},{5,9},{6,10},{7,11},{8,4},{9,5},... | collective-permute-start | bytes 491528 | tf_op jit(solution)/shard_map/ppermute | solution.py:90
  46.4 10.2 %shard_map.107 = (f32[8,256]{1,0:T(8,128)S(1)}, bf16[8,8,128]{2,1,0:T(8,128)(2,1)S(1)}, bf16[8,8,128]{2,1,0:T(8,128)(2,1)S(1)}) custom-call(s32[66]{0:T(128)S(1)} %pad_add_fusion.info.info_ref, bf16[20,32,128]{2,1,0:T(8,128)(2,1)S(1)} %get-tuple-element.32.refs_0_, bf16[20,32,128]{2,1,0:T(8,128)(2,1)S(1)} %collective-permute-done.8.refs_1_, ...), custom_call_target="tpu_custom_call" | custom-call | flops 80000000 | bytes 4000000 | tf_op jit(solution)/shard_map/pallas_call | solution.py:283
  56.5 4.1 %collective-permute-done.6 = bf16[20,32,128]{2,1,0:T(8,128)(2,1)S(1)} collective-permute-done((bf16[20,32,128]{2,1,0:T(8,128)(2,1)S(1)}, bf16[20,32,128]{2,1,0:T(8,128)(2,1)S(1)}, u32[]{:S(2)}, u32[]{:S(2)}) %collective-permute-start.6) | collective-permute-done | bytes 163872 | tf_op jit(solution)/shard_map/ppermute | solution.py:90
  61.2 10.0 %shard_map.108 = (f32[8,256]{1,0:T(8,128)S(1)}, bf16[8,8,128]{2,1,0:T(8,128)(2,1)S(1)}, bf16[8,8,128]{2,1,0:T(8,128)(2,1)S(1)}) custom-call(s32[66]{0:T(128)S(1)} %pad_add_fusion.info.info_ref, bf16[20,32,128]{2,1,0:T(8,128)(2,1)S(1)} %get-tuple-element.32.refs_0_, bf16[20,32,128]{2,1,0:T(8,128)(2,1)S(1)} %collective-permute-done.8.refs_1_, ...), custom_call_target="tpu_custom_call" | custom-call | flops 8000000000 | bytes 4000000 | tf_op jit(solution)/shard_map/pallas_call | solution.py:283
  71.2 2.0 %collective-permute-done.22.refs_3_ = bf16[3,20,32,128]{3,2,1,0:T(8,128)(2,1)S(1)} collective-permute-done((bf16[3,20,32,128]{3,2,1,0:T(8,128)(2,1)S(1)}, bf16[3,20,32,128]{3,2,1,0:T(8,128)(2,1)S(1)}, u32[]{:S(2)}, u32[]{:S(2)}) %collective-permute-start.22) | collective-permute-done | bytes 491552 | tf_op jit(solution)/shard_map/ppermute | solution.py:90
  73.7 1.6 %collective-permute-done.23.refs_4_ = bf16[20,32,128]{2,1,0:T(8,128)(2,1)S(1)} collective-permute-done((bf16[20,32,128]{2,1,0:T(8,128)(2,1)S(1)}, bf16[20,32,128]{2,1,0:T(8,128)(2,1)S(1)}, u32[]{:S(2)}, u32[]{:S(2)}) %collective-permute-start.23) | collective-permute-done | bytes 163872 | tf_op jit(solution)/shard_map/ppermute | solution.py:90
  75.5 18.1 %shard_map.109 = (f32[4,256]{1,0:T(4,128)S(1)}, f32[4,256]{1,0:T(4,128)S(1)}, bf16[16,8,128]{2,1,0:T(8,128)(2,1)S(1)}, bf16[16,8,128]{2,1,0:T(8,128)(2,1)S(1)}) custom-call(s32[66]{0:T(128)S(1)} %pad_add_fusion.info.info_ref, bf16[20,32,128]{2,1,0:T(8,128)(2,1)S(1)} %get-tuple-element.33.refs_0_, bf16[20,32,128]{2,1,0:T(8,128)(2,1)S(1)} %collective-permute-done.7.refs_1_, ...), custom_call_target="tpu_custom_call" | custom-call | flops 16000000000 | bytes 8000000 | tf_op jit(solution)/shard_map/pallas_call | solution.py:283
  94.3 1.5 %collective-permute-start.27 = (f32[4,256]{1,0:T(4,128)S(1)}, f32[4,256]{1,0:T(4,128)S(1)}, u32[]{:S(2)}, u32[]{:S(2)}) collective-permute-start(f32[4,256]{1,0:T(4,128)S(1)} %get-tuple-element.49), channel_id=1, source_target_pairs={{0,16},{16,0},{1,17},{17,1},{2,18},{18,2},{3,19},{19,3},{4,20},{20... | collective-permute-start | bytes 12296 | tf_op jit(solution)/shard_map/ppermute | solution.py:420
  95.8 2.3 %collective-permute-done.27 = f32[4,256]{1,0:T(4,128)S(1)} collective-permute-done((f32[4,256]{1,0:T(4,128)S(1)}, f32[4,256]{1,0:T(4,128)S(1)}, u32[]{:S(2)}, u32[]{:S(2)}) %collective-permute-start.27) | collective-permute-done | bytes 4128 | tf_op jit(solution)/shard_map/ppermute | solution.py:420
  98.1 1.2 %collective-permute-done.29 = f32[4,256]{1,0:T(4,128)S(1)} collective-permute-done((f32[4,256]{1,0:T(4,128)S(1)}, f32[4,256]{1,0:T(4,128)S(1)}, u32[]{:S(2)}, u32[]{:S(2)}) %collective-permute-start.29) | collective-permute-done | bytes 4128 | tf_op jit(solution)/shard_map/ppermute | solution.py:90
  99.7 3.1 %collective-permute-done.30 = f32[4,256]{1,0:T(4,128)S(1)} collective-permute-done((f32[4,256]{1,0:T(4,128)S(1)}, f32[4,256]{1,0:T(4,128)S(1)}, u32[]{:S(2)}, u32[]{:S(2)}) %collective-permute-start.30) | collective-permute-done | bytes 4128 | tf_op jit(solution)/shard_map/ppermute | solution.py:90
  102.8 1.6 %shard_map.110 = bf16[2,8,4096]{2,1,0:T(8,128)(2,1)} custom-call(s32[66]{0:T(128)S(1)} %pad_add_fusion.info.info_ref, bf16[8,8,128]{2,1,0:T(8,128)(2,1)S(1)} %get-tuple-element.54.kept_a, bf16[8,8,128]{2,1,0:T(8,128)(2,1)S(1)} %get-tuple-element.55.kept_b, bf16[16,8,128]{2,1,0:T(8,128)(2,1)S(1)} %get-tuple-element.56.kept_c, ...), custom_call_target="tpu_custom_call" | custom-call | tf_op jit(solution)/shard_map/pallas_call | solution.py:423
  104.5 2.0 %collective-permute-done.31 = f32[4,256]{1,0:T(4,128)S(1)} collective-permute-done((f32[4,256]{1,0:T(4,128)S(1)}, f32[4,256]{1,0:T(4,128)S(1)}, u32[]{:S(2)}, u32[]{:S(2)}) %collective-permute-start.31) | collective-permute-done | bytes 4128 | tf_op jit(solution)/shard_map/ppermute | solution.py:90
  106.8 4.2 %collective-permute-done.32 = f32[4,256]{1,0:T(4,128)S(1)} collective-permute-done((f32[4,256]{1,0:T(4,128)S(1)}, f32[4,256]{1,0:T(4,128)S(1)}, u32[]{:S(2)}, u32[]{:S(2)}) %collective-permute-start.32) | collective-permute-done | bytes 4128 | tf_op jit(solution)/shard_map/ppermute | solution.py:90
  (75 shorter events, 12.6 us)
Async XLA Ops:
  0.6 6.7 %collective-permute-start = (bf16[2,8,4096]{2,1,0:T(8,128)(2,1)}, bf16[2,8,4096]{2,1,0:T(8,128)(2,1)S(1)}, u32[]{:S(2)}, u32[]{:S(2)}) collective-permute-start(bf16[2,8,4096]{2,1,0:T(8,128)(2,1)} %own.2), channel_id=1, source_target_pairs={{0,16},{16,0},{1,17},{17,1},{2,18},{18,2},{3,19},{19,3},{4,20},{20... | collective-permute-start | bytes 393224 | tf_op jit(solution)/shard_map/ppermute | solution.py:341
  10.9 14.1 %collective-permute-start.15 = (bf16[2,128,768]{2,1,0:T(8,128)(2,1)}, bf16[2,128,768]{2,1,0:T(8,128)(2,1)S(1)}, u32[]{:S(2)}, u32[]{:S(2)}) collective-permute-start(bf16[2,128,768]{2,1,0:T(8,128)(2,1)} %own.3), channel_id=1, source_target_pairs={{0,16},{16,0},{1,17},{17,1},{2,18},{18,2},{3,19},{19,3},{4,20},{20... | collective-permute-start | bytes 1179656 | tf_op jit(solution)/shard_map/ppermute | solution.py:365
  12.7 8.5 %collective-permute-start.2 = (bf16[20,32,128]{2,1,0:T(8,128)(2,1)S(1)}, bf16[20,32,128]{2,1,0:T(8,128)(2,1)S(1)}, u32[]{:S(2)}, u32[]{:S(2)}) collective-permute-start(bf16[20,32,128]{2,1,0:T(8,128)(2,1)S(1)} %get-tuple-element.32.refs_0_), channel_id=1, source_target_pairs={{0,12},{1,13},{2,14},{3,15},{4,8},{5,9},{6,10},{7,11},{8,4},{9,5},... | collective-permute-start | bytes 491528 | tf_op jit(solution)/shard_map/ppermute | solution.py:90
  16.3 6.7 %collective-permute-start.1 = (bf16[20,32,128]{2,1,0:T(8,128)(2,1)S(1)}, bf16[20,32,128]{2,1,0:T(8,128)(2,1)S(1)}, u32[]{:S(2)}, u32[]{:S(2)}) collective-permute-start(bf16[20,32,128]{2,1,0:T(8,128)(2,1)S(1)} %get-tuple-element.32.refs_0_), channel_id=1, source_target_pairs={{0,4},{1,5},{2,6},{3,7},{4,0},{5,1},{6,2},{7,3},{8,12},{9,13},{10,... | collective-permute-start | bytes 491528 | tf_op jit(solution)/shard_map/ppermute | solution.py:90
  19.0 6.5 %collective-permute-start.9 = (bf16[20,32,128]{2,1,0:T(8,128)(2,1)S(1)}, bf16[20,32,128]{2,1,0:T(8,128)(2,1)S(1)}, u32[]{:S(2)}, u32[]{:S(2)}) collective-permute-start(bf16[20,32,128]{2,1,0:T(8,128)(2,1)S(1)} %get-tuple-element.32.refs_0_), channel_id=1, source_target_pairs={{0,2},{1,3},{2,0},{3,1},{4,6},{5,7},{6,4},{7,5},{8,10},{9,11},{10,... | collective-permute-start | bytes 491528 | tf_op jit(solution)/shard_map/ppermute | solution.py:90
  23.0 9.3 %collective-permute-start.3 = (bf16[20,32,128]{2,1,0:T(8,128)(2,1)S(1)}, bf16[20,32,128]{2,1,0:T(8,128)(2,1)S(1)}, u32[]{:S(2)}, u32[]{:S(2)}) collective-permute-start(bf16[20,32,128]{2,1,0:T(8,128)(2,1)S(1)} %get-tuple-element.32.refs_0_), channel_id=1, source_target_pairs={{0,8},{1,9},{2,10},{3,11},{4,12},{5,13},{6,14},{7,15},{8,0},{9,1},... | collective-permute-start | bytes 491528 | tf_op jit(solution)/shard_map/ppermute | solution.py:90
  23.5 8.8 %collective-permute-start.12 = (bf16[20,32,128]{2,1,0:T(8,128)(2,1)S(1)}, bf16[20,32,128]{2,1,0:T(8,128)(2,1)S(1)}, u32[]{:S(2)}, u32[]{:S(2)}) collective-permute-start(bf16[20,32,128]{2,1,0:T(8,128)(2,1)S(1)} %collective-permute-done.1.refs_4_), channel_id=1, source_target_pairs={{0,2},{1,3},{2,0},{3,1},{4,6},{5,7},{6,4},{7,5},{8,10},{9,11},{10,... | collective-permute-start | bytes 491528 | tf_op jit(solution)/shard_map/ppermute | solution.py:90
  25.0 7.2 %collective-permute-start.16 = (bf16[20,32,128]{2,1,0:T(8,128)(2,1)S(1)}, bf16[20,32,128]{2,1,0:T(8,128)(2,1)S(1)}, u32[]{:S(2)}, u32[]{:S(2)}) collective-permute-start(bf16[20,32,128]{2,1,0:T(8,128)(2,1)S(1)} %collective-permute-done.2.refs_12_), channel_id=1, source_target_pairs={{0,2},{1,3},{2,0},{3,1},{4,6},{5,7},{6,4},{7,5},{8,10},{9,11},{10,... | collective-permute-start | bytes 491528 | tf_op jit(solution)/shard_map/ppermute | solution.py:90
  25.5 15.6 %collective-permute-start.8 = (bf16[20,32,128]{2,1,0:T(8,128)(2,1)S(1)}, bf16[20,32,128]{2,1,0:T(8,128)(2,1)S(1)}, u32[]{:S(2)}, u32[]{:S(2)}) collective-permute-start(bf16[20,32,128]{2,1,0:T(8,128)(2,1)S(1)} %get-tuple-element.32.refs_0_), channel_id=1, source_target_pairs={{0,1},{1,0},{2,3},{3,2},{4,5},{5,4},{6,7},{7,6},{8,9},{9,8},{10,11... | collective-permute-start | bytes 491528 | tf_op jit(solution)/shard_map/ppermute | solution.py:90
  25.5 16.2 %collective-permute-start.19 = (bf16[20,32,128]{2,1,0:T(8,128)(2,1)S(1)}, bf16[20,32,128]{2,1,0:T(8,128)(2,1)S(1)}, u32[]{:S(2)}, u32[]{:S(2)}) collective-permute-start(bf16[20,32,128]{2,1,0:T(8,128)(2,1)S(1)} %collective-permute-done.2.refs_12_), channel_id=1, source_target_pairs={{0,1},{1,0},{2,3},{3,2},{4,5},{5,4},{6,7},{7,6},{8,9},{9,8},{10,11... | collective-permute-start | bytes 491528 | tf_op jit(solution)/shard_map/ppermute | solution.py:90
  32.2 9.6 %collective-permute-start.11 = (bf16[20,32,128]{2,1,0:T(8,128)(2,1)S(1)}, bf16[20,32,128]{2,1,0:T(8,128)(2,1)S(1)}, u32[]{:S(2)}, u32[]{:S(2)}) collective-permute-start(bf16[20,32,128]{2,1,0:T(8,128)(2,1)S(1)} %collective-permute-done.1.refs_4_), channel_id=1, source_target_pairs={{0,1},{1,0},{2,3},{3,2},{4,5},{5,4},{6,7},{7,6},{8,9},{9,8},{10,11... | collective-permute-start | bytes 491528 | tf_op jit(solution)/shard_map/ppermute | solution.py:90
  32.3 10.0 %collective-permute-start.17 = (bf16[20,32,128]{2,1,0:T(8,128)(2,1)S(1)}, bf16[20,32,128]{2,1,0:T(8,128)(2,1)S(1)}, u32[]{:S(2)}, u32[]{:S(2)}) collective-permute-start(bf16[20,32,128]{2,1,0:T(8,128)(2,1)S(1)} %collective-permute-done.3.refs_8_), channel_id=1, source_target_pairs={{0,2},{1,3},{2,0},{3,1},{4,6},{5,7},{6,4},{7,5},{8,10},{9,11},{10,... | collective-permute-start | bytes 491528 | tf_op jit(solution)/shard_map/ppermute | solution.py:90
  33.8 3.7 %collective-permute-start.20 = (s32[1,128]{1,0:T(1,128)}, s32[1,128]{1,0:T(1,128)S(1)}, u32[]{:S(2)}, u32[]{:S(2)}) collective-permute-start(s32[1,128]{1,0:T(1,128)} %bitcast.8), channel_id=1, source_target_pairs={{0,16},{16,0},{1,17},{17,1},{2,18},{18,2},{3,19},{19,3},{4,20},{20... | collective-permute-start | bytes 1544 | tf_op jit(solution)/shard_map/ppermute | solution.py:364
  37.5 4.8 %collective-permute-start.10 = (bf16[20,32,128]{2,1,0:T(8,128)(2,1)S(1)}, bf16[20,32,128]{2,1,0:T(8,128)(2,1)S(1)}, u32[]{:S(2)}, u32[]{:S(2)}) collective-permute-start(bf16[20,32,128]{2,1,0:T(8,128)(2,1)S(1)} %collective-permute-done.9.refs_2_), channel_id=1, source_target_pairs={{0,1},{1,0},{2,3},{3,2},{4,5},{5,4},{6,7},{7,6},{8,9},{9,8},{10,11... | collective-permute-start | bytes 491528 | tf_op jit(solution)/shard_map/ppermute | solution.py:90
  41.2 2.3 %collective-permute-start.14 = (bf16[20,32,128]{2,1,0:T(8,128)(2,1)S(1)}, bf16[20,32,128]{2,1,0:T(8,128)(2,1)S(1)}, u32[]{:S(2)}, u32[]{:S(2)}) collective-permute-start(bf16[20,32,128]{2,1,0:T(8,128)(2,1)S(1)} %collective-permute-done.3.refs_8_), channel_id=1, source_target_pairs={{0,1},{1,0},{2,3},{3,2},{4,5},{5,4},{6,7},{7,6},{8,9},{9,8},{10,11... | collective-permute-start | bytes 491528 | tf_op jit(solution)/shard_map/ppermute | solution.py:90
  41.7 3.7 %collective-permute-start.13 = (bf16[20,32,128]{2,1,0:T(8,128)(2,1)S(1)}, bf16[20,32,128]{2,1,0:T(8,128)(2,1)S(1)}, u32[]{:S(2)}, u32[]{:S(2)}) collective-permute-start(bf16[20,32,128]{2,1,0:T(8,128)(2,1)S(1)} %collective-permute-done.12.refs_6_), channel_id=1, source_target_pairs={{0,1},{1,0},{2,3},{3,2},{4,5},{5,4},{6,7},{7,6},{8,9},{9,8},{10,11... | collective-permute-start | bytes 491528 | tf_op jit(solution)/shard_map/ppermute | solution.py:90
  41.8 4.0 %collective-permute-start.21 = (bf16[20,32,128]{2,1,0:T(8,128)(2,1)S(1)}, bf16[20,32,128]{2,1,0:T(8,128)(2,1)S(1)}, u32[]{:S(2)}, u32[]{:S(2)}) collective-permute-start(bf16[20,32,128]{2,1,0:T(8,128)(2,1)S(1)} %collective-permute-done.16.refs_14_), channel_id=1, source_target_pairs={{0,1},{1,0},{2,3},{3,2},{4,5},{5,4},{6,7},{7,6},{8,9},{9,8},{10,11... | collective-permute-start | bytes 491528 | tf_op jit(solution)/shard_map/ppermute | solution.py:90
  42.3 4.1 %collective-permute-start.18 = (bf16[20,32,128]{2,1,0:T(8,128)(2,1)S(1)}, bf16[20,32,128]{2,1,0:T(8,128)(2,1)S(1)}, u32[]{:S(2)}, u32[]{:S(2)}) collective-permute-start(bf16[20,32,128]{2,1,0:T(8,128)(2,1)S(1)} %collective-permute-done.17.refs_10_), channel_id=1, source_target_pairs={{0,1},{1,0},{2,3},{3,2},{4,5},{5,4},{6,7},{7,6},{8,9},{9,8},{10,11... | collective-permute-start | bytes 491528 | tf_op jit(solution)/shard_map/ppermute | solution.py:90
  42.3 14.2 %collective-permute-start.4 = (bf16[20,32,128]{2,1,0:T(8,128)(2,1)S(1)}, bf16[20,32,128]{2,1,0:T(8,128)(2,1)S(1)}, u32[]{:S(2)}, u32[]{:S(2)}) collective-permute-start(bf16[20,32,128]{2,1,0:T(8,128)(2,1)S(1)} %get-tuple-element.33.refs_0_), channel_id=1, source_target_pairs={{0,4},{1,5},{2,6},{3,7},{4,0},{5,1},{6,2},{7,3},{8,12},{9,13},{10,... | collective-permute-start | bytes 491528 | tf_op jit(solution)/shard_map/ppermute | solution.py:90
  43.5 13.1 %collective-permute-start.5 = (bf16[20,32,128]{2,1,0:T(8,128)(2,1)S(1)}, bf16[20,32,128]{2,1,0:T(8,128)(2,1)S(1)}, u32[]{:S(2)}, u32[]{:S(2)}) collective-permute-start(bf16[20,32,128]{2,1,0:T(8,128)(2,1)S(1)} %get-tuple-element.33.refs_0_), channel_id=1, source_target_pairs={{0,12},{1,13},{2,14},{3,15},{4,8},{5,9},{6,10},{7,11},{8,4},{9,5},... | collective-permute-start | bytes 491528 | tf_op jit(solution)/shard_map/ppermute | solution.py:90
  45.5 15.1 %collective-permute-start.6 = (bf16[20,32,128]{2,1,0:T(8,128)(2,1)S(1)}, bf16[20,32,128]{2,1,0:T(8,128)(2,1)S(1)}, u32[]{:S(2)}, u32[]{:S(2)}) collective-permute-start(bf16[20,32,128]{2,1,0:T(8,128)(2,1)S(1)} %get-tuple-element.33.refs_0_), channel_id=1, source_target_pairs={{0,8},{1,9},{2,10},{3,11},{4,12},{5,13},{6,14},{7,15},{8,0},{9,1},... | collective-permute-start | bytes 491528 | tf_op jit(solution)/shard_map/ppermute | solution.py:90
  45.8 14.8 %collective-permute-start.7 = (bf16[20,32,128]{2,1,0:T(8,128)(2,1)S(1)}, bf16[20,32,128]{2,1,0:T(8,128)(2,1)S(1)}, u32[]{:S(2)}, u32[]{:S(2)}) collective-permute-start(bf16[20,32,128]{2,1,0:T(8,128)(2,1)S(1)} %get-tuple-element.33.refs_0_), channel_id=1, source_target_pairs={{0,2},{1,3},{2,0},{3,1},{4,6},{5,7},{6,4},{7,5},{8,10},{9,11},{10,... | collective-permute-start | bytes 491528 | tf_op jit(solution)/shard_map/ppermute | solution.py:90
  60.7 12.5 %collective-permute-start.22 = (bf16[3,20,32,128]{3,2,1,0:T(8,128)(2,1)S(1)}, bf16[3,20,32,128]{3,2,1,0:T(8,128)(2,1)S(1)}, u32[]{:S(2)}, u32[]{:S(2)}) collective-permute-start(bf16[3,20,32,128]{3,2,1,0:T(8,128)(2,1)S(1)} %pad_maximum_fusion.refs_2_), channel_id=1, source_target_pairs={{0,2},{1,3},{2,0},{3,1},{4,6},{5,7},{6,4},{7,5},{8,10},{9,11},{10,... | collective-permute-start | bytes 1474568 | tf_op jit(solution)/shard_map/ppermute | solution.py:90
  61.2 14.3 %collective-permute-start.25 = (bf16[3,20,32,128]{3,2,1,0:T(8,128)(2,1)S(1)}, bf16[3,20,32,128]{3,2,1,0:T(8,128)(2,1)S(1)}, u32[]{:S(2)}, u32[]{:S(2)}) collective-permute-start(bf16[3,20,32,128]{3,2,1,0:T(8,128)(2,1)S(1)} %pad_maximum_fusion.refs_2_), channel_id=1, source_target_pairs={{0,1},{1,0},{2,3},{3,2},{4,5},{5,4},{6,7},{7,6},{8,9},{9,8},{10,11... | collective-permute-start | bytes 1474568 | tf_op jit(solution)/shard_map/ppermute | solution.py:90
  73.2 2.3 %collective-permute-start.26 = (bf16[3,20,32,128]{3,2,1,0:T(8,128)(2,1)S(1)}, bf16[3,20,32,128]{3,2,1,0:T(8,128)(2,1)S(1)}, u32[]{:S(2)}, u32[]{:S(2)}) collective-permute-start(bf16[3,20,32,128]{3,2,1,0:T(8,128)(2,1)S(1)} %collective-permute-done.22.refs_3_), channel_id=1, source_target_pairs={{0,1},{1,0},{2,3},{3,2},{4,5},{5,4},{6,7},{7,6},{8,9},{9,8},{10,11... | collective-permute-start | bytes 1474568 | tf_op jit(solution)/shard_map/ppermute | solution.py:90
  73.2 2.1 %collective-permute-start.23 = (bf16[20,32,128]{2,1,0:T(8,128)(2,1)S(1)}, bf16[20,32,128]{2,1,0:T(8,128)(2,1)S(1)}, u32[]{:S(2)}, u32[]{:S(2)}) collective-permute-start(bf16[20,32,128]{2,1,0:T(8,128)(2,1)S(1)} %get-tuple-element.33.refs_0_), channel_id=1, source_target_pairs={{0,1},{1,0},{2,3},{3,2},{4,5},{5,4},{6,7},{7,6},{8,9},{9,8},{10,11... | collective-permute-start | bytes 491528 | tf_op jit(solution)/shard_map/ppermute | solution.py:90
  73.7 1.8 %collective-permute-start.24 = (bf16[20,32,128]{2,1,0:T(8,128)(2,1)S(1)}, bf16[20,32,128]{2,1,0:T(8,128)(2,1)S(1)}, u32[]{:S(2)}, u32[]{:S(2)}) collective-permute-start(bf16[20,32,128]{2,1,0:T(8,128)(2,1)S(1)} %collective-permute-done.7.refs_1_), channel_id=1, source_target_pairs={{0,1},{1,0},{2,3},{3,2},{4,5},{5,4},{6,7},{7,6},{8,9},{9,8},{10,11... | collective-permute-start | bytes 491528 | tf_op jit(solution)/shard_map/ppermute | solution.py:90
  93.7 4.4 %collective-permute-start.28 = (bf16[32,8,128]{2,1,0:T(8,128)(2,1)S(1)}, bf16[32,8,128]{2,1,0:T(8,128)(2,1)S(1)}, u32[]{:S(2)}, u32[]{:S(2)}) collective-permute-start(bf16[32,8,128]{2,1,0:T(8,128)(2,1)S(1)} %pad_maximum_fusion.1), channel_id=1, source_target_pairs={{0,16},{16,0},{1,17},{17,1},{2,18},{18,2},{3,19},{19,3},{4,20},{20... | collective-permute-start | bytes 196616 | tf_op jit(solution)/shard_map/ppermute | solution.py:421
  94.3 3.8 %collective-permute-start.27 = (f32[4,256]{1,0:T(4,128)S(1)}, f32[4,256]{1,0:T(4,128)S(1)}, u32[]{:S(2)}, u32[]{:S(2)}) collective-permute-start(f32[4,256]{1,0:T(4,128)S(1)} %get-tuple-element.49), channel_id=1, source_target_pairs={{0,16},{16,0},{1,17},{17,1},{2,18},{18,2},{3,19},{19,3},{4,20},{20... | collective-permute-start | bytes 12296 | tf_op jit(solution)/shard_map/ppermute | solution.py:420
  99.2 3.6 %collective-permute-start.30 = (f32[4,256]{1,0:T(4,128)S(1)}, f32[4,256]{1,0:T(4,128)S(1)}, u32[]{:S(2)}, u32[]{:S(2)}) collective-permute-start(f32[4,256]{1,0:T(4,128)S(1)} %add.16), channel_id=1, source_target_pairs={{0,2},{1,3},{2,0},{3,1},{4,6},{5,7},{6,4},{7,5},{8,10},{9,11},{10,... | collective-permute-start | bytes 12296 | tf_op jit(solution)/shard_map/ppermute | solution.py:90
  102.8 3.6 %collective-permute-start.31 = (f32[4,256]{1,0:T(4,128)S(1)}, f32[4,256]{1,0:T(4,128)S(1)}, u32[]{:S(2)}, u32[]{:S(2)}) collective-permute-start(f32[4,256]{1,0:T(4,128)S(1)} %add.17), channel_id=1, source_target_pairs={{0,4},{1,5},{2,6},{3,7},{4,0},{5,1},{6,2},{7,3},{8,12},{9,13},{10,... | collective-permute-start | bytes 12296 | tf_op jit(solution)/shard_map/ppermute | solution.py:90
  106.4 4.5 %collective-permute-start.32 = (f32[4,256]{1,0:T(4,128)S(1)}, f32[4,256]{1,0:T(4,128)S(1)}, u32[]{:S(2)}, u32[]{:S(2)}) collective-permute-start(f32[4,256]{1,0:T(4,128)S(1)} %add.18), channel_id=1, source_target_pairs={{0,8},{1,9},{2,10},{3,11},{4,12},{5,13},{6,14},{7,15},{8,0},{9,1},... | collective-permute-start | bytes 12296 | tf_op jit(solution)/shard_map/ppermute | solution.py:90
  (9 other events, 8.7 us)

commit v12 on v10

--- a/solution.py
+++ b/solution.py
@@ -394,24 +394,25 @@
 
     zero = jnp.zeros((GROUPS, TOKENS), jnp.float32)
     common = (grads, query_grads, codes, eigenvalues)
-    part0, kept_a, given_a = score_tiles(0, 8, False, info, units, places0, *common, zero)
+    part0, kept_a, given_a = score_tiles(0, 10, False, info, units, places0, *common, zero)
 
     second = after(packed[1], units[8])
     along = [hop(second, d) for d in (4, 12, 8)]
     near = hop(second, 2)
-    *along, near, _ = lax.optimization_barrier((*along, near, part0))
-    line = jnp.stack(along)
-    beside = hop(line, 2)
-    part1, kept_b, given_b = score_tiles(8, 8, False, info, units, places0, *common, part0)
-    beside = after(beside, part1)
-    arrays = [second, near, line, beside]
+    first, third, near, _ = lax.optimization_barrier((along[0], along[1], near, part0))
+    pair = jnp.stack([first, third])
+    pair_beside = hop(pair, 2)
+    last = after(along[2], part0)
+    last_beside = hop(last, 2)
+    part1, kept_b, given_b = score_tiles(10, 6, False, info, units, places0, *common, part0)
+    pair_beside, last_beside, _ = lax.optimization_barrier((pair_beside, last_beside, part1))
+    arrays = [second, near, pair, pair_beside, last, last_beside]
     arrays = arrays + [hop(array, 1) for array in arrays]
-    order = {4: 0, 12: 1, 8: 2}
+    held = {0: (0, None), 4: (2, 0), 12: (2, 1), 8: (4, None)}
     places1 = []
     for d in range(NQ):
-        across_y = (d & 2) // 2 + 4 * (d & 1)
-        far = d & 12
-        places1.append((across_y + 2, order[far]) if far else (across_y, None))
+        array, index = held[d & 12]
+        places1.append((array + (d & 2) // 2 + 6 * (d & 1), index))
     keep, give, kept1, given1 = score_tiles(
         16, 16, True, info, arrays, places1, *common, part1
     )

time: 110 us -> 109 us (level)
  waiting for transfers between devices: 31.2 us -> 24.6 us
  starting transfers between devices: 26 us -> 31.7 us
    ppermute x28 -> x31, waiting for transfers between devices: 25.3 us -> 18.7 us  [hop(): return lax.ppermute(value, 'query', [(i, i ^ bits) for i in range(NQ)])]
    ppermute x28 -> x31, starting transfers between devices: 20.1 us -> 25.8 us  [hop(): return lax.ppermute(value, 'query', [(i, i ^ bits) for i in range(NQ)])]
  transfers between devices with their start and end apart: 33 -> 36, of which waited for: 15 -> 15; matrix products, arithmetic and copies ran while one was open for 1% -> 1% of each run, Pallas kernels for 21% -> 21%
where the time goes in v12:
time: 109 us
  Pallas kernels  42.2 us (39%)
  starting transfers between devices  31.7 us (29%)
  waiting for transfers between devices  24.6 us (23%)
  local copies, waits for them, and re-layouts  8.07 us (7%)
  other arithmetic  1.59 us (1%)
    pallas_call x3, Pallas kernels, score_tiles(): pl.pallas_call(kernel, in_specs=[SMEM] + [VMEM] * len(arrays) + [VMEM, VM...  38.2 us
    ppermute x31, starting transfers between devices, hop(): return lax.ppermute(value, 'query', [(i, i ^ bits) for i in range(NQ)])  25.8 us
    ppermute x31, waiting for transfers between devices, hop(): return lax.ppermute(value, 'query', [(i, i ^ bits) for i in range(NQ)])  18.7 us
    unnamed x16, local copies, waits for them, and re-layouts  7.53 us
    ppermute x1, waiting for transfers between devices, paired_body(): ids_other = lax.ppermute(after(ids, mine), 'parts', SWAP)  3.41 us
    ppermute x1, starting transfers between devices, paired_body(): train_other = lax.ppermute(train_inputs, 'parts', SWAP)  3 us
    ppermute x1, waiting for transfers between devices, paired_body(): total = keep + lax.ppermute(give, 'parts', SWAP)  2.49 us
  transfers between devices with their start and end apart: 36, of which 15 were waited for; matrix products, arithmetic and copies ran while one was open for 1% of the time, Pallas kernels for 21%

profile of v12, /device:TPU:0, one launch (start us, length us, event | category | flops | bytes accessed | tf_op | source)
XLA Modules:
  0.0 109.0 jit_solution(577409129283777685)
XLA Ops:
  0.6 3.0 %collective-permute-start.1 = (bf16[2,8,4096]{2,1,0:T(8,128)(2,1)}, bf16[2,8,4096]{2,1,0:T(8,128)(2,1)S(1)}, u32[]{:S(2)}, u32[]{:S(2)}) collective-permute-start(bf16[2,8,4096]{2,1,0:T(8,128)(2,1)} %own.2), channel_id=1, source_target_pairs={{0,16},{16,0},{1,17},{17,1},{2,18},{18,2},{3,19},{19,3},{4,20},{20... | collective-permute-start | bytes 393224 | tf_op jit(solution)/shard_map/ppermute | solution.py:341
  5.0 3.4 %collective-permute-done.ids_other = s32[1,128]{1,0:T(1,128)S(1)} collective-permute-done((s32[1,128]{1,0:T(1,128)}, s32[1,128]{1,0:T(1,128)S(1)}, u32[]{:S(2)}, u32[]{:S(2)}) %collective-permute-start) | collective-permute-done | bytes 544 | tf_op jit(solution)/shard_map/ppermute | solution.py:348
  12.8 1.6 %collective-permute-start.2 = (bf16[20,32,128]{2,1,0:T(8,128)(2,1)S(1)}, bf16[20,32,128]{2,1,0:T(8,128)(2,1)S(1)}, u32[]{:S(2)}, u32[]{:S(2)}) collective-permute-start(bf16[20,32,128]{2,1,0:T(8,128)(2,1)S(1)} %get-tuple-element.36.refs_0_), channel_id=1, source_target_pairs={{0,4},{1,5},{2,6},{3,7},{4,0},{5,1},{6,2},{7,3},{8,12},{9,13},{10,... | collective-permute-start | bytes 491528 | tf_op jit(solution)/shard_map/ppermute | solution.py:90
  14.4 2.5 %collective-permute-start.3 = (bf16[20,32,128]{2,1,0:T(8,128)(2,1)S(1)}, bf16[20,32,128]{2,1,0:T(8,128)(2,1)S(1)}, u32[]{:S(2)}, u32[]{:S(2)}) collective-permute-start(bf16[20,32,128]{2,1,0:T(8,128)(2,1)S(1)} %get-tuple-element.36.refs_0_), channel_id=1, source_target_pairs={{0,12},{1,13},{2,14},{3,15},{4,8},{5,9},{6,10},{7,11},{8,4},{9,5},... | collective-permute-start | bytes 491528 | tf_op jit(solution)/shard_map/ppermute | solution.py:90
  16.8 1.5 %collective-permute-start.9 = (bf16[20,32,128]{2,1,0:T(8,128)(2,1)S(1)}, bf16[20,32,128]{2,1,0:T(8,128)(2,1)S(1)}, u32[]{:S(2)}, u32[]{:S(2)}) collective-permute-start(bf16[20,32,128]{2,1,0:T(8,128)(2,1)S(1)} %get-tuple-element.36.refs_0_), channel_id=1, source_target_pairs={{0,2},{1,3},{2,0},{3,1},{4,6},{5,7},{6,4},{7,5},{8,10},{9,11},{10,... | collective-permute-start | bytes 491528 | tf_op jit(solution)/shard_map/ppermute | solution.py:90
  18.4 1.0 copy-done
  19.4 1.1 %copy-done.2 = bf16[2,256,768]{2,1,0:T(8,128)(2,1)S(1)} copy-done((bf16[2,256,768]{2,1,0:T(8,128)(2,1)S(1)}, bf16[2,256,768]{2,1,0:T(8,128)(2,1)}, u32[]{:S(2)}) %copy-start.2) | copy-done | bytes 786456
  21.1 2.1 %collective-permute-done.3.refs_12_ = bf16[20,32,128]{2,1,0:T(8,128)(2,1)S(1)} collective-permute-done((bf16[20,32,128]{2,1,0:T(8,128)(2,1)S(1)}, bf16[20,32,128]{2,1,0:T(8,128)(2,1)S(1)}, u32[]{:S(2)}, u32[]{:S(2)}) %collective-permute-start.3) | collective-permute-done | bytes 163872 | tf_op jit(solution)/shard_map/ppermute | solution.py:90
  23.2 3.8 %collective-permute-start.4 = (bf16[20,32,128]{2,1,0:T(8,128)(2,1)S(1)}, bf16[20,32,128]{2,1,0:T(8,128)(2,1)S(1)}, u32[]{:S(2)}, u32[]{:S(2)}) collective-permute-start(bf16[20,32,128]{2,1,0:T(8,128)(2,1)S(1)} %get-tuple-element.36.refs_0_), channel_id=1, source_target_pairs={{0,8},{1,9},{2,10},{3,11},{4,12},{5,13},{6,14},{7,15},{8,0},{9,1},... | collective-permute-start | bytes 491528 | tf_op jit(solution)/shard_map/ppermute | solution.py:90
  26.9 1.5 %collective-permute-start.12 = (bf16[20,32,128]{2,1,0:T(8,128)(2,1)S(1)}, bf16[20,32,128]{2,1,0:T(8,128)(2,1)S(1)}, u32[]{:S(2)}, u32[]{:S(2)}) collective-permute-start(bf16[20,32,128]{2,1,0:T(8,128)(2,1)S(1)} %collective-permute-done.2.refs_4_), channel_id=1, source_target_pairs={{0,2},{1,3},{2,0},{3,1},{4,6},{5,7},{6,4},{7,5},{8,10},{9,11},{10,... | collective-permute-start | bytes 491528 | tf_op jit(solution)/shard_map/ppermute | solution.py:90
  29.5 2.5 %collective-permute-done.4.refs_8_ = bf16[20,32,128]{2,1,0:T(8,128)(2,1)S(1)} collective-permute-done((bf16[20,32,128]{2,1,0:T(8,128)(2,1)S(1)}, bf16[20,32,128]{2,1,0:T(8,128)(2,1)S(1)}, u32[]{:S(2)}, u32[]{:S(2)}) %collective-permute-start.4) | collective-permute-done | bytes 163872 | tf_op jit(solution)/shard_map/ppermute | solution.py:90
  32.3 1.8 %collective-permute-done.16.refs_14_ = bf16[20,32,128]{2,1,0:T(8,128)(2,1)S(1)} collective-permute-done((bf16[20,32,128]{2,1,0:T(8,128)(2,1)S(1)}, bf16[20,32,128]{2,1,0:T(8,128)(2,1)S(1)}, u32[]{:S(2)}, u32[]{:S(2)}) %collective-permute-start.16) | collective-permute-done | bytes 163872 | tf_op jit(solution)/shard_map/ppermute | solution.py:90
  34.0 1.5 %collective-permute-start.17 = (bf16[20,32,128]{2,1,0:T(8,128)(2,1)S(1)}, bf16[20,32,128]{2,1,0:T(8,128)(2,1)S(1)}, u32[]{:S(2)}, u32[]{:S(2)}) collective-permute-start(bf16[20,32,128]{2,1,0:T(8,128)(2,1)S(1)} %collective-permute-done.4.refs_8_), channel_id=1, source_target_pairs={{0,2},{1,3},{2,0},{3,1},{4,6},{5,7},{6,4},{7,5},{8,10},{9,11},{10,... | collective-permute-start | bytes 491528 | tf_op jit(solution)/shard_map/ppermute | solution.py:90
  36.1 1.0 copy-done.1
  37.1 1.0 copy-done.3
  40.4 1.4 %collective-permute-start.6 = (bf16[20,32,128]{2,1,0:T(8,128)(2,1)S(1)}, bf16[20,32,128]{2,1,0:T(8,128)(2,1)S(1)}, u32[]{:S(2)}, u32[]{:S(2)}) collective-permute-start(bf16[20,32,128]{2,1,0:T(8,128)(2,1)S(1)} %get-tuple-element.37.refs_0_), channel_id=1, source_target_pairs={{0,12},{1,13},{2,14},{3,15},{4,8},{5,9},{6,10},{7,11},{8,4},{9,5},... | collective-permute-start | bytes 491528 | tf_op jit(solution)/shard_map/ppermute | solution.py:90
  42.8 1.6 %collective-permute-start.22 = (bf16[20,32,128]{2,1,0:T(8,128)(2,1)S(1)}, bf16[20,32,128]{2,1,0:T(8,128)(2,1)S(1)}, u32[]{:S(2)}, u32[]{:S(2)}) collective-permute-start(bf16[20,32,128]{2,1,0:T(8,128)(2,1)S(1)} %get-tuple-element.37.refs_0_), channel_id=1, source_target_pairs={{0,8},{1,9},{2,10},{3,11},{4,12},{5,13},{6,14},{7,15},{8,0},{9,1},... | collective-permute-start | bytes 491528 | tf_op jit(solution)/shard_map/ppermute | solution.py:90
  44.4 12.2 %shard_map.107 = (f32[8,256]{1,0:T(8,128)S(1)}, bf16[10,8,128]{2,1,0:T(8,128)(2,1)S(1)}, bf16[10,8,128]{2,1,0:T(8,128)(2,1)S(1)}) custom-call(s32[66]{0:T(128)S(1)} %pad_add_fusion.info.info_ref, bf16[20,32,128]{2,1,0:T(8,128)(2,1)S(1)} %get-tuple-element.36.refs_0_, bf16[20,32,128]{2,1,0:T(8,128)(2,1)S(1)} %collective-permute-done.8.refs_1_, ...), custom_call_target="tpu_custom_call" | custom-call | flops 100000000 | bytes 5000000 | tf_op jit(solution)/shard_map/pallas_call | solution.py:283
  56.6 1.6 %collective-permute-start.21 = (bf16[2,20,32,128]{3,2,1,0:T(8,128)(2,1)S(1)}, bf16[2,20,32,128]{3,2,1,0:T(8,128)(2,1)S(1)}, u32[]{:S(2)}, u32[]{:S(2)}) collective-permute-start(bf16[2,20,32,128]{3,2,1,0:T(8,128)(2,1)S(1)} %pad_maximum_fusion.refs_2_), channel_id=1, source_target_pairs={{0,2},{1,3},{2,0},{3,1},{4,6},{5,7},{6,4},{7,5},{8,10},{9,11},{10,... | collective-permute-start | bytes 983048 | tf_op jit(solution)/shard_map/ppermute | solution.py:90
  59.2 8.0 %shard_map.108 = (f32[8,256]{1,0:T(8,128)S(1)}, bf16[6,8,128]{2,1,0:T(8,128)(2,1)S(1)}, bf16[6,8,128]{2,1,0:T(8,128)(2,1)S(1)}) custom-call(s32[66]{0:T(128)S(1)} %pad_add_fusion.info.info_ref, bf16[20,32,128]{2,1,0:T(8,128)(2,1)S(1)} %get-tuple-element.36.refs_0_, bf16[20,32,128]{2,1,0:T(8,128)(2,1)S(1)} %collective-permute-done.8.refs_1_, ...), custom_call_target="tpu_custom_call" | custom-call | flops 6000000000 | bytes 3000000 | tf_op jit(solution)/shard_map/pallas_call | solution.py:283
  67.2 3.2 %collective-permute-done.23.refs_5_ = bf16[20,32,128]{2,1,0:T(8,128)(2,1)S(1)} collective-permute-done((bf16[20,32,128]{2,1,0:T(8,128)(2,1)S(1)}, bf16[20,32,128]{2,1,0:T(8,128)(2,1)S(1)}, u32[]{:S(2)}, u32[]{:S(2)}) %collective-permute-start.23) | collective-permute-done | bytes 163872 | tf_op jit(solution)/shard_map/ppermute | solution.py:90
  72.7 18.1 %shard_map.109 = (f32[4,256]{1,0:T(4,128)S(1)}, f32[4,256]{1,0:T(4,128)S(1)}, bf16[16,8,128]{2,1,0:T(8,128)(2,1)S(1)}, bf16[16,8,128]{2,1,0:T(8,128)(2,1)S(1)}) custom-call(s32[66]{0:T(128)S(1)} %pad_add_fusion.info.info_ref, bf16[20,32,128]{2,1,0:T(8,128)(2,1)S(1)} %get-tuple-element.37.refs_0_, bf16[20,32,128]{2,1,0:T(8,128)(2,1)S(1)} %collective-permute-done.7.refs_1_, ...), custom_call_target="tpu_custom_call" | custom-call | flops 16000000000 | bytes 8000000 | tf_op jit(solution)/shard_map/pallas_call | solution.py:283
  91.7 1.1 %collective-permute-start.30 = (f32[4,256]{1,0:T(4,128)S(1)}, f32[4,256]{1,0:T(4,128)S(1)}, u32[]{:S(2)}, u32[]{:S(2)}) collective-permute-start(f32[4,256]{1,0:T(4,128)S(1)} %get-tuple-element.53), channel_id=1, source_target_pairs={{0,16},{16,0},{1,17},{17,1},{2,18},{18,2},{3,19},{19,3},{4,20},{20... | collective-permute-start | bytes 12296 | tf_op jit(solution)/shard_map/ppermute | solution.py:420
  92.9 2.5 %collective-permute-done.30 = f32[4,256]{1,0:T(4,128)S(1)} collective-permute-done((f32[4,256]{1,0:T(4,128)S(1)}, f32[4,256]{1,0:T(4,128)S(1)}, u32[]{:S(2)}, u32[]{:S(2)}) %collective-permute-start.30) | collective-permute-done | bytes 4128 | tf_op jit(solution)/shard_map/ppermute | solution.py:420
  95.4 1.2 %collective-permute-done.32 = f32[4,256]{1,0:T(4,128)S(1)} collective-permute-done((f32[4,256]{1,0:T(4,128)S(1)}, f32[4,256]{1,0:T(4,128)S(1)}, u32[]{:S(2)}, u32[]{:S(2)}) %collective-permute-start.32) | collective-permute-done | bytes 4128 | tf_op jit(solution)/shard_map/ppermute | solution.py:90
  96.5 1.5 %collective-permute-start.33 = (f32[4,256]{1,0:T(4,128)S(1)}, f32[4,256]{1,0:T(4,128)S(1)}, u32[]{:S(2)}, u32[]{:S(2)}) collective-permute-start(f32[4,256]{1,0:T(4,128)S(1)} %add.16), channel_id=1, source_target_pairs={{0,2},{1,3},{2,0},{3,1},{4,6},{5,7},{6,4},{7,5},{8,10},{9,11},{10,... | collective-permute-start | bytes 12296 | tf_op jit(solution)/shard_map/ppermute | solution.py:90
  98.0 2.1 %collective-permute-done.33 = f32[4,256]{1,0:T(4,128)S(1)} collective-permute-done((f32[4,256]{1,0:T(4,128)S(1)}, f32[4,256]{1,0:T(4,128)S(1)}, u32[]{:S(2)}, u32[]{:S(2)}) %collective-permute-start.33) | collective-permute-done | bytes 4128 | tf_op jit(solution)/shard_map/ppermute | solution.py:90
  100.1 1.0 collective-permute-start.34
  101.1 1.6 %shard_map.110 = bf16[2,8,4096]{2,1,0:T(8,128)(2,1)} custom-call(s32[66]{0:T(128)S(1)} %pad_add_fusion.info.info_ref, bf16[10,8,128]{2,1,0:T(8,128)(2,1)S(1)} %get-tuple-element.58.kept_a, bf16[6,8,128]{2,1,0:T(8,128)(2,1)S(1)} %get-tuple-element.59.kept_b, bf16[16,8,128]{2,1,0:T(8,128)(2,1)S(1)} %get-tuple-element.60.kept_c, ...), custom_call_target="tpu_custom_call" | custom-call | tf_op jit(solution)/shard_map/pallas_call | solution.py:423
  102.8 1.0 collective-permute-done.34
  103.8 1.3 %collective-permute-start.35 = (f32[4,256]{1,0:T(4,128)S(1)}, f32[4,256]{1,0:T(4,128)S(1)}, u32[]{:S(2)}, u32[]{:S(2)}) collective-permute-start(f32[4,256]{1,0:T(4,128)S(1)} %add.18), channel_id=1, source_target_pairs={{0,8},{1,9},{2,10},{3,11},{4,12},{5,13},{6,14},{7,15},{8,0},{9,1},... | collective-permute-start | bytes 12296 | tf_op jit(solution)/shard_map/ppermute | solution.py:90
  105.1 3.2 %collective-permute-done.35 = f32[4,256]{1,0:T(4,128)S(1)} collective-permute-done((f32[4,256]{1,0:T(4,128)S(1)}, f32[4,256]{1,0:T(4,128)S(1)}, u32[]{:S(2)}, u32[]{:S(2)}) %collective-permute-start.35) | collective-permute-done | bytes 4128 | tf_op jit(solution)/shard_map/ppermute | solution.py:90
  (81 shorter events, 16.4 us)
Async XLA Ops:
  0.6 7.8 %collective-permute-start.1 = (bf16[2,8,4096]{2,1,0:T(8,128)(2,1)}, bf16[2,8,4096]{2,1,0:T(8,128)(2,1)S(1)}, u32[]{:S(2)}, u32[]{:S(2)}) collective-permute-start(bf16[2,8,4096]{2,1,0:T(8,128)(2,1)} %own.2), channel_id=1, source_target_pairs={{0,16},{16,0},{1,17},{17,1},{2,18},{18,2},{3,19},{19,3},{4,20},{20... | collective-permute-start | bytes 393224 | tf_op jit(solution)/shard_map/ppermute | solution.py:341
  4.7 3.7 %collective-permute-start = (s32[1,128]{1,0:T(1,128)}, s32[1,128]{1,0:T(1,128)S(1)}, u32[]{:S(2)}, u32[]{:S(2)}) collective-permute-start(s32[1,128]{1,0:T(1,128)} %bitcast.7), channel_id=1, source_target_pairs={{0,16},{16,0},{1,17},{17,1},{2,18},{18,2},{3,19},{19,3},{4,20},{20... | collective-permute-start | bytes 1544 | tf_op jit(solution)/shard_map/ppermute | solution.py:348
  12.0 16.5 %collective-permute-start.15 = (bf16[2,128,768]{2,1,0:T(8,128)(2,1)}, bf16[2,128,768]{2,1,0:T(8,128)(2,1)S(1)}, u32[]{:S(2)}, u32[]{:S(2)}) collective-permute-start(bf16[2,128,768]{2,1,0:T(8,128)(2,1)} %own.3), channel_id=1, source_target_pairs={{0,16},{16,0},{1,17},{17,1},{2,18},{18,2},{3,19},{19,3},{4,20},{20... | collective-permute-start | bytes 1179656 | tf_op jit(solution)/shard_map/ppermute | solution.py:360
  12.8 8.3 %collective-permute-start.2 = (bf16[20,32,128]{2,1,0:T(8,128)(2,1)S(1)}, bf16[20,32,128]{2,1,0:T(8,128)(2,1)S(1)}, u32[]{:S(2)}, u32[]{:S(2)}) collective-permute-start(bf16[20,32,128]{2,1,0:T(8,128)(2,1)S(1)} %get-tuple-element.36.refs_0_), channel_id=1, source_target_pairs={{0,4},{1,5},{2,6},{3,7},{4,0},{5,1},{6,2},{7,3},{8,12},{9,13},{10,... | collective-permute-start | bytes 491528 | tf_op jit(solution)/shard_map/ppermute | solution.py:90
  14.4 8.8 %collective-permute-start.3 = (bf16[20,32,128]{2,1,0:T(8,128)(2,1)S(1)}, bf16[20,32,128]{2,1,0:T(8,128)(2,1)S(1)}, u32[]{:S(2)}, u32[]{:S(2)}) collective-permute-start(bf16[20,32,128]{2,1,0:T(8,128)(2,1)S(1)} %get-tuple-element.36.refs_0_), channel_id=1, source_target_pairs={{0,12},{1,13},{2,14},{3,15},{4,8},{5,9},{6,10},{7,11},{8,4},{9,5},... | collective-permute-start | bytes 491528 | tf_op jit(solution)/shard_map/ppermute | solution.py:90
  16.8 12.1 %collective-permute-start.9 = (bf16[20,32,128]{2,1,0:T(8,128)(2,1)S(1)}, bf16[20,32,128]{2,1,0:T(8,128)(2,1)S(1)}, u32[]{:S(2)}, u32[]{:S(2)}) collective-permute-start(bf16[20,32,128]{2,1,0:T(8,128)(2,1)S(1)} %get-tuple-element.36.refs_0_), channel_id=1, source_target_pairs={{0,2},{1,3},{2,0},{3,1},{4,6},{5,7},{6,4},{7,5},{8,10},{9,11},{10,... | collective-permute-start | bytes 491528 | tf_op jit(solution)/shard_map/ppermute | solution.py:90
  23.2 8.8 %collective-permute-start.4 = (bf16[20,32,128]{2,1,0:T(8,128)(2,1)S(1)}, bf16[20,32,128]{2,1,0:T(8,128)(2,1)S(1)}, u32[]{:S(2)}, u32[]{:S(2)}) collective-permute-start(bf16[20,32,128]{2,1,0:T(8,128)(2,1)S(1)} %get-tuple-element.36.refs_0_), channel_id=1, source_target_pairs={{0,8},{1,9},{2,10},{3,11},{4,12},{5,13},{6,14},{7,15},{8,0},{9,1},... | collective-permute-start | bytes 491528 | tf_op jit(solution)/shard_map/ppermute | solution.py:90
  26.9 5.3 %collective-permute-start.12 = (bf16[20,32,128]{2,1,0:T(8,128)(2,1)S(1)}, bf16[20,32,128]{2,1,0:T(8,128)(2,1)S(1)}, u32[]{:S(2)}, u32[]{:S(2)}) collective-permute-start(bf16[20,32,128]{2,1,0:T(8,128)(2,1)S(1)} %collective-permute-done.2.refs_4_), channel_id=1, source_target_pairs={{0,2},{1,3},{2,0},{3,1},{4,6},{5,7},{6,4},{7,5},{8,10},{9,11},{10,... | collective-permute-start | bytes 491528 | tf_op jit(solution)/shard_map/ppermute | solution.py:90
  28.5 5.6 %collective-permute-start.16 = (bf16[20,32,128]{2,1,0:T(8,128)(2,1)S(1)}, bf16[20,32,128]{2,1,0:T(8,128)(2,1)S(1)}, u32[]{:S(2)}, u32[]{:S(2)}) collective-permute-start(bf16[20,32,128]{2,1,0:T(8,128)(2,1)S(1)} %collective-permute-done.3.refs_12_), channel_id=1, source_target_pairs={{0,2},{1,3},{2,0},{3,1},{4,6},{5,7},{6,4},{7,5},{8,10},{9,11},{10,... | collective-permute-start | bytes 491528 | tf_op jit(solution)/shard_map/ppermute | solution.py:90
  29.0 6.6 %collective-permute-start.8 = (bf16[20,32,128]{2,1,0:T(8,128)(2,1)S(1)}, bf16[20,32,128]{2,1,0:T(8,128)(2,1)S(1)}, u32[]{:S(2)}, u32[]{:S(2)}) collective-permute-start(bf16[20,32,128]{2,1,0:T(8,128)(2,1)S(1)} %get-tuple-element.36.refs_0_), channel_id=1, source_target_pairs={{0,1},{1,0},{2,3},{3,2},{4,5},{5,4},{6,7},{7,6},{8,9},{9,8},{10,11... | collective-permute-start | bytes 491528 | tf_op jit(solution)/shard_map/ppermute | solution.py:90
  29.0 7.1 %collective-permute-start.11 = (bf16[20,32,128]{2,1,0:T(8,128)(2,1)S(1)}, bf16[20,32,128]{2,1,0:T(8,128)(2,1)S(1)}, u32[]{:S(2)}, u32[]{:S(2)}) collective-permute-start(bf16[20,32,128]{2,1,0:T(8,128)(2,1)S(1)} %collective-permute-done.2.refs_4_), channel_id=1, source_target_pairs={{0,1},{1,0},{2,3},{3,2},{4,5},{5,4},{6,7},{7,6},{8,9},{9,8},{10,11... | collective-permute-start | bytes 491528 | tf_op jit(solution)/shard_map/ppermute | solution.py:90
  32.0 7.8 %collective-permute-start.19 = (bf16[20,32,128]{2,1,0:T(8,128)(2,1)S(1)}, bf16[20,32,128]{2,1,0:T(8,128)(2,1)S(1)}, u32[]{:S(2)}, u32[]{:S(2)}) collective-permute-start(bf16[20,32,128]{2,1,0:T(8,128)(2,1)S(1)} %collective-permute-done.3.refs_12_), channel_id=1, source_target_pairs={{0,1},{1,0},{2,3},{3,2},{4,5},{5,4},{6,7},{7,6},{8,9},{9,8},{10,11... | collective-permute-start | bytes 491528 | tf_op jit(solution)/shard_map/ppermute | solution.py:90
  34.0 6.3 %collective-permute-start.17 = (bf16[20,32,128]{2,1,0:T(8,128)(2,1)S(1)}, bf16[20,32,128]{2,1,0:T(8,128)(2,1)S(1)}, u32[]{:S(2)}, u32[]{:S(2)}) collective-permute-start(bf16[20,32,128]{2,1,0:T(8,128)(2,1)S(1)} %collective-permute-done.4.refs_8_), channel_id=1, source_target_pairs={{0,2},{1,3},{2,0},{3,1},{4,6},{5,7},{6,4},{7,5},{8,10},{9,11},{10,... | collective-permute-start | bytes 491528 | tf_op jit(solution)/shard_map/ppermute | solution.py:90
  35.5 4.8 %collective-permute-start.10 = (bf16[20,32,128]{2,1,0:T(8,128)(2,1)S(1)}, bf16[20,32,128]{2,1,0:T(8,128)(2,1)S(1)}, u32[]{:S(2)}, u32[]{:S(2)}) collective-permute-start(bf16[20,32,128]{2,1,0:T(8,128)(2,1)S(1)} %collective-permute-done.9.refs_2_), channel_id=1, source_target_pairs={{0,1},{1,0},{2,3},{3,2},{4,5},{5,4},{6,7},{7,6},{8,9},{9,8},{10,11... | collective-permute-start | bytes 491528 | tf_op jit(solution)/shard_map/ppermute | solution.py:90
  35.5 4.8 %collective-permute-start.14 = (bf16[20,32,128]{2,1,0:T(8,128)(2,1)S(1)}, bf16[20,32,128]{2,1,0:T(8,128)(2,1)S(1)}, u32[]{:S(2)}, u32[]{:S(2)}) collective-permute-start(bf16[20,32,128]{2,1,0:T(8,128)(2,1)S(1)} %collective-permute-done.4.refs_8_), channel_id=1, source_target_pairs={{0,1},{1,0},{2,3},{3,2},{4,5},{5,4},{6,7},{7,6},{8,9},{9,8},{10,11... | collective-permute-start | bytes 491528 | tf_op jit(solution)/shard_map/ppermute | solution.py:90
  36.0 5.8 %collective-permute-start.13 = (bf16[20,32,128]{2,1,0:T(8,128)(2,1)S(1)}, bf16[20,32,128]{2,1,0:T(8,128)(2,1)S(1)}, u32[]{:S(2)}, u32[]{:S(2)}) collective-permute-start(bf16[20,32,128]{2,1,0:T(8,128)(2,1)S(1)} %collective-permute-done.12.refs_6_), channel_id=1, source_target_pairs={{0,1},{1,0},{2,3},{3,2},{4,5},{5,4},{6,7},{7,6},{8,9},{9,8},{10,11... | collective-permute-start | bytes 491528 | tf_op jit(solution)/shard_map/ppermute | solution.py:90
  39.8 3.0 %collective-permute-start.20 = (bf16[20,32,128]{2,1,0:T(8,128)(2,1)S(1)}, bf16[20,32,128]{2,1,0:T(8,128)(2,1)S(1)}, u32[]{:S(2)}, u32[]{:S(2)}) collective-permute-start(bf16[20,32,128]{2,1,0:T(8,128)(2,1)S(1)} %collective-permute-done.16.refs_14_), channel_id=1, source_target_pairs={{0,1},{1,0},{2,3},{3,2},{4,5},{5,4},{6,7},{7,6},{8,9},{9,8},{10,11... | collective-permute-start | bytes 491528 | tf_op jit(solution)/shard_map/ppermute | solution.py:90
  40.3 4.1 %collective-permute-start.18 = (bf16[20,32,128]{2,1,0:T(8,128)(2,1)S(1)}, bf16[20,32,128]{2,1,0:T(8,128)(2,1)S(1)}, u32[]{:S(2)}, u32[]{:S(2)}) collective-permute-start(bf16[20,32,128]{2,1,0:T(8,128)(2,1)S(1)} %collective-permute-done.17.refs_10_), channel_id=1, source_target_pairs={{0,1},{1,0},{2,3},{3,2},{4,5},{5,4},{6,7},{7,6},{8,9},{9,8},{10,11... | collective-permute-start | bytes 491528 | tf_op jit(solution)/shard_map/ppermute | solution.py:90
  40.4 16.2 %collective-permute-start.5 = (bf16[20,32,128]{2,1,0:T(8,128)(2,1)S(1)}, bf16[20,32,128]{2,1,0:T(8,128)(2,1)S(1)}, u32[]{:S(2)}, u32[]{:S(2)}) collective-permute-start(bf16[20,32,128]{2,1,0:T(8,128)(2,1)S(1)} %get-tuple-element.37.refs_0_), channel_id=1, source_target_pairs={{0,4},{1,5},{2,6},{3,7},{4,0},{5,1},{6,2},{7,3},{8,12},{9,13},{10,... | collective-permute-start | bytes 491528 | tf_op jit(solution)/shard_map/ppermute | solution.py:90
  40.4 16.2 %collective-permute-start.6 = (bf16[20,32,128]{2,1,0:T(8,128)(2,1)S(1)}, bf16[20,32,128]{2,1,0:T(8,128)(2,1)S(1)}, u32[]{:S(2)}, u32[]{:S(2)}) collective-permute-start(bf16[20,32,128]{2,1,0:T(8,128)(2,1)S(1)} %get-tuple-element.37.refs_0_), channel_id=1, source_target_pairs={{0,12},{1,13},{2,14},{3,15},{4,8},{5,9},{6,10},{7,11},{8,4},{9,5},... | collective-permute-start | bytes 491528 | tf_op jit(solution)/shard_map/ppermute | solution.py:90
  41.8 14.8 %collective-permute-start.7 = (bf16[20,32,128]{2,1,0:T(8,128)(2,1)S(1)}, bf16[20,32,128]{2,1,0:T(8,128)(2,1)S(1)}, u32[]{:S(2)}, u32[]{:S(2)}) collective-permute-start(bf16[20,32,128]{2,1,0:T(8,128)(2,1)S(1)} %get-tuple-element.37.refs_0_), channel_id=1, source_target_pairs={{0,2},{1,3},{2,0},{3,1},{4,6},{5,7},{6,4},{7,5},{8,10},{9,11},{10,... | collective-permute-start | bytes 491528 | tf_op jit(solution)/shard_map/ppermute | solution.py:90
  42.8 15.8 %collective-permute-start.22 = (bf16[20,32,128]{2,1,0:T(8,128)(2,1)S(1)}, bf16[20,32,128]{2,1,0:T(8,128)(2,1)S(1)}, u32[]{:S(2)}, u32[]{:S(2)}) collective-permute-start(bf16[20,32,128]{2,1,0:T(8,128)(2,1)S(1)} %get-tuple-element.37.refs_0_), channel_id=1, source_target_pairs={{0,8},{1,9},{2,10},{3,11},{4,12},{5,13},{6,14},{7,15},{8,0},{9,1},... | collective-permute-start | bytes 491528 | tf_op jit(solution)/shard_map/ppermute | solution.py:90
  44.4 26.5 %collective-permute-start.24 = (bf16[20,32,128]{2,1,0:T(8,128)(2,1)S(1)}, bf16[20,32,128]{2,1,0:T(8,128)(2,1)S(1)}, u32[]{:S(2)}, u32[]{:S(2)}) collective-permute-start(bf16[20,32,128]{2,1,0:T(8,128)(2,1)S(1)} %get-tuple-element.37.refs_0_), channel_id=1, source_target_pairs={{0,1},{1,0},{2,3},{3,2},{4,5},{5,4},{6,7},{7,6},{8,9},{9,8},{10,11... | collective-permute-start | bytes 491528 | tf_op jit(solution)/shard_map/ppermute | solution.py:90
  56.6 13.7 %collective-permute-start.21 = (bf16[2,20,32,128]{3,2,1,0:T(8,128)(2,1)S(1)}, bf16[2,20,32,128]{3,2,1,0:T(8,128)(2,1)S(1)}, u32[]{:S(2)}, u32[]{:S(2)}) collective-permute-start(bf16[2,20,32,128]{3,2,1,0:T(8,128)(2,1)S(1)} %pad_maximum_fusion.refs_2_), channel_id=1, source_target_pairs={{0,2},{1,3},{2,0},{3,1},{4,6},{5,7},{6,4},{7,5},{8,10},{9,11},{10,... | collective-permute-start | bytes 983048 | tf_op jit(solution)/shard_map/ppermute | solution.py:90
  58.2 14.2 %collective-permute-start.26 = (bf16[2,20,32,128]{3,2,1,0:T(8,128)(2,1)S(1)}, bf16[2,20,32,128]{3,2,1,0:T(8,128)(2,1)S(1)}, u32[]{:S(2)}, u32[]{:S(2)}) collective-permute-start(bf16[2,20,32,128]{3,2,1,0:T(8,128)(2,1)S(1)} %pad_maximum_fusion.refs_2_), channel_id=1, source_target_pairs={{0,1},{1,0},{2,3},{3,2},{4,5},{5,4},{6,7},{7,6},{8,9},{9,8},{10,11... | collective-permute-start | bytes 983048 | tf_op jit(solution)/shard_map/ppermute | solution.py:90
  58.6 11.7 %collective-permute-start.23 = (bf16[20,32,128]{2,1,0:T(8,128)(2,1)S(1)}, bf16[20,32,128]{2,1,0:T(8,128)(2,1)S(1)}, u32[]{:S(2)}, u32[]{:S(2)}) collective-permute-start(bf16[20,32,128]{2,1,0:T(8,128)(2,1)S(1)} %collective-permute-done.22.refs_4_), channel_id=1, source_target_pairs={{0,2},{1,3},{2,0},{3,1},{4,6},{5,7},{6,4},{7,5},{8,10},{9,11},{10,... | collective-permute-start | bytes 491528 | tf_op jit(solution)/shard_map/ppermute | solution.py:90
  70.3 2.3 %collective-permute-start.27 = (bf16[2,20,32,128]{3,2,1,0:T(8,128)(2,1)S(1)}, bf16[2,20,32,128]{3,2,1,0:T(8,128)(2,1)S(1)}, u32[]{:S(2)}, u32[]{:S(2)}) collective-permute-start(bf16[2,20,32,128]{3,2,1,0:T(8,128)(2,1)S(1)} %collective-permute-done.21.refs_3_), channel_id=1, source_target_pairs={{0,1},{1,0},{2,3},{3,2},{4,5},{5,4},{6,7},{7,6},{8,9},{9,8},{10,11... | collective-permute-start | bytes 983048 | tf_op jit(solution)/shard_map/ppermute | solution.py:90
  90.8 4.6 %collective-permute-start.31 = (bf16[32,8,128]{2,1,0:T(8,128)(2,1)S(1)}, bf16[32,8,128]{2,1,0:T(8,128)(2,1)S(1)}, u32[]{:S(2)}, u32[]{:S(2)}) collective-permute-start(bf16[32,8,128]{2,1,0:T(8,128)(2,1)S(1)} %pad_maximum_fusion.1), channel_id=1, source_target_pairs={{0,16},{16,0},{1,17},{17,1},{2,18},{18,2},{3,19},{19,3},{4,20},{20... | collective-permute-start | bytes 196616 | tf_op jit(solution)/shard_map/ppermute | solution.py:421
  91.7 3.6 %collective-permute-start.30 = (f32[4,256]{1,0:T(4,128)S(1)}, f32[4,256]{1,0:T(4,128)S(1)}, u32[]{:S(2)}, u32[]{:S(2)}) collective-permute-start(f32[4,256]{1,0:T(4,128)S(1)} %get-tuple-element.53), channel_id=1, source_target_pairs={{0,16},{16,0},{1,17},{17,1},{2,18},{18,2},{3,19},{19,3},{4,20},{20... | collective-permute-start | bytes 12296 | tf_op jit(solution)/shard_map/ppermute | solution.py:420
  96.5 3.6 %collective-permute-start.33 = (f32[4,256]{1,0:T(4,128)S(1)}, f32[4,256]{1,0:T(4,128)S(1)}, u32[]{:S(2)}, u32[]{:S(2)}) collective-permute-start(f32[4,256]{1,0:T(4,128)S(1)} %add.16), channel_id=1, source_target_pairs={{0,2},{1,3},{2,0},{3,1},{4,6},{5,7},{6,4},{7,5},{8,10},{9,11},{10,... | collective-permute-start | bytes 12296 | tf_op jit(solution)/shard_map/ppermute | solution.py:90
  100.1 3.6 %collective-permute-start.34 = (f32[4,256]{1,0:T(4,128)S(1)}, f32[4,256]{1,0:T(4,128)S(1)}, u32[]{:S(2)}, u32[]{:S(2)}) collective-permute-start(f32[4,256]{1,0:T(4,128)S(1)} %add.17), channel_id=1, source_target_pairs={{0,4},{1,5},{2,6},{3,7},{4,0},{5,1},{6,2},{7,3},{8,12},{9,13},{10,... | collective-permute-start | bytes 12296 | tf_op jit(solution)/shard_map/ppermute | solution.py:90
  103.8 4.5 %collective-permute-start.35 = (f32[4,256]{1,0:T(4,128)S(1)}, f32[4,256]{1,0:T(4,128)S(1)}, u32[]{:S(2)}, u32[]{:S(2)}) collective-permute-start(f32[4,256]{1,0:T(4,128)S(1)} %add.18), channel_id=1, source_target_pairs={{0,8},{1,9},{2,10},{3,11},{4,12},{5,13},{6,14},{7,15},{8,0},{9,1},... | collective-permute-start | bytes 12296 | tf_op jit(solution)/shard_map/ppermute | solution.py:90
  (12 other events, 14.0 us)

commit v13 on v12

--- a/solution.py
+++ b/solution.py
@@ -354,7 +354,7 @@
         in_specs=[SMEM, VMEM, VMEM, VMEM, VMEM],
         out_specs=[VMEM] * WAVES,
         out_shape=[jax.ShapeDtypeStruct((UNIT, 32, TILE_A), BF)] * WAVES,
-        compiler_params=pltpu.CompilerParams(vmem_limit_bytes=8 * 1024 * 1024),
+        compiler_params=pltpu.CompilerParams(vmem_limit_bytes=60 * 1024 * 1024),
     )(after(info, ids_other), train_inputs, train_other, query_inputs, input_basis)
 
     out_other = lax.ppermute(after(train_outgrads, packed[0]), "parts", SWAP)

time: 109 us -> 111 us (1.018)
  Pallas kernels: 42.2 us -> 43.5 us
    pallas_call x1, Pallas kernels: 0.81 us -> 2.11 us  [paired_body(): pl.pallas_call(pack_kernel, in_specs=[SMEM, VMEM, VMEM, VMEM, VMEM], out_...]
    unnamed x16 -> x20, local copies, waits for them, and re-layouts: 7.53 us -> 7.67 us
  transfers between devices with their start and end apart: 36 -> 36, of which waited for: 15 -> 14; matrix products, arithmetic and copies ran while one was open for 1% -> 2% of each run, Pallas kernels for 21% -> 21%
where the time goes in v13:
time: 111 us; the launch traced here: 110 us
  Pallas kernels  43.5 us (39%)
  starting transfers between devices  30.9 us (28%)
  waiting for transfers between devices  24.6 us (22%)
  local copies, waits for them, and re-layouts  8.21 us (7%)
  other arithmetic  2.17 us (2%)
    pallas_call x3, Pallas kernels, score_tiles(): pl.pallas_call(kernel, in_specs=[SMEM] + [VMEM] * len(arrays) + [VMEM, VM...  38.2 us
    ppermute x31, starting transfers between devices, hop(): return lax.ppermute(value, 'query', [(i, i ^ bits) for i in range(NQ)])  25.1 us
    ppermute x31, waiting for transfers between devices, hop(): return lax.ppermute(value, 'query', [(i, i ^ bits) for i in range(NQ)])  19.4 us
    unnamed x20, local copies, waits for them, and re-layouts  7.67 us
    ppermute x1, starting transfers between devices, paired_body(): train_other = lax.ppermute(train_inputs, 'parts', SWAP)  3 us
    ppermute x1, waiting for transfers between devices, paired_body(): ids_other = lax.ppermute(after(ids, mine), 'parts', SWAP)  2.83 us
    ppermute x1, waiting for transfers between devices, paired_body(): total = keep + lax.ppermute(give, 'parts', SWAP)  2.28 us
  transfers between devices with their start and end apart: 36, of which 14 were waited for; matrix products, arithmetic and copies ran while one was open for 2% of the time, Pallas kernels for 21%

profile of v13, /device:TPU:0, one launch (start us, length us, event | category | flops | bytes accessed | tf_op | source)
XLA Modules:
  0.0 110.2 jit_solution(6826662009231594717)
XLA Ops:
  0.6 3.0 %collective-permute-start.1 = (bf16[2,8,4096]{2,1,0:T(8,128)(2,1)}, bf16[2,8,4096]{2,1,0:T(8,128)(2,1)S(1)}, u32[]{:S(2)}, u32[]{:S(2)}) collective-permute-start(bf16[2,8,4096]{2,1,0:T(8,128)(2,1)} %own.2), channel_id=1, source_target_pairs={{0,16},{16,0},{1,17},{17,1},{2,18},{18,2},{3,19},{19,3},{4,20},{20... | collective-permute-start | bytes 393224 | tf_op jit(solution)/shard_map/ppermute | solution.py:341
  5.6 2.8 %collective-permute-done.ids_other = s32[1,128]{1,0:T(1,128)S(1)} collective-permute-done((s32[1,128]{1,0:T(1,128)}, s32[1,128]{1,0:T(1,128)S(1)}, u32[]{:S(2)}, u32[]{:S(2)}) %collective-permute-start) | collective-permute-done | bytes 544 | tf_op jit(solution)/shard_map/ppermute | solution.py:348
  9.1 2.1 %shard_map.104 = (bf16[20,32,128]{2,1,0:T(8,128)(2,1)}, bf16[20,32,128]{2,1,0:T(8,128)(2,1)}) custom-call(s32[66]{0:T(128)} %pad_add_fusion.info.info_ref, bf16[2,8,4096]{2,1,0:T(8,128)(2,1)} %own.2, bf16[2,8,4096]{2,1,0:T(8,128)(2,1)} %copy-done.9, bf16[2,16,4096]{2,1,0:T(8,128)(2,1)} %query.2, bf16[4,128,128]{2,1,0:T(8,128)(2,1)} %basis.1), custom_call_target="tpu_custom_call" | custom-call | tf_op jit(solution)/shard_map/pallas_call | solution.py:352
  11.9 1.6 %collective-permute-start.2 = (bf16[20,32,128]{2,1,0:T(8,128)(2,1)}, bf16[20,32,128]{2,1,0:T(8,128)(2,1)S(1)}, u32[]{:S(2)}, u32[]{:S(2)}) collective-permute-start(bf16[20,32,128]{2,1,0:T(8,128)(2,1)} %get-tuple-element.36.refs_0_), channel_id=1, source_target_pairs={{0,4},{1,5},{2,6},{3,7},{4,0},{5,1},{6,2},{7,3},{8,12},{9,13},{10,... | collective-permute-start | bytes 491528 | tf_op jit(solution)/shard_map/ppermute | solution.py:90
  13.5 2.5 %collective-permute-start.3 = (bf16[20,32,128]{2,1,0:T(8,128)(2,1)}, bf16[20,32,128]{2,1,0:T(8,128)(2,1)S(1)}, u32[]{:S(2)}, u32[]{:S(2)}) collective-permute-start(bf16[20,32,128]{2,1,0:T(8,128)(2,1)} %get-tuple-element.36.refs_0_), channel_id=1, source_target_pairs={{0,12},{1,13},{2,14},{3,15},{4,8},{5,9},{6,10},{7,11},{8,4},{9,5},... | collective-permute-start | bytes 491528 | tf_op jit(solution)/shard_map/ppermute | solution.py:90
  16.0 1.5 %collective-permute-start.9 = (bf16[20,32,128]{2,1,0:T(8,128)(2,1)}, bf16[20,32,128]{2,1,0:T(8,128)(2,1)S(1)}, u32[]{:S(2)}, u32[]{:S(2)}) collective-permute-start(bf16[20,32,128]{2,1,0:T(8,128)(2,1)} %get-tuple-element.36.refs_0_), channel_id=1, source_target_pairs={{0,2},{1,3},{2,0},{3,1},{4,6},{5,7},{6,4},{7,5},{8,10},{9,11},{10,... | collective-permute-start | bytes 491528 | tf_op jit(solution)/shard_map/ppermute | solution.py:90
  17.5 1.0 copy-done
  18.5 1.1 %copy-done.2 = bf16[2,256,768]{2,1,0:T(8,128)(2,1)S(1)} copy-done((bf16[2,256,768]{2,1,0:T(8,128)(2,1)S(1)}, bf16[2,256,768]{2,1,0:T(8,128)(2,1)}, u32[]{:S(2)}) %copy-start.2) | copy-done | bytes 786456
  20.2 2.3 %collective-permute-done.3.refs_12_ = bf16[20,32,128]{2,1,0:T(8,128)(2,1)S(1)} collective-permute-done((bf16[20,32,128]{2,1,0:T(8,128)(2,1)}, bf16[20,32,128]{2,1,0:T(8,128)(2,1)S(1)}, u32[]{:S(2)}, u32[]{:S(2)}) %collective-permute-start.3) | collective-permute-done | bytes 163872 | tf_op jit(solution)/shard_map/ppermute | solution.py:90
  22.5 3.6 %collective-permute-start.4 = (bf16[20,32,128]{2,1,0:T(8,128)(2,1)}, bf16[20,32,128]{2,1,0:T(8,128)(2,1)S(1)}, u32[]{:S(2)}, u32[]{:S(2)}) collective-permute-start(bf16[20,32,128]{2,1,0:T(8,128)(2,1)} %get-tuple-element.36.refs_0_), channel_id=1, source_target_pairs={{0,8},{1,9},{2,10},{3,11},{4,12},{5,13},{6,14},{7,15},{8,0},{9,1},... | collective-permute-start | bytes 491528 | tf_op jit(solution)/shard_map/ppermute | solution.py:90
  26.1 1.5 %collective-permute-start.12 = (bf16[20,32,128]{2,1,0:T(8,128)(2,1)S(1)}, bf16[20,32,128]{2,1,0:T(8,128)(2,1)S(1)}, u32[]{:S(2)}, u32[]{:S(2)}) collective-permute-start(bf16[20,32,128]{2,1,0:T(8,128)(2,1)S(1)} %collective-permute-done.2.refs_4_), channel_id=1, source_target_pairs={{0,2},{1,3},{2,0},{3,1},{4,6},{5,7},{6,4},{7,5},{8,10},{9,11},{10,... | collective-permute-start | bytes 491528 | tf_op jit(solution)/shard_map/ppermute | solution.py:90
  28.6 2.1 %collective-permute-done.4.refs_8_ = bf16[20,32,128]{2,1,0:T(8,128)(2,1)S(1)} collective-permute-done((bf16[20,32,128]{2,1,0:T(8,128)(2,1)}, bf16[20,32,128]{2,1,0:T(8,128)(2,1)S(1)}, u32[]{:S(2)}, u32[]{:S(2)}) %collective-permute-start.4) | collective-permute-done | bytes 163872 | tf_op jit(solution)/shard_map/ppermute | solution.py:90
  31.4 1.8 %collective-permute-done.16.refs_14_ = bf16[20,32,128]{2,1,0:T(8,128)(2,1)S(1)} collective-permute-done((bf16[20,32,128]{2,1,0:T(8,128)(2,1)S(1)}, bf16[20,32,128]{2,1,0:T(8,128)(2,1)S(1)}, u32[]{:S(2)}, u32[]{:S(2)}) %collective-permute-start.16) | collective-permute-done | bytes 163872 | tf_op jit(solution)/shard_map/ppermute | solution.py:90
  33.1 1.5 %collective-permute-start.17 = (bf16[20,32,128]{2,1,0:T(8,128)(2,1)S(1)}, bf16[20,32,128]{2,1,0:T(8,128)(2,1)S(1)}, u32[]{:S(2)}, u32[]{:S(2)}) collective-permute-start(bf16[20,32,128]{2,1,0:T(8,128)(2,1)S(1)} %collective-permute-done.4.refs_8_), channel_id=1, source_target_pairs={{0,2},{1,3},{2,0},{3,1},{4,6},{5,7},{6,4},{7,5},{8,10},{9,11},{10,... | collective-permute-start | bytes 491528 | tf_op jit(solution)/shard_map/ppermute | solution.py:90
  35.2 1.0 copy-done.1
  36.2 1.0 copy-done.4
  40.1 1.5 %collective-permute-start.6 = (bf16[20,32,128]{2,1,0:T(8,128)(2,1)}, bf16[20,32,128]{2,1,0:T(8,128)(2,1)S(1)}, u32[]{:S(2)}, u32[]{:S(2)}) collective-permute-start(bf16[20,32,128]{2,1,0:T(8,128)(2,1)} %get-tuple-element.37.refs_0_), channel_id=1, source_target_pairs={{0,12},{1,13},{2,14},{3,15},{4,8},{5,9},{6,10},{7,11},{8,4},{9,5},... | collective-permute-start | bytes 491528 | tf_op jit(solution)/shard_map/ppermute | solution.py:90
  42.1 2.0 %collective-permute-start.22 = (bf16[20,32,128]{2,1,0:T(8,128)(2,1)}, bf16[20,32,128]{2,1,0:T(8,128)(2,1)S(1)}, u32[]{:S(2)}, u32[]{:S(2)}) collective-permute-start(bf16[20,32,128]{2,1,0:T(8,128)(2,1)} %get-tuple-element.37.refs_0_), channel_id=1, source_target_pairs={{0,8},{1,9},{2,10},{3,11},{4,12},{5,13},{6,14},{7,15},{8,0},{9,1},... | collective-permute-start | bytes 491528 | tf_op jit(solution)/shard_map/ppermute | solution.py:90
  45.8 12.2 %shard_map.107 = (f32[8,256]{1,0:T(8,128)S(1)}, bf16[10,8,128]{2,1,0:T(8,128)(2,1)S(1)}, bf16[10,8,128]{2,1,0:T(8,128)(2,1)S(1)}) custom-call(s32[66]{0:T(128)S(1)} %copy-done.6, bf16[20,32,128]{2,1,0:T(8,128)(2,1)S(1)} %copy-done.3, bf16[20,32,128]{2,1,0:T(8,128)(2,1)S(1)} %collective-permute-done.8.refs_1_, ...), custom_call_target="tpu_custom_call" | custom-call | flops 100000000 | bytes 5000000 | tf_op jit(solution)/shard_map/pallas_call | solution.py:283
  58.0 1.6 %collective-permute-start.21 = (bf16[2,20,32,128]{3,2,1,0:T(8,128)(2,1)S(1)}, bf16[2,20,32,128]{3,2,1,0:T(8,128)(2,1)S(1)}, u32[]{:S(2)}, u32[]{:S(2)}) collective-permute-start(bf16[2,20,32,128]{3,2,1,0:T(8,128)(2,1)S(1)} %pad_maximum_fusion.refs_2_), channel_id=1, source_target_pairs={{0,2},{1,3},{2,0},{3,1},{4,6},{5,7},{6,4},{7,5},{8,10},{9,11},{10,... | collective-permute-start | bytes 983048 | tf_op jit(solution)/shard_map/ppermute | solution.py:90
  60.3 8.0 %shard_map.108 = (f32[8,256]{1,0:T(8,128)S(1)}, bf16[6,8,128]{2,1,0:T(8,128)(2,1)S(1)}, bf16[6,8,128]{2,1,0:T(8,128)(2,1)S(1)}) custom-call(s32[66]{0:T(128)S(1)} %copy-done.6, bf16[20,32,128]{2,1,0:T(8,128)(2,1)S(1)} %copy-done.3, bf16[20,32,128]{2,1,0:T(8,128)(2,1)S(1)} %collective-permute-done.8.refs_1_, ...), custom_call_target="tpu_custom_call" | custom-call | flops 6000000000 | bytes 3000000 | tf_op jit(solution)/shard_map/pallas_call | solution.py:283
  68.3 3.4 %collective-permute-done.23.refs_5_ = bf16[20,32,128]{2,1,0:T(8,128)(2,1)S(1)} collective-permute-done((bf16[20,32,128]{2,1,0:T(8,128)(2,1)S(1)}, bf16[20,32,128]{2,1,0:T(8,128)(2,1)S(1)}, u32[]{:S(2)}, u32[]{:S(2)}) %collective-permute-start.23) | collective-permute-done | bytes 163872 | tf_op jit(solution)/shard_map/ppermute | solution.py:90
  74.0 18.1 %shard_map.109 = (f32[4,256]{1,0:T(4,128)S(1)}, f32[4,256]{1,0:T(4,128)S(1)}, bf16[16,8,128]{2,1,0:T(8,128)(2,1)S(1)}, bf16[16,8,128]{2,1,0:T(8,128)(2,1)S(1)}) custom-call(s32[66]{0:T(128)S(1)} %copy-done.6, bf16[20,32,128]{2,1,0:T(8,128)(2,1)S(1)} %copy-done.8, bf16[20,32,128]{2,1,0:T(8,128)(2,1)S(1)} %collective-permute-done.7.refs_1_, ...), custom_call_target="tpu_custom_call" | custom-call | flops 16000000000 | bytes 8000000 | tf_op jit(solution)/shard_map/pallas_call | solution.py:283
  92.2 2.0 %collective-permute-start.30 = (f32[4,256]{1,0:T(4,128)S(1)}, f32[4,256]{1,0:T(4,128)S(1)}, u32[]{:S(2)}, u32[]{:S(2)}) collective-permute-start(f32[4,256]{1,0:T(4,128)S(1)} %get-tuple-element.53), channel_id=1, source_target_pairs={{0,16},{16,0},{1,17},{17,1},{2,18},{18,2},{3,19},{19,3},{4,20},{20... | collective-permute-start | bytes 12296 | tf_op jit(solution)/shard_map/ppermute | solution.py:420
  94.2 2.3 %collective-permute-done.30 = f32[4,256]{1,0:T(4,128)S(1)} collective-permute-done((f32[4,256]{1,0:T(4,128)S(1)}, f32[4,256]{1,0:T(4,128)S(1)}, u32[]{:S(2)}, u32[]{:S(2)}) %collective-permute-start.30) | collective-permute-done | bytes 4128 | tf_op jit(solution)/shard_map/ppermute | solution.py:420
  96.5 1.2 %collective-permute-done.32 = f32[4,256]{1,0:T(4,128)S(1)} collective-permute-done((f32[4,256]{1,0:T(4,128)S(1)}, f32[4,256]{1,0:T(4,128)S(1)}, u32[]{:S(2)}, u32[]{:S(2)}) %collective-permute-start.32) | collective-permute-done | bytes 4128 | tf_op jit(solution)/shard_map/ppermute | solution.py:90
  97.7 1.5 %collective-permute-start.33 = (f32[4,256]{1,0:T(4,128)S(1)}, f32[4,256]{1,0:T(4,128)S(1)}, u32[]{:S(2)}, u32[]{:S(2)}) collective-permute-start(f32[4,256]{1,0:T(4,128)S(1)} %add.16), channel_id=1, source_target_pairs={{0,2},{1,3},{2,0},{3,1},{4,6},{5,7},{6,4},{7,5},{8,10},{9,11},{10,... | collective-permute-start | bytes 12296 | tf_op jit(solution)/shard_map/ppermute | solution.py:90
  99.2 2.1 %collective-permute-done.33 = f32[4,256]{1,0:T(4,128)S(1)} collective-permute-done((f32[4,256]{1,0:T(4,128)S(1)}, f32[4,256]{1,0:T(4,128)S(1)}, u32[]{:S(2)}, u32[]{:S(2)}) %collective-permute-start.33) | collective-permute-done | bytes 4128 | tf_op jit(solution)/shard_map/ppermute | solution.py:90
  101.3 1.0 collective-permute-start.34
  102.3 1.6 %shard_map.110 = bf16[2,8,4096]{2,1,0:T(8,128)(2,1)} custom-call(s32[66]{0:T(128)S(1)} %copy-done.6, bf16[10,8,128]{2,1,0:T(8,128)(2,1)S(1)} %get-tuple-element.58.kept_a, bf16[6,8,128]{2,1,0:T(8,128)(2,1)S(1)} %get-tuple-element.59.kept_b, bf16[16,8,128]{2,1,0:T(8,128)(2,1)S(1)} %get-tuple-element.60.kept_c, ...), custom_call_target="tpu_custom_call" | custom-call | tf_op jit(solution)/shard_map/pallas_call | solution.py:423
  103.9 1.0 collective-permute-done.34
  105.8 3.6 %collective-permute-done.35 = f32[4,256]{1,0:T(4,128)S(1)} collective-permute-done((f32[4,256]{1,0:T(4,128)S(1)}, f32[4,256]{1,0:T(4,128)S(1)}, u32[]{:S(2)}, u32[]{:S(2)}) %collective-permute-start.35) | collective-permute-done | bytes 4128 | tf_op jit(solution)/shard_map/ppermute | solution.py:90
  (85 shorter events, 16.0 us)
Async XLA Ops:
  0.6 7.8 %collective-permute-start.1 = (bf16[2,8,4096]{2,1,0:T(8,128)(2,1)}, bf16[2,8,4096]{2,1,0:T(8,128)(2,1)S(1)}, u32[]{:S(2)}, u32[]{:S(2)}) collective-permute-start(bf16[2,8,4096]{2,1,0:T(8,128)(2,1)} %own.2), channel_id=1, source_target_pairs={{0,16},{16,0},{1,17},{17,1},{2,18},{18,2},{3,19},{19,3},{4,20},{20... | collective-permute-start | bytes 393224 | tf_op jit(solution)/shard_map/ppermute | solution.py:341
  4.7 3.7 %collective-permute-start = (s32[1,128]{1,0:T(1,128)}, s32[1,128]{1,0:T(1,128)S(1)}, u32[]{:S(2)}, u32[]{:S(2)}) collective-permute-start(s32[1,128]{1,0:T(1,128)} %bitcast.7), channel_id=1, source_target_pairs={{0,16},{16,0},{1,17},{17,1},{2,18},{18,2},{3,19},{19,3},{4,20},{20... | collective-permute-start | bytes 1544 | tf_op jit(solution)/shard_map/ppermute | solution.py:348
  11.2 16.4 %collective-permute-start.15 = (bf16[2,128,768]{2,1,0:T(8,128)(2,1)}, bf16[2,128,768]{2,1,0:T(8,128)(2,1)S(1)}, u32[]{:S(2)}, u32[]{:S(2)}) collective-permute-start(bf16[2,128,768]{2,1,0:T(8,128)(2,1)} %own.3), channel_id=1, source_target_pairs={{0,16},{16,0},{1,17},{17,1},{2,18},{18,2},{3,19},{19,3},{4,20},{20... | collective-permute-start | bytes 1179656 | tf_op jit(solution)/shard_map/ppermute | solution.py:360
  11.9 8.3 %collective-permute-start.2 = (bf16[20,32,128]{2,1,0:T(8,128)(2,1)}, bf16[20,32,128]{2,1,0:T(8,128)(2,1)S(1)}, u32[]{:S(2)}, u32[]{:S(2)}) collective-permute-start(bf16[20,32,128]{2,1,0:T(8,128)(2,1)} %get-tuple-element.36.refs_0_), channel_id=1, source_target_pairs={{0,4},{1,5},{2,6},{3,7},{4,0},{5,1},{6,2},{7,3},{8,12},{9,13},{10,... | collective-permute-start | bytes 491528 | tf_op jit(solution)/shard_map/ppermute | solution.py:90
  13.5 9.0 %collective-permute-start.3 = (bf16[20,32,128]{2,1,0:T(8,128)(2,1)}, bf16[20,32,128]{2,1,0:T(8,128)(2,1)S(1)}, u32[]{:S(2)}, u32[]{:S(2)}) collective-permute-start(bf16[20,32,128]{2,1,0:T(8,128)(2,1)} %get-tuple-element.36.refs_0_), channel_id=1, source_target_pairs={{0,12},{1,13},{2,14},{3,15},{4,8},{5,9},{6,10},{7,11},{8,4},{9,5},... | collective-permute-start | bytes 491528 | tf_op jit(solution)/shard_map/ppermute | solution.py:90
  16.0 12.1 %collective-permute-start.9 = (bf16[20,32,128]{2,1,0:T(8,128)(2,1)}, bf16[20,32,128]{2,1,0:T(8,128)(2,1)S(1)}, u32[]{:S(2)}, u32[]{:S(2)}) collective-permute-start(bf16[20,32,128]{2,1,0:T(8,128)(2,1)} %get-tuple-element.36.refs_0_), channel_id=1, source_target_pairs={{0,2},{1,3},{2,0},{3,1},{4,6},{5,7},{6,4},{7,5},{8,10},{9,11},{10,... | collective-permute-start | bytes 491528 | tf_op jit(solution)/shard_map/ppermute | solution.py:90
  22.5 8.2 %collective-permute-start.4 = (bf16[20,32,128]{2,1,0:T(8,128)(2,1)}, bf16[20,32,128]{2,1,0:T(8,128)(2,1)S(1)}, u32[]{:S(2)}, u32[]{:S(2)}) collective-permute-start(bf16[20,32,128]{2,1,0:T(8,128)(2,1)} %get-tuple-element.36.refs_0_), channel_id=1, source_target_pairs={{0,8},{1,9},{2,10},{3,11},{4,12},{5,13},{6,14},{7,15},{8,0},{9,1},... | collective-permute-start | bytes 491528 | tf_op jit(solution)/shard_map/ppermute | solution.py:90
  26.1 5.3 %collective-permute-start.12 = (bf16[20,32,128]{2,1,0:T(8,128)(2,1)S(1)}, bf16[20,32,128]{2,1,0:T(8,128)(2,1)S(1)}, u32[]{:S(2)}, u32[]{:S(2)}) collective-permute-start(bf16[20,32,128]{2,1,0:T(8,128)(2,1)S(1)} %collective-permute-done.2.refs_4_), channel_id=1, source_target_pairs={{0,2},{1,3},{2,0},{3,1},{4,6},{5,7},{6,4},{7,5},{8,10},{9,11},{10,... | collective-permute-start | bytes 491528 | tf_op jit(solution)/shard_map/ppermute | solution.py:90
  27.6 5.6 %collective-permute-start.16 = (bf16[20,32,128]{2,1,0:T(8,128)(2,1)S(1)}, bf16[20,32,128]{2,1,0:T(8,128)(2,1)S(1)}, u32[]{:S(2)}, u32[]{:S(2)}) collective-permute-start(bf16[20,32,128]{2,1,0:T(8,128)(2,1)S(1)} %collective-permute-done.3.refs_12_), channel_id=1, source_target_pairs={{0,2},{1,3},{2,0},{3,1},{4,6},{5,7},{6,4},{7,5},{8,10},{9,11},{10,... | collective-permute-start | bytes 491528 | tf_op jit(solution)/shard_map/ppermute | solution.py:90
  28.1 6.6 %collective-permute-start.8 = (bf16[20,32,128]{2,1,0:T(8,128)(2,1)}, bf16[20,32,128]{2,1,0:T(8,128)(2,1)S(1)}, u32[]{:S(2)}, u32[]{:S(2)}) collective-permute-start(bf16[20,32,128]{2,1,0:T(8,128)(2,1)} %get-tuple-element.36.refs_0_), channel_id=1, source_target_pairs={{0,1},{1,0},{2,3},{3,2},{4,5},{5,4},{6,7},{7,6},{8,9},{9,8},{10,11... | collective-permute-start | bytes 491528 | tf_op jit(solution)/shard_map/ppermute | solution.py:90
  28.1 7.1 %collective-permute-start.11 = (bf16[20,32,128]{2,1,0:T(8,128)(2,1)S(1)}, bf16[20,32,128]{2,1,0:T(8,128)(2,1)S(1)}, u32[]{:S(2)}, u32[]{:S(2)}) collective-permute-start(bf16[20,32,128]{2,1,0:T(8,128)(2,1)S(1)} %collective-permute-done.2.refs_4_), channel_id=1, source_target_pairs={{0,1},{1,0},{2,3},{3,2},{4,5},{5,4},{6,7},{7,6},{8,9},{9,8},{10,11... | collective-permute-start | bytes 491528 | tf_op jit(solution)/shard_map/ppermute | solution.py:90
  30.7 8.8 %collective-permute-start.19 = (bf16[20,32,128]{2,1,0:T(8,128)(2,1)S(1)}, bf16[20,32,128]{2,1,0:T(8,128)(2,1)S(1)}, u32[]{:S(2)}, u32[]{:S(2)}) collective-permute-start(bf16[20,32,128]{2,1,0:T(8,128)(2,1)S(1)} %collective-permute-done.3.refs_12_), channel_id=1, source_target_pairs={{0,1},{1,0},{2,3},{3,2},{4,5},{5,4},{6,7},{7,6},{8,9},{9,8},{10,11... | collective-permute-start | bytes 491528 | tf_op jit(solution)/shard_map/ppermute | solution.py:90
  33.1 6.9 %collective-permute-start.17 = (bf16[20,32,128]{2,1,0:T(8,128)(2,1)S(1)}, bf16[20,32,128]{2,1,0:T(8,128)(2,1)S(1)}, u32[]{:S(2)}, u32[]{:S(2)}) collective-permute-start(bf16[20,32,128]{2,1,0:T(8,128)(2,1)S(1)} %collective-permute-done.4.refs_8_), channel_id=1, source_target_pairs={{0,2},{1,3},{2,0},{3,1},{4,6},{5,7},{6,4},{7,5},{8,10},{9,11},{10,... | collective-permute-start | bytes 491528 | tf_op jit(solution)/shard_map/ppermute | solution.py:90
  34.7 5.5 %collective-permute-start.10 = (bf16[20,32,128]{2,1,0:T(8,128)(2,1)S(1)}, bf16[20,32,128]{2,1,0:T(8,128)(2,1)S(1)}, u32[]{:S(2)}, u32[]{:S(2)}) collective-permute-start(bf16[20,32,128]{2,1,0:T(8,128)(2,1)S(1)} %collective-permute-done.9.refs_2_), channel_id=1, source_target_pairs={{0,1},{1,0},{2,3},{3,2},{4,5},{5,4},{6,7},{7,6},{8,9},{9,8},{10,11... | collective-permute-start | bytes 491528 | tf_op jit(solution)/shard_map/ppermute | solution.py:90
  34.7 5.5 %collective-permute-start.14 = (bf16[20,32,128]{2,1,0:T(8,128)(2,1)S(1)}, bf16[20,32,128]{2,1,0:T(8,128)(2,1)S(1)}, u32[]{:S(2)}, u32[]{:S(2)}) collective-permute-start(bf16[20,32,128]{2,1,0:T(8,128)(2,1)S(1)} %collective-permute-done.4.refs_8_), channel_id=1, source_target_pairs={{0,1},{1,0},{2,3},{3,2},{4,5},{5,4},{6,7},{7,6},{8,9},{9,8},{10,11... | collective-permute-start | bytes 491528 | tf_op jit(solution)/shard_map/ppermute | solution.py:90
  35.2 6.4 %collective-permute-start.13 = (bf16[20,32,128]{2,1,0:T(8,128)(2,1)S(1)}, bf16[20,32,128]{2,1,0:T(8,128)(2,1)S(1)}, u32[]{:S(2)}, u32[]{:S(2)}) collective-permute-start(bf16[20,32,128]{2,1,0:T(8,128)(2,1)S(1)} %collective-permute-done.12.refs_6_), channel_id=1, source_target_pairs={{0,1},{1,0},{2,3},{3,2},{4,5},{5,4},{6,7},{7,6},{8,9},{9,8},{10,11... | collective-permute-start | bytes 491528 | tf_op jit(solution)/shard_map/ppermute | solution.py:90
  39.5 2.6 %collective-permute-start.20 = (bf16[20,32,128]{2,1,0:T(8,128)(2,1)S(1)}, bf16[20,32,128]{2,1,0:T(8,128)(2,1)S(1)}, u32[]{:S(2)}, u32[]{:S(2)}) collective-permute-start(bf16[20,32,128]{2,1,0:T(8,128)(2,1)S(1)} %collective-permute-done.16.refs_14_), channel_id=1, source_target_pairs={{0,1},{1,0},{2,3},{3,2},{4,5},{5,4},{6,7},{7,6},{8,9},{9,8},{10,11... | collective-permute-start | bytes 491528 | tf_op jit(solution)/shard_map/ppermute | solution.py:90
  40.1 4.1 %collective-permute-start.18 = (bf16[20,32,128]{2,1,0:T(8,128)(2,1)S(1)}, bf16[20,32,128]{2,1,0:T(8,128)(2,1)S(1)}, u32[]{:S(2)}, u32[]{:S(2)}) collective-permute-start(bf16[20,32,128]{2,1,0:T(8,128)(2,1)S(1)} %collective-permute-done.17.refs_10_), channel_id=1, source_target_pairs={{0,1},{1,0},{2,3},{3,2},{4,5},{5,4},{6,7},{7,6},{8,9},{9,8},{10,11... | collective-permute-start | bytes 491528 | tf_op jit(solution)/shard_map/ppermute | solution.py:90
  40.1 17.8 %collective-permute-start.5 = (bf16[20,32,128]{2,1,0:T(8,128)(2,1)}, bf16[20,32,128]{2,1,0:T(8,128)(2,1)S(1)}, u32[]{:S(2)}, u32[]{:S(2)}) collective-permute-start(bf16[20,32,128]{2,1,0:T(8,128)(2,1)} %get-tuple-element.37.refs_0_), channel_id=1, source_target_pairs={{0,4},{1,5},{2,6},{3,7},{4,0},{5,1},{6,2},{7,3},{8,12},{9,13},{10,... | collective-permute-start | bytes 491528 | tf_op jit(solution)/shard_map/ppermute | solution.py:90
  40.1 17.8 %collective-permute-start.6 = (bf16[20,32,128]{2,1,0:T(8,128)(2,1)}, bf16[20,32,128]{2,1,0:T(8,128)(2,1)S(1)}, u32[]{:S(2)}, u32[]{:S(2)}) collective-permute-start(bf16[20,32,128]{2,1,0:T(8,128)(2,1)} %get-tuple-element.37.refs_0_), channel_id=1, source_target_pairs={{0,12},{1,13},{2,14},{3,15},{4,8},{5,9},{6,10},{7,11},{8,4},{9,5},... | collective-permute-start | bytes 491528 | tf_op jit(solution)/shard_map/ppermute | solution.py:90
  41.6 16.4 %collective-permute-start.7 = (bf16[20,32,128]{2,1,0:T(8,128)(2,1)}, bf16[20,32,128]{2,1,0:T(8,128)(2,1)S(1)}, u32[]{:S(2)}, u32[]{:S(2)}) collective-permute-start(bf16[20,32,128]{2,1,0:T(8,128)(2,1)} %get-tuple-element.37.refs_0_), channel_id=1, source_target_pairs={{0,2},{1,3},{2,0},{3,1},{4,6},{5,7},{6,4},{7,5},{8,10},{9,11},{10,... | collective-permute-start | bytes 491528 | tf_op jit(solution)/shard_map/ppermute | solution.py:90
  42.1 17.7 %collective-permute-start.22 = (bf16[20,32,128]{2,1,0:T(8,128)(2,1)}, bf16[20,32,128]{2,1,0:T(8,128)(2,1)S(1)}, u32[]{:S(2)}, u32[]{:S(2)}) collective-permute-start(bf16[20,32,128]{2,1,0:T(8,128)(2,1)} %get-tuple-element.37.refs_0_), channel_id=1, source_target_pairs={{0,8},{1,9},{2,10},{3,11},{4,12},{5,13},{6,14},{7,15},{8,0},{9,1},... | collective-permute-start | bytes 491528 | tf_op jit(solution)/shard_map/ppermute | solution.py:90
  44.2 28.1 %collective-permute-start.24 = (bf16[20,32,128]{2,1,0:T(8,128)(2,1)}, bf16[20,32,128]{2,1,0:T(8,128)(2,1)S(1)}, u32[]{:S(2)}, u32[]{:S(2)}) collective-permute-start(bf16[20,32,128]{2,1,0:T(8,128)(2,1)} %get-tuple-element.37.refs_0_), channel_id=1, source_target_pairs={{0,1},{1,0},{2,3},{3,2},{4,5},{5,4},{6,7},{7,6},{8,9},{9,8},{10,11... | collective-permute-start | bytes 491528 | tf_op jit(solution)/shard_map/ppermute | solution.py:90
  58.0 13.7 %collective-permute-start.21 = (bf16[2,20,32,128]{3,2,1,0:T(8,128)(2,1)S(1)}, bf16[2,20,32,128]{3,2,1,0:T(8,128)(2,1)S(1)}, u32[]{:S(2)}, u32[]{:S(2)}) collective-permute-start(bf16[2,20,32,128]{3,2,1,0:T(8,128)(2,1)S(1)} %pad_maximum_fusion.refs_2_), channel_id=1, source_target_pairs={{0,2},{1,3},{2,0},{3,1},{4,6},{5,7},{6,4},{7,5},{8,10},{9,11},{10,... | collective-permute-start | bytes 983048 | tf_op jit(solution)/shard_map/ppermute | solution.py:90
  59.6 14.2 %collective-permute-start.26 = (bf16[2,20,32,128]{3,2,1,0:T(8,128)(2,1)S(1)}, bf16[2,20,32,128]{3,2,1,0:T(8,128)(2,1)S(1)}, u32[]{:S(2)}, u32[]{:S(2)}) collective-permute-start(bf16[2,20,32,128]{3,2,1,0:T(8,128)(2,1)S(1)} %pad_maximum_fusion.refs_2_), channel_id=1, source_target_pairs={{0,1},{1,0},{2,3},{3,2},{4,5},{5,4},{6,7},{7,6},{8,9},{9,8},{10,11... | collective-permute-start | bytes 983048 | tf_op jit(solution)/shard_map/ppermute | solution.py:90
  59.8 11.9 %collective-permute-start.23 = (bf16[20,32,128]{2,1,0:T(8,128)(2,1)S(1)}, bf16[20,32,128]{2,1,0:T(8,128)(2,1)S(1)}, u32[]{:S(2)}, u32[]{:S(2)}) collective-permute-start(bf16[20,32,128]{2,1,0:T(8,128)(2,1)S(1)} %collective-permute-done.22.refs_4_), channel_id=1, source_target_pairs={{0,2},{1,3},{2,0},{3,1},{4,6},{5,7},{6,4},{7,5},{8,10},{9,11},{10,... | collective-permute-start | bytes 491528 | tf_op jit(solution)/shard_map/ppermute | solution.py:90
  71.7 2.3 %collective-permute-start.27 = (bf16[2,20,32,128]{3,2,1,0:T(8,128)(2,1)S(1)}, bf16[2,20,32,128]{3,2,1,0:T(8,128)(2,1)S(1)}, u32[]{:S(2)}, u32[]{:S(2)}) collective-permute-start(bf16[2,20,32,128]{3,2,1,0:T(8,128)(2,1)S(1)} %collective-permute-done.21.refs_3_), channel_id=1, source_target_pairs={{0,1},{1,0},{2,3},{3,2},{4,5},{5,4},{6,7},{7,6},{8,9},{9,8},{10,11... | collective-permute-start | bytes 983048 | tf_op jit(solution)/shard_map/ppermute | solution.py:90
  92.1 4.4 %collective-permute-start.31 = (bf16[32,8,128]{2,1,0:T(8,128)(2,1)S(1)}, bf16[32,8,128]{2,1,0:T(8,128)(2,1)S(1)}, u32[]{:S(2)}, u32[]{:S(2)}) collective-permute-start(bf16[32,8,128]{2,1,0:T(8,128)(2,1)S(1)} %pad_maximum_fusion.1), channel_id=1, source_target_pairs={{0,16},{16,0},{1,17},{17,1},{2,18},{18,2},{3,19},{19,3},{4,20},{20... | collective-permute-start | bytes 196616 | tf_op jit(solution)/shard_map/ppermute | solution.py:421
  92.2 4.3 %collective-permute-start.30 = (f32[4,256]{1,0:T(4,128)S(1)}, f32[4,256]{1,0:T(4,128)S(1)}, u32[]{:S(2)}, u32[]{:S(2)}) collective-permute-start(f32[4,256]{1,0:T(4,128)S(1)} %get-tuple-element.53), channel_id=1, source_target_pairs={{0,16},{16,0},{1,17},{17,1},{2,18},{18,2},{3,19},{19,3},{4,20},{20... | collective-permute-start | bytes 12296 | tf_op jit(solution)/shard_map/ppermute | solution.py:420
  97.7 3.6 %collective-permute-start.33 = (f32[4,256]{1,0:T(4,128)S(1)}, f32[4,256]{1,0:T(4,128)S(1)}, u32[]{:S(2)}, u32[]{:S(2)}) collective-permute-start(f32[4,256]{1,0:T(4,128)S(1)} %add.16), channel_id=1, source_target_pairs={{0,2},{1,3},{2,0},{3,1},{4,6},{5,7},{6,4},{7,5},{8,10},{9,11},{10,... | collective-permute-start | bytes 12296 | tf_op jit(solution)/shard_map/ppermute | solution.py:90
  101.3 3.6 %collective-permute-start.34 = (f32[4,256]{1,0:T(4,128)S(1)}, f32[4,256]{1,0:T(4,128)S(1)}, u32[]{:S(2)}, u32[]{:S(2)}) collective-permute-start(f32[4,256]{1,0:T(4,128)S(1)} %add.17), channel_id=1, source_target_pairs={{0,4},{1,5},{2,6},{3,7},{4,0},{5,1},{6,2},{7,3},{8,12},{9,13},{10,... | collective-permute-start | bytes 12296 | tf_op jit(solution)/shard_map/ppermute | solution.py:90
  104.9 4.5 %collective-permute-start.35 = (f32[4,256]{1,0:T(4,128)S(1)}, f32[4,256]{1,0:T(4,128)S(1)}, u32[]{:S(2)}, u32[]{:S(2)}) collective-permute-start(f32[4,256]{1,0:T(4,128)S(1)} %add.18), channel_id=1, source_target_pairs={{0,8},{1,9},{2,10},{3,11},{4,12},{5,13},{6,14},{7,15},{8,0},{9,1},... | collective-permute-start | bytes 12296 | tf_op jit(solution)/shard_map/ppermute | solution.py:90
  (14 other events, 42.4 us)
